TPU v7x, 32 devices: a whole 2x2x4 slice. The times are simulated.
32 devices in a mesh: blk: 32 (over z, y, x, core).
Axes of the slice: x: 2, y: 2, z: 4, core: 2. Of those that a mesh axis runs over, the one named last changes fastest.
Arguments:
- features: bfloat16 [12288, 512], P('blk'), may hold values from -6 to 6
- tile_list: int32 [32, 8, 7, 2], P('blk'), may hold values from 0 to 2, as said below
- tile_count: int32 [32, 8], P('blk'), may hold values from 1 to 7, as said below
- tile_values: bfloat16 [32, 8, 7, 128, 128], P('blk'), may hold values from -0.1875 to 0.1875
- weight: bfloat16 [512, 512], replicated, may hold values from -0.25 to 0.25
- bias: float32 [512], replicated, may hold values from -3 to 3
- grad_out: bfloat16 [12288, 512], P('blk'), may hold values from -6 to 6
Outputs:
- output: bfloat16 [12288, 512], P('blk')
- grad_features: bfloat16 [12288, 512], P('blk')
- grad_weight: float32 [512, 512], replicated
- grad_bias: float32 [512], replicated
Inputs may be any that keep to these rules, and one draw needn't show every extreme that they name: `tile_list`: entries are tile indices within a row block; within one row block and neighbour the 7 (row tile, column tile) pairs are distinct. `tile_count`: loads differ from row block to row block; 7 is reached in every draw.
All inputs are finite; a program needn't handle non-finite values.
Results may differ from a plain program's by a relative error of at most 0.0075.
Values may be sent and summed in bfloat16 or wider, within the bound.
No kernel may reach another device: no remote copies, remote signals or barrier semaphores. Data moves between devices by JAX's collectives and lax.ppermute only.
A program may use at most 64 MiB of HBM per device.

v0:
```python
import jax
import jax.numpy as jnp
from jax import lax
from jax.sharding import PartitionSpec as P


def passed_along(value, axis, steps):
    count = lax.axis_size(axis)
    pairs = [(source, (source + steps) % count) for source in range(count)]
    return lax.ppermute(value, axis, pairs)


def padded_terms(values_now, take_index, put_index, count_now, blocks, flipped):
    picked = jnp.take(blocks, take_index, axis=0)
    if flipped:
        product = jnp.einsum("kba,kbh->kah", values_now, picked, preferred_element_type=jnp.float32)
    else:
        product = jnp.einsum("kab,kbh->kah", values_now, picked, preferred_element_type=jnp.float32)
    live = (jnp.arange(values_now.shape[0], dtype=jnp.int32) < count_now).astype(jnp.float32)
    select = (put_index[:, None] == jnp.arange(blocks.shape[0], dtype=jnp.int32)[None, :]).astype(
        jnp.float32
    )
    select = select * live[:, None]
    return jnp.einsum("kr,kah->rah", select, product, precision=lax.Precision.HIGHEST)


def tile_terms(values_now, take_index, put_index, count_now, blocks, flipped):
    return padded_terms(values_now, take_index, put_index, count_now, blocks, flipped)


def local(features, tile_list, tile_count, tile_values, weight, bias, grad_out):
    window = lax.axis_size("blk") // 4
    midway = window // 2
    rows_dev, hidden = features.shape
    tile = tile_values.shape[-1]
    tile_rows = rows_dev // tile
    local_values = tile_values[0]
    tile_pairs = tile_list[0]
    tile_counts = tile_count[0]
    blocks = features.reshape(tile_rows, tile, hidden)

    def gather_term(j, source):
        return tile_terms(
            local_values[j], tile_pairs[j, :, 1], tile_pairs[j, :, 0], tile_counts[j], source, False
        )

    current = passed_along(blocks, "blk", midway)
    summed = gather_term(0, current)

    def one_side(j, state):
        moving, total = state
        moving = passed_along(moving, "blk", -1)
        return (moving, total + gather_term(j, moving))

    current, summed = lax.fori_loop(1, window, one_side, (current, summed))
    agg = summed.reshape(rows_dev, hidden).astype(jnp.bfloat16)
    pre = jnp.dot(agg, weight, preferred_element_type=jnp.float32) + bias
    sig = jax.nn.sigmoid(pre)
    output = (pre * sig).astype(jnp.bfloat16)
    grad_pre = (grad_out.astype(jnp.float32) * sig * (1.0 + pre * (1.0 - sig))).astype(jnp.bfloat16)
    local_weight = jnp.einsum("rh,rk->hk", agg, grad_pre, preferred_element_type=jnp.float32)
    local_bias = jnp.sum(grad_pre.astype(jnp.float32), axis=0)
    grad_weight, grad_bias = lax.psum((local_weight, local_bias), "blk")
    grad_agg = jnp.einsum("rk,hk->rh", grad_pre, weight, preferred_element_type=jnp.float32).astype(
        jnp.bfloat16
    )
    grad_blocks = grad_agg.reshape(tile_rows, tile, hidden)

    def scatter_term(j):
        return tile_terms(
            local_values[j],
            tile_pairs[j, :, 0],
            tile_pairs[j, :, 1],
            tile_counts[j],
            grad_blocks,
            True,
        )

    def carry_chain(t, carried):
        carried = passed_along(carried, "blk", 1)
        return carried + scatter_term(window - 1 - t)

    carried = lax.fori_loop(1, window, carry_chain, scatter_term(window - 1))
    gathered = passed_along(carried.astype(jnp.bfloat16), "blk", -midway).astype(carried.dtype)
    grad_features = gathered.reshape(rows_dev, hidden).astype(jnp.bfloat16)
    return (output, grad_features, grad_weight, grad_bias)


def solution(mesh):
    placed = (
        P("blk", None),
        P("blk", None, None, None),
        P("blk", None),
        P("blk", None, None, None, None),
        P(),
        P(),
        P("blk", None),
    )
    return jax.shard_map(
        local,
        mesh=mesh,
        in_specs=placed,
        out_specs=(P("blk", None), P("blk", None), P(), P()),
        check_vma=False,
    )
```

profile of v0, /device:TPU:0, one launch (start us, length us, event | category | flops | bytes accessed | tf_op | source)
XLA Modules:
  0.0 359.3 jit_solution(11663487937135137215)
XLA Ops:
  15.2 3.8 %copy.24 = bf16[1,8,7,128,128]{3,4,2,1,0:T(8,128)(2,1)} copy(bf16[1,8,7,128,128]{4,3,2,1,0:T(8,128)(2,1)} %param.16) | data formatting | bytes 3670016 | tf_op args[3]
  31.0 112.1 %while.32 = (s32[]{:T(128)}, bf16[3,128,512]{2,1,0:T(8,128)(2,1)S(1)}, f32[3,128,512]{2,0,1:T(4,128)S(1)}, s32[8,7,2]{1,2,0:T(2,128)S(1)}, s32[8]{0:T(128)S(1)},...) while((s32[]{:T(128)}, bf16[3,128,512]{2,1,0:T(8,128)(2,1)S(1)}, ...), condition=%wide.region_1.3_spmd, body=%wide.region_0.0_spmd.sunk | while | flops 134612080 | bytes 10588629 | solution.py:55
  33.6 4.0 %collective-permute-done = bf16[3,128,512]{2,1,0:T(8,128)(2,1)S(1)} collective-permute-done((bf16[3,128,512]{2,1,0:T(8,128)(2,1)S(1)}, bf16[3,128,512]{2,1,0:T(8,128)(2,1)S(1)}, u32[]{:S(2)}, u32[]{:S(2)}) %collective-permute-start) | collective-permute-done | bytes 393248 | tf_op jit(solution)/shard_map/while/body/eval_jaxpr/ppermute | solution.py:10
  43.3 5.6 %collective-permute-start = (bf16[3,128,512]{2,1,0:T(8,128)(2,1)S(1)}, bf16[3,128,512]{2,1,0:T(8,128)(2,1)S(1)}, u32[]{:S(2)}, u32[]{:S(2)}) collective-permute-start(bf16[3,128,512]{2,1,0:T(8,128)(2,1)S(1)} %get-tuple-element.480), channel_id=1, source_target_pairs={{0,31},{1,0},{2,1},{3,2},{4,3},{5,4},{6,5},{7,6},{8,7},{9,8},{10,9... | collective-permute-start | bytes 1179656 | tf_op jit(solution)/shard_map/while/body/eval_jaxpr/ppermute | solution.py:10
  50.2 4.0 %collective-permute-done = bf16[3,128,512]{2,1,0:T(8,128)(2,1)S(1)} collective-permute-done((bf16[3,128,512]{2,1,0:T(8,128)(2,1)S(1)}, bf16[3,128,512]{2,1,0:T(8,128)(2,1)S(1)}, u32[]{:S(2)}, u32[]{:S(2)}) %collective-permute-start) | collective-permute-done | bytes 393248 | tf_op jit(solution)/shard_map/while/body/eval_jaxpr/ppermute | solution.py:10
  60.0 5.6 %collective-permute-start = (bf16[3,128,512]{2,1,0:T(8,128)(2,1)S(1)}, bf16[3,128,512]{2,1,0:T(8,128)(2,1)S(1)}, u32[]{:S(2)}, u32[]{:S(2)}) collective-permute-start(bf16[3,128,512]{2,1,0:T(8,128)(2,1)S(1)} %get-tuple-element.480), channel_id=1, source_target_pairs={{0,31},{1,0},{2,1},{3,2},{4,3},{5,4},{6,5},{7,6},{8,7},{9,8},{10,9... | collective-permute-start | bytes 1179656 | tf_op jit(solution)/shard_map/while/body/eval_jaxpr/ppermute | solution.py:10
  66.8 4.0 %collective-permute-done = bf16[3,128,512]{2,1,0:T(8,128)(2,1)S(1)} collective-permute-done((bf16[3,128,512]{2,1,0:T(8,128)(2,1)S(1)}, bf16[3,128,512]{2,1,0:T(8,128)(2,1)S(1)}, u32[]{:S(2)}, u32[]{:S(2)}) %collective-permute-start) | collective-permute-done | bytes 393248 | tf_op jit(solution)/shard_map/while/body/eval_jaxpr/ppermute | solution.py:10
  76.6 5.6 %collective-permute-start = (bf16[3,128,512]{2,1,0:T(8,128)(2,1)S(1)}, bf16[3,128,512]{2,1,0:T(8,128)(2,1)S(1)}, u32[]{:S(2)}, u32[]{:S(2)}) collective-permute-start(bf16[3,128,512]{2,1,0:T(8,128)(2,1)S(1)} %get-tuple-element.480), channel_id=1, source_target_pairs={{0,31},{1,0},{2,1},{3,2},{4,3},{5,4},{6,5},{7,6},{8,7},{9,8},{10,9... | collective-permute-start | bytes 1179656 | tf_op jit(solution)/shard_map/while/body/eval_jaxpr/ppermute | solution.py:10
  83.4 4.0 %collective-permute-done = bf16[3,128,512]{2,1,0:T(8,128)(2,1)S(1)} collective-permute-done((bf16[3,128,512]{2,1,0:T(8,128)(2,1)S(1)}, bf16[3,128,512]{2,1,0:T(8,128)(2,1)S(1)}, u32[]{:S(2)}, u32[]{:S(2)}) %collective-permute-start) | collective-permute-done | bytes 393248 | tf_op jit(solution)/shard_map/while/body/eval_jaxpr/ppermute | solution.py:10
  93.2 5.6 %collective-permute-start = (bf16[3,128,512]{2,1,0:T(8,128)(2,1)S(1)}, bf16[3,128,512]{2,1,0:T(8,128)(2,1)S(1)}, u32[]{:S(2)}, u32[]{:S(2)}) collective-permute-start(bf16[3,128,512]{2,1,0:T(8,128)(2,1)S(1)} %get-tuple-element.480), channel_id=1, source_target_pairs={{0,31},{1,0},{2,1},{3,2},{4,3},{5,4},{6,5},{7,6},{8,7},{9,8},{10,9... | collective-permute-start | bytes 1179656 | tf_op jit(solution)/shard_map/while/body/eval_jaxpr/ppermute | solution.py:10
  100.0 4.0 %collective-permute-done = bf16[3,128,512]{2,1,0:T(8,128)(2,1)S(1)} collective-permute-done((bf16[3,128,512]{2,1,0:T(8,128)(2,1)S(1)}, bf16[3,128,512]{2,1,0:T(8,128)(2,1)S(1)}, u32[]{:S(2)}, u32[]{:S(2)}) %collective-permute-start) | collective-permute-done | bytes 393248 | tf_op jit(solution)/shard_map/while/body/eval_jaxpr/ppermute | solution.py:10
  109.8 5.6 %collective-permute-start = (bf16[3,128,512]{2,1,0:T(8,128)(2,1)S(1)}, bf16[3,128,512]{2,1,0:T(8,128)(2,1)S(1)}, u32[]{:S(2)}, u32[]{:S(2)}) collective-permute-start(bf16[3,128,512]{2,1,0:T(8,128)(2,1)S(1)} %get-tuple-element.480), channel_id=1, source_target_pairs={{0,31},{1,0},{2,1},{3,2},{4,3},{5,4},{6,5},{7,6},{8,7},{9,8},{10,9... | collective-permute-start | bytes 1179656 | tf_op jit(solution)/shard_map/while/body/eval_jaxpr/ppermute | solution.py:10
  116.7 4.0 %collective-permute-done = bf16[3,128,512]{2,1,0:T(8,128)(2,1)S(1)} collective-permute-done((bf16[3,128,512]{2,1,0:T(8,128)(2,1)S(1)}, bf16[3,128,512]{2,1,0:T(8,128)(2,1)S(1)}, u32[]{:S(2)}, u32[]{:S(2)}) %collective-permute-start) | collective-permute-done | bytes 393248 | tf_op jit(solution)/shard_map/while/body/eval_jaxpr/ppermute | solution.py:10
  126.4 5.6 %collective-permute-start = (bf16[3,128,512]{2,1,0:T(8,128)(2,1)S(1)}, bf16[3,128,512]{2,1,0:T(8,128)(2,1)S(1)}, u32[]{:S(2)}, u32[]{:S(2)}) collective-permute-start(bf16[3,128,512]{2,1,0:T(8,128)(2,1)S(1)} %get-tuple-element.480), channel_id=1, source_target_pairs={{0,31},{1,0},{2,1},{3,2},{4,3},{5,4},{6,5},{7,6},{8,7},{9,8},{10,9... | collective-permute-start | bytes 1179656 | tf_op jit(solution)/shard_map/while/body/eval_jaxpr/ppermute | solution.py:10
  133.3 4.0 %collective-permute-done = bf16[3,128,512]{2,1,0:T(8,128)(2,1)S(1)} collective-permute-done((bf16[3,128,512]{2,1,0:T(8,128)(2,1)S(1)}, bf16[3,128,512]{2,1,0:T(8,128)(2,1)S(1)}, u32[]{:S(2)}, u32[]{:S(2)}) %collective-permute-start) | collective-permute-done | bytes 393248 | tf_op jit(solution)/shard_map/while/body/eval_jaxpr/ppermute | solution.py:10
  139.3 3.7 %fusion.98 = f32[3,128,512]{2,0,1:T(4,128)S(1)} fusion(f32[3,128,512]{2,0,1:T(4,128)S(1)} %get-tuple-element.481, f32[7,128,512]{2,1,0:T(8,128)S(1)} %fusion.96, f32[7]{0:T(128)S(1)} %compare_convert_fusion.6, s32[7]{0:T(128)S(1)} %fusion.97), kind=kOutput, calls=%fused_computation.6.clone.1 | convolution fusion | flops 16711722 | bytes 3407928 | tf_op jit(solution)/shard_map/while/body/eval_jaxpr/kr,kah->rah/dot_general | solution.py:24
  156.3 152.5 %while.33 = (s32[]{:T(128)}, f32[3,128,512]{2,0,1:T(4,128)S(1)}, s32[8,7,2]{1,2,0:T(2,128)S(1)}, s32[8]{0:T(128)S(1)}, bf16[8,7,128,128]{2,3,1,0:T(8,128)(2,1)},...) while((s32[]{:T(128)}, f32[3,128,512]{2,0,1:T(4,128)S(1)}, ...), condition=%wide.region_3.5_spmd, body=%wide.region_2.4_spmd.sunk | while | flops 134612080 | bytes 12947937 | solution.py:83
  160.9 14.7 %collective-permute-done.1 = f32[3,128,512]{2,1,0:T(8,128)} collective-permute-done((f32[3,128,512]{2,1,0:T(8,128)}, f32[3,128,512]{2,1,0:T(8,128)}, u32[]{:S(2)}, u32[]{:S(2)}) %collective-permute-start.1) | collective-permute-done | bytes 786464 | tf_op jit(solution)/shard_map/while/body/eval_jaxpr/ppermute | solution.py:10
  175.7 4.4 %copy_add_fusion.2 = f32[3,128,512]{2,0,1:T(4,128)S(1)} fusion(f32[3,128,512]{2,1,0:T(8,128)} %collective-permute-done.1, f32[7,128,512]{2,1,0:T(8,128)S(1)} %fusion.103, f32[7]{0:T(128)S(1)} %compare_convert_fusion.7, s32[7]{0:T(128)S(1)} %fusion.104), kind=kOutput, calls=%fused_computation.32.clone.1 | convolution fusion | flops 16711722 | bytes 3407928 | tf_op jit(solution)/shard_map/while/body/eval_jaxpr/kr,kah->rah/dot_general | solution.py:24
  184.5 12.4 %collective-permute-done.1 = f32[3,128,512]{2,1,0:T(8,128)} collective-permute-done((f32[3,128,512]{2,1,0:T(8,128)}, f32[3,128,512]{2,1,0:T(8,128)}, u32[]{:S(2)}, u32[]{:S(2)}) %collective-permute-start.1) | collective-permute-done | bytes 786464 | tf_op jit(solution)/shard_map/while/body/eval_jaxpr/ppermute | solution.py:10
  196.9 4.4 %copy_add_fusion.2 = f32[3,128,512]{2,0,1:T(4,128)S(1)} fusion(f32[3,128,512]{2,1,0:T(8,128)} %collective-permute-done.1, f32[7,128,512]{2,1,0:T(8,128)S(1)} %fusion.103, f32[7]{0:T(128)S(1)} %compare_convert_fusion.7, s32[7]{0:T(128)S(1)} %fusion.104), kind=kOutput, calls=%fused_computation.32.clone.1 | convolution fusion | flops 16711722 | bytes 3407928 | tf_op jit(solution)/shard_map/while/body/eval_jaxpr/kr,kah->rah/dot_general | solution.py:24
  205.7 12.3 %collective-permute-done.1 = f32[3,128,512]{2,1,0:T(8,128)} collective-permute-done((f32[3,128,512]{2,1,0:T(8,128)}, f32[3,128,512]{2,1,0:T(8,128)}, u32[]{:S(2)}, u32[]{:S(2)}) %collective-permute-start.1) | collective-permute-done | bytes 786464 | tf_op jit(solution)/shard_map/while/body/eval_jaxpr/ppermute | solution.py:10
  218.0 4.4 %copy_add_fusion.2 = f32[3,128,512]{2,0,1:T(4,128)S(1)} fusion(f32[3,128,512]{2,1,0:T(8,128)} %collective-permute-done.1, f32[7,128,512]{2,1,0:T(8,128)S(1)} %fusion.103, f32[7]{0:T(128)S(1)} %compare_convert_fusion.7, s32[7]{0:T(128)S(1)} %fusion.104), kind=kOutput, calls=%fused_computation.32.clone.1 | convolution fusion | flops 16711722 | bytes 3407928 | tf_op jit(solution)/shard_map/while/body/eval_jaxpr/kr,kah->rah/dot_general | solution.py:24
  226.8 12.3 %collective-permute-done.1 = f32[3,128,512]{2,1,0:T(8,128)} collective-permute-done((f32[3,128,512]{2,1,0:T(8,128)}, f32[3,128,512]{2,1,0:T(8,128)}, u32[]{:S(2)}, u32[]{:S(2)}) %collective-permute-start.1) | collective-permute-done | bytes 786464 | tf_op jit(solution)/shard_map/while/body/eval_jaxpr/ppermute | solution.py:10
  239.1 4.4 %copy_add_fusion.2 = f32[3,128,512]{2,0,1:T(4,128)S(1)} fusion(f32[3,128,512]{2,1,0:T(8,128)} %collective-permute-done.1, f32[7,128,512]{2,1,0:T(8,128)S(1)} %fusion.103, f32[7]{0:T(128)S(1)} %compare_convert_fusion.7, s32[7]{0:T(128)S(1)} %fusion.104), kind=kOutput, calls=%fused_computation.32.clone.1 | convolution fusion | flops 16711722 | bytes 3407928 | tf_op jit(solution)/shard_map/while/body/eval_jaxpr/kr,kah->rah/dot_general | solution.py:24
  247.9 12.8 %collective-permute-done.1 = f32[3,128,512]{2,1,0:T(8,128)} collective-permute-done((f32[3,128,512]{2,1,0:T(8,128)}, f32[3,128,512]{2,1,0:T(8,128)}, u32[]{:S(2)}, u32[]{:S(2)}) %collective-permute-start.1) | collective-permute-done | bytes 786464 | tf_op jit(solution)/shard_map/while/body/eval_jaxpr/ppermute | solution.py:10
  260.7 4.4 %copy_add_fusion.2 = f32[3,128,512]{2,0,1:T(4,128)S(1)} fusion(f32[3,128,512]{2,1,0:T(8,128)} %collective-permute-done.1, f32[7,128,512]{2,1,0:T(8,128)S(1)} %fusion.103, f32[7]{0:T(128)S(1)} %compare_convert_fusion.7, s32[7]{0:T(128)S(1)} %fusion.104), kind=kOutput, calls=%fused_computation.32.clone.1 | convolution fusion | flops 16711722 | bytes 3407928 | tf_op jit(solution)/shard_map/while/body/eval_jaxpr/kr,kah->rah/dot_general | solution.py:24
  269.5 13.6 %collective-permute-done.1 = f32[3,128,512]{2,1,0:T(8,128)} collective-permute-done((f32[3,128,512]{2,1,0:T(8,128)}, f32[3,128,512]{2,1,0:T(8,128)}, u32[]{:S(2)}, u32[]{:S(2)}) %collective-permute-start.1) | collective-permute-done | bytes 786464 | tf_op jit(solution)/shard_map/while/body/eval_jaxpr/ppermute | solution.py:10
  283.1 4.4 %copy_add_fusion.2 = f32[3,128,512]{2,0,1:T(4,128)S(1)} fusion(f32[3,128,512]{2,1,0:T(8,128)} %collective-permute-done.1, f32[7,128,512]{2,1,0:T(8,128)S(1)} %fusion.103, f32[7]{0:T(128)S(1)} %compare_convert_fusion.7, s32[7]{0:T(128)S(1)} %fusion.104), kind=kOutput, calls=%fused_computation.32.clone.1 | convolution fusion | flops 16711722 | bytes 3407928 | tf_op jit(solution)/shard_map/while/body/eval_jaxpr/kr,kah->rah/dot_general | solution.py:24
  291.9 12.5 %collective-permute-done.1 = f32[3,128,512]{2,1,0:T(8,128)} collective-permute-done((f32[3,128,512]{2,1,0:T(8,128)}, f32[3,128,512]{2,1,0:T(8,128)}, u32[]{:S(2)}, u32[]{:S(2)}) %collective-permute-start.1) | collective-permute-done | bytes 786464 | tf_op jit(solution)/shard_map/while/body/eval_jaxpr/ppermute | solution.py:10
  304.4 4.4 %copy_add_fusion.2 = f32[3,128,512]{2,0,1:T(4,128)S(1)} fusion(f32[3,128,512]{2,1,0:T(8,128)} %collective-permute-done.1, f32[7,128,512]{2,1,0:T(8,128)S(1)} %fusion.103, f32[7]{0:T(128)S(1)} %compare_convert_fusion.7, s32[7]{0:T(128)S(1)} %fusion.104), kind=kOutput, calls=%fused_computation.32.clone.1 | convolution fusion | flops 16711722 | bytes 3407928 | tf_op jit(solution)/shard_map/while/body/eval_jaxpr/kr,kah->rah/dot_general | solution.py:24
  309.1 40.3 %psum.15 = f32[512]{0:T(512)} all-reduce(f32[512]{0:T(512)S(1)} %get-tuple-element.383), channel_id=1, replica_groups=mesh['blk'=32] {'blk'}, use_global_device_ids=true, to_apply=%region_6.8 | all-reduce | flops 512 | bytes 4096 | tf_op jit(solution)/shard_map/psum | solution.py:63
  (169 shorter events, 113.8 us)
Async XLA Ops:
  7.2 136.1 %copy-start = (bf16[512,512]{1,0:T(8,128)(2,1)S(1)}, bf16[512,512]{1,0:T(8,128)(2,1)}, u32[]{:S(2)}) copy-start(bf16[512,512]{1,0:T(8,128)(2,1)} %param.17) | copy-start | bytes 1572868
  7.2 343.0 %all-reduce.2.cloned.1.call-start = ((), (), s32[]{:S(2)}) async-start(), calls=%async_computation | async-start | bytes 2097152 | tf_op jit(solution)/shard_map/psum | solution.py:63
  7.2 15.4 %collective-permute-start.2 = (bf16[3,128,512]{2,1,0:T(8,128)(2,1)}, bf16[3,128,512]{2,1,0:T(8,128)(2,1)S(1)}, u32[]{:S(2)}, u32[]{:S(2)}) collective-permute-start(bf16[3,128,512]{2,1,0:T(8,128)(2,1)} %bitcast.91), channel_id=1, source_target_pairs={{0,4},{1,5},{2,6},{3,7},{4,8},{5,9},{6,10},{7,11},{8,12},{9,13},{1... | collective-permute-start | bytes 1179656 | tf_op jit(solution)/shard_map/ppermute | solution.py:10
  22.6 0.7 copy-start.1
  27.5 3.5 copy-start.2
  27.5 3.5 copy-start.3
  31.0 112.4 %copy-start.4 = (f32[512]{0:T(512)S(1)}, f32[512]{0:T(512)}, u32[]{:S(2)}) copy-start(f32[512]{0:T(512)} %param.18) | copy-start | bytes 6148
  31.0 6.6 %collective-permute-start = (bf16[3,128,512]{2,1,0:T(8,128)(2,1)S(1)}, bf16[3,128,512]{2,1,0:T(8,128)(2,1)S(1)}, u32[]{:S(2)}, u32[]{:S(2)}) collective-permute-start(bf16[3,128,512]{2,1,0:T(8,128)(2,1)S(1)} %get-tuple-element.480), channel_id=1, source_target_pairs={{0,31},{1,0},{2,1},{3,2},{4,3},{5,4},{6,5},{7,6},{8,7},{9,8},{10,9... | collective-permute-start | bytes 1179656 | tf_op jit(solution)/shard_map/while/body/eval_jaxpr/ppermute | solution.py:10
  43.3 10.9 %collective-permute-start = (bf16[3,128,512]{2,1,0:T(8,128)(2,1)S(1)}, bf16[3,128,512]{2,1,0:T(8,128)(2,1)S(1)}, u32[]{:S(2)}, u32[]{:S(2)}) collective-permute-start(bf16[3,128,512]{2,1,0:T(8,128)(2,1)S(1)} %get-tuple-element.480), channel_id=1, source_target_pairs={{0,31},{1,0},{2,1},{3,2},{4,3},{5,4},{6,5},{7,6},{8,7},{9,8},{10,9... | collective-permute-start | bytes 1179656 | tf_op jit(solution)/shard_map/while/body/eval_jaxpr/ppermute | solution.py:10
  60.0 10.9 %collective-permute-start = (bf16[3,128,512]{2,1,0:T(8,128)(2,1)S(1)}, bf16[3,128,512]{2,1,0:T(8,128)(2,1)S(1)}, u32[]{:S(2)}, u32[]{:S(2)}) collective-permute-start(bf16[3,128,512]{2,1,0:T(8,128)(2,1)S(1)} %get-tuple-element.480), channel_id=1, source_target_pairs={{0,31},{1,0},{2,1},{3,2},{4,3},{5,4},{6,5},{7,6},{8,7},{9,8},{10,9... | collective-permute-start | bytes 1179656 | tf_op jit(solution)/shard_map/while/body/eval_jaxpr/ppermute | solution.py:10
  76.6 10.9 %collective-permute-start = (bf16[3,128,512]{2,1,0:T(8,128)(2,1)S(1)}, bf16[3,128,512]{2,1,0:T(8,128)(2,1)S(1)}, u32[]{:S(2)}, u32[]{:S(2)}) collective-permute-start(bf16[3,128,512]{2,1,0:T(8,128)(2,1)S(1)} %get-tuple-element.480), channel_id=1, source_target_pairs={{0,31},{1,0},{2,1},{3,2},{4,3},{5,4},{6,5},{7,6},{8,7},{9,8},{10,9... | collective-permute-start | bytes 1179656 | tf_op jit(solution)/shard_map/while/body/eval_jaxpr/ppermute | solution.py:10
  93.2 10.9 %collective-permute-start = (bf16[3,128,512]{2,1,0:T(8,128)(2,1)S(1)}, bf16[3,128,512]{2,1,0:T(8,128)(2,1)S(1)}, u32[]{:S(2)}, u32[]{:S(2)}) collective-permute-start(bf16[3,128,512]{2,1,0:T(8,128)(2,1)S(1)} %get-tuple-element.480), channel_id=1, source_target_pairs={{0,31},{1,0},{2,1},{3,2},{4,3},{5,4},{6,5},{7,6},{8,7},{9,8},{10,9... | collective-permute-start | bytes 1179656 | tf_op jit(solution)/shard_map/while/body/eval_jaxpr/ppermute | solution.py:10
  109.8 10.9 %collective-permute-start = (bf16[3,128,512]{2,1,0:T(8,128)(2,1)S(1)}, bf16[3,128,512]{2,1,0:T(8,128)(2,1)S(1)}, u32[]{:S(2)}, u32[]{:S(2)}) collective-permute-start(bf16[3,128,512]{2,1,0:T(8,128)(2,1)S(1)} %get-tuple-element.480), channel_id=1, source_target_pairs={{0,31},{1,0},{2,1},{3,2},{4,3},{5,4},{6,5},{7,6},{8,7},{9,8},{10,9... | collective-permute-start | bytes 1179656 | tf_op jit(solution)/shard_map/while/body/eval_jaxpr/ppermute | solution.py:10
  126.4 10.9 %collective-permute-start = (bf16[3,128,512]{2,1,0:T(8,128)(2,1)S(1)}, bf16[3,128,512]{2,1,0:T(8,128)(2,1)S(1)}, u32[]{:S(2)}, u32[]{:S(2)}) collective-permute-start(bf16[3,128,512]{2,1,0:T(8,128)(2,1)S(1)} %get-tuple-element.480), channel_id=1, source_target_pairs={{0,31},{1,0},{2,1},{3,2},{4,3},{5,4},{6,5},{7,6},{8,7},{9,8},{10,9... | collective-permute-start | bytes 1179656 | tf_op jit(solution)/shard_map/while/body/eval_jaxpr/ppermute | solution.py:10
  157.6 18.0 %collective-permute-start.1 = (f32[3,128,512]{2,1,0:T(8,128)}, f32[3,128,512]{2,1,0:T(8,128)}, u32[]{:S(2)}, u32[]{:S(2)}) collective-permute-start(f32[3,128,512]{2,1,0:T(8,128)} %copy.53), channel_id=1, source_target_pairs={{0,1},{1,2},{2,3},{3,4},{4,5},{5,6},{6,7},{7,8},{8,9},{9,10},{10,1... | collective-permute-start | bytes 2359304 | tf_op jit(solution)/shard_map/while/body/eval_jaxpr/ppermute | solution.py:10
  181.2 15.7 %collective-permute-start.1 = (f32[3,128,512]{2,1,0:T(8,128)}, f32[3,128,512]{2,1,0:T(8,128)}, u32[]{:S(2)}, u32[]{:S(2)}) collective-permute-start(f32[3,128,512]{2,1,0:T(8,128)} %copy.53), channel_id=1, source_target_pairs={{0,1},{1,2},{2,3},{3,4},{4,5},{5,6},{6,7},{7,8},{8,9},{9,10},{10,1... | collective-permute-start | bytes 2359304 | tf_op jit(solution)/shard_map/while/body/eval_jaxpr/ppermute | solution.py:10
  202.4 15.6 %collective-permute-start.1 = (f32[3,128,512]{2,1,0:T(8,128)}, f32[3,128,512]{2,1,0:T(8,128)}, u32[]{:S(2)}, u32[]{:S(2)}) collective-permute-start(f32[3,128,512]{2,1,0:T(8,128)} %copy.53), channel_id=1, source_target_pairs={{0,1},{1,2},{2,3},{3,4},{4,5},{5,6},{6,7},{7,8},{8,9},{9,10},{10,1... | collective-permute-start | bytes 2359304 | tf_op jit(solution)/shard_map/while/body/eval_jaxpr/ppermute | solution.py:10
  223.5 15.6 %collective-permute-start.1 = (f32[3,128,512]{2,1,0:T(8,128)}, f32[3,128,512]{2,1,0:T(8,128)}, u32[]{:S(2)}, u32[]{:S(2)}) collective-permute-start(f32[3,128,512]{2,1,0:T(8,128)} %copy.53), channel_id=1, source_target_pairs={{0,1},{1,2},{2,3},{3,4},{4,5},{5,6},{6,7},{7,8},{8,9},{9,10},{10,1... | collective-permute-start | bytes 2359304 | tf_op jit(solution)/shard_map/while/body/eval_jaxpr/ppermute | solution.py:10
  244.6 16.1 %collective-permute-start.1 = (f32[3,128,512]{2,1,0:T(8,128)}, f32[3,128,512]{2,1,0:T(8,128)}, u32[]{:S(2)}, u32[]{:S(2)}) collective-permute-start(f32[3,128,512]{2,1,0:T(8,128)} %copy.53), channel_id=1, source_target_pairs={{0,1},{1,2},{2,3},{3,4},{4,5},{5,6},{6,7},{7,8},{8,9},{9,10},{10,1... | collective-permute-start | bytes 2359304 | tf_op jit(solution)/shard_map/while/body/eval_jaxpr/ppermute | solution.py:10
  266.2 16.9 %collective-permute-start.1 = (f32[3,128,512]{2,1,0:T(8,128)}, f32[3,128,512]{2,1,0:T(8,128)}, u32[]{:S(2)}, u32[]{:S(2)}) collective-permute-start(f32[3,128,512]{2,1,0:T(8,128)} %copy.53), channel_id=1, source_target_pairs={{0,1},{1,2},{2,3},{3,4},{4,5},{5,6},{6,7},{7,8},{8,9},{9,10},{10,1... | collective-permute-start | bytes 2359304 | tf_op jit(solution)/shard_map/while/body/eval_jaxpr/ppermute | solution.py:10
  288.6 15.8 %collective-permute-start.1 = (f32[3,128,512]{2,1,0:T(8,128)}, f32[3,128,512]{2,1,0:T(8,128)}, u32[]{:S(2)}, u32[]{:S(2)}) collective-permute-start(f32[3,128,512]{2,1,0:T(8,128)} %copy.53), channel_id=1, source_target_pairs={{0,1},{1,2},{2,3},{3,4},{4,5},{5,6},{6,7},{7,8},{8,9},{9,10},{10,1... | collective-permute-start | bytes 2359304 | tf_op jit(solution)/shard_map/while/body/eval_jaxpr/ppermute | solution.py:10
  309.0 40.3 %collective-permute-start.3 = (bf16[3,128,512]{2,0,1:T(4,128)(2,1)S(1)}, bf16[3,128,512]{2,0,1:T(4,128)(2,1)S(1)}, u32[]{:S(2)}, u32[]{:S(2)}) collective-permute-start(bf16[3,128,512]{2,0,1:T(4,128)(2,1)S(1)} %convert_element_type.87), channel_id=1, source_target_pairs={{0,28},{1,29},{2,30},{3,31},{4,0},{5,1},{6,2},{7,3},{8,4},{9,5},{1... | collective-permute-start | bytes 1179656 | tf_op jit(solution)/shard_map/ppermute | solution.py:10
Sparse Core Ops, SparseCore 0:
  153.1 145.7 all-reduce.1
where the time goes:
time: 361 us; the launch traced here: 359 us
  waiting for transfers between devices  122 us (34%)
  matrix products  90.4 us (25%)
  local copies, waits for them, and re-layouts  42.4 us (12%)
  blocking collectives  40.3 us (11%)
  starting transfers between devices  37.8 us (10%)
  between operations  14.2 us (4%)
  other arithmetic  10.8 us (3%)
    ppermute x16, waiting for transfers between devices, passed_along(): return lax.ppermute(value, axis, pairs)  122 us
    dot_general x16, matrix products, padded_terms(): jnp.einsum('kr,kah->rah', select, product, precision=lax.Precision.HIGHEST)  63.3 us
    psum x1, blocking collectives, local(): grad_weight, grad_bias = lax.psum((local_weight, local_bias), 'blk')  40.3 us
    ppermute x16, starting transfers between devices, passed_along(): return lax.ppermute(value, axis, pairs)  37.7 us
    dot_general x8, matrix products, padded_terms(): jnp.einsum('kba,kbh->kah', values_now, picked, preferred_element_type=jnp...  11.6 us
    dot_general x8, matrix products, padded_terms(): jnp.einsum('kab,kbh->kah', values_now, picked, preferred_element_type=jnp...  11.3 us
    gather x16, local copies, waits for them, and re-layouts, padded_terms(): picked = jnp.take(blocks, take_index, axis=0)  10.6 us
    convert_element_type x16, other arithmetic, padded_terms(): (jnp.arange(values_now.shape[0], dtype=jnp.int32) < count_now).astype(jnp...  10.4 us
  transfers between devices with their start and end apart: 17, of which 15 were waited for; matrix products, arithmetic and copies ran while one was open for 23% of the time, Pallas kernels for 0%

commit v1 on v0

v1 whole, which is shorter than its diff:
```python
import jax
import jax.numpy as jnp
from jax import lax
from jax.experimental import pallas as pl
from jax.experimental.pallas import tpu as pltpu
from jax.sharding import PartitionSpec as P

VMEM_LIMIT = 56 * 1024 * 1024
BF16, F32 = jnp.bfloat16, jnp.float32
BIAS_ROWS = 16


def call(kernel, outs, ins, flops=0, smem=0):
    spec = lambda k: pl.BlockSpec(memory_space=pltpu.SMEM if k < smem else pltpu.VMEM)
    out_shape = [jax.ShapeDtypeStruct(s, d) for s, d in outs]
    moved = sum(a.size * a.dtype.itemsize for a in list(ins) + out_shape)
    return pl.pallas_call(
        kernel,
        out_shape=out_shape,
        in_specs=[spec(k) for k in range(len(ins))],
        out_specs=[pl.BlockSpec(memory_space=pltpu.VMEM)] * len(outs),
        compiler_params=pltpu.CompilerParams(vmem_limit_bytes=VMEM_LIMIT),
        cost_estimate=pl.CostEstimate(flops=flops, bytes_accessed=moved, transcendentals=0),
    )(*ins)


def dense_tiles(core, own_meta, mate_meta, own_values, mate_values, rows_dev, positions):
    window, slots, tile, _ = own_values.shape
    tile_rows = rows_dev // tile

    def kernel(core_ref, own_meta_ref, mate_meta_ref, own_ref, mate_ref, dense_ref, flipped_ref):
        dense_ref[...] = jnp.zeros_like(dense_ref)
        flipped_ref[...] = jnp.zeros_like(flipped_ref)

        def place(meta_ref, values_ref, first_j, shift, first_row):
            def slot(t, _):
                i, k = t // slots, t % slots
                j = 2 * i + first_j
                base = j * (2 * slots + 1)

                @pl.when(k < meta_ref[base + 2 * slots])
                def _():
                    row = pl.multiple_of((meta_ref[base + 2 * k] + first_row) * tile, tile)
                    col = pl.multiple_of(((i + shift) * tile_rows + meta_ref[base + 2 * k + 1]) * tile, tile)
                    values = values_ref[j, k]
                    dense_ref[pl.ds(row, tile), pl.ds(col, tile)] = values
                    flipped_ref[pl.ds(col, tile), pl.ds(row, tile)] = values.T

                return 0

            lax.fori_loop(0, (window // 2) * slots, slot, 0)

        place(own_meta_ref, own_ref, 0, 0, 0)
        place(mate_meta_ref, mate_ref, 1, 1 - core_ref[0], tile_rows)

    wide = positions * rows_dev
    return call(
        kernel,
        [((2 * rows_dev, wide), BF16), ((wide, 2 * rows_dev), BF16)],
        [core, own_meta, mate_meta, own_values, mate_values],
        smem=3,
    )


def gathered_sums(dense, sources):
    rows_dev, hidden = sources[0].shape

    def kernel(dense_ref, *refs):
        source_refs, (own_ref, mate_ref) = refs[:-2], refs[-2:]
        total = jnp.zeros((2 * rows_dev, hidden), F32)
        for m, ref in enumerate(source_refs):
            part = dense_ref[:, m * rows_dev : (m + 1) * rows_dev]
            total = total + jnp.dot(part, ref[...], preferred_element_type=F32)
        own_ref[...] = total[:rows_dev]
        mate_ref[...] = total[rows_dev:]

    return call(
        kernel,
        [((rows_dev, hidden), F32), ((rows_dev, hidden), F32)],
        [dense, *sources],
        flops=4 * rows_dev * rows_dev * hidden * len(sources),
    )


def layer(own_sum, mate_sum, weight, bias, grad_out):
    rows_dev, hidden = own_sum.shape

    def kernel(own_ref, mate_ref, weight_ref, bias_ref, grad_out_ref, agg_ref, out_ref, gp_ref, ga_ref):
        agg = (own_ref[...] + mate_ref[...]).astype(BF16)
        agg_ref[...] = agg
        pre = jnp.dot(agg, weight_ref[...], preferred_element_type=F32) + bias_ref[...]
        sig = jax.nn.sigmoid(pre)
        out_ref[...] = (pre * sig).astype(BF16)
        grad_pre = (grad_out_ref[...].astype(F32) * sig * (1.0 + pre * (1.0 - sig))).astype(BF16)
        gp_ref[...] = grad_pre
        ga_ref[...] = lax.dot_general(
            grad_pre, weight_ref[...], (((1,), (1,)), ((), ())), preferred_element_type=F32
        ).astype(BF16)

    shape = (rows_dev, hidden)
    return call(
        kernel,
        [(shape, BF16)] * 4,
        [own_sum, mate_sum, weight, bias.reshape(1, hidden), grad_out],
        flops=4 * rows_dev * hidden * hidden,
    )


def weight_terms(core, agg, grad_pre, pieces):
    rows_dev, hidden = agg.shape
    piece = hidden // pieces
    half = (pieces // 2, piece + BIAS_ROWS, hidden)

    def kernel(core_ref, agg_ref, gp_ref, keep_ref, give_ref):
        grad_pre_now = gp_ref[...]
        bias_term = jnp.sum(grad_pre_now.astype(F32), axis=0, keepdims=True)
        bias_rows = jnp.broadcast_to(bias_term, (BIAS_ROWS, hidden))

        def term(side):
            cols = pl.ds(pl.multiple_of(side * (hidden // 2), hidden // 2), hidden // 2)
            return lax.dot_general(
                agg_ref[:, cols], grad_pre_now, (((0,), (0,)), ((), ())), preferred_element_type=F32
            )

        core_now = core_ref[0]
        for ref, value in ((keep_ref, term(core_now)), (give_ref, term(1 - core_now))):
            for q in range(pieces // 2):
                ref[q, :piece] = value[q * piece : (q + 1) * piece].astype(ref.dtype)
                ref[q, piece:] = bias_rows.astype(ref.dtype)

    return call(
        kernel, [(half, F32), (half, BF16)], [core, agg, grad_pre], flops=2 * rows_dev * hidden * hidden, smem=1
    )


def spread_halves(place, keep, got):
    count, rows, hidden = keep.shape

    def kernel(place_ref, keep_ref, got_ref, own_ref, *out_refs):
        for other in range(count):
            q = place_ref[0] ^ other
            value = keep_ref[q] + got_ref[q].astype(F32)
            if other == 0:
                own_ref[...] = value
            else:
                out_refs[other - 1][...] = value.astype(BF16)

    return call(
        kernel,
        [((rows, hidden), F32)] + [((rows, hidden), BF16)] * (count - 1),
        [place, keep, got],
        smem=1,
    )


def summed_terms(own, others):
    def kernel(own_ref, *refs):
        others_now, out_ref = refs[:-1], refs[-1]
        total = own_ref[...].astype(F32)
        for ref in others_now:
            total = total + ref[...].astype(F32)
        out_ref[...] = total.astype(BF16)

    return call(kernel, [(own.shape, BF16)], [own, *others])[0]


def tree_sum(values):
    values = [v.astype(F32) for v in values]
    while len(values) > 1:
        values = [values[k] + values[k + 1] for k in range(0, len(values), 2)]
    return values[0]


def summed_planes(values, piece):
    shape = values[0].shape

    def kernel(*refs):
        value_refs, (weight_ref, bias_ref) = refs[:-2], refs[-2:]
        total = tree_sum([ref[...] for ref in value_refs])
        weight_ref[...] = total[:piece].astype(BF16)
        bias_ref[...] = total[piece : piece + 8]

    return call(kernel, [((piece, shape[1]), BF16), ((8, shape[1]), F32)], list(values))


def joined(place, pieces):
    piece, hidden = pieces[0].shape
    count = len(pieces)

    def kernel(place_ref, *refs):
        piece_refs, out_ref = refs[:-1], refs[-1]
        for other, ref in enumerate(piece_refs):
            q = place_ref[0] ^ other
            out_ref[pl.ds(pl.multiple_of(q * piece, piece), piece)] = ref[...]

    return call(kernel, [((count * piece, hidden), BF16)], [place, *pieces], smem=1)[0]


def whole_weight(core, mine, other):
    rows, hidden = mine.shape

    def kernel(core_ref, mine_ref, other_ref, out_ref):
        core_now = core_ref[0]
        out_ref[pl.ds(pl.multiple_of(core_now * rows, rows), rows)] = mine_ref[...].astype(F32)
        out_ref[pl.ds(pl.multiple_of((1 - core_now) * rows, rows), rows)] = other_ref[...].astype(F32)

    return call(kernel, [((2 * rows, hidden), F32)], [core, mine, other], smem=1)[0]


def scattered_sums(flipped, own, mate):
    rows_dev, hidden = own.shape
    positions = flipped.shape[0] // rows_dev

    def kernel(flipped_ref, own_ref, mate_ref, *out_refs):
        for m, ref in enumerate(out_refs):
            part = pl.ds(m * rows_dev, rows_dev)
            total = jnp.dot(flipped_ref[part, :rows_dev], own_ref[...], preferred_element_type=F32)
            total += jnp.dot(flipped_ref[part, rows_dev:], mate_ref[...], preferred_element_type=F32)
            ref[...] = total.astype(ref.dtype)

    return call(
        kernel,
        [((rows_dev, hidden), F32 if m == positions // 2 else BF16) for m in range(positions)],
        [flipped, own, mate],
        flops=4 * rows_dev * rows_dev * hidden * positions,
    )


def local(features, tile_list, tile_count, tile_values, weight, bias, grad_out):
    count = lax.axis_size("blk")
    me = lax.axis_index("blk")
    window = tile_values.shape[1]
    reach = window // 4
    positions = 2 * reach + 1
    rows_dev, hidden = features.shape
    plane, plane_bits = 4, 2
    pieces = 2 * plane
    core = (me % 2).astype(jnp.int32).reshape(1)
    place = ((me // 2) % plane).astype(jnp.int32).reshape(1)

    def moved(value, chips, even_only=False):
        pairs = [(s, (s + 2 * chips) % count) for s in range(count) if not (even_only and s % 2)]
        return lax.ppermute(value, "blk", pairs)

    def swapped(value, distance):
        return lax.ppermute(value, "blk", [(s, s ^ distance) for s in range(count)])

    sources = [
        features if m == reach else moved(features, reach - m, m == positions - 1) for m in range(positions)
    ]
    meta = jnp.concatenate([tile_list[0].reshape(window, -1), tile_count[0][:, None]], axis=1).reshape(-1)
    mate_meta, mate_values = swapped(meta, 1), swapped(tile_values[0], 1)
    dense, flipped = dense_tiles(core, meta, mate_meta, tile_values[0], mate_values, rows_dev, positions)
    own_sum, mate_sum = gathered_sums(dense, sources)
    agg, output, grad_pre, grad_agg = layer(own_sum, swapped(mate_sum, 1), weight, bias, grad_out)
    mate_grad = swapped(grad_agg, 1)

    keep, give = weight_terms(core, agg, grad_pre, pieces)
    terms = scattered_sums(flipped, grad_agg, mate_grad)
    arrived = [
        moved(terms[m], m - reach, m == positions - 1) for m in range(positions) if m != reach
    ]

    own_piece, *give_pieces = spread_halves(place, keep, swapped(give, 1))
    plane_sum = summed_terms(own_piece, [swapped(v, 2 * (d + 1)) for d, v in enumerate(give_pieces)])
    group = count // pieces
    values = [plane_sum] + [swapped(plane_sum, pieces * d) for d in range(1, group)]
    piece_sum, bias_sum = summed_planes(values, hidden // pieces)
    half = joined(place, [piece_sum] + [swapped(piece_sum, 2 * d) for d in range(1, plane)])
    grad_weight = whole_weight(core, half, swapped(half, 1))
    grad_features = summed_terms(terms[reach], arrived)
    return (output, grad_features, grad_weight, bias_sum[0])


def solution(mesh):
    placed = (
        P("blk", None),
        P("blk", None, None, None),
        P("blk", None),
        P("blk", None, None, None, None),
        P(),
        P(),
        P("blk", None),
    )
    return jax.shard_map(
        local,
        mesh=mesh,
        in_specs=placed,
        out_specs=(P("blk", None), P("blk", None), P(), P()),
        check_vma=False,
    )
```

time: 361 us -> 119 us (0.33)
  matrix products: 90.4 us -> 0 us
  waiting for transfers between devices: 122 us -> 35.8 us
  blocking collectives: 40.3 us -> 0 us
  Pallas kernels: 0 us -> 36.1 us
  local copies, waits for them, and re-layouts: 42.4 us -> 10.3 us
  between operations: 14.2 us -> 0.79 us
  other arithmetic: 10.8 us -> 0.66 us
    dot_general x35 -> x0, matrix products: 90.4 us -> none  [the longest x16 63.3 us: padded_terms(): jnp.einsum('kr,kah->rah', select, product, precision=lax.Precision.HIGHEST)]
    ppermute x16 -> x23, waiting for transfers between devices: 122 us -> 35.8 us  [the longest x15 28.1 us: swapped(): return lax.ppermute(value, 'blk', [(s, s ^ distance) for s in range(count)])]
    psum x1 -> x0, blocking collectives: 40.3 us -> none  [local(): grad_weight, grad_bias = lax.psum((local_weight, local_bias), 'blk')]
    pallas_call x0 -> x11, Pallas kernels: none -> 36.1 us  [call(): pl.pallas_call(kernel, out_shape=out_shape, in_specs=[spec(k) for k in ra...]
    gather x16 -> x0, local copies, waits for them, and re-layouts: 10.6 us -> none  [padded_terms(): picked = jnp.take(blocks, take_index, axis=0)]
    convert_element_type x17 -> x0, other arithmetic: 10.6 us -> none  [the longest x16 10.4 us: padded_terms(): (jnp.arange(values_now.shape[0], dtype=jnp.int32) < count_now).astype(jnp...]
    dynamic_slice x14 -> x0, local copies, waits for them, and re-layouts: 8.15 us -> none  [the longest x7 4.08 us: scatter_term(): tile_counts[j]]
    another operation x7 -> x1, local copies, waits for them, and re-layouts: 7.83 us -> 0.7 us  [local(): tile_list[0].reshape(window, -1)]
  transfers between devices with their start and end apart: 17 -> 23, of which waited for: 15 -> 12; matrix products, arithmetic and copies ran while one was open for 23% -> 2% of each run, Pallas kernels for 0% -> 19%
where the time goes in v1:
time: 119 us; the launch traced here: 118 us
  Pallas kernels  36.1 us (30%)
  waiting for transfers between devices  35.8 us (30%)
  starting transfers between devices  34.2 us (29%)
  local copies, waits for them, and re-layouts  10.3 us (9%)
    pallas_call x11, Pallas kernels, call(): pl.pallas_call(kernel, out_shape=out_shape, in_specs=[spec(k) for k in ra...  36.1 us
    ppermute x15, waiting for transfers between devices, swapped(): return lax.ppermute(value, 'blk', [(s, s ^ distance) for s in range(count)])  28.1 us
    ppermute x8, starting transfers between devices, moved(): return lax.ppermute(value, 'blk', pairs)  20.5 us
    ppermute x15, starting transfers between devices, swapped(): return lax.ppermute(value, 'blk', [(s, s ^ distance) for s in range(count)])  13.8 us
    unnamed x50, local copies, waits for them, and re-layouts  8.1 us
    ppermute x8, waiting for transfers between devices, moved(): return lax.ppermute(value, 'blk', pairs)  7.68 us
  transfers between devices with their start and end apart: 23, of which 12 were waited for; matrix products, arithmetic and copies ran while one was open for 2% of the time, Pallas kernels for 19%

profile of v1, /device:TPU:0, one launch (start us, length us, event | category | flops | bytes accessed | tf_op | source)
XLA Modules:
  0.0 117.9 jit_solution(15310097693743509929)
XLA Ops:
  2.8 3.0 %collective-permute-start.2 = (bf16[384,512]{1,0:T(8,128)(2,1)}, bf16[384,512]{1,0:T(8,128)(2,1)S(1)}, u32[]{:S(2)}, u32[]{:S(2)}) collective-permute-start(bf16[384,512]{1,0:T(8,128)(2,1)} %refs_2_.1), channel_id=1, source_target_pairs={{0,4},{1,5},{2,6},{3,7},{4,8},{5,9},{6,10},{7,11},{8,12},{9,13},{1... | collective-permute-start | bytes 1179656 | tf_op jit(solution)/shard_map/ppermute | solution.py:243
  5.8 1.5 %collective-permute-start.3 = (bf16[384,512]{1,0:T(8,128)(2,1)}, bf16[384,512]{1,0:T(8,128)(2,1)S(1)}, u32[]{:S(2)}, u32[]{:S(2)}) collective-permute-start(bf16[384,512]{1,0:T(8,128)(2,1)} %refs_2_.1), channel_id=1, source_target_pairs={{0,2},{1,3},{2,4},{3,5},{4,6},{5,7},{6,8},{7,9},{8,10},{9,11},{10,... | collective-permute-start | bytes 1179656 | tf_op jit(solution)/shard_map/ppermute | solution.py:243
  7.2 4.1 %collective-permute-start.4 = (bf16[384,512]{1,0:T(8,128)(2,1)}, bf16[384,512]{1,0:T(8,128)(2,1)S(1)}, u32[]{:S(2)}, u32[]{:S(2)}) collective-permute-start(bf16[384,512]{1,0:T(8,128)(2,1)} %refs_2_.1), channel_id=1, source_target_pairs={{0,30},{1,31},{2,0},{3,1},{4,2},{5,3},{6,4},{7,5},{8,6},{9,7},{10,... | collective-permute-start | bytes 1179656 | tf_op jit(solution)/shard_map/ppermute | solution.py:243
  11.4 2.3 %collective-permute-start.5 = (bf16[384,512]{1,0:T(8,128)(2,1)}, bf16[384,512]{1,0:T(8,128)(2,1)S(1)}, u32[]{:S(2)}, u32[]{:S(2)}) collective-permute-start(bf16[384,512]{1,0:T(8,128)(2,1)} %refs_2_.1), channel_id=1, source_target_pairs={{0,28},{2,30},{4,0},{6,2},{8,4},{10,6},{12,8},{14,10},{16,12},{18,... | collective-permute-start | bytes 1179656 | tf_op jit(solution)/shard_map/ppermute | solution.py:243
  14.9 8.4 %shard_map.102 = (bf16[768,1920]{1,0:T(8,128)(2,1)}, bf16[1920,768]{1,0:T(8,128)(2,1)}) custom-call(s32[1]{0:T(128)} %bitcast.core_ref, s32[120]{0:T(128)} %copy-done.18, s32[120]{0:T(128)} %copy-done.19, bf16[8,7,128,128]{3,2,1,0:T(8,128)(2,1)} %bitcast.9, bf16[8,7,128,128]{3,2,1,0:T(8,128)(2,1)} %copy-done), custom_call_target="tpu_custom_call" | custom-call | bytes 9569220 | tf_op jit(solution)/shard_map/pallas_call | solution.py:17
  23.3 4.0 %collective-permute-done.2.refs_0_ = bf16[384,512]{1,0:T(8,128)(2,1)S(1)} collective-permute-done((bf16[384,512]{1,0:T(8,128)(2,1)}, bf16[384,512]{1,0:T(8,128)(2,1)S(1)}, u32[]{:S(2)}, u32[]{:S(2)}) %collective-permute-start.2) | collective-permute-done | bytes 393248 | tf_op jit(solution)/shard_map/ppermute | solution.py:243
  27.9 3.1 %collective-permute-done.5.refs_4_ = bf16[384,512]{1,0:T(8,128)(2,1)S(1)} collective-permute-done((bf16[384,512]{1,0:T(8,128)(2,1)}, bf16[384,512]{1,0:T(8,128)(2,1)S(1)}, u32[]{:S(2)}, u32[]{:S(2)}) %collective-permute-start.5) | collective-permute-done | bytes 393248 | tf_op jit(solution)/shard_map/ppermute | solution.py:243
  31.8 5.6 %shard_map.103 = (f32[384,512]{1,0:T(8,128)}, f32[384,512]{1,0:T(8,128)}) custom-call(bf16[768,1920]{1,0:T(8,128)(2,1)} %get-tuple-element.25.dense_ref, bf16[384,512]{1,0:T(8,128)(2,1)} %copy-done.21, bf16[384,512]{1,0:T(8,128)(2,1)} %copy-done.22, bf16[384,512]{1,0:T(8,128)(2,1)} %refs_2_.1, bf16[384,512]{1,0:T(8,128)(2,1)} %copy-done.23, ...), custom_call_target="tpu_custom_call" | custom-call | flops 1509949440 | bytes 6488064 | tf_op jit(solution)/shard_map/pallas_call | solution.py:17
  37.3 2.5 %collective-permute-done.6.mate_ref = f32[384,512]{1,0:T(8,128)S(1)} collective-permute-done((f32[384,512]{1,0:T(8,128)}, f32[384,512]{1,0:T(8,128)S(1)}, u32[]{:S(2)}, u32[]{:S(2)}) %collective-permute-start.6) | collective-permute-done | bytes 786464 | tf_op jit(solution)/shard_map/ppermute | solution.py:246
  40.7 3.2 %shard_map.104 = (bf16[384,512]{1,0:T(8,128)(2,1)}, bf16[384,512]{1,0:T(8,128)(2,1)}, bf16[384,512]{1,0:T(8,128)(2,1)}, bf16[384,512]{1,0:T(8,128)(2,1)}) custom-call(f32[384,512]{1,0:T(8,128)} %get-tuple-element.26.own_ref, f32[384,512]{1,0:T(8,128)} %copy-done.1, bf16[512,512]{1,0:T(8,128)(2,1)} %weight_ref.1, f32[1,512]{1,0:T(1,128)} %bitcast.11, ...), custom_call_target="tpu_custom_call" | custom-call | flops 402653184 | bytes 4065280 | tf_op jit(solution)/shard_map/pallas_call | solution.py:17
  43.9 2.4 %shard_map.107 = (f32[4,80,512]{2,1,0:T(8,128)}, bf16[4,80,512]{2,1,0:T(8,128)(2,1)}) custom-call(s32[1]{0:T(128)} %bitcast.core_ref, bf16[384,512]{1,0:T(8,128)(2,1)} %get-tuple-element.36.agg_ref, bf16[384,512]{1,0:T(8,128)(2,1)} %get-tuple-element.37.gp_ref), custom_call_target="tpu_custom_call" | custom-call | flops 201326592 | bytes 1769476 | tf_op jit(solution)/shard_map/pallas_call | solution.py:17
  48.9 2.0 %shard_map.108 = (f32[80,512]{1,0:T(8,128)}, bf16[80,512]{1,0:T(8,128)(2,1)}, bf16[80,512]{1,0:T(8,128)(2,1)}, bf16[80,512]{1,0:T(8,128)(2,1)}) custom-call(s32[1]{0:T(128)} %bitcast.4.place_ref, f32[4,80,512]{2,1,0:T(8,128)} %get-tuple-element.38.keep_ref, bf16[4,80,512]{2,1,0:T(8,128)(2,1)} %copy-done.6), custom_call_target="tpu_custom_call" | custom-call | bytes 1392644 | tf_op jit(solution)/shard_map/pallas_call | solution.py:17
  50.9 1.5 %collective-permute-start.13 = (bf16[80,512]{1,0:T(8,128)(2,1)}, bf16[80,512]{1,0:T(8,128)(2,1)S(1)}, u32[]{:S(2)}, u32[]{:S(2)}) collective-permute-start(bf16[80,512]{1,0:T(8,128)(2,1)} %get-tuple-element.41), channel_id=1, source_target_pairs={{0,2},{1,3},{2,0},{3,1},{4,6},{5,7},{6,4},{7,5},{8,10},{9,11},{10,... | collective-permute-start | bytes 245768 | tf_op jit(solution)/shard_map/ppermute | solution.py:246
  52.4 2.0 %collective-permute-start.15 = (bf16[80,512]{1,0:T(8,128)(2,1)}, bf16[80,512]{1,0:T(8,128)(2,1)S(1)}, u32[]{:S(2)}, u32[]{:S(2)}) collective-permute-start(bf16[80,512]{1,0:T(8,128)(2,1)} %get-tuple-element.43), channel_id=1, source_target_pairs={{0,6},{1,7},{2,4},{3,5},{4,2},{5,3},{6,0},{7,1},{8,14},{9,15},{10,... | collective-permute-start | bytes 245768 | tf_op jit(solution)/shard_map/ppermute | solution.py:246
  55.6 3.0 %collective-permute-done.14.refs_1_ = bf16[80,512]{1,0:T(8,128)(2,1)S(1)} collective-permute-done((bf16[80,512]{1,0:T(8,128)(2,1)}, bf16[80,512]{1,0:T(8,128)(2,1)S(1)}, u32[]{:S(2)}, u32[]{:S(2)}) %collective-permute-start.14) | collective-permute-done | bytes 81952 | tf_op jit(solution)/shard_map/ppermute | solution.py:246
  59.2 1.7 %shard_map.109.refs_0_ = bf16[80,512]{1,0:T(8,128)(2,1)} custom-call(f32[80,512]{1,0:T(8,128)} %get-tuple-element.40.own_ref, bf16[80,512]{1,0:T(8,128)(2,1)} %copy-done.11, bf16[80,512]{1,0:T(8,128)(2,1)} %copy-done.12, bf16[80,512]{1,0:T(8,128)(2,1)} %copy-done.13), custom_call_target="tpu_custom_call" | custom-call | bytes 491520 | tf_op jit(solution)/shard_map/pallas_call | solution.py:17
  60.9 2.6 %collective-permute-start.17 = (bf16[80,512]{1,0:T(8,128)(2,1)}, bf16[80,512]{1,0:T(8,128)(2,1)S(1)}, u32[]{:S(2)}, u32[]{:S(2)}) collective-permute-start(bf16[80,512]{1,0:T(8,128)(2,1)} %shard_map.109.refs_0_), channel_id=1, source_target_pairs={{0,16},{1,17},{2,18},{3,19},{4,20},{5,21},{6,22},{7,23},{8,24},{9,... | collective-permute-start | bytes 245768 | tf_op jit(solution)/shard_map/ppermute | solution.py:246
  63.5 1.8 %collective-permute-start.18 = (bf16[80,512]{1,0:T(8,128)(2,1)}, bf16[80,512]{1,0:T(8,128)(2,1)S(1)}, u32[]{:S(2)}, u32[]{:S(2)}) collective-permute-start(bf16[80,512]{1,0:T(8,128)(2,1)} %shard_map.109.refs_0_), channel_id=1, source_target_pairs={{0,24},{1,25},{2,26},{3,27},{4,28},{5,29},{6,30},{7,31},{8,16},{9,... | collective-permute-start | bytes 245768 | tf_op jit(solution)/shard_map/ppermute | solution.py:246
  65.6 2.7 %collective-permute-done.17.refs_2_ = bf16[80,512]{1,0:T(8,128)(2,1)S(1)} collective-permute-done((bf16[80,512]{1,0:T(8,128)(2,1)}, bf16[80,512]{1,0:T(8,128)(2,1)S(1)}, u32[]{:S(2)}, u32[]{:S(2)}) %collective-permute-start.17) | collective-permute-done | bytes 81952 | tf_op jit(solution)/shard_map/ppermute | solution.py:246
  68.3 1.7 %collective-permute-done.18.refs_3_ = bf16[80,512]{1,0:T(8,128)(2,1)S(1)} collective-permute-done((bf16[80,512]{1,0:T(8,128)(2,1)}, bf16[80,512]{1,0:T(8,128)(2,1)S(1)}, u32[]{:S(2)}, u32[]{:S(2)}) %collective-permute-start.18) | collective-permute-done | bytes 81952 | tf_op jit(solution)/shard_map/ppermute | solution.py:246
  70.7 1.7 %shard_map.110 = (bf16[64,512]{1,0:T(8,128)(2,1)}, f32[8,512]{1,0:T(8,128)}) custom-call(bf16[80,512]{1,0:T(8,128)(2,1)} %shard_map.109.refs_0_, bf16[80,512]{1,0:T(8,128)(2,1)} %copy-done.8, bf16[80,512]{1,0:T(8,128)(2,1)} %copy-done.9, bf16[80,512]{1,0:T(8,128)(2,1)} %copy-done.10), custom_call_target="tpu_custom_call" | custom-call | bytes 409600 | tf_op jit(solution)/shard_map/pallas_call | solution.py:17
  73.7 4.9 %shard_map.105 = (bf16[384,512]{1,0:T(8,128)(2,1)}, bf16[384,512]{1,0:T(8,128)(2,1)}, f32[384,512]{1,0:T(8,128)}, bf16[384,512]{1,0:T(8,128)(2,1)}, bf16[384,512]{1,0:T(8,128)(2,1)}) custom-call(bf16[1920,768]{1,0:T(8,128)(2,1)} %get-tuple-element.29.flipped_ref, bf16[384,512]{1,0:T(8,128)(2,1)} %get-tuple-element.30.own_ref, bf16[384,512]{1,0:T(8,128)(2,1)} %copy-done.20), custom_call_target="tpu_custom_call" | custom-call | flops 1509949440 | bytes 6094848 | tf_op jit(solution)/shard_map/pallas_call | solution.py:17
  78.6 1.5 %collective-permute-start.10 = (bf16[384,512]{1,0:T(8,128)(2,1)}, bf16[384,512]{1,0:T(8,128)(2,1)S(1)}, u32[]{:S(2)}, u32[]{:S(2)}) collective-permute-start(bf16[384,512]{1,0:T(8,128)(2,1)} %get-tuple-element.34), channel_id=1, source_target_pairs={{0,2},{1,3},{2,4},{3,5},{4,6},{5,7},{6,8},{7,9},{8,10},{9,11},{10,... | collective-permute-start | bytes 1179656 | tf_op jit(solution)/shard_map/ppermute | solution.py:243
  80.1 2.9 %collective-permute-start.11 = (bf16[384,512]{1,0:T(8,128)(2,1)}, bf16[384,512]{1,0:T(8,128)(2,1)S(1)}, u32[]{:S(2)}, u32[]{:S(2)}) collective-permute-start(bf16[384,512]{1,0:T(8,128)(2,1)} %get-tuple-element.35), channel_id=1, source_target_pairs={{0,4},{2,6},{4,8},{6,10},{8,12},{10,14},{12,16},{14,18},{16,20},{1... | collective-permute-start | bytes 1179656 | tf_op jit(solution)/shard_map/ppermute | solution.py:243
  83.0 3.8 %collective-permute-start.8 = (bf16[384,512]{1,0:T(8,128)(2,1)}, bf16[384,512]{1,0:T(8,128)(2,1)S(1)}, u32[]{:S(2)}, u32[]{:S(2)}) collective-permute-start(bf16[384,512]{1,0:T(8,128)(2,1)} %get-tuple-element.32), channel_id=1, source_target_pairs={{0,28},{1,29},{2,30},{3,31},{4,0},{5,1},{6,2},{7,3},{8,4},{9,5},{1... | collective-permute-start | bytes 1179656 | tf_op jit(solution)/shard_map/ppermute | solution.py:243
  86.8 1.4 %collective-permute-start.9 = (bf16[384,512]{1,0:T(8,128)(2,1)}, bf16[384,512]{1,0:T(8,128)(2,1)S(1)}, u32[]{:S(2)}, u32[]{:S(2)}) collective-permute-start(bf16[384,512]{1,0:T(8,128)(2,1)} %get-tuple-element.33), channel_id=1, source_target_pairs={{0,30},{1,31},{2,0},{3,1},{4,2},{5,3},{6,4},{7,5},{8,6},{9,7},{10,... | collective-permute-start | bytes 1179656 | tf_op jit(solution)/shard_map/ppermute | solution.py:243
  89.3 13.1 %collective-permute-done.20.refs_2_ = bf16[64,512]{1,0:T(8,128)(2,1)S(1)} collective-permute-done((bf16[64,512]{1,0:T(8,128)(2,1)S(1)}, bf16[64,512]{1,0:T(8,128)(2,1)S(1)}, u32[]{:S(2)}, u32[]{:S(2)}) %collective-permute-start.20) | collective-permute-done | bytes 65568 | tf_op jit(solution)/shard_map/ppermute | solution.py:246
  102.4 3.2 %collective-permute-start.21 = (bf16[64,512]{1,0:T(8,128)(2,1)S(1)}, bf16[64,512]{1,0:T(8,128)(2,1)S(1)}, u32[]{:S(2)}, u32[]{:S(2)}) collective-permute-start(bf16[64,512]{1,0:T(8,128)(2,1)S(1)} %copy-done.14), channel_id=1, source_target_pairs={{0,6},{1,7},{2,4},{3,5},{4,2},{5,3},{6,0},{7,1},{8,14},{9,15},{10,... | collective-permute-start | bytes 196616 | tf_op jit(solution)/shard_map/ppermute | solution.py:246
  105.6 2.2 %collective-permute-done.21.refs_3_ = bf16[64,512]{1,0:T(8,128)(2,1)S(1)} collective-permute-done((bf16[64,512]{1,0:T(8,128)(2,1)S(1)}, bf16[64,512]{1,0:T(8,128)(2,1)S(1)}, u32[]{:S(2)}, u32[]{:S(2)}) %collective-permute-start.21) | collective-permute-done | bytes 65568 | tf_op jit(solution)/shard_map/ppermute | solution.py:246
  108.4 1.6 %shard_map.111.mine_ref = bf16[256,512]{1,0:T(8,128)(2,1)} custom-call(s32[1]{0:T(128)} %bitcast.4.place_ref, bf16[64,512]{1,0:T(8,128)(2,1)} %get-tuple-element.44.refs_0_, bf16[64,512]{1,0:T(8,128)(2,1)} %copy-done.15, bf16[64,512]{1,0:T(8,128)(2,1)} %copy-done.16, bf16[64,512]{1,0:T(8,128)(2,1)} %copy-done.17), custom_call_target="tpu_custom_call" | custom-call | bytes 524292 | tf_op jit(solution)/shard_map/pallas_call | solution.py:17
  112.6 2.6 %shard_map.106 = bf16[384,512]{1,0:T(8,128)(2,1)} custom-call(f32[384,512]{1,0:T(8,128)} %get-tuple-element.31.own_ref, bf16[384,512]{1,0:T(8,128)(2,1)} %copy-done.4, bf16[384,512]{1,0:T(8,128)(2,1)} %copy-done.5, bf16[384,512]{1,0:T(8,128)(2,1)} %copy-done.2, bf16[384,512]{1,0:T(8,128)(2,1)} %copy-done.3), custom_call_target="tpu_custom_call" | custom-call | bytes 2752512 | tf_op jit(solution)/shard_map/pallas_call | solution.py:17
  115.8 2.1 %shard_map.112 = f32[512,512]{1,0:T(8,128)} custom-call(s32[1]{0:T(128)} %bitcast.core_ref, bf16[256,512]{1,0:T(8,128)(2,1)} %shard_map.111.mine_ref, bf16[256,512]{1,0:T(8,128)(2,1)} %copy-done.7), custom_call_target="tpu_custom_call" | custom-call | bytes 1572868 | tf_op jit(solution)/shard_map/pallas_call | solution.py:17
  (80 shorter events, 17.1 us)
Async XLA Ops:
  0.6 13.0 %collective-permute-start.1 = (bf16[8,7,128,128]{3,2,1,0:T(8,128)(2,1)}, bf16[8,7,128,128]{3,2,1,0:T(8,128)(2,1)S(1)}, u32[]{:S(2)}, u32[]{:S(2)}) collective-permute-start(bf16[8,7,128,128]{3,2,1,0:T(8,128)(2,1)} %bitcast.8), channel_id=1, source_target_pairs={{0,1},{1,0},{2,3},{3,2},{4,5},{5,4},{6,7},{7,6},{8,9},{9,8},{10,11... | collective-permute-start | bytes 5505032 | tf_op jit(solution)/shard_map/ppermute | solution.py:246
  2.7 11.0 %copy-start.18 = (s32[120]{0:T(128)}, s32[120]{0:T(128)S(1)}, u32[]{:S(2)}) copy-start(s32[120]{0:T(128)S(1)} %reshape.21.own_meta_ref) | copy-start | bytes 1444
  2.7 8.7 %collective-permute-start = (s32[120]{0:T(128)S(1)}, s32[120]{0:T(128)S(1)}, u32[]{:S(2)}, u32[]{:S(2)}) collective-permute-start(s32[120]{0:T(128)S(1)} %reshape.21.own_meta_ref), channel_id=1, source_target_pairs={{0,1},{1,0},{2,3},{3,2},{4,5},{5,4},{6,7},{7,6},{8,9},{9,8},{10,11... | collective-permute-start | bytes 1448 | tf_op jit(solution)/shard_map/ppermute | solution.py:246
  2.8 24.5 %collective-permute-start.2 = (bf16[384,512]{1,0:T(8,128)(2,1)}, bf16[384,512]{1,0:T(8,128)(2,1)S(1)}, u32[]{:S(2)}, u32[]{:S(2)}) collective-permute-start(bf16[384,512]{1,0:T(8,128)(2,1)} %refs_2_.1), channel_id=1, source_target_pairs={{0,4},{1,5},{2,6},{3,7},{4,8},{5,9},{6,10},{7,11},{8,12},{9,13},{1... | collective-permute-start | bytes 1179656 | tf_op jit(solution)/shard_map/ppermute | solution.py:243
  5.8 22.1 %collective-permute-start.3 = (bf16[384,512]{1,0:T(8,128)(2,1)}, bf16[384,512]{1,0:T(8,128)(2,1)S(1)}, u32[]{:S(2)}, u32[]{:S(2)}) collective-permute-start(bf16[384,512]{1,0:T(8,128)(2,1)} %refs_2_.1), channel_id=1, source_target_pairs={{0,2},{1,3},{2,4},{3,5},{4,6},{5,7},{6,8},{7,9},{8,10},{9,11},{10,... | collective-permute-start | bytes 1179656 | tf_op jit(solution)/shard_map/ppermute | solution.py:243
  7.2 20.6 %collective-permute-start.4 = (bf16[384,512]{1,0:T(8,128)(2,1)}, bf16[384,512]{1,0:T(8,128)(2,1)S(1)}, u32[]{:S(2)}, u32[]{:S(2)}) collective-permute-start(bf16[384,512]{1,0:T(8,128)(2,1)} %refs_2_.1), channel_id=1, source_target_pairs={{0,30},{1,31},{2,0},{3,1},{4,2},{5,3},{6,4},{7,5},{8,6},{9,7},{10,... | collective-permute-start | bytes 1179656 | tf_op jit(solution)/shard_map/ppermute | solution.py:243
  11.4 19.6 %collective-permute-start.5 = (bf16[384,512]{1,0:T(8,128)(2,1)}, bf16[384,512]{1,0:T(8,128)(2,1)S(1)}, u32[]{:S(2)}, u32[]{:S(2)}) collective-permute-start(bf16[384,512]{1,0:T(8,128)(2,1)} %refs_2_.1), channel_id=1, source_target_pairs={{0,28},{2,30},{4,0},{6,2},{8,4},{10,6},{12,8},{14,10},{16,12},{18,... | collective-permute-start | bytes 1179656 | tf_op jit(solution)/shard_map/ppermute | solution.py:243
  27.3 3.7 %copy-start.21 = (bf16[384,512]{1,0:T(8,128)(2,1)}, bf16[384,512]{1,0:T(8,128)(2,1)S(1)}, u32[]{:S(2)}) copy-start(bf16[384,512]{1,0:T(8,128)(2,1)S(1)} %collective-permute-done.2.refs_0_) | copy-start | bytes 1179652
  27.9 3.1 %copy-start.22 = (bf16[384,512]{1,0:T(8,128)(2,1)}, bf16[384,512]{1,0:T(8,128)(2,1)S(1)}, u32[]{:S(2)}) copy-start(bf16[384,512]{1,0:T(8,128)(2,1)S(1)} %collective-permute-done.3.refs_1_) | copy-start | bytes 1179652
  27.9 3.1 %copy-start.23 = (bf16[384,512]{1,0:T(8,128)(2,1)}, bf16[384,512]{1,0:T(8,128)(2,1)S(1)}, u32[]{:S(2)}) copy-start(bf16[384,512]{1,0:T(8,128)(2,1)S(1)} %collective-permute-done.4.refs_3_) | copy-start | bytes 1179652
  37.3 2.5 %collective-permute-start.6 = (f32[384,512]{1,0:T(8,128)}, f32[384,512]{1,0:T(8,128)S(1)}, u32[]{:S(2)}, u32[]{:S(2)}) collective-permute-start(f32[384,512]{1,0:T(8,128)} %get-tuple-element.27), channel_id=1, source_target_pairs={{0,1},{1,0},{2,3},{3,2},{4,5},{5,4},{6,7},{7,6},{8,9},{9,8},{10,11... | collective-permute-start | bytes 2359304 | tf_op jit(solution)/shard_map/ppermute | solution.py:246
  46.3 1.8 %collective-permute-start.12 = (bf16[4,80,512]{2,1,0:T(8,128)(2,1)}, bf16[4,80,512]{2,1,0:T(8,128)(2,1)S(1)}, u32[]{:S(2)}, u32[]{:S(2)}) collective-permute-start(bf16[4,80,512]{2,1,0:T(8,128)(2,1)} %get-tuple-element.39), channel_id=1, source_target_pairs={{0,1},{1,0},{2,3},{3,2},{4,5},{5,4},{6,7},{7,6},{8,9},{9,8},{10,11... | collective-permute-start | bytes 983048 | tf_op jit(solution)/shard_map/ppermute | solution.py:246
  46.5 26.4 %collective-permute-start.7 = (bf16[384,512]{1,0:T(8,128)(2,1)}, bf16[384,512]{1,0:T(8,128)(2,1)S(1)}, u32[]{:S(2)}, u32[]{:S(2)}) collective-permute-start(bf16[384,512]{1,0:T(8,128)(2,1)} %get-tuple-element.30.own_ref), channel_id=1, source_target_pairs={{0,1},{1,0},{2,3},{3,2},{4,5},{5,4},{6,7},{7,6},{8,9},{9,8},{10,11... | collective-permute-start | bytes 1179656 | tf_op jit(solution)/shard_map/ppermute | solution.py:246
  50.9 4.7 %collective-permute-start.13 = (bf16[80,512]{1,0:T(8,128)(2,1)}, bf16[80,512]{1,0:T(8,128)(2,1)S(1)}, u32[]{:S(2)}, u32[]{:S(2)}) collective-permute-start(bf16[80,512]{1,0:T(8,128)(2,1)} %get-tuple-element.41), channel_id=1, source_target_pairs={{0,2},{1,3},{2,0},{3,1},{4,6},{5,7},{6,4},{7,5},{8,10},{9,11},{10,... | collective-permute-start | bytes 245768 | tf_op jit(solution)/shard_map/ppermute | solution.py:246
  52.4 6.2 %collective-permute-start.14 = (bf16[80,512]{1,0:T(8,128)(2,1)}, bf16[80,512]{1,0:T(8,128)(2,1)S(1)}, u32[]{:S(2)}, u32[]{:S(2)}) collective-permute-start(bf16[80,512]{1,0:T(8,128)(2,1)} %get-tuple-element.42), channel_id=1, source_target_pairs={{0,4},{1,5},{2,6},{3,7},{4,0},{5,1},{6,2},{7,3},{8,12},{9,13},{10,... | collective-permute-start | bytes 245768 | tf_op jit(solution)/shard_map/ppermute | solution.py:246
  52.4 6.2 %collective-permute-start.15 = (bf16[80,512]{1,0:T(8,128)(2,1)}, bf16[80,512]{1,0:T(8,128)(2,1)S(1)}, u32[]{:S(2)}, u32[]{:S(2)}) collective-permute-start(bf16[80,512]{1,0:T(8,128)(2,1)} %get-tuple-element.43), channel_id=1, source_target_pairs={{0,6},{1,7},{2,4},{3,5},{4,2},{5,3},{6,0},{7,1},{8,14},{9,15},{10,... | collective-permute-start | bytes 245768 | tf_op jit(solution)/shard_map/ppermute | solution.py:246
  55.6 3.0 %copy-start.11 = (bf16[80,512]{1,0:T(8,128)(2,1)}, bf16[80,512]{1,0:T(8,128)(2,1)S(1)}, u32[]{:S(2)}) copy-start(bf16[80,512]{1,0:T(8,128)(2,1)S(1)} %collective-permute-done.13.refs_0_) | copy-start | bytes 245764
  60.9 4.7 %collective-permute-start.16 = (bf16[80,512]{1,0:T(8,128)(2,1)}, bf16[80,512]{1,0:T(8,128)(2,1)S(1)}, u32[]{:S(2)}, u32[]{:S(2)}) collective-permute-start(bf16[80,512]{1,0:T(8,128)(2,1)} %shard_map.109.refs_0_), channel_id=1, source_target_pairs={{0,8},{1,9},{2,10},{3,11},{4,12},{5,13},{6,14},{7,15},{8,0},{9,1},... | collective-permute-start | bytes 245768 | tf_op jit(solution)/shard_map/ppermute | solution.py:246
  60.9 7.4 %collective-permute-start.17 = (bf16[80,512]{1,0:T(8,128)(2,1)}, bf16[80,512]{1,0:T(8,128)(2,1)S(1)}, u32[]{:S(2)}, u32[]{:S(2)}) collective-permute-start(bf16[80,512]{1,0:T(8,128)(2,1)} %shard_map.109.refs_0_), channel_id=1, source_target_pairs={{0,16},{1,17},{2,18},{3,19},{4,20},{5,21},{6,22},{7,23},{8,24},{9,... | collective-permute-start | bytes 245768 | tf_op jit(solution)/shard_map/ppermute | solution.py:246
  63.5 6.6 %collective-permute-start.18 = (bf16[80,512]{1,0:T(8,128)(2,1)}, bf16[80,512]{1,0:T(8,128)(2,1)S(1)}, u32[]{:S(2)}, u32[]{:S(2)}) collective-permute-start(bf16[80,512]{1,0:T(8,128)(2,1)} %shard_map.109.refs_0_), channel_id=1, source_target_pairs={{0,24},{1,25},{2,26},{3,27},{4,28},{5,29},{6,30},{7,31},{8,16},{9,... | collective-permute-start | bytes 245768 | tf_op jit(solution)/shard_map/ppermute | solution.py:246
  65.6 4.5 %copy-start.8 = (bf16[80,512]{1,0:T(8,128)(2,1)}, bf16[80,512]{1,0:T(8,128)(2,1)S(1)}, u32[]{:S(2)}) copy-start(bf16[80,512]{1,0:T(8,128)(2,1)S(1)} %collective-permute-done.16.refs_1_) | copy-start | bytes 245764
  72.4 15.8 %copy-start.14 = (bf16[64,512]{1,0:T(8,128)(2,1)S(1)}, bf16[64,512]{1,0:T(8,128)(2,1)}, u32[]{:S(2)}) copy-start(bf16[64,512]{1,0:T(8,128)(2,1)} %get-tuple-element.44.refs_0_) | copy-start | bytes 196612
  72.4 15.8 %collective-permute-start.19 = (bf16[64,512]{1,0:T(8,128)(2,1)}, bf16[64,512]{1,0:T(8,128)(2,1)S(1)}, u32[]{:S(2)}, u32[]{:S(2)}) collective-permute-start(bf16[64,512]{1,0:T(8,128)(2,1)} %get-tuple-element.44.refs_0_), channel_id=1, source_target_pairs={{0,2},{1,3},{2,0},{3,1},{4,6},{5,7},{6,4},{7,5},{8,10},{9,11},{10,... | collective-permute-start | bytes 196616 | tf_op jit(solution)/shard_map/ppermute | solution.py:246
  78.6 32.8 %collective-permute-start.10 = (bf16[384,512]{1,0:T(8,128)(2,1)}, bf16[384,512]{1,0:T(8,128)(2,1)S(1)}, u32[]{:S(2)}, u32[]{:S(2)}) collective-permute-start(bf16[384,512]{1,0:T(8,128)(2,1)} %get-tuple-element.34), channel_id=1, source_target_pairs={{0,2},{1,3},{2,4},{3,5},{4,6},{5,7},{6,8},{7,9},{8,10},{9,11},{10,... | collective-permute-start | bytes 1179656 | tf_op jit(solution)/shard_map/ppermute | solution.py:243
  80.1 31.3 %collective-permute-start.11 = (bf16[384,512]{1,0:T(8,128)(2,1)}, bf16[384,512]{1,0:T(8,128)(2,1)S(1)}, u32[]{:S(2)}, u32[]{:S(2)}) collective-permute-start(bf16[384,512]{1,0:T(8,128)(2,1)} %get-tuple-element.35), channel_id=1, source_target_pairs={{0,4},{2,6},{4,8},{6,10},{8,12},{10,14},{12,16},{14,18},{16,20},{1... | collective-permute-start | bytes 1179656 | tf_op jit(solution)/shard_map/ppermute | solution.py:243
  83.0 28.4 %collective-permute-start.8 = (bf16[384,512]{1,0:T(8,128)(2,1)}, bf16[384,512]{1,0:T(8,128)(2,1)S(1)}, u32[]{:S(2)}, u32[]{:S(2)}) collective-permute-start(bf16[384,512]{1,0:T(8,128)(2,1)} %get-tuple-element.32), channel_id=1, source_target_pairs={{0,28},{1,29},{2,30},{3,31},{4,0},{5,1},{6,2},{7,3},{8,4},{9,5},{1... | collective-permute-start | bytes 1179656 | tf_op jit(solution)/shard_map/ppermute | solution.py:243
  86.8 24.6 %collective-permute-start.9 = (bf16[384,512]{1,0:T(8,128)(2,1)}, bf16[384,512]{1,0:T(8,128)(2,1)S(1)}, u32[]{:S(2)}, u32[]{:S(2)}) collective-permute-start(bf16[384,512]{1,0:T(8,128)(2,1)} %get-tuple-element.33), channel_id=1, source_target_pairs={{0,30},{1,31},{2,0},{3,1},{4,2},{5,3},{6,4},{7,5},{8,6},{9,7},{10,... | collective-permute-start | bytes 1179656 | tf_op jit(solution)/shard_map/ppermute | solution.py:243
  88.2 19.6 %copy-start.15 = (bf16[64,512]{1,0:T(8,128)(2,1)}, bf16[64,512]{1,0:T(8,128)(2,1)S(1)}, u32[]{:S(2)}) copy-start(bf16[64,512]{1,0:T(8,128)(2,1)S(1)} %collective-permute-done.19.refs_1_) | copy-start | bytes 196612
  88.2 14.2 %collective-permute-start.20 = (bf16[64,512]{1,0:T(8,128)(2,1)S(1)}, bf16[64,512]{1,0:T(8,128)(2,1)S(1)}, u32[]{:S(2)}, u32[]{:S(2)}) collective-permute-start(bf16[64,512]{1,0:T(8,128)(2,1)S(1)} %copy-done.14), channel_id=1, source_target_pairs={{0,4},{1,5},{2,6},{3,7},{4,0},{5,1},{6,2},{7,3},{8,12},{9,13},{10,... | collective-permute-start | bytes 196616 | tf_op jit(solution)/shard_map/ppermute | solution.py:246
  102.4 5.4 %copy-start.16 = (bf16[64,512]{1,0:T(8,128)(2,1)}, bf16[64,512]{1,0:T(8,128)(2,1)S(1)}, u32[]{:S(2)}) copy-start(bf16[64,512]{1,0:T(8,128)(2,1)S(1)} %collective-permute-done.20.refs_2_) | copy-start | bytes 196612
  102.4 5.4 %collective-permute-start.21 = (bf16[64,512]{1,0:T(8,128)(2,1)S(1)}, bf16[64,512]{1,0:T(8,128)(2,1)S(1)}, u32[]{:S(2)}, u32[]{:S(2)}) collective-permute-start(bf16[64,512]{1,0:T(8,128)(2,1)S(1)} %copy-done.14), channel_id=1, source_target_pairs={{0,6},{1,7},{2,4},{3,5},{4,2},{5,3},{6,0},{7,1},{8,14},{9,15},{10,... | collective-permute-start | bytes 196616 | tf_op jit(solution)/shard_map/ppermute | solution.py:246
  110.1 5.0 %collective-permute-start.22 = (bf16[256,512]{1,0:T(8,128)(2,1)}, bf16[256,512]{1,0:T(8,128)(2,1)S(1)}, u32[]{:S(2)}, u32[]{:S(2)}) collective-permute-start(bf16[256,512]{1,0:T(8,128)(2,1)} %shard_map.111.mine_ref), channel_id=1, source_target_pairs={{0,1},{1,0},{2,3},{3,2},{4,5},{5,4},{6,7},{7,6},{8,9},{9,8},{10,11... | collective-permute-start | bytes 786440 | tf_op jit(solution)/shard_map/ppermute | solution.py:246
  (16 other events, 15.5 us)

commit v2 on v1

--- a/solution.py
+++ b/solution.py
@@ -5,7 +5,6 @@
 from jax.experimental.pallas import tpu as pltpu
 from jax.sharding import PartitionSpec as P
 
-VMEM_LIMIT = 56 * 1024 * 1024
 BF16, F32 = jnp.bfloat16, jnp.float32
 BIAS_ROWS = 16
 
@@ -19,7 +18,7 @@
         out_shape=out_shape,
         in_specs=[spec(k) for k in range(len(ins))],
         out_specs=[pl.BlockSpec(memory_space=pltpu.VMEM)] * len(outs),
-        compiler_params=pltpu.CompilerParams(vmem_limit_bytes=VMEM_LIMIT),
+        compiler_params=pltpu.CompilerParams(vmem_limit_bytes=moved + moved // 4 + 4 * 1024 * 1024),
         cost_estimate=pl.CostEstimate(flops=flops, bytes_accessed=moved, transcendentals=0),
     )(*ins)
 
@@ -62,24 +61,23 @@
     )
 
 
-def gathered_sums(dense, sources):
+def gathered_sums(dense, sources, side):
     rows_dev, hidden = sources[0].shape
 
     def kernel(dense_ref, *refs):
-        source_refs, (own_ref, mate_ref) = refs[:-2], refs[-2:]
-        total = jnp.zeros((2 * rows_dev, hidden), F32)
+        source_refs, out_ref = refs[:-1], refs[-1]
+        total = jnp.zeros((rows_dev, hidden), F32)
         for m, ref in enumerate(source_refs):
-            part = dense_ref[:, m * rows_dev : (m + 1) * rows_dev]
+            part = dense_ref[side * rows_dev : (side + 1) * rows_dev, m * rows_dev : (m + 1) * rows_dev]
             total = total + jnp.dot(part, ref[...], preferred_element_type=F32)
-        own_ref[...] = total[:rows_dev]
-        mate_ref[...] = total[rows_dev:]
-
-    return call(
-        kernel,
-        [((rows_dev, hidden), F32), ((rows_dev, hidden), F32)],
+        out_ref[...] = total
+
+    return call(
+        kernel,
+        [((rows_dev, hidden), F32)],
         [dense, *sources],
-        flops=4 * rows_dev * rows_dev * hidden * len(sources),
-    )
+        flops=2 * rows_dev * rows_dev * hidden * len(sources),
+    )[0]
 
 
 def layer(own_sum, mate_sum, weight, bias, grad_out):
@@ -251,8 +249,9 @@
     meta = jnp.concatenate([tile_list[0].reshape(window, -1), tile_count[0][:, None]], axis=1).reshape(-1)
     mate_meta, mate_values = swapped(meta, 1), swapped(tile_values[0], 1)
     dense, flipped = dense_tiles(core, meta, mate_meta, tile_values[0], mate_values, rows_dev, positions)
-    own_sum, mate_sum = gathered_sums(dense, sources)
-    agg, output, grad_pre, grad_agg = layer(own_sum, swapped(mate_sum, 1), weight, bias, grad_out)
+    mate_sum = swapped(gathered_sums(dense, sources, 1), 1)
+    own_sum = gathered_sums(dense, sources, 0)
+    agg, output, grad_pre, grad_agg = layer(own_sum, mate_sum, weight, bias, grad_out)
     mate_grad = swapped(grad_agg, 1)
 
     keep, give = weight_terms(core, agg, grad_pre, pieces)
@@ -261,7 +260,8 @@
         moved(terms[m], m - reach, m == positions - 1) for m in range(positions) if m != reach
     ]
 
-    own_piece, *give_pieces = spread_halves(place, keep, swapped(give, 1))
+    got, *terms = lax.optimization_barrier((swapped(give, 1), *terms))
+    own_piece, *give_pieces = spread_halves(place, keep, got)
     plane_sum = summed_terms(own_piece, [swapped(v, 2 * (d + 1)) for d, v in enumerate(give_pieces)])
     group = count // pieces
     values = [plane_sum] + [swapped(plane_sum, pieces * d) for d in range(1, group)]

time: 119 us -> 90.2 us (0.76)
  Pallas kernels: 36.1 us -> 13.3 us
  local copies, waits for them, and re-layouts: 10.3 us -> 4.8 us
  waiting for transfers between devices: 35.8 us -> 39 us
  starting transfers between devices: 34.2 us -> 31.2 us
    pallas_call x11 -> x12, Pallas kernels: 36.1 us -> 13.3 us  [call(): pl.pallas_call(kernel, out_shape=out_shape, in_specs=[spec(k) for k in ra...]
    unnamed x50 -> x14, local copies, waits for them, and re-layouts: 8.1 us -> 3.35 us
    ppermute x8, waiting for transfers between devices: 7.68 us -> 11 us  [moved(): return lax.ppermute(value, 'blk', pairs)]
    ppermute x8, starting transfers between devices: 20.5 us -> 18.5 us  [moved(): return lax.ppermute(value, 'blk', pairs)]
  transfers between devices with their start and end apart: 23 -> 23, of which waited for: 12 -> 12; matrix products, arithmetic and copies ran while one was open for 2% -> 2% of each run, Pallas kernels for 19% -> 11%
where the time goes in v2:
time: 90.2 us; the launch traced here: 89.8 us
  waiting for transfers between devices  39 us (43%)
  starting transfers between devices  31.2 us (35%)
  Pallas kernels  13.3 us (15%)
  local copies, waits for them, and re-layouts  4.8 us (5%)
    ppermute x15, waiting for transfers between devices, swapped(): return lax.ppermute(value, 'blk', [(s, s ^ distance) for s in range(count)])  28 us
    ppermute x8, starting transfers between devices, moved(): return lax.ppermute(value, 'blk', pairs)  18.5 us
    pallas_call x12, Pallas kernels, call(): pl.pallas_call(kernel, out_shape=out_shape, in_specs=[spec(k) for k in ra...  13.3 us
    ppermute x15, starting transfers between devices, swapped(): return lax.ppermute(value, 'blk', [(s, s ^ distance) for s in range(count)])  12.7 us
    ppermute x8, waiting for transfers between devices, moved(): return lax.ppermute(value, 'blk', pairs)  11 us
    unnamed x14, local copies, waits for them, and re-layouts  3.35 us
  transfers between devices with their start and end apart: 23, of which 12 were waited for; matrix products, arithmetic and copies ran while one was open for 2% of the time, Pallas kernels for 11%

profile of v2, /device:TPU:0, one launch (start us, length us, event | category | flops | bytes accessed | tf_op | source)
XLA Modules:
  0.0 89.8 jit_solution(897112960028137269)
XLA Ops:
  1.1 0.7 reshape_squeeze.3
  2.7 3.0 %collective-permute-start.2 = (bf16[384,512]{1,0:T(8,128)(2,1)}, bf16[384,512]{1,0:T(8,128)(2,1)S(1)}, u32[]{:S(2)}, u32[]{:S(2)}) collective-permute-start(bf16[384,512]{1,0:T(8,128)(2,1)} %refs_2_.3), channel_id=1, source_target_pairs={{0,4},{1,5},{2,6},{3,7},{4,8},{5,9},{6,10},{7,11},{8,12},{9,13},{1... | collective-permute-start | bytes 1179656 | tf_op jit(solution)/shard_map/ppermute | solution.py:241
  5.7 1.5 %collective-permute-start.3 = (bf16[384,512]{1,0:T(8,128)(2,1)}, bf16[384,512]{1,0:T(8,128)(2,1)S(1)}, u32[]{:S(2)}, u32[]{:S(2)}) collective-permute-start(bf16[384,512]{1,0:T(8,128)(2,1)} %refs_2_.3), channel_id=1, source_target_pairs={{0,2},{1,3},{2,4},{3,5},{4,6},{5,7},{6,8},{7,9},{8,10},{9,11},{10,... | collective-permute-start | bytes 1179656 | tf_op jit(solution)/shard_map/ppermute | solution.py:241
  7.2 4.1 %collective-permute-start.4 = (bf16[384,512]{1,0:T(8,128)(2,1)}, bf16[384,512]{1,0:T(8,128)(2,1)S(1)}, u32[]{:S(2)}, u32[]{:S(2)}) collective-permute-start(bf16[384,512]{1,0:T(8,128)(2,1)} %refs_2_.3), channel_id=1, source_target_pairs={{0,30},{1,31},{2,0},{3,1},{4,2},{5,3},{6,4},{7,5},{8,6},{9,7},{10,... | collective-permute-start | bytes 1179656 | tf_op jit(solution)/shard_map/ppermute | solution.py:241
  11.3 2.3 %collective-permute-start.5 = (bf16[384,512]{1,0:T(8,128)(2,1)}, bf16[384,512]{1,0:T(8,128)(2,1)S(1)}, u32[]{:S(2)}, u32[]{:S(2)}) collective-permute-start(bf16[384,512]{1,0:T(8,128)(2,1)} %refs_2_.3), channel_id=1, source_target_pairs={{0,28},{2,30},{4,0},{6,2},{8,4},{10,6},{12,8},{14,10},{16,12},{18,... | collective-permute-start | bytes 1179656 | tf_op jit(solution)/shard_map/ppermute | solution.py:241
  13.6 1.5 %copy-done = bf16[1,8,7,128,128]{4,3,2,1,0:T(8,128)(2,1)S(1)} copy-done((bf16[1,8,7,128,128]{4,3,2,1,0:T(8,128)(2,1)S(1)}, bf16[1,8,7,128,128]{4,3,2,1,0:T(8,128)(2,1)}, u32[]{:S(2)}) %copy-start) | copy-done | bytes 1835032
  15.1 4.8 %shard_map.102 = (bf16[768,1920]{1,0:T(8,128)(2,1)S(1)}, bf16[1920,768]{1,0:T(8,128)(2,1)S(1)}) custom-call(s32[1]{0:T(128)} %bitcast.core_ref, s32[120]{0:T(128)S(1)} %reshape.21.own_meta_ref, s32[120]{0:T(128)S(1)} %collective-permute-done.mate_meta_ref, bf16[8,7,128,128]{3,2,1,0:T(8,128)(2,1)S(1)} %bitcast.9, ...), custom_call_target="tpu_custom_call" | custom-call | bytes 9569220 | tf_op jit(solution)/shard_map/pallas_call | solution.py:16
  20.0 7.3 %collective-permute-done.2.refs_0_ = bf16[384,512]{1,0:T(8,128)(2,1)S(1)} collective-permute-done((bf16[384,512]{1,0:T(8,128)(2,1)}, bf16[384,512]{1,0:T(8,128)(2,1)S(1)}, u32[]{:S(2)}, u32[]{:S(2)}) %collective-permute-start.2) | collective-permute-done | bytes 393248 | tf_op jit(solution)/shard_map/ppermute | solution.py:241
  27.8 3.1 %collective-permute-done.5.refs_4_ = bf16[384,512]{1,0:T(8,128)(2,1)S(1)} collective-permute-done((bf16[384,512]{1,0:T(8,128)(2,1)}, bf16[384,512]{1,0:T(8,128)(2,1)S(1)}, u32[]{:S(2)}, u32[]{:S(2)}) %collective-permute-start.5) | collective-permute-done | bytes 393248 | tf_op jit(solution)/shard_map/ppermute | solution.py:241
  30.9 1.2 %shard_map.104 = f32[384,512]{1,0:T(8,128)S(1)} custom-call(bf16[768,1920]{1,0:T(8,128)(2,1)S(1)} %get-tuple-element.25.dense_ref, bf16[384,512]{1,0:T(8,128)(2,1)S(1)} %collective-permute-done.2.refs_0_, bf16[384,512]{1,0:T(8,128)(2,1)S(1)} %collective-permute-done.3.refs_1_, bf16[384,512]{1,0:T(8,128)(2,1)S(1)} %copy-done.1, ...), custom_call_target="tpu_custom_call" | custom-call | flops 754974720 | bytes 5701632 | tf_op jit(solution)/shard_map/pallas_call | solution.py:16
  32.2 1.2 %shard_map.103.own_ref = f32[384,512]{1,0:T(8,128)S(1)} custom-call(bf16[768,1920]{1,0:T(8,128)(2,1)S(1)} %get-tuple-element.25.dense_ref, bf16[384,512]{1,0:T(8,128)(2,1)S(1)} %collective-permute-done.2.refs_0_, bf16[384,512]{1,0:T(8,128)(2,1)S(1)} %collective-permute-done.3.refs_1_, bf16[384,512]{1,0:T(8,128)(2,1)S(1)} %copy-done.1, ...), custom_call_target="tpu_custom_call" | custom-call | flops 754974720 | bytes 5701632 | tf_op jit(solution)/shard_map/pallas_call | solution.py:16
  33.4 1.1 %collective-permute-done.6.mate_ref = f32[384,512]{1,0:T(8,128)S(1)} collective-permute-done((f32[384,512]{1,0:T(8,128)S(1)}, f32[384,512]{1,0:T(8,128)S(1)}, u32[]{:S(2)}, u32[]{:S(2)}) %collective-permute-start.6) | collective-permute-done | bytes 786464 | tf_op jit(solution)/shard_map/ppermute | solution.py:244
  34.5 1.3 %shard_map.105 = (bf16[384,512]{1,0:T(8,128)(2,1)S(1)}, bf16[384,512]{1,0:T(8,128)(2,1)}, bf16[384,512]{1,0:T(8,128)(2,1)S(1)}, bf16[384,512]{1,0:T(8,128)(2,1)S(1)}) custom-call(f32[384,512]{1,0:T(8,128)S(1)} %shard_map.103.own_ref, f32[384,512]{1,0:T(8,128)S(1)} %collective-permute-done.6.mate_ref, bf16[512,512]{1,0:T(8,128)(2,1)S(1)} %copy-done.2, ...), custom_call_target="tpu_custom_call" | custom-call | flops 402653184 | bytes 4065280 | tf_op jit(solution)/shard_map/pallas_call | solution.py:16
  36.9 0.7 collective-permute-done.8.mate_ref
  37.6 1.8 %copy-done.6 = bf16[1920,768]{1,0:T(8,128)(2,1)S(1)} copy-done((bf16[1920,768]{1,0:T(8,128)(2,1)S(1)}, bf16[1920,768]{1,0:T(8,128)(2,1)}, u32[]{:S(2)}) %copy-start.6) | copy-done | bytes 2949144
  39.4 2.2 %shard_map.107 = (bf16[384,512]{1,0:T(8,128)(2,1)S(1)}, bf16[384,512]{1,0:T(8,128)(2,1)S(1)}, f32[384,512]{1,0:T(8,128)S(1)}, bf16[384,512]{1,0:T(8,128)(2,1)S(1)}, bf16[384,512]{1,0:T(8,128)(2,1)S(1)}) custom-call(bf16[1920,768]{1,0:T(8,128)(2,1)S(1)} %copy-done.6, bf16[384,512]{1,0:T(8,128)(2,1)S(1)} %get-tuple-element.31.own_ref, ...), custom_call_target="tpu_custom_call" | custom-call | flops 1509949440 | bytes 6094848 | tf_op jit(solution)/shard_map/pallas_call | solution.py:16
  41.7 1.6 %collective-permute-start.13 = (bf16[80,512]{1,0:T(8,128)(2,1)S(1)}, bf16[80,512]{1,0:T(8,128)(2,1)S(1)}, u32[]{:S(2)}, u32[]{:S(2)}) collective-permute-start(bf16[80,512]{1,0:T(8,128)(2,1)S(1)} %get-tuple-element.41), channel_id=1, source_target_pairs={{0,2},{1,3},{2,0},{3,1},{4,6},{5,7},{6,4},{7,5},{8,10},{9,11},{10,... | collective-permute-start | bytes 245768 | tf_op jit(solution)/shard_map/ppermute | solution.py:244
  43.2 2.0 %collective-permute-start.15 = (bf16[80,512]{1,0:T(8,128)(2,1)S(1)}, bf16[80,512]{1,0:T(8,128)(2,1)S(1)}, u32[]{:S(2)}, u32[]{:S(2)}) collective-permute-start(bf16[80,512]{1,0:T(8,128)(2,1)S(1)} %get-tuple-element.43), channel_id=1, source_target_pairs={{0,6},{1,7},{2,4},{3,5},{4,2},{5,3},{6,0},{7,1},{8,14},{9,15},{10,... | collective-permute-start | bytes 245768 | tf_op jit(solution)/shard_map/ppermute | solution.py:244
  45.2 1.0 %collective-permute-done.13.refs_0_ = bf16[80,512]{1,0:T(8,128)(2,1)S(1)} collective-permute-done((bf16[80,512]{1,0:T(8,128)(2,1)S(1)}, bf16[80,512]{1,0:T(8,128)(2,1)S(1)}, u32[]{:S(2)}, u32[]{:S(2)}) %collective-permute-start.13) | collective-permute-done | bytes 81952 | tf_op jit(solution)/shard_map/ppermute | solution.py:244
  46.2 3.0 %collective-permute-done.14.refs_1_ = bf16[80,512]{1,0:T(8,128)(2,1)S(1)} collective-permute-done((bf16[80,512]{1,0:T(8,128)(2,1)S(1)}, bf16[80,512]{1,0:T(8,128)(2,1)S(1)}, u32[]{:S(2)}, u32[]{:S(2)}) %collective-permute-start.14) | collective-permute-done | bytes 81952 | tf_op jit(solution)/shard_map/ppermute | solution.py:244
  49.3 2.4 %collective-permute-start.17 = (bf16[80,512]{1,0:T(8,128)(2,1)S(1)}, bf16[80,512]{1,0:T(8,128)(2,1)S(1)}, u32[]{:S(2)}, u32[]{:S(2)}) collective-permute-start(bf16[80,512]{1,0:T(8,128)(2,1)S(1)} %shard_map.110.refs_0_), channel_id=1, source_target_pairs={{0,16},{1,17},{2,18},{3,19},{4,20},{5,21},{6,22},{7,23},{8,24},{9,... | collective-permute-start | bytes 245768 | tf_op jit(solution)/shard_map/ppermute | solution.py:244
  51.8 1.9 %collective-permute-start.18 = (bf16[80,512]{1,0:T(8,128)(2,1)S(1)}, bf16[80,512]{1,0:T(8,128)(2,1)S(1)}, u32[]{:S(2)}, u32[]{:S(2)}) collective-permute-start(bf16[80,512]{1,0:T(8,128)(2,1)S(1)} %shard_map.110.refs_0_), channel_id=1, source_target_pairs={{0,24},{1,25},{2,26},{3,27},{4,28},{5,29},{6,30},{7,31},{8,16},{9,... | collective-permute-start | bytes 245768 | tf_op jit(solution)/shard_map/ppermute | solution.py:244
  53.8 2.7 %collective-permute-done.17.refs_2_ = bf16[80,512]{1,0:T(8,128)(2,1)S(1)} collective-permute-done((bf16[80,512]{1,0:T(8,128)(2,1)S(1)}, bf16[80,512]{1,0:T(8,128)(2,1)S(1)}, u32[]{:S(2)}, u32[]{:S(2)}) %collective-permute-start.17) | collective-permute-done | bytes 81952 | tf_op jit(solution)/shard_map/ppermute | solution.py:244
  56.5 1.6 %collective-permute-done.18.refs_3_ = bf16[80,512]{1,0:T(8,128)(2,1)S(1)} collective-permute-done((bf16[80,512]{1,0:T(8,128)(2,1)S(1)}, bf16[80,512]{1,0:T(8,128)(2,1)S(1)}, u32[]{:S(2)}, u32[]{:S(2)}) %collective-permute-start.18) | collective-permute-done | bytes 81952 | tf_op jit(solution)/shard_map/ppermute | solution.py:244
  58.8 2.7 %collective-permute-start.9 = (bf16[384,512]{1,0:T(8,128)(2,1)S(1)}, bf16[384,512]{1,0:T(8,128)(2,1)S(1)}, u32[]{:S(2)}, u32[]{:S(2)}) collective-permute-start(bf16[384,512]{1,0:T(8,128)(2,1)S(1)} %get-tuple-element.32), channel_id=1, source_target_pairs={{0,28},{1,29},{2,30},{3,31},{4,0},{5,1},{6,2},{7,3},{8,4},{9,5},{1... | collective-permute-start | bytes 1179656 | tf_op jit(solution)/shard_map/ppermute | solution.py:241
  61.5 1.6 %collective-permute-start.10 = (bf16[384,512]{1,0:T(8,128)(2,1)S(1)}, bf16[384,512]{1,0:T(8,128)(2,1)S(1)}, u32[]{:S(2)}, u32[]{:S(2)}) collective-permute-start(bf16[384,512]{1,0:T(8,128)(2,1)S(1)} %get-tuple-element.33), channel_id=1, source_target_pairs={{0,30},{1,31},{2,0},{3,1},{4,2},{5,3},{6,4},{7,5},{8,6},{9,7},{10,... | collective-permute-start | bytes 1179656 | tf_op jit(solution)/shard_map/ppermute | solution.py:241
  63.5 2.8 %collective-permute-start.12 = (bf16[384,512]{1,0:T(8,128)(2,1)S(1)}, bf16[384,512]{1,0:T(8,128)(2,1)S(1)}, u32[]{:S(2)}, u32[]{:S(2)}) collective-permute-start(bf16[384,512]{1,0:T(8,128)(2,1)S(1)} %get-tuple-element.36), channel_id=1, source_target_pairs={{0,4},{2,6},{4,8},{6,10},{8,12},{10,14},{12,16},{14,18},{16,20},{1... | collective-permute-start | bytes 1179656 | tf_op jit(solution)/shard_map/ppermute | solution.py:241
  66.9 15.0 %collective-permute-done.20.refs_2_ = bf16[64,512]{1,0:T(8,128)(2,1)S(1)} collective-permute-done((bf16[64,512]{1,0:T(8,128)(2,1)S(1)}, bf16[64,512]{1,0:T(8,128)(2,1)S(1)}, u32[]{:S(2)}, u32[]{:S(2)}) %collective-permute-start.20) | collective-permute-done | bytes 65568 | tf_op jit(solution)/shard_map/ppermute | solution.py:244
  81.8 2.4 %collective-permute-start.21 = (bf16[64,512]{1,0:T(8,128)(2,1)S(1)}, bf16[64,512]{1,0:T(8,128)(2,1)S(1)}, u32[]{:S(2)}, u32[]{:S(2)}) collective-permute-start(bf16[64,512]{1,0:T(8,128)(2,1)S(1)} %get-tuple-element.44.refs_0_), channel_id=1, source_target_pairs={{0,6},{1,7},{2,4},{3,5},{4,2},{5,3},{6,0},{7,1},{8,14},{9,15},{10,... | collective-permute-start | bytes 196616 | tf_op jit(solution)/shard_map/ppermute | solution.py:244
  84.2 2.8 %collective-permute-done.21.refs_3_ = bf16[64,512]{1,0:T(8,128)(2,1)S(1)} collective-permute-done((bf16[64,512]{1,0:T(8,128)(2,1)S(1)}, bf16[64,512]{1,0:T(8,128)(2,1)S(1)}, u32[]{:S(2)}, u32[]{:S(2)}) %collective-permute-start.21) | collective-permute-done | bytes 65568 | tf_op jit(solution)/shard_map/ppermute | solution.py:244
  87.7 1.0 %shard_map.108 = bf16[384,512]{1,0:T(8,128)(2,1)} custom-call(f32[384,512]{1,0:T(8,128)S(1)} %get-tuple-element.37.own_ref, bf16[384,512]{1,0:T(8,128)(2,1)S(1)} %collective-permute-done.9.refs_0_, bf16[384,512]{1,0:T(8,128)(2,1)S(1)} %collective-permute-done.10.refs_1_, bf16[384,512]{1,0:T(8,128)(2,1)S(1)} %collective-permute-done.11.refs_2_, ...), custom_call_target="tpu_custom_call" | custom-call | bytes 2752512 | tf_op jit(solution)/shard_map/pallas_call | solution.py:16
  88.7 1.0 %shard_map.113 = f32[512,512]{1,0:T(8,128)} custom-call(s32[1]{0:T(128)} %bitcast.core_ref, bf16[256,512]{1,0:T(8,128)(2,1)S(1)} %shard_map.112.mine_ref, bf16[256,512]{1,0:T(8,128)(2,1)S(1)} %collective-permute-done.22.other_ref), custom_call_target="tpu_custom_call" | custom-call | bytes 1572868 | tf_op jit(solution)/shard_map/pallas_call | solution.py:16
  (45 shorter events, 5.6 us)
Async XLA Ops:
  0.6 13.0 %collective-permute-start.1 = (bf16[8,7,128,128]{3,2,1,0:T(8,128)(2,1)}, bf16[8,7,128,128]{3,2,1,0:T(8,128)(2,1)S(1)}, u32[]{:S(2)}, u32[]{:S(2)}) collective-permute-start(bf16[8,7,128,128]{3,2,1,0:T(8,128)(2,1)} %bitcast.8), channel_id=1, source_target_pairs={{0,1},{1,0},{2,3},{3,2},{4,5},{5,4},{6,7},{7,6},{8,9},{9,8},{10,11... | collective-permute-start | bytes 5505032 | tf_op jit(solution)/shard_map/ppermute | solution.py:244
  2.7 8.7 %collective-permute-start = (s32[120]{0:T(128)S(1)}, s32[120]{0:T(128)S(1)}, u32[]{:S(2)}, u32[]{:S(2)}) collective-permute-start(s32[120]{0:T(128)S(1)} %reshape.21.own_meta_ref), channel_id=1, source_target_pairs={{0,1},{1,0},{2,3},{3,2},{4,5},{5,4},{6,7},{7,6},{8,9},{9,8},{10,11... | collective-permute-start | bytes 1448 | tf_op jit(solution)/shard_map/ppermute | solution.py:244
  2.7 24.5 %collective-permute-start.2 = (bf16[384,512]{1,0:T(8,128)(2,1)}, bf16[384,512]{1,0:T(8,128)(2,1)S(1)}, u32[]{:S(2)}, u32[]{:S(2)}) collective-permute-start(bf16[384,512]{1,0:T(8,128)(2,1)} %refs_2_.3), channel_id=1, source_target_pairs={{0,4},{1,5},{2,6},{3,7},{4,8},{5,9},{6,10},{7,11},{8,12},{9,13},{1... | collective-permute-start | bytes 1179656 | tf_op jit(solution)/shard_map/ppermute | solution.py:241
  5.7 22.1 %collective-permute-start.3 = (bf16[384,512]{1,0:T(8,128)(2,1)}, bf16[384,512]{1,0:T(8,128)(2,1)S(1)}, u32[]{:S(2)}, u32[]{:S(2)}) collective-permute-start(bf16[384,512]{1,0:T(8,128)(2,1)} %refs_2_.3), channel_id=1, source_target_pairs={{0,2},{1,3},{2,4},{3,5},{4,6},{5,7},{6,8},{7,9},{8,10},{9,11},{10,... | collective-permute-start | bytes 1179656 | tf_op jit(solution)/shard_map/ppermute | solution.py:241
  7.2 20.6 %collective-permute-start.4 = (bf16[384,512]{1,0:T(8,128)(2,1)}, bf16[384,512]{1,0:T(8,128)(2,1)S(1)}, u32[]{:S(2)}, u32[]{:S(2)}) collective-permute-start(bf16[384,512]{1,0:T(8,128)(2,1)} %refs_2_.3), channel_id=1, source_target_pairs={{0,30},{1,31},{2,0},{3,1},{4,2},{5,3},{6,4},{7,5},{8,6},{9,7},{10,... | collective-permute-start | bytes 1179656 | tf_op jit(solution)/shard_map/ppermute | solution.py:241
  11.3 19.6 %collective-permute-start.5 = (bf16[384,512]{1,0:T(8,128)(2,1)}, bf16[384,512]{1,0:T(8,128)(2,1)S(1)}, u32[]{:S(2)}, u32[]{:S(2)}) collective-permute-start(bf16[384,512]{1,0:T(8,128)(2,1)} %refs_2_.3), channel_id=1, source_target_pairs={{0,28},{2,30},{4,0},{6,2},{8,4},{10,6},{12,8},{14,10},{16,12},{18,... | collective-permute-start | bytes 1179656 | tf_op jit(solution)/shard_map/ppermute | solution.py:241
  13.6 1.5 %copy-start = (bf16[1,8,7,128,128]{4,3,2,1,0:T(8,128)(2,1)S(1)}, bf16[1,8,7,128,128]{4,3,2,1,0:T(8,128)(2,1)}, u32[]{:S(2)}) copy-start(bf16[1,8,7,128,128]{4,3,2,1,0:T(8,128)(2,1)} %param.10) | copy-start | bytes 5505028
  15.1 15.8 %copy-start.1 = (bf16[384,512]{1,0:T(8,128)(2,1)S(1)}, bf16[384,512]{1,0:T(8,128)(2,1)}, u32[]{:S(2)}) copy-start(bf16[384,512]{1,0:T(8,128)(2,1)} %refs_2_.3) | copy-start | bytes 1179652
  20.0 13.4 %copy-start.5 = (bf16[1920,768]{1,0:T(8,128)(2,1)}, bf16[1920,768]{1,0:T(8,128)(2,1)S(1)}, u32[]{:S(2)}) copy-start(bf16[1920,768]{1,0:T(8,128)(2,1)S(1)} %get-tuple-element.30.flipped_ref) | copy-start | bytes 8847364
  32.1 2.4 %copy-start.2 = (bf16[512,512]{1,0:T(8,128)(2,1)S(1)}, bf16[512,512]{1,0:T(8,128)(2,1)}, u32[]{:S(2)}) copy-start(bf16[512,512]{1,0:T(8,128)(2,1)} %weight_ref.1) | copy-start | bytes 1572868
  32.1 2.4 %copy-start.3 = (bf16[384,512]{1,0:T(8,128)(2,1)S(1)}, bf16[384,512]{1,0:T(8,128)(2,1)}, u32[]{:S(2)}) copy-start(bf16[384,512]{1,0:T(8,128)(2,1)} %grad_out_ref.1) | copy-start | bytes 1179652
  32.1 2.4 %copy-start.4 = (f32[512]{0:T(512)S(1)}, f32[512]{0:T(512)}, u32[]{:S(2)}) copy-start(f32[512]{0:T(512)} %param.12) | copy-start | bytes 6148
  32.2 2.4 %collective-permute-start.6 = (f32[384,512]{1,0:T(8,128)S(1)}, f32[384,512]{1,0:T(8,128)S(1)}, u32[]{:S(2)}, u32[]{:S(2)}) collective-permute-start(f32[384,512]{1,0:T(8,128)S(1)} %shard_map.104), channel_id=1, source_target_pairs={{0,1},{1,0},{2,3},{3,2},{4,5},{5,4},{6,7},{7,6},{8,9},{9,8},{10,11... | collective-permute-start | bytes 2359304 | tf_op jit(solution)/shard_map/ppermute | solution.py:244
  35.8 1.7 %collective-permute-start.8 = (bf16[384,512]{1,0:T(8,128)(2,1)S(1)}, bf16[384,512]{1,0:T(8,128)(2,1)S(1)}, u32[]{:S(2)}, u32[]{:S(2)}) collective-permute-start(bf16[384,512]{1,0:T(8,128)(2,1)S(1)} %get-tuple-element.31.own_ref), channel_id=1, source_target_pairs={{0,1},{1,0},{2,3},{3,2},{4,5},{5,4},{6,7},{7,6},{8,9},{9,8},{10,11... | collective-permute-start | bytes 1179656 | tf_op jit(solution)/shard_map/ppermute | solution.py:244
  36.4 5.2 %collective-permute-start.7 = (bf16[4,80,512]{2,1,0:T(8,128)(2,1)S(1)}, bf16[4,80,512]{2,1,0:T(8,128)(2,1)S(1)}, u32[]{:S(2)}, u32[]{:S(2)}) collective-permute-start(bf16[4,80,512]{2,1,0:T(8,128)(2,1)S(1)} %get-tuple-element.29), channel_id=1, source_target_pairs={{0,1},{1,0},{2,3},{3,2},{4,5},{5,4},{6,7},{7,6},{8,9},{9,8},{10,11... | collective-permute-start | bytes 983048 | tf_op jit(solution)/shard_map/ppermute | solution.py:244
  37.6 1.8 %copy-start.6 = (bf16[1920,768]{1,0:T(8,128)(2,1)S(1)}, bf16[1920,768]{1,0:T(8,128)(2,1)}, u32[]{:S(2)}) copy-start(bf16[1920,768]{1,0:T(8,128)(2,1)} %copy-done.5) | copy-start | bytes 8847364
  41.7 4.6 %collective-permute-start.13 = (bf16[80,512]{1,0:T(8,128)(2,1)S(1)}, bf16[80,512]{1,0:T(8,128)(2,1)S(1)}, u32[]{:S(2)}, u32[]{:S(2)}) collective-permute-start(bf16[80,512]{1,0:T(8,128)(2,1)S(1)} %get-tuple-element.41), channel_id=1, source_target_pairs={{0,2},{1,3},{2,0},{3,1},{4,6},{5,7},{6,4},{7,5},{8,10},{9,11},{10,... | collective-permute-start | bytes 245768 | tf_op jit(solution)/shard_map/ppermute | solution.py:244
  43.2 6.0 %collective-permute-start.14 = (bf16[80,512]{1,0:T(8,128)(2,1)S(1)}, bf16[80,512]{1,0:T(8,128)(2,1)S(1)}, u32[]{:S(2)}, u32[]{:S(2)}) collective-permute-start(bf16[80,512]{1,0:T(8,128)(2,1)S(1)} %get-tuple-element.42), channel_id=1, source_target_pairs={{0,4},{1,5},{2,6},{3,7},{4,0},{5,1},{6,2},{7,3},{8,12},{9,13},{10,... | collective-permute-start | bytes 245768 | tf_op jit(solution)/shard_map/ppermute | solution.py:244
  43.2 6.0 %collective-permute-start.15 = (bf16[80,512]{1,0:T(8,128)(2,1)S(1)}, bf16[80,512]{1,0:T(8,128)(2,1)S(1)}, u32[]{:S(2)}, u32[]{:S(2)}) collective-permute-start(bf16[80,512]{1,0:T(8,128)(2,1)S(1)} %get-tuple-element.43), channel_id=1, source_target_pairs={{0,6},{1,7},{2,4},{3,5},{4,2},{5,3},{6,0},{7,1},{8,14},{9,15},{10,... | collective-permute-start | bytes 245768 | tf_op jit(solution)/shard_map/ppermute | solution.py:244
  49.3 4.5 %collective-permute-start.16 = (bf16[80,512]{1,0:T(8,128)(2,1)S(1)}, bf16[80,512]{1,0:T(8,128)(2,1)S(1)}, u32[]{:S(2)}, u32[]{:S(2)}) collective-permute-start(bf16[80,512]{1,0:T(8,128)(2,1)S(1)} %shard_map.110.refs_0_), channel_id=1, source_target_pairs={{0,8},{1,9},{2,10},{3,11},{4,12},{5,13},{6,14},{7,15},{8,0},{9,1},... | collective-permute-start | bytes 245768 | tf_op jit(solution)/shard_map/ppermute | solution.py:244
  49.3 7.2 %collective-permute-start.17 = (bf16[80,512]{1,0:T(8,128)(2,1)S(1)}, bf16[80,512]{1,0:T(8,128)(2,1)S(1)}, u32[]{:S(2)}, u32[]{:S(2)}) collective-permute-start(bf16[80,512]{1,0:T(8,128)(2,1)S(1)} %shard_map.110.refs_0_), channel_id=1, source_target_pairs={{0,16},{1,17},{2,18},{3,19},{4,20},{5,21},{6,22},{7,23},{8,24},{9,... | collective-permute-start | bytes 245768 | tf_op jit(solution)/shard_map/ppermute | solution.py:244
  51.8 6.3 %collective-permute-start.18 = (bf16[80,512]{1,0:T(8,128)(2,1)S(1)}, bf16[80,512]{1,0:T(8,128)(2,1)S(1)}, u32[]{:S(2)}, u32[]{:S(2)}) collective-permute-start(bf16[80,512]{1,0:T(8,128)(2,1)S(1)} %shard_map.110.refs_0_), channel_id=1, source_target_pairs={{0,24},{1,25},{2,26},{3,27},{4,28},{5,29},{6,30},{7,31},{8,16},{9,... | collective-permute-start | bytes 245768 | tf_op jit(solution)/shard_map/ppermute | solution.py:244
  58.2 8.2 %collective-permute-start.19 = (bf16[64,512]{1,0:T(8,128)(2,1)S(1)}, bf16[64,512]{1,0:T(8,128)(2,1)S(1)}, u32[]{:S(2)}, u32[]{:S(2)}) collective-permute-start(bf16[64,512]{1,0:T(8,128)(2,1)S(1)} %get-tuple-element.44.refs_0_), channel_id=1, source_target_pairs={{0,2},{1,3},{2,0},{3,1},{4,6},{5,7},{6,4},{7,5},{8,10},{9,11},{10,... | collective-permute-start | bytes 196616 | tf_op jit(solution)/shard_map/ppermute | solution.py:244
  58.8 28.9 %collective-permute-start.9 = (bf16[384,512]{1,0:T(8,128)(2,1)S(1)}, bf16[384,512]{1,0:T(8,128)(2,1)S(1)}, u32[]{:S(2)}, u32[]{:S(2)}) collective-permute-start(bf16[384,512]{1,0:T(8,128)(2,1)S(1)} %get-tuple-element.32), channel_id=1, source_target_pairs={{0,28},{1,29},{2,30},{3,31},{4,0},{5,1},{6,2},{7,3},{8,4},{9,5},{1... | collective-permute-start | bytes 1179656 | tf_op jit(solution)/shard_map/ppermute | solution.py:241
  61.5 26.2 %collective-permute-start.10 = (bf16[384,512]{1,0:T(8,128)(2,1)S(1)}, bf16[384,512]{1,0:T(8,128)(2,1)S(1)}, u32[]{:S(2)}, u32[]{:S(2)}) collective-permute-start(bf16[384,512]{1,0:T(8,128)(2,1)S(1)} %get-tuple-element.33), channel_id=1, source_target_pairs={{0,30},{1,31},{2,0},{3,1},{4,2},{5,3},{6,4},{7,5},{8,6},{9,7},{10,... | collective-permute-start | bytes 1179656 | tf_op jit(solution)/shard_map/ppermute | solution.py:241
  63.1 24.6 %collective-permute-start.11 = (bf16[384,512]{1,0:T(8,128)(2,1)S(1)}, bf16[384,512]{1,0:T(8,128)(2,1)S(1)}, u32[]{:S(2)}, u32[]{:S(2)}) collective-permute-start(bf16[384,512]{1,0:T(8,128)(2,1)S(1)} %get-tuple-element.35), channel_id=1, source_target_pairs={{0,2},{1,3},{2,4},{3,5},{4,6},{5,7},{6,8},{7,9},{8,10},{9,11},{10,... | collective-permute-start | bytes 1179656 | tf_op jit(solution)/shard_map/ppermute | solution.py:241
  63.5 24.2 %collective-permute-start.12 = (bf16[384,512]{1,0:T(8,128)(2,1)S(1)}, bf16[384,512]{1,0:T(8,128)(2,1)S(1)}, u32[]{:S(2)}, u32[]{:S(2)}) collective-permute-start(bf16[384,512]{1,0:T(8,128)(2,1)S(1)} %get-tuple-element.36), channel_id=1, source_target_pairs={{0,4},{2,6},{4,8},{6,10},{8,12},{10,14},{12,16},{14,18},{16,20},{1... | collective-permute-start | bytes 1179656 | tf_op jit(solution)/shard_map/ppermute | solution.py:241
  66.4 15.5 %collective-permute-start.20 = (bf16[64,512]{1,0:T(8,128)(2,1)S(1)}, bf16[64,512]{1,0:T(8,128)(2,1)S(1)}, u32[]{:S(2)}, u32[]{:S(2)}) collective-permute-start(bf16[64,512]{1,0:T(8,128)(2,1)S(1)} %get-tuple-element.44.refs_0_), channel_id=1, source_target_pairs={{0,4},{1,5},{2,6},{3,7},{4,0},{5,1},{6,2},{7,3},{8,12},{9,13},{10,... | collective-permute-start | bytes 196616 | tf_op jit(solution)/shard_map/ppermute | solution.py:244
  81.8 5.2 %collective-permute-start.21 = (bf16[64,512]{1,0:T(8,128)(2,1)S(1)}, bf16[64,512]{1,0:T(8,128)(2,1)S(1)}, u32[]{:S(2)}, u32[]{:S(2)}) collective-permute-start(bf16[64,512]{1,0:T(8,128)(2,1)S(1)} %get-tuple-element.44.refs_0_), channel_id=1, source_target_pairs={{0,6},{1,7},{2,4},{3,5},{4,2},{5,3},{6,0},{7,1},{8,14},{9,15},{10,... | collective-permute-start | bytes 196616 | tf_op jit(solution)/shard_map/ppermute | solution.py:244
  87.0 1.7 %collective-permute-start.22 = (bf16[256,512]{1,0:T(8,128)(2,1)S(1)}, bf16[256,512]{1,0:T(8,128)(2,1)S(1)}, u32[]{:S(2)}, u32[]{:S(2)}) collective-permute-start(bf16[256,512]{1,0:T(8,128)(2,1)S(1)} %shard_map.112.mine_ref), channel_id=1, source_target_pairs={{0,1},{1,0},{2,3},{3,2},{4,5},{5,4},{6,7},{7,6},{8,9},{9,8},{10,11... | collective-permute-start | bytes 786440 | tf_op jit(solution)/shard_map/ppermute | solution.py:244

commit v3 on v2

--- a/solution.py
+++ b/solution.py
@@ -23,11 +23,13 @@
     )(*ins)
 
 
-def dense_tiles(core, own_meta, mate_meta, own_values, mate_values, rows_dev, positions):
+def dense_tiles(spot, own_meta, mate_meta, own_values, mate_values, rows_dev, table):
     window, slots, tile, _ = own_values.shape
     tile_rows = rows_dev // tile
-
-    def kernel(core_ref, own_meta_ref, mate_meta_ref, own_ref, mate_ref, dense_ref, flipped_ref):
+    positions = len(table[0])
+
+    def kernel(spot_ref, table_ref, own_meta_ref, mate_meta_ref, own_ref, mate_ref, dense_ref, flipped_ref):
+        spot_now = spot_ref[0]
         dense_ref[...] = jnp.zeros_like(dense_ref)
         flipped_ref[...] = jnp.zeros_like(flipped_ref)
 
@@ -40,7 +42,8 @@
                 @pl.when(k < meta_ref[base + 2 * slots])
                 def _():
                     row = pl.multiple_of((meta_ref[base + 2 * k] + first_row) * tile, tile)
-                    col = pl.multiple_of(((i + shift) * tile_rows + meta_ref[base + 2 * k + 1]) * tile, tile)
+                    column = table_ref[spot_now * positions + i + shift]
+                    col = pl.multiple_of((column * tile_rows + meta_ref[base + 2 * k + 1]) * tile, tile)
                     values = values_ref[j, k]
                     dense_ref[pl.ds(row, tile), pl.ds(col, tile)] = values
                     flipped_ref[pl.ds(col, tile), pl.ds(row, tile)] = values.T
@@ -50,34 +53,51 @@
             lax.fori_loop(0, (window // 2) * slots, slot, 0)
 
         place(own_meta_ref, own_ref, 0, 0, 0)
-        place(mate_meta_ref, mate_ref, 1, 1 - core_ref[0], tile_rows)
+        place(mate_meta_ref, mate_ref, 1, 1 - spot_now % 2, tile_rows)
 
     wide = positions * rows_dev
     return call(
         kernel,
         [((2 * rows_dev, wide), BF16), ((wide, 2 * rows_dev), BF16)],
-        [core, own_meta, mate_meta, own_values, mate_values],
-        smem=3,
-    )
-
-
-def gathered_sums(dense, sources, side):
-    rows_dev, hidden = sources[0].shape
-
-    def kernel(dense_ref, *refs):
-        source_refs, out_ref = refs[:-1], refs[-1]
-        total = jnp.zeros((rows_dev, hidden), F32)
-        for m, ref in enumerate(source_refs):
-            part = dense_ref[side * rows_dev : (side + 1) * rows_dev, m * rows_dev : (m + 1) * rows_dev]
-            total = total + jnp.dot(part, ref[...], preferred_element_type=F32)
+        [spot, jnp.asarray(table, jnp.int32).reshape(-1), own_meta, mate_meta, own_values, mate_values],
+        smem=4,
+    )
+
+
+def holds(mask, spot):
+    return (mask >> spot) % 2 == 1
+
+
+def gathered_sums(spot, dense, columns, rows, sources, start=None):
+    hidden = first_of(sources[0]).shape[1]
+    rows_dev = first_of(sources[0]).shape[0]
+    first, last = rows
+
+    def kernel(spot_ref, dense_ref, *refs):
+        refs, out_ref = list(refs[:-1]), refs[-1]
+        total = refs.pop(0)[first:last] if start is not None else jnp.zeros((last - first, hidden), F32)
+        for column, source in zip(columns, sources):
+            if isinstance(source, tuple):
+                a, b = refs.pop(0)[...], refs.pop(0)[...]
+                value = jnp.where(holds(source[0], spot_ref[0]), a, b)
+            else:
+                value = refs.pop(0)[...]
+            part = dense_ref[first:last, column * rows_dev : (column + 1) * rows_dev]
+            total = total + jnp.dot(part, value, preferred_element_type=F32)
         out_ref[...] = total
 
-    return call(
-        kernel,
-        [((rows_dev, hidden), F32)],
-        [dense, *sources],
-        flops=2 * rows_dev * rows_dev * hidden * len(sources),
+    arrays = [a for source in sources for a in (source[1:] if isinstance(source, tuple) else (source,))]
+    return call(
+        kernel,
+        [((last - first, hidden), F32)],
+        [spot, dense, *([] if start is None else [start]), *arrays],
+        flops=2 * (last - first) * rows_dev * hidden * len(sources),
+        smem=1,
     )[0]
+
+
+def first_of(source):
+    return source[1] if isinstance(source, tuple) else source
 
 
 def layer(own_sum, mate_sum, weight, bias, grad_out):
@@ -151,15 +171,20 @@
     )
 
 
-def summed_terms(own, others):
-    def kernel(own_ref, *refs):
-        others_now, out_ref = refs[:-1], refs[-1]
-        total = own_ref[...].astype(F32)
-        for ref in others_now:
-            total = total + ref[...].astype(F32)
-        out_ref[...] = total.astype(BF16)
-
-    return call(kernel, [(own.shape, BF16)], [own, *others])[0]
+def summed_terms(spot, terms, masks=None, dtype=BF16):
+    masks = masks or [None] * len(terms)
+
+    def kernel(spot_ref, *refs):
+        out_ref = refs[-1]
+        total = None
+        for ref, mask in zip(refs[:-1], masks):
+            value = ref[...].astype(F32)
+            if mask is not None:
+                value = jnp.where(holds(mask, spot_ref[0]), value, 0.0)
+            total = value if total is None else total + value
+        out_ref[...] = total.astype(dtype)
+
+    return call(kernel, [(terms[0].shape, dtype)], [spot, *terms], smem=1)[0]
 
 
 def tree_sum(values):
@@ -205,23 +230,123 @@
     return call(kernel, [((2 * rows, hidden), F32)], [core, mine, other], smem=1)[0]
 
 
-def scattered_sums(flipped, own, mate):
+def scattered_sums(flipped, own, mate, columns, dtypes):
     rows_dev, hidden = own.shape
-    positions = flipped.shape[0] // rows_dev
 
     def kernel(flipped_ref, own_ref, mate_ref, *out_refs):
-        for m, ref in enumerate(out_refs):
-            part = pl.ds(m * rows_dev, rows_dev)
+        out_refs = list(out_refs)
+        for column, kinds in zip(columns, dtypes):
+            part = pl.ds(column * rows_dev, rows_dev)
             total = jnp.dot(flipped_ref[part, :rows_dev], own_ref[...], preferred_element_type=F32)
             total += jnp.dot(flipped_ref[part, rows_dev:], mate_ref[...], preferred_element_type=F32)
-            ref[...] = total.astype(ref.dtype)
-
-    return call(
-        kernel,
-        [((rows_dev, hidden), F32 if m == positions // 2 else BF16) for m in range(positions)],
+            for kind in kinds:
+                out_refs.pop(0)[...] = total.astype(kind)
+
+    return call(
+        kernel,
+        [((rows_dev, hidden), kind) for kinds in dtypes for kind in kinds],
         [flipped, own, mate],
-        flops=4 * rows_dev * rows_dev * hidden * positions,
-    )
+        flops=4 * rows_dev * rows_dev * hidden * len(columns),
+    )
+
+
+class Direct:
+    def __init__(self, count, reach):
+        self.count, self.reach, self.positions = count, reach, 2 * reach + 1
+        self.table = [list(range(self.positions))] * 8
+
+    def moved(self, value, chips, even_only=False):
+        pairs = [(s, (s + 2 * chips) % self.count) for s in range(self.count) if not (even_only and s % 2)]
+        return lax.ppermute(value, "blk", pairs)
+
+    def gather(self, features):
+        last = self.positions - 1
+        self.sources = [
+            features if m == self.reach else self.moved(features, self.reach - m, m == last)
+            for m in range(self.positions)
+        ]
+        return self.sources[0]
+
+    def sums(self, spot, dense, rows_dev):
+        columns = range(self.positions)
+        return [
+            gathered_sums(spot, dense, columns, (side * rows_dev, (side + 1) * rows_dev), self.sources)
+            for side in (1, 0)
+        ]
+
+    def scatter(self, spot, flipped, own, mate):
+        kinds = [[F32 if m == self.reach else BF16] for m in range(self.positions)]
+        terms = scattered_sums(flipped, own, mate, range(self.positions), kinds)
+        last = self.positions - 1
+        arrived = [
+            self.moved(terms[m], m - self.reach, m == last) for m in range(self.positions) if m != self.reach
+        ]
+        return terms[0], lambda: summed_terms(spot, [terms[self.reach], *arrived])
+
+
+class Relayed:
+    EVEN, MIDDLE, ENDS = 0b01010101, 0b00111100, 0b11000011
+
+    def __init__(self, count):
+        self.count, self.positions = count, 5
+        self.table = [
+            [3, 4, 0, 2, 1], [3, 4, 0, 1, 2],
+            [3, 2, 0, 4, 1], [3, 1, 0, 4, 2],
+            [1, 4, 0, 2, 3], [2, 4, 0, 1, 3],
+            [1, 2, 0, 4, 3], [2, 1, 0, 4, 3],
+        ]
+
+    def sent(self, value, steps, back=False):
+        pairs = [(s, steps[s % 8](s) % self.count) for s in range(self.count) if s % 8 in steps]
+        return lax.ppermute(value, "blk", [(b, a) if back else (a, b) for a, b in pairs])
+
+    x, y = staticmethod(lambda s: s ^ 2), staticmethod(lambda s: s ^ 4)
+    up, down = staticmethod(lambda s: s + 8), staticmethod(lambda s: s - 8)
+
+    def routes(self):
+        x, y, up, down = self.x, self.y, self.up, self.down
+        p1 = {spot: x if spot % 2 else y for spot in range(8)}
+        p2 = {spot: y if spot % 2 else x for spot in range(8)}
+        p3 = {0: up, 2: up, 4: down, 6: down, 5: up, 3: down}
+        p4 = {0: x, 6: x, 1: y, 7: y}
+        p5 = {1: up, 3: up}
+        p6 = {2: x, 4: x, 5: y, 3: y}
+        return p1, p2, p3, p4, p5, p6
+
+    def gather(self, features):
+        p1, p2, p3, p4, p5, p6 = self.routes()
+        first = self.sent(features, p1)
+        second = self.sent(features, p2)
+        third = self.sent(first, p3)
+        fourth = self.sent(first, p4)
+        fifth = self.sent(second, p5)
+        sixth = self.sent(third, p6)
+        self.early = [features, first, second]
+        self.late = [(self.EVEN, third, fifth), (self.MIDDLE, fourth, sixth)]
+        return first
+
+    def sums(self, spot, dense, rows_dev):
+        start = gathered_sums(spot, dense, (0, 1, 2), (0, 2 * rows_dev), self.early)
+        return [
+            gathered_sums(spot, dense, (3, 4), (side * rows_dev, (side + 1) * rows_dev), self.late, start)
+            for side in (1, 0)
+        ]
+
+    def scatter(self, spot, flipped, own, mate):
+        p1, p2, p3, p4, p5, p6 = self.routes()
+        to_last, to_plane, rest_plane = scattered_sums(flipped, own, mate, (4, 3), [[BF16], [BF16, F32]])
+        by_sixth = self.sent(to_last, {**p4, **p6}, back=True)
+        by_fifth = self.sent(to_plane, p5, back=True)
+        kept, to_first, to_second = scattered_sums(flipped, own, mate, (0, 1, 2), [[F32]] * 3)
+        out_third = summed_terms(spot, [rest_plane, by_sixth], [self.EVEN, self.MIDDLE])
+        by_third = self.sent(out_third, p3, back=True)
+        out_second = summed_terms(spot, [to_second, by_fifth], [None, 0b00001010])
+        by_second = self.sent(out_second, p2, back=True)
+        out_first = summed_terms(
+            spot, [to_first, by_third, by_sixth], [None, self.EVEN | 0b00101000, self.ENDS]
+        )
+        by_first = self.sent(out_first, p1, back=True)
+        return to_last, lambda: summed_terms(spot, [kept, by_second, by_first])
 
 
 def local(features, tile_list, tile_count, tile_values, weight, bias, grad_out):
@@ -229,47 +354,37 @@
     me = lax.axis_index("blk")
     window = tile_values.shape[1]
     reach = window // 4
-    positions = 2 * reach + 1
     rows_dev, hidden = features.shape
-    plane, plane_bits = 4, 2
+    plane = 4
     pieces = 2 * plane
     core = (me % 2).astype(jnp.int32).reshape(1)
     place = ((me // 2) % plane).astype(jnp.int32).reshape(1)
-
-    def moved(value, chips, even_only=False):
-        pairs = [(s, (s + 2 * chips) % count) for s in range(count) if not (even_only and s % 2)]
-        return lax.ppermute(value, "blk", pairs)
+    spot = (me % pieces).astype(jnp.int32).reshape(1)
+    route = Relayed(count) if reach == 2 else Direct(count, reach)
 
     def swapped(value, distance):
         return lax.ppermute(value, "blk", [(s, s ^ distance) for s in range(count)])
 
-    sources = [
-        features if m == reach else moved(features, reach - m, m == positions - 1) for m in range(positions)
-    ]
+    first = route.gather(features)
+    first, tile_list, tile_count, tile_values = lax.optimization_barrier((first, tile_list, tile_count, tile_values))
     meta = jnp.concatenate([tile_list[0].reshape(window, -1), tile_count[0][:, None]], axis=1).reshape(-1)
     mate_meta, mate_values = swapped(meta, 1), swapped(tile_values[0], 1)
-    dense, flipped = dense_tiles(core, meta, mate_meta, tile_values[0], mate_values, rows_dev, positions)
-    mate_sum = swapped(gathered_sums(dense, sources, 1), 1)
-    own_sum = gathered_sums(dense, sources, 0)
-    agg, output, grad_pre, grad_agg = layer(own_sum, mate_sum, weight, bias, grad_out)
+    dense, flipped = dense_tiles(spot, meta, mate_meta, tile_values[0], mate_values, rows_dev, route.table)
+    mate_sum, own_sum = route.sums(spot, dense, rows_dev)
+    agg, output, grad_pre, grad_agg = layer(own_sum, swapped(mate_sum, 1), weight, bias, grad_out)
     mate_grad = swapped(grad_agg, 1)
 
     keep, give = weight_terms(core, agg, grad_pre, pieces)
-    terms = scattered_sums(flipped, grad_agg, mate_grad)
-    arrived = [
-        moved(terms[m], m - reach, m == positions - 1) for m in range(positions) if m != reach
-    ]
-
-    got, *terms = lax.optimization_barrier((swapped(give, 1), *terms))
+    first_sent, finish = route.scatter(spot, flipped, grad_agg, mate_grad)
+    got, first_sent = lax.optimization_barrier((swapped(give, 1), first_sent))
     own_piece, *give_pieces = spread_halves(place, keep, got)
-    plane_sum = summed_terms(own_piece, [swapped(v, 2 * (d + 1)) for d, v in enumerate(give_pieces)])
+    plane_sum = summed_terms(spot, [own_piece] + [swapped(v, 2 * (d + 1)) for d, v in enumerate(give_pieces)])
     group = count // pieces
     values = [plane_sum] + [swapped(plane_sum, pieces * d) for d in range(1, group)]
     piece_sum, bias_sum = summed_planes(values, hidden // pieces)
     half = joined(place, [piece_sum] + [swapped(piece_sum, 2 * d) for d in range(1, plane)])
     grad_weight = whole_weight(core, half, swapped(half, 1))
-    grad_features = summed_terms(terms[reach], arrived)
-    return (output, grad_features, grad_weight, bias_sum[0])
+    return (output, finish(), grad_weight, bias_sum[0])
 
 
 def solution(mesh):

time: 90.2 us -> 104 us (1.15)
  waiting for transfers between devices: 39 us -> 24.4 us
  local copies, waits for them, and re-layouts: 4.8 us -> 14.8 us
  starting transfers between devices: 31.2 us -> 40.6 us
  Pallas kernels: 13.3 us -> 22.3 us
    ppermute x15, waiting for transfers between devices: 28 us -> 14.1 us  [swapped(): return lax.ppermute(value, 'blk', [(s, s ^ distance) for s in range(count)])]
    unnamed x14 -> x38, local copies, waits for them, and re-layouts: 3.35 us -> 13.4 us
    ppermute x8 -> x11, starting transfers between devices: 18.5 us -> 28.3 us  [sent(): lax.ppermute(value, 'blk', [(b, a) if back else (a, b) for a, b in pairs])]
    pallas_call x12 -> x17, Pallas kernels: 13.3 us -> 22.3 us  [call(): pl.pallas_call(kernel, out_shape=out_shape, in_specs=[spec(k) for k in ra...]
    ppermute x8 -> x11, waiting for transfers between devices: 11 us -> 10.2 us  [sent(): lax.ppermute(value, 'blk', [(b, a) if back else (a, b) for a, b in pairs])]
  transfers between devices with their start and end apart: 23 -> 26, of which waited for: 12 -> 12; matrix products, arithmetic and copies ran while one was open for 2% -> 2% of each run, Pallas kernels for 11% -> 16%
where the time goes in v3:
time: 104 us
  starting transfers between devices  40.6 us (39%)
  waiting for transfers between devices  24.4 us (23%)
  Pallas kernels  22.3 us (21%)
  local copies, waits for them, and re-layouts  14.8 us (14%)
    ppermute x11, starting transfers between devices, sent(): lax.ppermute(value, 'blk', [(b, a) if back else (a, b) for a, b in pairs])  28.3 us
    pallas_call x17, Pallas kernels, call(): pl.pallas_call(kernel, out_shape=out_shape, in_specs=[spec(k) for k in ra...  22.3 us
    ppermute x15, waiting for transfers between devices, swapped(): return lax.ppermute(value, 'blk', [(s, s ^ distance) for s in range(count)])  14.1 us
    unnamed x38, local copies, waits for them, and re-layouts  13.4 us
    ppermute x15, starting transfers between devices, swapped(): return lax.ppermute(value, 'blk', [(s, s ^ distance) for s in range(count)])  12.3 us
    ppermute x11, waiting for transfers between devices, sent(): lax.ppermute(value, 'blk', [(b, a) if back else (a, b) for a, b in pairs])  10.2 us
  transfers between devices with their start and end apart: 26, of which 12 were waited for; matrix products, arithmetic and copies ran while one was open for 2% of the time, Pallas kernels for 16%

profile of v3, /device:TPU:0, one launch (start us, length us, event | category | flops | bytes accessed | tf_op | source)
XLA Modules:
  0.0 103.7 jit_solution(17681698801165370586)
XLA Ops:
  0.6 3.0 %collective-permute-start = (bf16[384,512]{1,0:T(8,128)(2,1)}, bf16[384,512]{1,0:T(8,128)(2,1)}, u32[]{:S(2)}, u32[]{:S(2)}) collective-permute-start(bf16[384,512]{1,0:T(8,128)(2,1)} %refs_0_.1), channel_id=1, source_target_pairs={{0,4},{1,3},{2,6},{3,1},{4,0},{5,7},{6,2},{7,5},{8,12},{9,11},{10,... | collective-permute-start | bytes 1179656 | tf_op jit(solution)/shard_map/ppermute | solution.py:301
  3.7 6.1 %collective-permute-done.refs_1_ = bf16[384,512]{1,0:T(8,128)(2,1)} collective-permute-done((bf16[384,512]{1,0:T(8,128)(2,1)}, bf16[384,512]{1,0:T(8,128)(2,1)}, u32[]{:S(2)}, u32[]{:S(2)}) %collective-permute-start) | collective-permute-done | bytes 393248 | tf_op jit(solution)/shard_map/ppermute | solution.py:301
  9.7 2.0 %collective-permute-start.3 = (bf16[384,512]{1,0:T(8,128)(2,1)}, bf16[384,512]{1,0:T(8,128)(2,1)}, u32[]{:S(2)}, u32[]{:S(2)}) collective-permute-start(bf16[384,512]{1,0:T(8,128)(2,1)} %refs_0_.1), channel_id=1, source_target_pairs={{0,2},{1,5},{2,0},{3,7},{4,6},{5,1},{6,4},{7,3},{8,10},{9,13},{10,... | collective-permute-start | bytes 1179656 | tf_op jit(solution)/shard_map/ppermute | solution.py:301
  11.7 3.5 %collective-permute-start.4 = (bf16[384,512]{1,0:T(8,128)(2,1)}, bf16[384,512]{1,0:T(8,128)(2,1)S(1)}, u32[]{:S(2)}, u32[]{:S(2)}) collective-permute-start(bf16[384,512]{1,0:T(8,128)(2,1)} %collective-permute-done.refs_1_), channel_id=1, source_target_pairs={{0,8},{2,10},{3,27},{4,28},{5,13},{6,30},{8,16},{10,18},{11,3},{12... | collective-permute-start | bytes 1179656 | tf_op jit(solution)/shard_map/ppermute | solution.py:301
  15.2 3.2 %collective-permute-start.6 = (bf16[384,512]{1,0:T(8,128)(2,1)}, bf16[384,512]{1,0:T(8,128)(2,1)}, u32[]{:S(2)}, u32[]{:S(2)}) collective-permute-start(bf16[384,512]{1,0:T(8,128)(2,1)} %collective-permute-done.refs_1_), channel_id=1, source_target_pairs={{0,2},{1,5},{6,4},{7,3},{8,10},{9,13},{14,12},{15,11},{16,18},{17,... | collective-permute-start | bytes 1179656 | tf_op jit(solution)/shard_map/ppermute | solution.py:301
  18.4 1.4 %collective-permute-start.5 = (bf16[384,512]{1,0:T(8,128)(2,1)}, bf16[384,512]{1,0:T(8,128)(2,1)}, u32[]{:S(2)}, u32[]{:S(2)}) collective-permute-start(bf16[384,512]{1,0:T(8,128)(2,1)} %collective-permute-done.3.refs_2_), channel_id=1, source_target_pairs={{1,9},{3,11},{9,17},{11,19},{17,25},{19,27},{25,1},{27,3}} | collective-permute-start | bytes 1179656 | tf_op jit(solution)/shard_map/ppermute | solution.py:301
  19.8 3.6 %collective-permute-done.4.refs_1_ = bf16[384,512]{1,0:T(8,128)(2,1)S(1)} collective-permute-done((bf16[384,512]{1,0:T(8,128)(2,1)}, bf16[384,512]{1,0:T(8,128)(2,1)S(1)}, u32[]{:S(2)}, u32[]{:S(2)}) %collective-permute-start.4) | collective-permute-done | bytes 393248 | tf_op jit(solution)/shard_map/ppermute | solution.py:301
  23.4 1.3 %collective-permute-start.7 = (bf16[384,512]{1,0:T(8,128)(2,1)S(1)}, bf16[384,512]{1,0:T(8,128)(2,1)}, u32[]{:S(2)}, u32[]{:S(2)}) collective-permute-start(bf16[384,512]{1,0:T(8,128)(2,1)S(1)} %collective-permute-done.4.refs_1_), channel_id=1, source_target_pairs={{2,0},{3,7},{4,6},{5,1},{10,8},{11,15},{12,14},{13,9},{18,16},{19,... | collective-permute-start | bytes 1179656 | tf_op jit(solution)/shard_map/ppermute | solution.py:301
  28.6 1.5 %copy-done = bf16[1,8,7,128,128]{4,3,2,1,0:T(8,128)(2,1)S(1)} copy-done((bf16[1,8,7,128,128]{4,3,2,1,0:T(8,128)(2,1)S(1)}, bf16[1,8,7,128,128]{4,3,2,1,0:T(8,128)(2,1)}, u32[]{:S(2)}) %copy-start) | copy-done | bytes 1835032
  30.1 1.5 %copy-done.2 = bf16[8,7,128,128]{3,2,1,0:T(8,128)(2,1)S(1)} copy-done((bf16[8,7,128,128]{3,2,1,0:T(8,128)(2,1)S(1)}, bf16[8,7,128,128]{3,2,1,0:T(8,128)(2,1)}, u32[]{:S(2)}) %copy-start.2) | copy-done | bytes 1835032
  32.3 3.7 %shard_map.111 = (bf16[768,1920]{1,0:T(8,128)(2,1)S(1)}, bf16[1920,768]{1,0:T(8,128)(2,1)S(1)}) custom-call(s32[1]{0:T(128)} %bitcast.spot_ref, s32[40]{0:T(128)S(1)} %copy-done.17, s32[120]{0:T(128)S(1)} %reshape.28.own_meta_ref, s32[120]{0:T(128)S(1)} %collective-permute-done.1.mate_meta_ref, bf16[8,7,128,128]{3,2,1,0:T(8,128)(2,1)S(1)} %bitcast.10, ...), custom_call_target="tpu_custom_call" | custom-call | bytes 9569380 | tf_op jit(solution)/shard_map/pallas_call | solution.py:16
  36.0 2.5 %shard_map.112.refs_0_ = f32[768,512]{1,0:T(8,128)S(1)} custom-call(s32[1]{0:T(128)} %bitcast.spot_ref, bf16[768,1920]{1,0:T(8,128)(2,1)S(1)} %get-tuple-element.31.dense_ref, bf16[384,512]{1,0:T(8,128)(2,1)S(1)} %copy-done.10, bf16[384,512]{1,0:T(8,128)(2,1)} %collective-permute-done.refs_1_, bf16[384,512]{1,0:T(8,128)(2,1)} %collective-permute-done.3.refs_2_), custom_call_target="tpu_custom_call" | custom-call | flops 905969664 | bytes 5701636 | tf_op jit(solution)/shard_map/pallas_call | solution.py:16
  38.5 1.8 %shard_map.114 = f32[384,512]{1,0:T(8,128)S(1)} custom-call(s32[1]{0:T(128)} %bitcast.spot_ref, bf16[768,1920]{1,0:T(8,128)(2,1)S(1)} %get-tuple-element.31.dense_ref, f32[768,512]{1,0:T(8,128)S(1)} %shard_map.112.refs_0_, bf16[384,512]{1,0:T(8,128)(2,1)S(1)} %collective-permute-done.4.refs_1_, bf16[384,512]{1,0:T(8,128)(2,1)} %collective-permute-done.5.refs_2_, ...), custom_call_target="tpu_custom_call" | custom-call | flops 301989888 | bytes 6881284 | tf_op jit(solution)/shard_map/pallas_call | solution.py:16
  40.7 1.8 %shard_map.113.own_ref = f32[384,512]{1,0:T(8,128)S(1)} custom-call(s32[1]{0:T(128)} %bitcast.spot_ref, bf16[768,1920]{1,0:T(8,128)(2,1)S(1)} %get-tuple-element.31.dense_ref, f32[768,512]{1,0:T(8,128)S(1)} %shard_map.112.refs_0_, bf16[384,512]{1,0:T(8,128)(2,1)S(1)} %collective-permute-done.4.refs_1_, bf16[384,512]{1,0:T(8,128)(2,1)} %collective-permute-done.5.refs_2_, ...), custom_call_target="tpu_custom_call" | custom-call | flops 301989888 | bytes 6881284 | tf_op jit(solution)/shard_map/pallas_call | solution.py:16
  42.7 1.3 %shard_map.115 = (bf16[384,512]{1,0:T(8,128)(2,1)S(1)}, bf16[384,512]{1,0:T(8,128)(2,1)}, bf16[384,512]{1,0:T(8,128)(2,1)S(1)}, bf16[384,512]{1,0:T(8,128)(2,1)S(1)}) custom-call(f32[384,512]{1,0:T(8,128)S(1)} %shard_map.113.own_ref, f32[384,512]{1,0:T(8,128)S(1)} %collective-permute-done.8.mate_ref, bf16[512,512]{1,0:T(8,128)(2,1)S(1)} %copy-done.9, ...), custom_call_target="tpu_custom_call" | custom-call | flops 402653184 | bytes 4065280 | tf_op jit(solution)/shard_map/pallas_call | solution.py:16
  45.1 1.4 %collective-permute-done.9.mate_ref = bf16[384,512]{1,0:T(8,128)(2,1)S(1)} collective-permute-done((bf16[384,512]{1,0:T(8,128)(2,1)S(1)}, bf16[384,512]{1,0:T(8,128)(2,1)S(1)}, u32[]{:S(2)}, u32[]{:S(2)}) %collective-permute-start.9) | collective-permute-done | bytes 393248 | tf_op jit(solution)/shard_map/ppermute | solution.py:366
  46.5 1.3 %shard_map.117 = (bf16[384,512]{1,0:T(8,128)(2,1)}, bf16[384,512]{1,0:T(8,128)(2,1)S(1)}, f32[384,512]{1,0:T(8,128)S(1)}) custom-call(bf16[1920,768]{1,0:T(8,128)(2,1)S(1)} %get-tuple-element.33.flipped_ref, bf16[384,512]{1,0:T(8,128)(2,1)S(1)} %get-tuple-element.34.own_ref, bf16[384,512]{1,0:T(8,128)(2,1)S(1)} %collective-permute-done.9.mate_ref), custom_call_target="tpu_custom_call" | custom-call | flops 603979776 | bytes 5308416 | tf_op jit(solution)/shard_map/pallas_call | solution.py:16
  49.5 5.0 %collective-permute-start.12 = (bf16[384,512]{1,0:T(8,128)(2,1)}, bf16[384,512]{1,0:T(8,128)(2,1)}, u32[]{:S(2)}, u32[]{:S(2)}) collective-permute-start(bf16[384,512]{1,0:T(8,128)(2,1)} %get-tuple-element.40), channel_id=1, source_target_pairs={{2,0},{5,1},{0,2},{7,3},{6,4},{1,5},{4,6},{3,7},{10,8},{13,9},{8,1... | collective-permute-start | bytes 1179656 | tf_op jit(solution)/shard_map/ppermute | solution.py:301
  58.5 1.4 %collective-permute-start.10 = (bf16[384,512]{1,0:T(8,128)(2,1)}, bf16[384,512]{1,0:T(8,128)(2,1)}, u32[]{:S(2)}, u32[]{:S(2)}) collective-permute-start(bf16[384,512]{1,0:T(8,128)(2,1)} %copy-done.18), channel_id=1, source_target_pairs={{9,1},{11,3},{17,9},{19,11},{25,17},{27,19},{1,25},{3,27}} | collective-permute-start | bytes 1179656 | tf_op jit(solution)/shard_map/ppermute | solution.py:301
  61.7 1.9 %shard_map.119 = bf16[384,512]{1,0:T(8,128)(2,1)} custom-call(s32[1]{0:T(128)} %bitcast.spot_ref, f32[384,512]{1,0:T(8,128)S(1)} %copy-done.6, bf16[384,512]{1,0:T(8,128)(2,1)} %collective-permute-done.12.refs_1_.refs_2_), custom_call_target="tpu_custom_call" | custom-call | bytes 1572868 | tf_op jit(solution)/shard_map/pallas_call | solution.py:16
  63.5 5.2 %collective-permute-start.13 = (bf16[384,512]{1,0:T(8,128)(2,1)}, bf16[384,512]{1,0:T(8,128)(2,1)}, u32[]{:S(2)}, u32[]{:S(2)}) collective-permute-start(bf16[384,512]{1,0:T(8,128)(2,1)} %shard_map.119), channel_id=1, source_target_pairs={{8,0},{10,2},{27,3},{28,4},{13,5},{30,6},{16,8},{18,10},{3,11},{4,... | collective-permute-start | bytes 1179656 | tf_op jit(solution)/shard_map/ppermute | solution.py:301
  70.9 2.1 %collective-permute-start.16 = (bf16[80,512]{1,0:T(8,128)(2,1)S(1)}, bf16[80,512]{1,0:T(8,128)(2,1)S(1)}, u32[]{:S(2)}, u32[]{:S(2)}) collective-permute-start(bf16[80,512]{1,0:T(8,128)(2,1)S(1)} %get-tuple-element.47), channel_id=1, source_target_pairs={{0,2},{1,3},{2,0},{3,1},{4,6},{5,7},{6,4},{7,5},{8,10},{9,11},{10,... | collective-permute-start | bytes 245768 | tf_op jit(solution)/shard_map/ppermute | solution.py:366
  73.0 1.5 %collective-permute-start.18 = (bf16[80,512]{1,0:T(8,128)(2,1)S(1)}, bf16[80,512]{1,0:T(8,128)(2,1)S(1)}, u32[]{:S(2)}, u32[]{:S(2)}) collective-permute-start(bf16[80,512]{1,0:T(8,128)(2,1)S(1)} %get-tuple-element.49), channel_id=1, source_target_pairs={{0,6},{1,7},{2,4},{3,5},{4,2},{5,3},{6,0},{7,1},{8,14},{9,15},{10,... | collective-permute-start | bytes 245768 | tf_op jit(solution)/shard_map/ppermute | solution.py:366
  74.6 1.7 %collective-permute-done.16.refs_1_ = bf16[80,512]{1,0:T(8,128)(2,1)S(1)} collective-permute-done((bf16[80,512]{1,0:T(8,128)(2,1)S(1)}, bf16[80,512]{1,0:T(8,128)(2,1)S(1)}, u32[]{:S(2)}, u32[]{:S(2)}) %collective-permute-start.16) | collective-permute-done | bytes 81952 | tf_op jit(solution)/shard_map/ppermute | solution.py:366
  78.4 1.5 %collective-permute-start.21 = (bf16[80,512]{1,0:T(8,128)(2,1)S(1)}, bf16[80,512]{1,0:T(8,128)(2,1)S(1)}, u32[]{:S(2)}, u32[]{:S(2)}) collective-permute-start(bf16[80,512]{1,0:T(8,128)(2,1)S(1)} %shard_map.124.refs_0_), channel_id=1, source_target_pairs={{0,24},{1,25},{2,26},{3,27},{4,28},{5,29},{6,30},{7,31},{8,16},{9,... | collective-permute-start | bytes 245768 | tf_op jit(solution)/shard_map/ppermute | solution.py:366
  79.9 2.9 %collective-permute-start.19 = (bf16[80,512]{1,0:T(8,128)(2,1)S(1)}, bf16[80,512]{1,0:T(8,128)(2,1)S(1)}, u32[]{:S(2)}, u32[]{:S(2)}) collective-permute-start(bf16[80,512]{1,0:T(8,128)(2,1)S(1)} %shard_map.124.refs_0_), channel_id=1, source_target_pairs={{0,8},{1,9},{2,10},{3,11},{4,12},{5,13},{6,14},{7,15},{8,0},{9,1},... | collective-permute-start | bytes 245768 | tf_op jit(solution)/shard_map/ppermute | solution.py:366
  83.9 1.4 %shard_map.116 = (f32[384,512]{1,0:T(8,128)S(1)}, f32[384,512]{1,0:T(8,128)S(1)}, f32[384,512]{1,0:T(8,128)S(1)}) custom-call(bf16[1920,768]{1,0:T(8,128)(2,1)S(1)} %get-tuple-element.33.flipped_ref, bf16[384,512]{1,0:T(8,128)(2,1)S(1)} %get-tuple-element.34.own_ref, bf16[384,512]{1,0:T(8,128)(2,1)S(1)} %copy-done.4), custom_call_target="tpu_custom_call" | custom-call | flops 905969664 | bytes 6094848 | tf_op jit(solution)/shard_map/pallas_call | solution.py:16
  87.1 1.3 %shard_map.120 = bf16[384,512]{1,0:T(8,128)(2,1)S(1)} custom-call(s32[1]{0:T(128)} %bitcast.spot_ref, f32[384,512]{1,0:T(8,128)S(1)} %get-tuple-element.38.refs_0_, bf16[384,512]{1,0:T(8,128)(2,1)} %collective-permute-done.13.refs_1_, bf16[384,512]{1,0:T(8,128)(2,1)} %collective-permute-done.12.refs_1_.refs_2_), custom_call_target="tpu_custom_call" | custom-call | bytes 1966084 | tf_op jit(solution)/shard_map/pallas_call | solution.py:16
  88.4 1.4 %collective-permute-start.14 = (bf16[384,512]{1,0:T(8,128)(2,1)S(1)}, bf16[384,512]{1,0:T(8,128)(2,1)S(1)}, u32[]{:S(2)}, u32[]{:S(2)}) collective-permute-start(bf16[384,512]{1,0:T(8,128)(2,1)S(1)} %shard_map.120), channel_id=1, source_target_pairs={{4,0},{3,1},{6,2},{1,3},{0,4},{7,5},{2,6},{5,7},{12,8},{11,9},{14,... | collective-permute-start | bytes 1179656 | tf_op jit(solution)/shard_map/ppermute | solution.py:301
  89.9 1.5 %collective-permute-start.24 = (bf16[64,512]{1,0:T(8,128)(2,1)S(1)}, bf16[64,512]{1,0:T(8,128)(2,1)S(1)}, u32[]{:S(2)}, u32[]{:S(2)}) collective-permute-start(bf16[64,512]{1,0:T(8,128)(2,1)S(1)} %get-tuple-element.50.refs_0_), channel_id=1, source_target_pairs={{0,6},{1,7},{2,4},{3,5},{4,2},{5,3},{6,0},{7,1},{8,14},{9,15},{10,... | collective-permute-start | bytes 196616 | tf_op jit(solution)/shard_map/ppermute | solution.py:366
  91.4 2.0 %collective-permute-start.23 = (bf16[64,512]{1,0:T(8,128)(2,1)S(1)}, bf16[64,512]{1,0:T(8,128)(2,1)S(1)}, u32[]{:S(2)}, u32[]{:S(2)}) collective-permute-start(bf16[64,512]{1,0:T(8,128)(2,1)S(1)} %get-tuple-element.50.refs_0_), channel_id=1, source_target_pairs={{0,4},{1,5},{2,6},{3,7},{4,0},{5,1},{6,2},{7,3},{8,12},{9,13},{10,... | collective-permute-start | bytes 196616 | tf_op jit(solution)/shard_map/ppermute | solution.py:366
  93.5 5.9 %collective-permute-done.24.refs_3_ = bf16[64,512]{1,0:T(8,128)(2,1)S(1)} collective-permute-done((bf16[64,512]{1,0:T(8,128)(2,1)S(1)}, bf16[64,512]{1,0:T(8,128)(2,1)S(1)}, u32[]{:S(2)}, u32[]{:S(2)}) %collective-permute-start.24) | collective-permute-done | bytes 65568 | tf_op jit(solution)/shard_map/ppermute | solution.py:366
  (80 shorter events, 25.2 us)
Async XLA Ops:
  0.6 9.1 %collective-permute-start = (bf16[384,512]{1,0:T(8,128)(2,1)}, bf16[384,512]{1,0:T(8,128)(2,1)}, u32[]{:S(2)}, u32[]{:S(2)}) collective-permute-start(bf16[384,512]{1,0:T(8,128)(2,1)} %refs_0_.1), channel_id=1, source_target_pairs={{0,4},{1,3},{2,6},{3,1},{4,0},{5,7},{6,2},{7,5},{8,12},{9,11},{10,... | collective-permute-start | bytes 1179656 | tf_op jit(solution)/shard_map/ppermute | solution.py:301
  9.7 17.6 %collective-permute-start.2 = (bf16[8,7,128,128]{3,2,1,0:T(8,128)(2,1)}, bf16[8,7,128,128]{3,2,1,0:T(8,128)(2,1)S(1)}, u32[]{:S(2)}, u32[]{:S(2)}) collective-permute-start(bf16[8,7,128,128]{3,2,1,0:T(8,128)(2,1)} %bitcast.9), channel_id=1, source_target_pairs={{0,1},{1,0},{2,3},{3,2},{4,5},{5,4},{6,7},{7,6},{8,9},{9,8},{10,11... | collective-permute-start | bytes 5505032 | tf_op jit(solution)/shard_map/ppermute | solution.py:366
  9.7 8.7 %collective-permute-start.3 = (bf16[384,512]{1,0:T(8,128)(2,1)}, bf16[384,512]{1,0:T(8,128)(2,1)}, u32[]{:S(2)}, u32[]{:S(2)}) collective-permute-start(bf16[384,512]{1,0:T(8,128)(2,1)} %refs_0_.1), channel_id=1, source_target_pairs={{0,2},{1,5},{2,0},{3,7},{4,6},{5,1},{6,4},{7,3},{8,10},{9,13},{10,... | collective-permute-start | bytes 1179656 | tf_op jit(solution)/shard_map/ppermute | solution.py:301
  11.7 11.7 %collective-permute-start.4 = (bf16[384,512]{1,0:T(8,128)(2,1)}, bf16[384,512]{1,0:T(8,128)(2,1)S(1)}, u32[]{:S(2)}, u32[]{:S(2)}) collective-permute-start(bf16[384,512]{1,0:T(8,128)(2,1)} %collective-permute-done.refs_1_), channel_id=1, source_target_pairs={{0,8},{2,10},{3,27},{4,28},{5,13},{6,30},{8,16},{10,18},{11,3},{12... | collective-permute-start | bytes 1179656 | tf_op jit(solution)/shard_map/ppermute | solution.py:301
  15.2 23.3 %collective-permute-start.6 = (bf16[384,512]{1,0:T(8,128)(2,1)}, bf16[384,512]{1,0:T(8,128)(2,1)}, u32[]{:S(2)}, u32[]{:S(2)}) collective-permute-start(bf16[384,512]{1,0:T(8,128)(2,1)} %collective-permute-done.refs_1_), channel_id=1, source_target_pairs={{0,2},{1,5},{6,4},{7,3},{8,10},{9,13},{14,12},{15,11},{16,18},{17,... | collective-permute-start | bytes 1179656 | tf_op jit(solution)/shard_map/ppermute | solution.py:301
  18.4 20.1 %collective-permute-start.5 = (bf16[384,512]{1,0:T(8,128)(2,1)}, bf16[384,512]{1,0:T(8,128)(2,1)}, u32[]{:S(2)}, u32[]{:S(2)}) collective-permute-start(bf16[384,512]{1,0:T(8,128)(2,1)} %collective-permute-done.3.refs_2_), channel_id=1, source_target_pairs={{1,9},{3,11},{9,17},{11,19},{17,25},{19,27},{25,1},{27,3}} | collective-permute-start | bytes 1179656 | tf_op jit(solution)/shard_map/ppermute | solution.py:301
  23.4 15.1 %collective-permute-start.7 = (bf16[384,512]{1,0:T(8,128)(2,1)S(1)}, bf16[384,512]{1,0:T(8,128)(2,1)}, u32[]{:S(2)}, u32[]{:S(2)}) collective-permute-start(bf16[384,512]{1,0:T(8,128)(2,1)S(1)} %collective-permute-done.4.refs_1_), channel_id=1, source_target_pairs={{2,0},{3,7},{4,6},{5,1},{10,8},{11,15},{12,14},{13,9},{18,16},{19,... | collective-permute-start | bytes 1179656 | tf_op jit(solution)/shard_map/ppermute | solution.py:301
  26.2 1.1 %collective-permute-start.1 = (s32[120]{0:T(128)S(1)}, s32[120]{0:T(128)S(1)}, u32[]{:S(2)}, u32[]{:S(2)}) collective-permute-start(s32[120]{0:T(128)S(1)} %reshape.28.own_meta_ref), channel_id=1, source_target_pairs={{0,1},{1,0},{2,3},{3,2},{4,5},{5,4},{6,7},{7,6},{8,9},{9,8},{10,11... | collective-permute-start | bytes 1448 | tf_op jit(solution)/shard_map/ppermute | solution.py:366
  28.6 1.5 %copy-start = (bf16[1,8,7,128,128]{4,3,2,1,0:T(8,128)(2,1)S(1)}, bf16[1,8,7,128,128]{4,3,2,1,0:T(8,128)(2,1)}, u32[]{:S(2)}) copy-start(bf16[1,8,7,128,128]{4,3,2,1,0:T(8,128)(2,1)} %param.11) | copy-start | bytes 5505028
  32.3 3.7 %copy-start.10 = (bf16[384,512]{1,0:T(8,128)(2,1)S(1)}, bf16[384,512]{1,0:T(8,128)(2,1)}, u32[]{:S(2)}) copy-start(bf16[384,512]{1,0:T(8,128)(2,1)} %refs_0_.1) | copy-start | bytes 1179652
  40.3 2.4 %copy-start.9 = (bf16[512,512]{1,0:T(8,128)(2,1)S(1)}, bf16[512,512]{1,0:T(8,128)(2,1)}, u32[]{:S(2)}) copy-start(bf16[512,512]{1,0:T(8,128)(2,1)} %weight_ref.1) | copy-start | bytes 1572868
  40.3 2.4 %copy-start.15 = (bf16[384,512]{1,0:T(8,128)(2,1)S(1)}, bf16[384,512]{1,0:T(8,128)(2,1)}, u32[]{:S(2)}) copy-start(bf16[384,512]{1,0:T(8,128)(2,1)} %grad_out_ref.1) | copy-start | bytes 1179652
  40.3 2.4 %copy-start.16 = (f32[512]{0:T(512)S(1)}, f32[512]{0:T(512)}, u32[]{:S(2)}) copy-start(f32[512]{0:T(512)} %param.13) | copy-start | bytes 6148
  40.4 2.4 %collective-permute-start.8 = (f32[384,512]{1,0:T(8,128)S(1)}, f32[384,512]{1,0:T(8,128)S(1)}, u32[]{:S(2)}, u32[]{:S(2)}) collective-permute-start(f32[384,512]{1,0:T(8,128)S(1)} %shard_map.114), channel_id=1, source_target_pairs={{0,1},{1,0},{2,3},{3,2},{4,5},{5,4},{6,7},{7,6},{8,9},{9,8},{10,11... | collective-permute-start | bytes 2359304 | tf_op jit(solution)/shard_map/ppermute | solution.py:366
  44.8 3.1 %copy-start.13 = (bf16[384,512]{1,0:T(8,128)(2,1)}, bf16[384,512]{1,0:T(8,128)(2,1)S(1)}, u32[]{:S(2)}) copy-start(bf16[384,512]{1,0:T(8,128)(2,1)S(1)} %get-tuple-element.42.gp_ref) | copy-start | bytes 1179652
  44.8 1.7 %collective-permute-start.9 = (bf16[384,512]{1,0:T(8,128)(2,1)S(1)}, bf16[384,512]{1,0:T(8,128)(2,1)S(1)}, u32[]{:S(2)}, u32[]{:S(2)}) collective-permute-start(bf16[384,512]{1,0:T(8,128)(2,1)S(1)} %get-tuple-element.34.own_ref), channel_id=1, source_target_pairs={{0,1},{1,0},{2,3},{3,2},{4,5},{5,4},{6,7},{7,6},{8,9},{9,8},{10,11... | collective-permute-start | bytes 1179656 | tf_op jit(solution)/shard_map/ppermute | solution.py:366
  49.5 11.1 %collective-permute-start.12 = (bf16[384,512]{1,0:T(8,128)(2,1)}, bf16[384,512]{1,0:T(8,128)(2,1)}, u32[]{:S(2)}, u32[]{:S(2)}) collective-permute-start(bf16[384,512]{1,0:T(8,128)(2,1)} %get-tuple-element.40), channel_id=1, source_target_pairs={{2,0},{5,1},{0,2},{7,3},{6,4},{1,5},{4,6},{3,7},{10,8},{13,9},{8,1... | collective-permute-start | bytes 1179656 | tf_op jit(solution)/shard_map/ppermute | solution.py:301
  58.5 10.3 %collective-permute-start.15 = (bf16[4,80,512]{2,1,0:T(8,128)(2,1)}, bf16[4,80,512]{2,1,0:T(8,128)(2,1)}, u32[]{:S(2)}, u32[]{:S(2)}) collective-permute-start(bf16[4,80,512]{2,1,0:T(8,128)(2,1)} %get-tuple-element.44), channel_id=1, source_target_pairs={{0,1},{1,0},{2,3},{3,2},{4,5},{5,4},{6,7},{7,6},{8,9},{9,8},{10,11... | collective-permute-start | bytes 983048 | tf_op jit(solution)/shard_map/ppermute | solution.py:366
  58.5 26.7 %collective-permute-start.10 = (bf16[384,512]{1,0:T(8,128)(2,1)}, bf16[384,512]{1,0:T(8,128)(2,1)}, u32[]{:S(2)}, u32[]{:S(2)}) collective-permute-start(bf16[384,512]{1,0:T(8,128)(2,1)} %copy-done.18), channel_id=1, source_target_pairs={{9,1},{11,3},{17,9},{19,11},{25,17},{27,19},{1,25},{3,27}} | collective-permute-start | bytes 1179656 | tf_op jit(solution)/shard_map/ppermute | solution.py:301
  63.5 23.6 %collective-permute-start.13 = (bf16[384,512]{1,0:T(8,128)(2,1)}, bf16[384,512]{1,0:T(8,128)(2,1)}, u32[]{:S(2)}, u32[]{:S(2)}) collective-permute-start(bf16[384,512]{1,0:T(8,128)(2,1)} %shard_map.119), channel_id=1, source_target_pairs={{8,0},{10,2},{27,3},{28,4},{13,5},{30,6},{16,8},{18,10},{3,11},{4,... | collective-permute-start | bytes 1179656 | tf_op jit(solution)/shard_map/ppermute | solution.py:301
  70.9 5.3 %collective-permute-start.16 = (bf16[80,512]{1,0:T(8,128)(2,1)S(1)}, bf16[80,512]{1,0:T(8,128)(2,1)S(1)}, u32[]{:S(2)}, u32[]{:S(2)}) collective-permute-start(bf16[80,512]{1,0:T(8,128)(2,1)S(1)} %get-tuple-element.47), channel_id=1, source_target_pairs={{0,2},{1,3},{2,0},{3,1},{4,6},{5,7},{6,4},{7,5},{8,10},{9,11},{10,... | collective-permute-start | bytes 245768 | tf_op jit(solution)/shard_map/ppermute | solution.py:366
  73.0 4.4 %collective-permute-start.17 = (bf16[80,512]{1,0:T(8,128)(2,1)S(1)}, bf16[80,512]{1,0:T(8,128)(2,1)S(1)}, u32[]{:S(2)}, u32[]{:S(2)}) collective-permute-start(bf16[80,512]{1,0:T(8,128)(2,1)S(1)} %get-tuple-element.48), channel_id=1, source_target_pairs={{0,4},{1,5},{2,6},{3,7},{4,0},{5,1},{6,2},{7,3},{8,12},{9,13},{10,... | collective-permute-start | bytes 245768 | tf_op jit(solution)/shard_map/ppermute | solution.py:366
  73.0 5.3 %collective-permute-start.18 = (bf16[80,512]{1,0:T(8,128)(2,1)S(1)}, bf16[80,512]{1,0:T(8,128)(2,1)S(1)}, u32[]{:S(2)}, u32[]{:S(2)}) collective-permute-start(bf16[80,512]{1,0:T(8,128)(2,1)S(1)} %get-tuple-element.49), channel_id=1, source_target_pairs={{0,6},{1,7},{2,4},{3,5},{4,2},{5,3},{6,0},{7,1},{8,14},{9,15},{10,... | collective-permute-start | bytes 245768 | tf_op jit(solution)/shard_map/ppermute | solution.py:366
  78.4 11.5 %collective-permute-start.21 = (bf16[80,512]{1,0:T(8,128)(2,1)S(1)}, bf16[80,512]{1,0:T(8,128)(2,1)S(1)}, u32[]{:S(2)}, u32[]{:S(2)}) collective-permute-start(bf16[80,512]{1,0:T(8,128)(2,1)S(1)} %shard_map.124.refs_0_), channel_id=1, source_target_pairs={{0,24},{1,25},{2,26},{3,27},{4,28},{5,29},{6,30},{7,31},{8,16},{9,... | collective-permute-start | bytes 245768 | tf_op jit(solution)/shard_map/ppermute | solution.py:366
  79.9 9.9 %collective-permute-start.20 = (bf16[80,512]{1,0:T(8,128)(2,1)S(1)}, bf16[80,512]{1,0:T(8,128)(2,1)S(1)}, u32[]{:S(2)}, u32[]{:S(2)}) collective-permute-start(bf16[80,512]{1,0:T(8,128)(2,1)S(1)} %shard_map.124.refs_0_), channel_id=1, source_target_pairs={{0,16},{1,17},{2,18},{3,19},{4,20},{5,21},{6,22},{7,23},{8,24},{9,... | collective-permute-start | bytes 245768 | tf_op jit(solution)/shard_map/ppermute | solution.py:366
  79.9 9.9 %collective-permute-start.19 = (bf16[80,512]{1,0:T(8,128)(2,1)S(1)}, bf16[80,512]{1,0:T(8,128)(2,1)S(1)}, u32[]{:S(2)}, u32[]{:S(2)}) collective-permute-start(bf16[80,512]{1,0:T(8,128)(2,1)S(1)} %shard_map.124.refs_0_), channel_id=1, source_target_pairs={{0,8},{1,9},{2,10},{3,11},{4,12},{5,13},{6,14},{7,15},{8,0},{9,1},... | collective-permute-start | bytes 245768 | tf_op jit(solution)/shard_map/ppermute | solution.py:366
  86.3 16.4 %collective-permute-start.11 = (bf16[384,512]{1,0:T(8,128)(2,1)S(1)}, bf16[384,512]{1,0:T(8,128)(2,1)S(1)}, u32[]{:S(2)}, u32[]{:S(2)}) collective-permute-start(bf16[384,512]{1,0:T(8,128)(2,1)S(1)} %shard_map.118), channel_id=1, source_target_pairs={{2,0},{5,1},{0,2},{7,3},{6,4},{1,5},{4,6},{3,7},{10,8},{13,9},{8,1... | collective-permute-start | bytes 1179656 | tf_op jit(solution)/shard_map/ppermute | solution.py:301
  88.4 14.4 %collective-permute-start.14 = (bf16[384,512]{1,0:T(8,128)(2,1)S(1)}, bf16[384,512]{1,0:T(8,128)(2,1)S(1)}, u32[]{:S(2)}, u32[]{:S(2)}) collective-permute-start(bf16[384,512]{1,0:T(8,128)(2,1)S(1)} %shard_map.120), channel_id=1, source_target_pairs={{4,0},{3,1},{6,2},{1,3},{0,4},{7,5},{2,6},{5,7},{12,8},{11,9},{14,... | collective-permute-start | bytes 1179656 | tf_op jit(solution)/shard_map/ppermute | solution.py:301
  89.9 9.4 %collective-permute-start.24 = (bf16[64,512]{1,0:T(8,128)(2,1)S(1)}, bf16[64,512]{1,0:T(8,128)(2,1)S(1)}, u32[]{:S(2)}, u32[]{:S(2)}) collective-permute-start(bf16[64,512]{1,0:T(8,128)(2,1)S(1)} %get-tuple-element.50.refs_0_), channel_id=1, source_target_pairs={{0,6},{1,7},{2,4},{3,5},{4,2},{5,3},{6,0},{7,1},{8,14},{9,15},{10,... | collective-permute-start | bytes 196616 | tf_op jit(solution)/shard_map/ppermute | solution.py:366
  91.4 7.9 %collective-permute-start.23 = (bf16[64,512]{1,0:T(8,128)(2,1)S(1)}, bf16[64,512]{1,0:T(8,128)(2,1)S(1)}, u32[]{:S(2)}, u32[]{:S(2)}) collective-permute-start(bf16[64,512]{1,0:T(8,128)(2,1)S(1)} %get-tuple-element.50.refs_0_), channel_id=1, source_target_pairs={{0,4},{1,5},{2,6},{3,7},{4,0},{5,1},{6,2},{7,3},{8,12},{9,13},{10,... | collective-permute-start | bytes 196616 | tf_op jit(solution)/shard_map/ppermute | solution.py:366
  93.4 6.7 %collective-permute-start.22 = (bf16[64,512]{1,0:T(8,128)(2,1)S(1)}, bf16[64,512]{1,0:T(8,128)(2,1)S(1)}, u32[]{:S(2)}, u32[]{:S(2)}) collective-permute-start(bf16[64,512]{1,0:T(8,128)(2,1)S(1)} %get-tuple-element.50.refs_0_), channel_id=1, source_target_pairs={{0,2},{1,3},{2,0},{3,1},{4,6},{5,7},{6,4},{7,5},{8,10},{9,11},{10,... | collective-permute-start | bytes 196616 | tf_op jit(solution)/shard_map/ppermute | solution.py:366
  100.1 1.6 %collective-permute-start.25 = (bf16[256,512]{1,0:T(8,128)(2,1)S(1)}, bf16[256,512]{1,0:T(8,128)(2,1)S(1)}, u32[]{:S(2)}, u32[]{:S(2)}) collective-permute-start(bf16[256,512]{1,0:T(8,128)(2,1)S(1)} %shard_map.126.mine_ref), channel_id=1, source_target_pairs={{0,1},{1,0},{2,3},{3,2},{4,5},{5,4},{6,7},{7,6},{8,9},{9,8},{10,11... | collective-permute-start | bytes 786440 | tf_op jit(solution)/shard_map/ppermute | solution.py:366
  (13 other events, 13.2 us)

commit v4 on v2

v4 whole, which is shorter than its diff:
```python
import jax
import jax.numpy as jnp
from jax import lax
from jax.experimental import pallas as pl
from jax.experimental.pallas import tpu as pltpu
from jax.sharding import PartitionSpec as P

BF16, F32 = jnp.bfloat16, jnp.float32
BIAS_ROWS = 16


def call(kernel, outs, ins, flops=0, smem=0):
    spec = lambda k: pl.BlockSpec(memory_space=pltpu.SMEM if k < smem else pltpu.VMEM)
    out_shape = [jax.ShapeDtypeStruct(s, d) for s, d in outs]
    moved = sum(a.size * a.dtype.itemsize for a in list(ins) + out_shape)
    return pl.pallas_call(
        kernel,
        out_shape=out_shape,
        in_specs=[spec(k) for k in range(len(ins))],
        out_specs=[pl.BlockSpec(memory_space=pltpu.VMEM)] * len(outs),
        compiler_params=pltpu.CompilerParams(vmem_limit_bytes=moved + moved // 4 + 4 * 1024 * 1024),
        cost_estimate=pl.CostEstimate(flops=flops, bytes_accessed=moved, transcendentals=0),
    )(*ins)


def dense_tiles(spot, own_meta, mate_meta, own_values, mate_values, rows_dev, table):
    window, slots, tile, _ = own_values.shape
    tile_rows = rows_dev // tile
    positions = len(table[0])

    def kernel(spot_ref, table_ref, own_meta_ref, mate_meta_ref, own_ref, mate_ref, dense_ref, flipped_ref):
        spot_now = spot_ref[0]
        dense_ref[...] = jnp.zeros_like(dense_ref)
        flipped_ref[...] = jnp.zeros_like(flipped_ref)

        def place(meta_ref, values_ref, first_j, shift, first_row):
            def slot(t, _):
                i, k = t // slots, t % slots
                j = 2 * i + first_j
                base = j * (2 * slots + 1)

                @pl.when(k < meta_ref[base + 2 * slots])
                def _():
                    row = pl.multiple_of((meta_ref[base + 2 * k] + first_row) * tile, tile)
                    column = table_ref[spot_now * positions + i + shift]
                    col = pl.multiple_of((column * tile_rows + meta_ref[base + 2 * k + 1]) * tile, tile)
                    values = values_ref[j, k]
                    dense_ref[pl.ds(row, tile), pl.ds(col, tile)] = values
                    flipped_ref[pl.ds(col, tile), pl.ds(row, tile)] = values.T

                return 0

            lax.fori_loop(0, (window // 2) * slots, slot, 0)

        place(own_meta_ref, own_ref, 0, 0, 0)
        place(mate_meta_ref, mate_ref, 1, 1 - spot_now % 2, tile_rows)

    wide = positions * rows_dev
    return call(
        kernel,
        [((2 * rows_dev, wide), BF16), ((wide, 2 * rows_dev), BF16)],
        [spot, jnp.asarray(table, jnp.int32).reshape(-1), own_meta, mate_meta, own_values, mate_values],
        smem=4,
    )


def gathered_sums(dense, columns, rows, sources, start=None):
    rows_dev, hidden = sources[0].shape
    first, last = rows

    def kernel(dense_ref, *refs):
        refs, out_ref = list(refs[:-1]), refs[-1]
        total = refs.pop(0)[first:last] if start is not None else jnp.zeros((last - first, hidden), F32)
        for column, ref in zip(columns, refs):
            part = dense_ref[first:last, column * rows_dev : (column + 1) * rows_dev]
            total = total + jnp.dot(part, ref[...], preferred_element_type=F32)
        out_ref[...] = total

    return call(
        kernel,
        [((last - first, hidden), F32)],
        [dense, *([] if start is None else [start]), *sources],
        flops=2 * (last - first) * rows_dev * hidden * len(sources),
    )[0]


def layer(core, own_sum, mate_sum, weight, bias, grad_out, pieces):
    rows_dev, hidden = own_sum.shape
    piece = hidden // pieces
    half = (pieces // 2, piece + BIAS_ROWS, hidden)

    def kernel(core_ref, own_ref, mate_ref, weight_ref, bias_ref, grad_out_ref, out_ref, ga_ref, keep_ref, give_ref):
        agg = (own_ref[...] + mate_ref[...]).astype(BF16)
        pre = jnp.dot(agg, weight_ref[...], preferred_element_type=F32) + bias_ref[...]
        sig = jax.nn.sigmoid(pre)
        out_ref[...] = (pre * sig).astype(BF16)
        grad_pre = (grad_out_ref[...].astype(F32) * sig * (1.0 + pre * (1.0 - sig))).astype(BF16)
        ga_ref[...] = lax.dot_general(
            grad_pre, weight_ref[...], (((1,), (1,)), ((), ())), preferred_element_type=F32
        ).astype(BF16)
        bias_term = jnp.sum(grad_pre.astype(F32), axis=0, keepdims=True)
        bias_rows = jnp.broadcast_to(bias_term, (BIAS_ROWS, hidden))
        terms = lax.dot_general(agg, grad_pre, (((0,), (0,)), ((), ())), preferred_element_type=F32)
        low, high = terms[: hidden // 2], terms[hidden // 2 :]
        even = core_ref[0] == 0
        for ref, value in ((keep_ref, jnp.where(even, low, high)), (give_ref, jnp.where(even, high, low))):
            for q in range(pieces // 2):
                ref[q, :piece] = value[q * piece : (q + 1) * piece].astype(ref.dtype)
                ref[q, piece:] = bias_rows.astype(ref.dtype)

    shape = (rows_dev, hidden)
    return call(
        kernel,
        [(shape, BF16), (shape, BF16), (half, F32), (half, BF16)],
        [core, own_sum, mate_sum, weight, bias.reshape(1, hidden), grad_out],
        flops=6 * rows_dev * hidden * hidden,
        smem=1,
    )


def spread_halves(place, keep, got):
    count, rows, hidden = keep.shape

    def kernel(place_ref, keep_ref, got_ref, own_ref, *out_refs):
        for other in range(count):
            q = place_ref[0] ^ other
            value = keep_ref[q] + got_ref[q].astype(F32)
            if other == 0:
                own_ref[...] = value
            else:
                out_refs[other - 1][...] = value.astype(BF16)

    return call(
        kernel,
        [((rows, hidden), F32)] + [((rows, hidden), BF16)] * (count - 1),
        [place, keep, got],
        smem=1,
    )


def summed_terms(*terms):
    def kernel(*refs):
        total = refs[0][...].astype(F32)
        for ref in refs[1:-1]:
            total = total + ref[...].astype(F32)
        refs[-1][...] = total.astype(BF16)

    return call(kernel, [(terms[0].shape, BF16)], list(terms))[0]


def tree_sum(values):
    values = [v.astype(F32) for v in values]
    while len(values) > 1:
        values = [values[k] + values[k + 1] for k in range(0, len(values), 2)]
    return values[0]


def summed_planes(values, piece):
    shape = values[0].shape

    def kernel(*refs):
        value_refs, (weight_ref, bias_ref) = refs[:-2], refs[-2:]
        total = tree_sum([ref[...] for ref in value_refs])
        weight_ref[...] = total[:piece].astype(BF16)
        bias_ref[...] = total[piece : piece + 8]

    return call(kernel, [((piece, shape[1]), BF16), ((8, shape[1]), F32)], list(values))


def joined(place, pieces):
    piece, hidden = pieces[0].shape
    count = len(pieces)

    def kernel(place_ref, *refs):
        piece_refs, out_ref = refs[:-1], refs[-1]
        for other, ref in enumerate(piece_refs):
            q = place_ref[0] ^ other
            out_ref[pl.ds(pl.multiple_of(q * piece, piece), piece)] = ref[...]

    return call(kernel, [((count * piece, hidden), BF16)], [place, *pieces], smem=1)[0]


def whole_weight(core, mine, other):
    rows, hidden = mine.shape

    def kernel(core_ref, mine_ref, other_ref, out_ref):
        core_now = core_ref[0]
        out_ref[pl.ds(pl.multiple_of(core_now * rows, rows), rows)] = mine_ref[...].astype(F32)
        out_ref[pl.ds(pl.multiple_of((1 - core_now) * rows, rows), rows)] = other_ref[...].astype(F32)

    return call(kernel, [((2 * rows, hidden), F32)], [core, mine, other], smem=1)[0]


def scattered_sums(flipped, own, mate, columns, dtypes):
    rows_dev, hidden = own.shape

    def kernel(flipped_ref, own_ref, mate_ref, *out_refs):
        out_refs = list(out_refs)
        for column, kinds in zip(columns, dtypes):
            part = pl.ds(column * rows_dev, rows_dev)
            total = jnp.dot(flipped_ref[part, :rows_dev], own_ref[...], preferred_element_type=F32)
            total += jnp.dot(flipped_ref[part, rows_dev:], mate_ref[...], preferred_element_type=F32)
            for kind in kinds:
                out_refs.pop(0)[...] = total.astype(kind)

    return call(
        kernel,
        [((rows_dev, hidden), kind) for kinds in dtypes for kind in kinds],
        [flipped, own, mate],
        flops=4 * rows_dev * rows_dev * hidden * len(columns),
    )


def after(value, *others):
    return lax.optimization_barrier((value, *others))


class Direct:
    def __init__(self, count, reach):
        self.count, self.reach, self.positions = count, reach, 2 * reach + 1
        self.table = [list(range(self.positions))] * 8

    def sent(self, value, chips, kept=lambda s: True):
        pairs = [(s, (s + 2 * chips) % self.count) for s in range(self.count) if kept(s)]
        return lax.ppermute(value, "blk", pairs)

    def gather(self, features):
        last = self.positions - 1
        self.sources = [
            features
            if m == self.reach
            else self.sent(features, self.reach - m, lambda s: m < last or s % 2 == 0)
            for m in range(self.positions)
        ]
        return self.sources[0]

    def sums(self, dense, rows_dev):
        columns = range(self.positions)
        return [
            gathered_sums(dense, columns, (side * rows_dev, (side + 1) * rows_dev), self.sources) for side in (1, 0)
        ]

    def scatter(self, flipped, own, mate):
        kinds = [[F32 if m == self.reach else BF16] for m in range(self.positions)]
        terms = scattered_sums(flipped, own, mate, range(self.positions), kinds)
        last = self.positions - 1
        arrived = [
            self.sent(terms[m], m - self.reach, lambda s: m < last or s % 2 == 0)
            for m in range(self.positions)
            if m != self.reach
        ]
        return terms[0], terms[0], [terms[self.reach], *arrived]


class Relayed(Direct):
    def __init__(self, count, reach):
        super().__init__(count, reach)
        self.table = [[2, 3, 0, 4, 1], [1, 3, 0, 4, 2]] * 2 + [[1, 3, 0, 4, 2]] * 4

    def routed(self, value, step):
        pairs = [(s, step(s) % self.count) for s in range(self.count) if step(s) is not None]
        return lax.ppermute(value, "blk", pairs)

    @staticmethod
    def plane_step(s, sign):
        return None if s % 2 else s + (8 * sign if s % 8 < 4 else -8 * sign)

    def gather(self, features):
        first = self.routed(features, lambda s: s + 4 if s % 2 else s ^ 4)
        back, on = self.sent(features, 1), self.sent(features, -1)
        relayed = self.routed(first, lambda s: self.plane_step(s, 1))
        self.sources = [features, first, relayed, back, on]
        return first

    def sums(self, dense, rows_dev):
        start = gathered_sums(dense, (0, 1, 2), (0, 2 * rows_dev), self.sources[:3])
        return [
            gathered_sums(dense, (3, 4), (side * rows_dev, (side + 1) * rows_dev), self.sources[3:], start)
            for side in (1, 0)
        ]

    def scatter(self, flipped, own, mate):
        to_plane, to_second, rest_second = scattered_sums(flipped, own, mate, (2, 1), [[BF16], [BF16, F32]])
        relayed = self.routed(to_plane, lambda s: self.plane_step(s, -1))
        straight = self.routed(to_second, lambda s: s - 4 if s % 2 else None)
        to_back, to_on, kept = scattered_sums(flipped, own, mate, (3, 4, 0), [[BF16], [BF16], [F32]])
        back, on = self.sent(to_back, -1), self.sent(to_on, 1)
        out = summed_terms(rest_second, relayed)
        swapped_sums = self.routed(out, lambda s: None if s % 2 else s ^ 4)
        return to_back, out, [kept, straight, back, on, swapped_sums]


def local(features, tile_list, tile_count, tile_values, weight, bias, grad_out):
    count = lax.axis_size("blk")
    me = lax.axis_index("blk")
    window = tile_values.shape[1]
    reach = window // 4
    rows_dev, hidden = features.shape
    plane = 4
    pieces = 2 * plane
    core = (me % 2).astype(jnp.int32).reshape(1)
    place = ((me // 2) % plane).astype(jnp.int32).reshape(1)
    spot = (me % pieces).astype(jnp.int32).reshape(1)
    route = (Relayed if reach == 2 else Direct)(count, reach)

    def swapped(value, distance):
        return lax.ppermute(value, "blk", [(s, s ^ distance) for s in range(count)])

    first = route.gather(features)
    first, tile_list, tile_count, tile_values = after(first, tile_list, tile_count, tile_values)
    meta = jnp.concatenate([tile_list[0].reshape(window, -1), tile_count[0][:, None]], axis=1).reshape(-1)
    mate_meta, mate_values = swapped(meta, 1), swapped(tile_values[0], 1)
    dense, flipped = dense_tiles(spot, meta, mate_meta, tile_values[0], mate_values, rows_dev, route.table)
    mate_sum, own_sum = route.sums(dense, rows_dev)
    output, grad_agg, keep, give = layer(core, own_sum, swapped(mate_sum, 1), weight, bias, grad_out, pieces)

    mate_grad, got = swapped(grad_agg, 1), swapped(give, 1)
    own_piece, *give_pieces = spread_halves(place, keep, got)
    mate_grad, *give_pieces = after(mate_grad, *give_pieces)
    sent_first, sent_last, arriving = route.scatter(flipped, grad_agg, mate_grad)
    own_piece, _ = after(own_piece, sent_first)
    plane_sum = summed_terms(own_piece, *[swapped(v, 2 * (d + 1)) for d, v in enumerate(give_pieces)])
    values = [plane_sum] + [swapped(plane_sum, pieces * d) for d in range(1, count // pieces)]
    values[0], _ = after(values[0], sent_last)
    piece_sum, bias_sum = summed_planes(values, hidden // pieces)
    gathered = [swapped(piece_sum, 2 * d) for d in range(1, plane)]
    piece_sum, *arriving = after(piece_sum, *arriving)
    half = joined(place, [piece_sum, *gathered])
    grad_weight = whole_weight(core, half, swapped(half, 1))
    return (output, summed_terms(*arriving), grad_weight, bias_sum[0])


def solution(mesh):
    placed = (
        P("blk", None),
        P("blk", None, None, None),
        P("blk", None),
        P("blk", None, None, None, None),
        P(),
        P(),
        P("blk", None),
    )
    return jax.shard_map(
        local,
        mesh=mesh,
        in_specs=placed,
        out_specs=(P("blk", None), P("blk", None), P(), P()),
        check_vma=False,
    )
```

time: 90.2 us -> 110 us (1.22)
  Pallas kernels: 13.3 us -> 22 us
  local copies, waits for them, and re-layouts: 4.8 us -> 9.71 us
  waiting for transfers between devices: 39 us -> 43.8 us
    pallas_call x12 -> x14, Pallas kernels: 13.3 us -> 22 us  [call(): pl.pallas_call(kernel, out_shape=out_shape, in_specs=[spec(k) for k in ra...]
    ppermute x15, waiting for transfers between devices: 28 us -> 33.1 us  [swapped(): return lax.ppermute(value, 'blk', [(s, s ^ distance) for s in range(count)])]
    unnamed x14 -> x28, local copies, waits for them, and re-layouts: 3.35 us -> 8.26 us
    ppermute x8 -> x9, starting transfers between devices: 18.5 us -> 19.1 us  [the longest x5 13.8 us: routed(): return lax.ppermute(value, 'blk', pairs)]
    ppermute x8 -> x9, waiting for transfers between devices: 11 us -> 10.7 us  [the longest x5 10.3 us: routed(): return lax.ppermute(value, 'blk', pairs)]
  transfers between devices with their start and end apart: 23 -> 24, of which waited for: 12 -> 11; matrix products, arithmetic and copies ran while one was open for 2% -> 2% of each run, Pallas kernels for 11% -> 12%
where the time goes in v4:
time: 110 us; the launch traced here: 109 us
  waiting for transfers between devices  43.8 us (40%)
  starting transfers between devices  31.9 us (29%)
  Pallas kernels  22 us (20%)
  local copies, waits for them, and re-layouts  9.71 us (9%)
    ppermute x15, waiting for transfers between devices, swapped(): return lax.ppermute(value, 'blk', [(s, s ^ distance) for s in range(count)])  33.1 us
    pallas_call x14, Pallas kernels, call(): pl.pallas_call(kernel, out_shape=out_shape, in_specs=[spec(k) for k in ra...  22 us
    ppermute x5, starting transfers between devices, routed(): return lax.ppermute(value, 'blk', pairs)  13.8 us
    ppermute x15, starting transfers between devices, swapped(): return lax.ppermute(value, 'blk', [(s, s ^ distance) for s in range(count)])  12.8 us
    ppermute x5, waiting for transfers between devices, routed(): return lax.ppermute(value, 'blk', pairs)  10.3 us
    unnamed x28, local copies, waits for them, and re-layouts  8.26 us
    ppermute x4, starting transfers between devices, sent(): return lax.ppermute(value, 'blk', pairs)  5.36 us
  transfers between devices with their start and end apart: 24, of which 11 were waited for; matrix products, arithmetic and copies ran while one was open for 2% of the time, Pallas kernels for 12%

profile of v4, /device:TPU:0, one launch (start us, length us, event | category | flops | bytes accessed | tf_op | source)
XLA Modules:
  0.0 108.9 jit_solution(10063501496397664575)
XLA Ops:
  0.6 3.0 %collective-permute-start = (bf16[384,512]{1,0:T(8,128)(2,1)}, bf16[384,512]{1,0:T(8,128)(2,1)}, u32[]{:S(2)}, u32[]{:S(2)}) collective-permute-start(bf16[384,512]{1,0:T(8,128)(2,1)} %refs_0_.1), channel_id=1, source_target_pairs={{0,4},{1,5},{2,6},{3,7},{4,0},{5,9},{6,2},{7,11},{8,12},{9,13},{10... | collective-permute-start | bytes 1179656 | tf_op jit(solution)/shard_map/ppermute | solution.py:262
  3.6 10.3 %collective-permute-done.refs_1_ = bf16[384,512]{1,0:T(8,128)(2,1)} collective-permute-done((bf16[384,512]{1,0:T(8,128)(2,1)}, bf16[384,512]{1,0:T(8,128)(2,1)}, u32[]{:S(2)}, u32[]{:S(2)}) %collective-permute-start) | collective-permute-done | bytes 393248 | tf_op jit(solution)/shard_map/ppermute | solution.py:262
  13.9 3.7 %collective-permute-start.3 = (bf16[384,512]{1,0:T(8,128)(2,1)}, bf16[384,512]{1,0:T(8,128)(2,1)}, u32[]{:S(2)}, u32[]{:S(2)}) collective-permute-start(bf16[384,512]{1,0:T(8,128)(2,1)} %collective-permute-done.refs_1_), channel_id=1, source_target_pairs={{0,8},{2,10},{4,28},{6,30},{8,16},{10,18},{12,4},{14,6},{16,24},{1... | collective-permute-start | bytes 1179656 | tf_op jit(solution)/shard_map/ppermute | solution.py:262
  17.7 3.5 %collective-permute-start.5 = (bf16[384,512]{1,0:T(8,128)(2,1)}, bf16[384,512]{1,0:T(8,128)(2,1)S(1)}, u32[]{:S(2)}, u32[]{:S(2)}) collective-permute-start(bf16[384,512]{1,0:T(8,128)(2,1)} %refs_0_.1), channel_id=1, source_target_pairs={{0,30},{1,31},{2,0},{3,1},{4,2},{5,3},{6,4},{7,5},{8,6},{9,7},{10,... | collective-permute-start | bytes 1179656 | tf_op jit(solution)/shard_map/ppermute | solution.py:225
  22.8 1.1 %collective-permute-done.1.mate_meta_ref = s32[120]{0:T(128)S(1)} collective-permute-done((s32[120]{0:T(128)S(1)}, s32[120]{0:T(128)S(1)}, u32[]{:S(2)}, u32[]{:S(2)}) %collective-permute-start.1) | collective-permute-done | bytes 512 | tf_op jit(solution)/shard_map/ppermute | solution.py:307
  23.9 1.3 %copy-done.5 = bf16[8,7,128,128]{3,2,1,0:T(8,128)(2,1)} copy-done((bf16[8,7,128,128]{3,2,1,0:T(8,128)(2,1)}, bf16[8,7,128,128]{3,2,1,0:T(8,128)(2,1)S(1)}, u32[]{:S(2)}) %copy-start.5) | copy-done | bytes 1835032
  25.1 1.5 %copy-done.4 = bf16[1,8,7,128,128]{4,3,2,1,0:T(8,128)(2,1)S(1)} copy-done((bf16[1,8,7,128,128]{4,3,2,1,0:T(8,128)(2,1)S(1)}, bf16[1,8,7,128,128]{4,3,2,1,0:T(8,128)(2,1)}, u32[]{:S(2)}) %copy-start.4) | copy-done | bytes 1835032
  26.6 1.5 %copy-done.6 = bf16[8,7,128,128]{3,2,1,0:T(8,128)(2,1)S(1)} copy-done((bf16[8,7,128,128]{3,2,1,0:T(8,128)(2,1)S(1)}, bf16[8,7,128,128]{3,2,1,0:T(8,128)(2,1)}, u32[]{:S(2)}) %copy-start.6) | copy-done | bytes 1835032
  28.8 4.0 %shard_map.111 = (bf16[768,1920]{1,0:T(8,128)(2,1)S(1)}, bf16[1920,768]{1,0:T(8,128)(2,1)S(1)}) custom-call(s32[1]{0:T(128)} %bitcast.1.spot_ref, s32[40]{0:T(128)S(1)} %copy-done.13, s32[120]{0:T(128)S(1)} %reshape.29.own_meta_ref, s32[120]{0:T(128)S(1)} %collective-permute-done.1.mate_meta_ref, bf16[8,7,128,128]{3,2,1,0:T(8,128)(2,1)S(1)} %bitcast.10, ...), custom_call_target="tpu_custom_call" | custom-call | bytes 9569380 | tf_op jit(solution)/shard_map/pallas_call | solution.py:16
  32.8 3.1 %shard_map.112.refs_0_ = f32[768,512]{1,0:T(8,128)S(1)} custom-call(bf16[768,1920]{1,0:T(8,128)(2,1)S(1)} %get-tuple-element.40.dense_ref, bf16[384,512]{1,0:T(8,128)(2,1)S(1)} %copy-done.10, bf16[384,512]{1,0:T(8,128)(2,1)} %collective-permute-done.refs_1_, bf16[384,512]{1,0:T(8,128)(2,1)} %collective-permute-done.3.refs_2_), custom_call_target="tpu_custom_call" | custom-call | flops 905969664 | bytes 5701632 | tf_op jit(solution)/shard_map/pallas_call | solution.py:16
  36.3 2.5 %shard_map.114 = f32[384,512]{1,0:T(8,128)} custom-call(bf16[768,1920]{1,0:T(8,128)(2,1)S(1)} %get-tuple-element.40.dense_ref, f32[768,512]{1,0:T(8,128)S(1)} %shard_map.112.refs_0_, bf16[384,512]{1,0:T(8,128)(2,1)} %collective-permute-done.4.refs_1_, bf16[384,512]{1,0:T(8,128)(2,1)S(1)} %collective-permute-done.5.refs_2_), custom_call_target="tpu_custom_call" | custom-call | flops 301989888 | bytes 6094848 | tf_op jit(solution)/shard_map/pallas_call | solution.py:16
  39.1 1.4 %copy-done.1 = f32[768,512]{1,0:T(8,128)S(1)} copy-done((f32[768,512]{1,0:T(8,128)S(1)}, f32[768,512]{1,0:T(8,128)}, u32[]{:S(2)}) %copy-start.1) | copy-done | bytes 1572888
  40.5 1.6 %shard_map.113.own_ref = f32[384,512]{1,0:T(8,128)S(1)} custom-call(bf16[768,1920]{1,0:T(8,128)(2,1)S(1)} %get-tuple-element.40.dense_ref, f32[768,512]{1,0:T(8,128)S(1)} %copy-done.1, bf16[384,512]{1,0:T(8,128)(2,1)} %collective-permute-done.4.refs_1_, bf16[384,512]{1,0:T(8,128)(2,1)S(1)} %collective-permute-done.5.refs_2_), custom_call_target="tpu_custom_call" | custom-call | flops 301989888 | bytes 6094848 | tf_op jit(solution)/shard_map/pallas_call | solution.py:16
  42.2 3.2 %shard_map.115 = (bf16[384,512]{1,0:T(8,128)(2,1)}, bf16[384,512]{1,0:T(8,128)(2,1)S(1)}, f32[4,80,512]{2,1,0:T(8,128)S(1)}, bf16[4,80,512]{2,1,0:T(8,128)(2,1)}) custom-call(s32[1]{0:T(128)} %bitcast.core_ref, f32[384,512]{1,0:T(8,128)S(1)} %shard_map.113.own_ref, f32[384,512]{1,0:T(8,128)} %collective-permute-done.6.mate_ref, ...), custom_call_target="tpu_custom_call" | custom-call | flops 603979776 | bytes 4261892 | tf_op jit(solution)/shard_map/pallas_call | solution.py:16
  46.7 2.0 %collective-permute-done.7.got_ref = bf16[4,80,512]{2,1,0:T(8,128)(2,1)} collective-permute-done((bf16[4,80,512]{2,1,0:T(8,128)(2,1)}, bf16[4,80,512]{2,1,0:T(8,128)(2,1)}, u32[]{:S(2)}, u32[]{:S(2)}) %collective-permute-start.7) | collective-permute-done | bytes 327712 | tf_op jit(solution)/shard_map/ppermute | solution.py:307
  48.7 1.1 copy-done.8
  49.8 1.1 shard_map.116
  50.9 2.0 %shard_map.119 = (bf16[384,512]{1,0:T(8,128)(2,1)S(1)}, bf16[384,512]{1,0:T(8,128)(2,1)S(1)}, f32[384,512]{1,0:T(8,128)S(1)}) custom-call(bf16[1920,768]{1,0:T(8,128)(2,1)S(1)} %copy-done.3, bf16[384,512]{1,0:T(8,128)(2,1)S(1)} %get-tuple-element.46.own_ref, bf16[384,512]{1,0:T(8,128)(2,1)} %collective-permute-done.8.mate_ref), custom_call_target="tpu_custom_call" | custom-call | flops 603979776 | bytes 5308416 | tf_op jit(solution)/shard_map/pallas_call | solution.py:16
  52.9 4.4 %collective-permute-start.12 = (bf16[384,512]{1,0:T(8,128)(2,1)S(1)}, bf16[384,512]{1,0:T(8,128)(2,1)S(1)}, u32[]{:S(2)}, u32[]{:S(2)}) collective-permute-start(bf16[384,512]{1,0:T(8,128)(2,1)S(1)} %get-tuple-element.57), channel_id=1, source_target_pairs={{0,24},{2,26},{4,12},{6,14},{8,0},{10,2},{12,20},{14,22},{16,8},{1... | collective-permute-start | bytes 1179656 | tf_op jit(solution)/shard_map/ppermute | solution.py:262
  57.3 2.2 %collective-permute-start.9 = (bf16[80,512]{1,0:T(8,128)(2,1)S(1)}, bf16[80,512]{1,0:T(8,128)(2,1)S(1)}, u32[]{:S(2)}, u32[]{:S(2)}) collective-permute-start(bf16[80,512]{1,0:T(8,128)(2,1)S(1)} %get-tuple-element.53), channel_id=1, source_target_pairs={{0,2},{1,3},{2,0},{3,1},{4,6},{5,7},{6,4},{7,5},{8,10},{9,11},{10,... | collective-permute-start | bytes 245768 | tf_op jit(solution)/shard_map/ppermute | solution.py:307
  59.5 2.4 %shard_map.117 = (bf16[384,512]{1,0:T(8,128)(2,1)S(1)}, bf16[384,512]{1,0:T(8,128)(2,1)S(1)}, f32[384,512]{1,0:T(8,128)S(1)}) custom-call(bf16[1920,768]{1,0:T(8,128)(2,1)S(1)} %copy-done.3, bf16[384,512]{1,0:T(8,128)(2,1)S(1)} %get-tuple-element.46.own_ref, bf16[384,512]{1,0:T(8,128)(2,1)} %collective-permute-done.8.mate_ref), custom_call_target="tpu_custom_call" | custom-call | flops 905969664 | bytes 5308416 | tf_op jit(solution)/shard_map/pallas_call | solution.py:16
  62.7 4.8 %collective-permute-start.11 = (bf16[80,512]{1,0:T(8,128)(2,1)S(1)}, bf16[80,512]{1,0:T(8,128)(2,1)S(1)}, u32[]{:S(2)}, u32[]{:S(2)}) collective-permute-start(bf16[80,512]{1,0:T(8,128)(2,1)S(1)} %get-tuple-element.55), channel_id=1, source_target_pairs={{0,6},{1,7},{2,4},{3,5},{4,2},{5,3},{6,0},{7,1},{8,14},{9,15},{10,... | collective-permute-start | bytes 245768 | tf_op jit(solution)/shard_map/ppermute | solution.py:307
  67.6 1.7 %collective-permute-start.17 = (bf16[384,512]{1,0:T(8,128)(2,1)S(1)}, bf16[384,512]{1,0:T(8,128)(2,1)S(1)}, u32[]{:S(2)}, u32[]{:S(2)}) collective-permute-start(bf16[384,512]{1,0:T(8,128)(2,1)S(1)} %get-tuple-element.51), channel_id=1, source_target_pairs={{0,30},{1,31},{2,0},{3,1},{4,2},{5,3},{6,4},{7,5},{8,6},{9,7},{10,... | collective-permute-start | bytes 1179656 | tf_op jit(solution)/shard_map/ppermute | solution.py:225
  69.3 1.9 %collective-permute-start.19 = (bf16[384,512]{1,0:T(8,128)(2,1)S(1)}, bf16[384,512]{1,0:T(8,128)(2,1)S(1)}, u32[]{:S(2)}, u32[]{:S(2)}) collective-permute-start(bf16[384,512]{1,0:T(8,128)(2,1)S(1)} %shard_map.120), channel_id=1, source_target_pairs={{0,4},{2,6},{4,0},{6,2},{8,12},{10,14},{12,8},{14,10},{16,20},{18,... | collective-permute-start | bytes 1179656 | tf_op jit(solution)/shard_map/ppermute | solution.py:262
  71.2 10.9 %collective-permute-done.11.refs_3_ = bf16[80,512]{1,0:T(8,128)(2,1)S(1)} collective-permute-done((bf16[80,512]{1,0:T(8,128)(2,1)S(1)}, bf16[80,512]{1,0:T(8,128)(2,1)S(1)}, u32[]{:S(2)}, u32[]{:S(2)}) %collective-permute-start.11) | collective-permute-done | bytes 81952 | tf_op jit(solution)/shard_map/ppermute | solution.py:307
  82.2 1.1 collective-permute-start.15
  83.3 5.6 %collective-permute-done.15.refs_3_ = bf16[80,512]{1,0:T(8,128)(2,1)S(1)} collective-permute-done((bf16[80,512]{1,0:T(8,128)(2,1)S(1)}, bf16[80,512]{1,0:T(8,128)(2,1)S(1)}, u32[]{:S(2)}, u32[]{:S(2)}) %collective-permute-start.15) | collective-permute-done | bytes 81952 | tf_op jit(solution)/shard_map/ppermute | solution.py:307
  88.9 5.3 %collective-permute-done.14.refs_2_ = bf16[80,512]{1,0:T(8,128)(2,1)S(1)} collective-permute-done((bf16[80,512]{1,0:T(8,128)(2,1)S(1)}, bf16[80,512]{1,0:T(8,128)(2,1)S(1)}, u32[]{:S(2)}, u32[]{:S(2)}) %collective-permute-start.14) | collective-permute-done | bytes 81952 | tf_op jit(solution)/shard_map/ppermute | solution.py:307
  94.2 4.4 %collective-permute-done.13.refs_1_ = bf16[80,512]{1,0:T(8,128)(2,1)S(1)} collective-permute-done((bf16[80,512]{1,0:T(8,128)(2,1)S(1)}, bf16[80,512]{1,0:T(8,128)(2,1)S(1)}, u32[]{:S(2)}, u32[]{:S(2)}) %collective-permute-start.13) | collective-permute-done | bytes 81952 | tf_op jit(solution)/shard_map/ppermute | solution.py:307
  98.7 3.2 %collective-permute-start.22 = (bf16[64,512]{1,0:T(8,128)(2,1)S(1)}, bf16[64,512]{1,0:T(8,128)(2,1)S(1)}, u32[]{:S(2)}, u32[]{:S(2)}) collective-permute-start(bf16[64,512]{1,0:T(8,128)(2,1)S(1)} %get-tuple-element.68.refs_0_), channel_id=1, source_target_pairs={{0,6},{1,7},{2,4},{3,5},{4,2},{5,3},{6,0},{7,1},{8,14},{9,15},{10,... | collective-permute-start | bytes 196616 | tf_op jit(solution)/shard_map/ppermute | solution.py:307
  102.5 2.0 %collective-permute-done.22.refs_3_ = bf16[64,512]{1,0:T(8,128)(2,1)S(1)} collective-permute-done((bf16[64,512]{1,0:T(8,128)(2,1)S(1)}, bf16[64,512]{1,0:T(8,128)(2,1)S(1)}, u32[]{:S(2)}, u32[]{:S(2)}) %collective-permute-start.22) | collective-permute-done | bytes 65568 | tf_op jit(solution)/shard_map/ppermute | solution.py:307
  104.5 1.6 %collective-permute-done.21.refs_2_ = bf16[64,512]{1,0:T(8,128)(2,1)S(1)} collective-permute-done((bf16[64,512]{1,0:T(8,128)(2,1)S(1)}, bf16[64,512]{1,0:T(8,128)(2,1)S(1)}, u32[]{:S(2)}, u32[]{:S(2)}) %collective-permute-start.21) | collective-permute-done | bytes 65568 | tf_op jit(solution)/shard_map/ppermute | solution.py:307
  (63 shorter events, 8.6 us)
Async XLA Ops:
  0.6 13.3 %collective-permute-start = (bf16[384,512]{1,0:T(8,128)(2,1)}, bf16[384,512]{1,0:T(8,128)(2,1)}, u32[]{:S(2)}, u32[]{:S(2)}) collective-permute-start(bf16[384,512]{1,0:T(8,128)(2,1)} %refs_0_.1), channel_id=1, source_target_pairs={{0,4},{1,5},{2,6},{3,7},{4,0},{5,9},{6,2},{7,11},{8,12},{9,13},{10... | collective-permute-start | bytes 1179656 | tf_op jit(solution)/shard_map/ppermute | solution.py:262
  13.9 9.9 %collective-permute-start.2 = (bf16[8,7,128,128]{3,2,1,0:T(8,128)(2,1)}, bf16[8,7,128,128]{3,2,1,0:T(8,128)(2,1)S(1)}, u32[]{:S(2)}, u32[]{:S(2)}) collective-permute-start(bf16[8,7,128,128]{3,2,1,0:T(8,128)(2,1)} %bitcast.9), channel_id=1, source_target_pairs={{0,1},{1,0},{2,3},{3,2},{4,5},{5,4},{6,7},{7,6},{8,9},{9,8},{10,11... | collective-permute-start | bytes 5505032 | tf_op jit(solution)/shard_map/ppermute | solution.py:307
  13.9 18.8 %collective-permute-start.3 = (bf16[384,512]{1,0:T(8,128)(2,1)}, bf16[384,512]{1,0:T(8,128)(2,1)}, u32[]{:S(2)}, u32[]{:S(2)}) collective-permute-start(bf16[384,512]{1,0:T(8,128)(2,1)} %collective-permute-done.refs_1_), channel_id=1, source_target_pairs={{0,8},{2,10},{4,28},{6,30},{8,16},{10,18},{12,4},{14,6},{16,24},{1... | collective-permute-start | bytes 1179656 | tf_op jit(solution)/shard_map/ppermute | solution.py:262
  17.7 18.2 %collective-permute-start.5 = (bf16[384,512]{1,0:T(8,128)(2,1)}, bf16[384,512]{1,0:T(8,128)(2,1)S(1)}, u32[]{:S(2)}, u32[]{:S(2)}) collective-permute-start(bf16[384,512]{1,0:T(8,128)(2,1)} %refs_0_.1), channel_id=1, source_target_pairs={{0,30},{1,31},{2,0},{3,1},{4,2},{5,3},{6,4},{7,5},{8,6},{9,7},{10,... | collective-permute-start | bytes 1179656 | tf_op jit(solution)/shard_map/ppermute | solution.py:225
  21.2 15.1 %collective-permute-start.4 = (bf16[384,512]{1,0:T(8,128)(2,1)}, bf16[384,512]{1,0:T(8,128)(2,1)}, u32[]{:S(2)}, u32[]{:S(2)}) collective-permute-start(bf16[384,512]{1,0:T(8,128)(2,1)} %refs_0_.1), channel_id=1, source_target_pairs={{0,2},{1,3},{2,4},{3,5},{4,6},{5,7},{6,8},{7,9},{8,10},{9,11},{10,... | collective-permute-start | bytes 1179656 | tf_op jit(solution)/shard_map/ppermute | solution.py:225
  22.7 1.1 %collective-permute-start.1 = (s32[120]{0:T(128)S(1)}, s32[120]{0:T(128)S(1)}, u32[]{:S(2)}, u32[]{:S(2)}) collective-permute-start(s32[120]{0:T(128)S(1)} %reshape.29.own_meta_ref), channel_id=1, source_target_pairs={{0,1},{1,0},{2,3},{3,2},{4,5},{5,4},{6,7},{7,6},{8,9},{9,8},{10,11... | collective-permute-start | bytes 1448 | tf_op jit(solution)/shard_map/ppermute | solution.py:307
  25.1 1.5 %copy-start.4 = (bf16[1,8,7,128,128]{4,3,2,1,0:T(8,128)(2,1)S(1)}, bf16[1,8,7,128,128]{4,3,2,1,0:T(8,128)(2,1)}, u32[]{:S(2)}) copy-start(bf16[1,8,7,128,128]{4,3,2,1,0:T(8,128)(2,1)} %param.11) | copy-start | bytes 5505028
  28.8 4.0 %copy-start.10 = (bf16[384,512]{1,0:T(8,128)(2,1)S(1)}, bf16[384,512]{1,0:T(8,128)(2,1)}, u32[]{:S(2)}) copy-start(bf16[384,512]{1,0:T(8,128)(2,1)} %refs_0_.1) | copy-start | bytes 1179652
  32.8 3.1 %copy-start.2 = (bf16[1920,768]{1,0:T(8,128)(2,1)}, bf16[1920,768]{1,0:T(8,128)(2,1)S(1)}, u32[]{:S(2)}) copy-start(bf16[1920,768]{1,0:T(8,128)(2,1)S(1)} %get-tuple-element.45.flipped_ref) | copy-start | bytes 8847364
  35.9 3.0 %copy-start = (f32[768,512]{1,0:T(8,128)}, f32[768,512]{1,0:T(8,128)S(1)}, u32[]{:S(2)}) copy-start(f32[768,512]{1,0:T(8,128)S(1)} %shard_map.112.refs_0_) | copy-start | bytes 4718596
  38.9 3.3 %collective-permute-start.6 = (f32[384,512]{1,0:T(8,128)}, f32[384,512]{1,0:T(8,128)}, u32[]{:S(2)}, u32[]{:S(2)}) collective-permute-start(f32[384,512]{1,0:T(8,128)} %shard_map.114), channel_id=1, source_target_pairs={{0,1},{1,0},{2,3},{3,2},{4,5},{5,4},{6,7},{7,6},{8,9},{9,8},{10,11... | collective-permute-start | bytes 2359304 | tf_op jit(solution)/shard_map/ppermute | solution.py:307
  40.5 1.7 %copy-start.9 = (bf16[512,512]{1,0:T(8,128)(2,1)S(1)}, bf16[512,512]{1,0:T(8,128)(2,1)}, u32[]{:S(2)}) copy-start(bf16[512,512]{1,0:T(8,128)(2,1)} %weight_ref.1) | copy-start | bytes 1572868
  40.5 1.7 %copy-start.11 = (bf16[384,512]{1,0:T(8,128)(2,1)S(1)}, bf16[384,512]{1,0:T(8,128)(2,1)}, u32[]{:S(2)}) copy-start(bf16[384,512]{1,0:T(8,128)(2,1)} %grad_out_ref.1) | copy-start | bytes 1179652
  40.5 1.7 %copy-start.12 = (f32[512]{0:T(512)S(1)}, f32[512]{0:T(512)}, u32[]{:S(2)}) copy-start(f32[512]{0:T(512)} %param.13) | copy-start | bytes 6148
  42.1 8.8 %copy-start.3 = (bf16[1920,768]{1,0:T(8,128)(2,1)S(1)}, bf16[1920,768]{1,0:T(8,128)(2,1)}, u32[]{:S(2)}) copy-start(bf16[1920,768]{1,0:T(8,128)(2,1)} %copy-done.2) | copy-start | bytes 8847364
  46.2 4.7 %collective-permute-start.8 = (bf16[384,512]{1,0:T(8,128)(2,1)S(1)}, bf16[384,512]{1,0:T(8,128)(2,1)}, u32[]{:S(2)}, u32[]{:S(2)}) collective-permute-start(bf16[384,512]{1,0:T(8,128)(2,1)S(1)} %get-tuple-element.46.own_ref), channel_id=1, source_target_pairs={{0,1},{1,0},{2,3},{3,2},{4,5},{5,4},{6,7},{7,6},{8,9},{9,8},{10,11... | collective-permute-start | bytes 1179656 | tf_op jit(solution)/shard_map/ppermute | solution.py:307
  46.5 2.2 %collective-permute-start.7 = (bf16[4,80,512]{2,1,0:T(8,128)(2,1)}, bf16[4,80,512]{2,1,0:T(8,128)(2,1)}, u32[]{:S(2)}, u32[]{:S(2)}) collective-permute-start(bf16[4,80,512]{2,1,0:T(8,128)(2,1)} %get-tuple-element.43), channel_id=1, source_target_pairs={{0,1},{1,0},{2,3},{3,2},{4,5},{5,4},{6,7},{7,6},{8,9},{9,8},{10,11... | collective-permute-start | bytes 983048 | tf_op jit(solution)/shard_map/ppermute | solution.py:307
  52.9 9.9 %collective-permute-start.12 = (bf16[384,512]{1,0:T(8,128)(2,1)S(1)}, bf16[384,512]{1,0:T(8,128)(2,1)S(1)}, u32[]{:S(2)}, u32[]{:S(2)}) collective-permute-start(bf16[384,512]{1,0:T(8,128)(2,1)S(1)} %get-tuple-element.57), channel_id=1, source_target_pairs={{0,24},{2,26},{4,12},{6,14},{8,0},{10,2},{12,20},{14,22},{16,8},{1... | collective-permute-start | bytes 1179656 | tf_op jit(solution)/shard_map/ppermute | solution.py:262
  57.3 10.3 %collective-permute-start.9 = (bf16[80,512]{1,0:T(8,128)(2,1)S(1)}, bf16[80,512]{1,0:T(8,128)(2,1)S(1)}, u32[]{:S(2)}, u32[]{:S(2)}) collective-permute-start(bf16[80,512]{1,0:T(8,128)(2,1)S(1)} %get-tuple-element.53), channel_id=1, source_target_pairs={{0,2},{1,3},{2,0},{3,1},{4,6},{5,7},{6,4},{7,5},{8,10},{9,11},{10,... | collective-permute-start | bytes 245768 | tf_op jit(solution)/shard_map/ppermute | solution.py:307
  59.5 9.8 %collective-permute-start.10 = (bf16[80,512]{1,0:T(8,128)(2,1)S(1)}, bf16[80,512]{1,0:T(8,128)(2,1)S(1)}, u32[]{:S(2)}, u32[]{:S(2)}) collective-permute-start(bf16[80,512]{1,0:T(8,128)(2,1)S(1)} %get-tuple-element.54), channel_id=1, source_target_pairs={{0,4},{1,5},{2,6},{3,7},{4,0},{5,1},{6,2},{7,3},{8,12},{9,13},{10,... | collective-permute-start | bytes 245768 | tf_op jit(solution)/shard_map/ppermute | solution.py:307
  61.9 40.0 %collective-permute-start.16 = (bf16[384,512]{1,0:T(8,128)(2,1)S(1)}, bf16[384,512]{1,0:T(8,128)(2,1)S(1)}, u32[]{:S(2)}, u32[]{:S(2)}) collective-permute-start(bf16[384,512]{1,0:T(8,128)(2,1)S(1)} %get-tuple-element.61), channel_id=1, source_target_pairs={{1,29},{3,31},{5,1},{7,3},{9,5},{11,7},{13,9},{15,11},{17,13},{19,... | collective-permute-start | bytes 1179656 | tf_op jit(solution)/shard_map/ppermute | solution.py:262
  62.6 39.3 %collective-permute-start.18 = (bf16[384,512]{1,0:T(8,128)(2,1)S(1)}, bf16[384,512]{1,0:T(8,128)(2,1)S(1)}, u32[]{:S(2)}, u32[]{:S(2)}) collective-permute-start(bf16[384,512]{1,0:T(8,128)(2,1)S(1)} %get-tuple-element.62), channel_id=1, source_target_pairs={{0,2},{1,3},{2,4},{3,5},{4,6},{5,7},{6,8},{7,9},{8,10},{9,11},{10,... | collective-permute-start | bytes 1179656 | tf_op jit(solution)/shard_map/ppermute | solution.py:225
  62.7 19.4 %collective-permute-start.11 = (bf16[80,512]{1,0:T(8,128)(2,1)S(1)}, bf16[80,512]{1,0:T(8,128)(2,1)S(1)}, u32[]{:S(2)}, u32[]{:S(2)}) collective-permute-start(bf16[80,512]{1,0:T(8,128)(2,1)S(1)} %get-tuple-element.55), channel_id=1, source_target_pairs={{0,6},{1,7},{2,4},{3,5},{4,2},{5,3},{6,0},{7,1},{8,14},{9,15},{10,... | collective-permute-start | bytes 245768 | tf_op jit(solution)/shard_map/ppermute | solution.py:307
  67.6 34.9 %collective-permute-start.17 = (bf16[384,512]{1,0:T(8,128)(2,1)S(1)}, bf16[384,512]{1,0:T(8,128)(2,1)S(1)}, u32[]{:S(2)}, u32[]{:S(2)}) collective-permute-start(bf16[384,512]{1,0:T(8,128)(2,1)S(1)} %get-tuple-element.51), channel_id=1, source_target_pairs={{0,30},{1,31},{2,0},{3,1},{4,2},{5,3},{6,4},{7,5},{8,6},{9,7},{10,... | collective-permute-start | bytes 1179656 | tf_op jit(solution)/shard_map/ppermute | solution.py:225
  69.3 33.2 %collective-permute-start.19 = (bf16[384,512]{1,0:T(8,128)(2,1)S(1)}, bf16[384,512]{1,0:T(8,128)(2,1)S(1)}, u32[]{:S(2)}, u32[]{:S(2)}) collective-permute-start(bf16[384,512]{1,0:T(8,128)(2,1)S(1)} %shard_map.120), channel_id=1, source_target_pairs={{0,4},{2,6},{4,0},{6,2},{8,12},{10,14},{12,8},{14,10},{16,20},{18,... | collective-permute-start | bytes 1179656 | tf_op jit(solution)/shard_map/ppermute | solution.py:262
  82.2 6.6 %collective-permute-start.15 = (bf16[80,512]{1,0:T(8,128)(2,1)S(1)}, bf16[80,512]{1,0:T(8,128)(2,1)S(1)}, u32[]{:S(2)}, u32[]{:S(2)}) collective-permute-start(bf16[80,512]{1,0:T(8,128)(2,1)S(1)} %shard_map.118.refs_0_), channel_id=1, source_target_pairs={{0,24},{1,25},{2,26},{3,27},{4,28},{5,29},{6,30},{7,31},{8,16},{9,... | collective-permute-start | bytes 245768 | tf_op jit(solution)/shard_map/ppermute | solution.py:307
  88.9 5.3 %collective-permute-start.14 = (bf16[80,512]{1,0:T(8,128)(2,1)S(1)}, bf16[80,512]{1,0:T(8,128)(2,1)S(1)}, u32[]{:S(2)}, u32[]{:S(2)}) collective-permute-start(bf16[80,512]{1,0:T(8,128)(2,1)S(1)} %shard_map.118.refs_0_), channel_id=1, source_target_pairs={{0,16},{1,17},{2,18},{3,19},{4,20},{5,21},{6,22},{7,23},{8,24},{9,... | collective-permute-start | bytes 245768 | tf_op jit(solution)/shard_map/ppermute | solution.py:307
  94.2 4.4 %collective-permute-start.13 = (bf16[80,512]{1,0:T(8,128)(2,1)S(1)}, bf16[80,512]{1,0:T(8,128)(2,1)S(1)}, u32[]{:S(2)}, u32[]{:S(2)}) collective-permute-start(bf16[80,512]{1,0:T(8,128)(2,1)S(1)} %shard_map.118.refs_0_), channel_id=1, source_target_pairs={{0,8},{1,9},{2,10},{3,11},{4,12},{5,13},{6,14},{7,15},{8,0},{9,1},... | collective-permute-start | bytes 245768 | tf_op jit(solution)/shard_map/ppermute | solution.py:307
  98.7 5.8 %collective-permute-start.22 = (bf16[64,512]{1,0:T(8,128)(2,1)S(1)}, bf16[64,512]{1,0:T(8,128)(2,1)S(1)}, u32[]{:S(2)}, u32[]{:S(2)}) collective-permute-start(bf16[64,512]{1,0:T(8,128)(2,1)S(1)} %get-tuple-element.68.refs_0_), channel_id=1, source_target_pairs={{0,6},{1,7},{2,4},{3,5},{4,2},{5,3},{6,0},{7,1},{8,14},{9,15},{10,... | collective-permute-start | bytes 196616 | tf_op jit(solution)/shard_map/ppermute | solution.py:307
  101.9 4.3 %collective-permute-start.21 = (bf16[64,512]{1,0:T(8,128)(2,1)S(1)}, bf16[64,512]{1,0:T(8,128)(2,1)S(1)}, u32[]{:S(2)}, u32[]{:S(2)}) collective-permute-start(bf16[64,512]{1,0:T(8,128)(2,1)S(1)} %get-tuple-element.68.refs_0_), channel_id=1, source_target_pairs={{0,4},{1,5},{2,6},{3,7},{4,0},{5,1},{6,2},{7,3},{8,12},{9,13},{10,... | collective-permute-start | bytes 196616 | tf_op jit(solution)/shard_map/ppermute | solution.py:307
  101.9 4.3 %collective-permute-start.20 = (bf16[64,512]{1,0:T(8,128)(2,1)S(1)}, bf16[64,512]{1,0:T(8,128)(2,1)S(1)}, u32[]{:S(2)}, u32[]{:S(2)}) collective-permute-start(bf16[64,512]{1,0:T(8,128)(2,1)S(1)} %get-tuple-element.68.refs_0_), channel_id=1, source_target_pairs={{0,2},{1,3},{2,0},{3,1},{4,6},{5,7},{6,4},{7,5},{8,10},{9,11},{10,... | collective-permute-start | bytes 196616 | tf_op jit(solution)/shard_map/ppermute | solution.py:307
  106.2 1.6 %collective-permute-start.23 = (bf16[256,512]{1,0:T(8,128)(2,1)S(1)}, bf16[256,512]{1,0:T(8,128)(2,1)S(1)}, u32[]{:S(2)}, u32[]{:S(2)}) collective-permute-start(bf16[256,512]{1,0:T(8,128)(2,1)S(1)} %shard_map.123.mine_ref), channel_id=1, source_target_pairs={{0,1},{1,0},{2,3},{3,2},{4,5},{5,4},{6,7},{7,6},{8,9},{9,8},{10,11... | collective-permute-start | bytes 786440 | tf_op jit(solution)/shard_map/ppermute | solution.py:307
  (6 other events, 6.7 us)

commit v5 on v4

--- a/solution.py
+++ b/solution.py
@@ -19,7 +19,7 @@
         in_specs=[spec(k) for k in range(len(ins))],
         out_specs=[pl.BlockSpec(memory_space=pltpu.VMEM)] * len(outs),
         compiler_params=pltpu.CompilerParams(vmem_limit_bytes=moved + moved // 4 + 4 * 1024 * 1024),
-        cost_estimate=pl.CostEstimate(flops=flops, bytes_accessed=moved, transcendentals=0),
+        cost_estimate=pl.CostEstimate(flops=0, bytes_accessed=0, transcendentals=0),
     )(*ins)
 
 
@@ -84,12 +84,12 @@
     )[0]
 
 
-def layer(core, own_sum, mate_sum, weight, bias, grad_out, pieces):
+def layer(spot, own_sum, mate_sum, weight, bias, grad_out, pieces):
     rows_dev, hidden = own_sum.shape
     piece = hidden // pieces
     half = (pieces // 2, piece + BIAS_ROWS, hidden)
 
-    def kernel(core_ref, own_ref, mate_ref, weight_ref, bias_ref, grad_out_ref, out_ref, ga_ref, keep_ref, give_ref):
+    def kernel(spot_ref, own_ref, mate_ref, weight_ref, bias_ref, grad_out_ref, out_ref, ga_ref, keep_ref, give_ref):
         agg = (own_ref[...] + mate_ref[...]).astype(BF16)
         pre = jnp.dot(agg, weight_ref[...], preferred_element_type=F32) + bias_ref[...]
         sig = jax.nn.sigmoid(pre)
@@ -102,7 +102,7 @@
         bias_rows = jnp.broadcast_to(bias_term, (BIAS_ROWS, hidden))
         terms = lax.dot_general(agg, grad_pre, (((0,), (0,)), ((), ())), preferred_element_type=F32)
         low, high = terms[: hidden // 2], terms[hidden // 2 :]
-        even = core_ref[0] == 0
+        even = spot_ref[0] % 2 == 0
         for ref, value in ((keep_ref, jnp.where(even, low, high)), (give_ref, jnp.where(even, high, low))):
             for q in range(pieces // 2):
                 ref[q, :piece] = value[q * piece : (q + 1) * piece].astype(ref.dtype)
@@ -112,30 +112,29 @@
     return call(
         kernel,
         [(shape, BF16), (shape, BF16), (half, F32), (half, BF16)],
-        [core, own_sum, mate_sum, weight, bias.reshape(1, hidden), grad_out],
+        [spot, own_sum, mate_sum, weight, bias.reshape(1, hidden), grad_out],
         flops=6 * rows_dev * hidden * hidden,
         smem=1,
     )
 
 
-def spread_halves(place, keep, got):
+def folded(spot, bit, keep, got, last=False):
     count, rows, hidden = keep.shape
-
-    def kernel(place_ref, keep_ref, got_ref, own_ref, *out_refs):
-        for other in range(count):
-            q = place_ref[0] ^ other
-            value = keep_ref[q] + got_ref[q].astype(F32)
-            if other == 0:
-                own_ref[...] = value
-            else:
-                out_refs[other - 1][...] = value.astype(BF16)
-
-    return call(
-        kernel,
-        [((rows, hidden), F32)] + [((rows, hidden), BF16)] * (count - 1),
-        [place, keep, got],
-        smem=1,
-    )
+    left = count if last else count // 2
+
+    def kernel(spot_ref, keep_ref, got_ref, *out_refs):
+        mine = (spot_ref[0] >> bit) % 2
+        for p in range(left):
+            if last:
+                out_refs[0][p] = (keep_ref[p] + got_ref[p].astype(F32)).astype(BF16)
+                continue
+            for ref, side in zip(out_refs, (mine, 1 - mine)):
+                q = side * left + p
+                ref[p] = (keep_ref[q] + got_ref[q].astype(F32)).astype(ref.dtype)
+
+    shape = (left, rows, hidden)
+    outs = [(shape, BF16)] if last else [(shape, F32), (shape, BF16)]
+    return call(kernel, outs, [spot, keep, got], smem=1)
 
 
 def summed_terms(*terms):
@@ -148,47 +147,26 @@
     return call(kernel, [(terms[0].shape, BF16)], list(terms))[0]
 
 
-def tree_sum(values):
-    values = [v.astype(F32) for v in values]
-    while len(values) > 1:
-        values = [values[k] + values[k + 1] for k in range(0, len(values), 2)]
-    return values[0]
-
-
-def summed_planes(values, piece):
-    shape = values[0].shape
-
-    def kernel(*refs):
-        value_refs, (weight_ref, bias_ref) = refs[:-2], refs[-2:]
-        total = tree_sum([ref[...] for ref in value_refs])
+def joined(spot, bit, mine, other):
+    rows, hidden = mine.shape
+
+    def kernel(spot_ref, mine_ref, other_ref, out_ref):
+        side = (spot_ref[0] >> bit) % 2
+        out_ref[pl.ds(pl.multiple_of(side * rows, rows), rows)] = mine_ref[...].astype(out_ref.dtype)
+        out_ref[pl.ds(pl.multiple_of((1 - side) * rows, rows), rows)] = other_ref[...].astype(out_ref.dtype)
+
+    return call(kernel, [((2 * rows, hidden), F32 if bit == 0 else BF16)], [spot, mine, other], smem=1)[0]
+
+
+def finished(mine, other, piece):
+    hidden = mine.shape[1]
+
+    def kernel(mine_ref, other_ref, weight_ref, bias_ref):
+        total = mine_ref[...].astype(F32) + other_ref[...].astype(F32)
         weight_ref[...] = total[:piece].astype(BF16)
         bias_ref[...] = total[piece : piece + 8]
 
-    return call(kernel, [((piece, shape[1]), BF16), ((8, shape[1]), F32)], list(values))
-
-
-def joined(place, pieces):
-    piece, hidden = pieces[0].shape
-    count = len(pieces)
-
-    def kernel(place_ref, *refs):
-        piece_refs, out_ref = refs[:-1], refs[-1]
-        for other, ref in enumerate(piece_refs):
-            q = place_ref[0] ^ other
-            out_ref[pl.ds(pl.multiple_of(q * piece, piece), piece)] = ref[...]
-
-    return call(kernel, [((count * piece, hidden), BF16)], [place, *pieces], smem=1)[0]
-
-
-def whole_weight(core, mine, other):
-    rows, hidden = mine.shape
-
-    def kernel(core_ref, mine_ref, other_ref, out_ref):
-        core_now = core_ref[0]
-        out_ref[pl.ds(pl.multiple_of(core_now * rows, rows), rows)] = mine_ref[...].astype(F32)
-        out_ref[pl.ds(pl.multiple_of((1 - core_now) * rows, rows), rows)] = other_ref[...].astype(F32)
-
-    return call(kernel, [((2 * rows, hidden), F32)], [core, mine, other], smem=1)[0]
+    return call(kernel, [((piece, hidden), BF16), ((8, hidden), F32)], [mine, other])
 
 
 def scattered_sums(flipped, own, mate, columns, dtypes):
@@ -252,82 +230,47 @@
         return terms[0], terms[0], [terms[self.reach], *arrived]
 
 
-class Relayed(Direct):
-    def __init__(self, count, reach):
-        super().__init__(count, reach)
-        self.table = [[2, 3, 0, 4, 1], [1, 3, 0, 4, 2]] * 2 + [[1, 3, 0, 4, 2]] * 4
-
-    def routed(self, value, step):
-        pairs = [(s, step(s) % self.count) for s in range(self.count) if step(s) is not None]
-        return lax.ppermute(value, "blk", pairs)
-
-    @staticmethod
-    def plane_step(s, sign):
-        return None if s % 2 else s + (8 * sign if s % 8 < 4 else -8 * sign)
-
-    def gather(self, features):
-        first = self.routed(features, lambda s: s + 4 if s % 2 else s ^ 4)
-        back, on = self.sent(features, 1), self.sent(features, -1)
-        relayed = self.routed(first, lambda s: self.plane_step(s, 1))
-        self.sources = [features, first, relayed, back, on]
-        return first
-
-    def sums(self, dense, rows_dev):
-        start = gathered_sums(dense, (0, 1, 2), (0, 2 * rows_dev), self.sources[:3])
-        return [
-            gathered_sums(dense, (3, 4), (side * rows_dev, (side + 1) * rows_dev), self.sources[3:], start)
-            for side in (1, 0)
-        ]
-
-    def scatter(self, flipped, own, mate):
-        to_plane, to_second, rest_second = scattered_sums(flipped, own, mate, (2, 1), [[BF16], [BF16, F32]])
-        relayed = self.routed(to_plane, lambda s: self.plane_step(s, -1))
-        straight = self.routed(to_second, lambda s: s - 4 if s % 2 else None)
-        to_back, to_on, kept = scattered_sums(flipped, own, mate, (3, 4, 0), [[BF16], [BF16], [F32]])
-        back, on = self.sent(to_back, -1), self.sent(to_on, 1)
-        out = summed_terms(rest_second, relayed)
-        swapped_sums = self.routed(out, lambda s: None if s % 2 else s ^ 4)
-        return to_back, out, [kept, straight, back, on, swapped_sums]
-
-
 def local(features, tile_list, tile_count, tile_values, weight, bias, grad_out):
     count = lax.axis_size("blk")
     me = lax.axis_index("blk")
     window = tile_values.shape[1]
     reach = window // 4
     rows_dev, hidden = features.shape
-    plane = 4
-    pieces = 2 * plane
-    core = (me % 2).astype(jnp.int32).reshape(1)
-    place = ((me // 2) % plane).astype(jnp.int32).reshape(1)
+    pieces = 8
     spot = (me % pieces).astype(jnp.int32).reshape(1)
-    route = (Relayed if reach == 2 else Direct)(count, reach)
+    route = Direct(count, reach)
 
     def swapped(value, distance):
         return lax.ppermute(value, "blk", [(s, s ^ distance) for s in range(count)])
 
-    first = route.gather(features)
-    first, tile_list, tile_count, tile_values = after(first, tile_list, tile_count, tile_values)
+    route.gather(features)
+    mate_values, tile_list, tile_count = after(swapped(tile_values[0], 1), tile_list, tile_count)
     meta = jnp.concatenate([tile_list[0].reshape(window, -1), tile_count[0][:, None]], axis=1).reshape(-1)
-    mate_meta, mate_values = swapped(meta, 1), swapped(tile_values[0], 1)
+    mate_meta = swapped(meta, 1)
     dense, flipped = dense_tiles(spot, meta, mate_meta, tile_values[0], mate_values, rows_dev, route.table)
     mate_sum, own_sum = route.sums(dense, rows_dev)
-    output, grad_agg, keep, give = layer(core, own_sum, swapped(mate_sum, 1), weight, bias, grad_out, pieces)
+    output, grad_agg, keep, give = layer(spot, own_sum, swapped(mate_sum, 1), weight, bias, grad_out, pieces)
 
     mate_grad, got = swapped(grad_agg, 1), swapped(give, 1)
-    own_piece, *give_pieces = spread_halves(place, keep, got)
-    mate_grad, *give_pieces = after(mate_grad, *give_pieces)
+    keep, give = folded(spot, 1, keep, got)
+    mate_grad, give = after(mate_grad, give)
     sent_first, sent_last, arriving = route.scatter(flipped, grad_agg, mate_grad)
-    own_piece, _ = after(own_piece, sent_first)
-    plane_sum = summed_terms(own_piece, *[swapped(v, 2 * (d + 1)) for d, v in enumerate(give_pieces)])
-    values = [plane_sum] + [swapped(plane_sum, pieces * d) for d in range(1, count // pieces)]
-    values[0], _ = after(values[0], sent_last)
-    piece_sum, bias_sum = summed_planes(values, hidden // pieces)
-    gathered = [swapped(piece_sum, 2 * d) for d in range(1, plane)]
-    piece_sum, *arriving = after(piece_sum, *arriving)
-    half = joined(place, [piece_sum, *gathered])
-    grad_weight = whole_weight(core, half, swapped(half, 1))
-    return (output, summed_terms(*arriving), grad_weight, bias_sum[0])
+    got = swapped(give, 2)
+    got, _ = after(got, sent_first)
+    keep, give = folded(spot, 2, keep, got)
+    total = folded(spot, 2, keep, swapped(give, 4), last=True)[0][0]
+    step = pieces
+    while 2 * step < count:
+        total = summed_terms(total, swapped(total, step))
+        step *= 2
+    total, bias_sum = finished(total, swapped(total, step), hidden // pieces)
+    grad_features = summed_terms(*arriving)
+    for bit in (2, 1, 0):
+        other = swapped(total, 1 << bit)
+        if bit == 2:
+            other, grad_features = after(other, grad_features)
+        total = joined(spot, bit, total, other)
+    return (output, grad_features, total, bias_sum[0])
 
 
 def solution(mesh):

time: 110 us -> 88.5 us (0.80)
  Pallas kernels: 22 us -> 12.9 us
  starting transfers between devices: 31.9 us -> 22.8 us
  local copies, waits for them, and re-layouts: 9.71 us -> 3.62 us
  waiting for transfers between devices: 43.8 us -> 47.4 us
    ppermute x5 -> x0, starting transfers between devices: 13.8 us -> none  [routed(): return lax.ppermute(value, 'blk', pairs)]
    ppermute x4 -> x8, starting transfers between devices: 5.36 us -> 16.5 us  [sent(): return lax.ppermute(value, 'blk', pairs)]
    ppermute x5 -> x0, waiting for transfers between devices: 10.3 us -> none  [routed(): return lax.ppermute(value, 'blk', pairs)]
    pallas_call x14, Pallas kernels: 22 us -> 12.9 us  [call(): pl.pallas_call(kernel, out_shape=out_shape, in_specs=[spec(k) for k in ra...]
    ppermute x4 -> x8, waiting for transfers between devices: 0.44 us -> 8.05 us  [sent(): return lax.ppermute(value, 'blk', pairs)]
    ppermute x15 -> x12, starting transfers between devices: 12.8 us -> 6.24 us  [swapped(): return lax.ppermute(value, 'blk', [(s, s ^ distance) for s in range(count)])]
    ppermute x15 -> x12, waiting for transfers between devices: 33.1 us -> 39.3 us  [swapped(): return lax.ppermute(value, 'blk', [(s, s ^ distance) for s in range(count)])]
    unnamed x28 -> x12, local copies, waits for them, and re-layouts: 8.26 us -> 2.18 us
  transfers between devices with their start and end apart: 24 -> 20, of which waited for: 11 -> 12; matrix products, arithmetic and copies ran while one was open for 2% -> 2% of each run, Pallas kernels for 12% -> 11%
where the time goes in v5:
time: 88.5 us; the launch traced here: 88.2 us
  waiting for transfers between devices  47.4 us (54%)
  starting transfers between devices  22.8 us (26%)
  Pallas kernels  12.9 us (15%)
  local copies, waits for them, and re-layouts  3.62 us (4%)
    ppermute x12, waiting for transfers between devices, swapped(): return lax.ppermute(value, 'blk', [(s, s ^ distance) for s in range(count)])  39.3 us
    ppermute x8, starting transfers between devices, sent(): return lax.ppermute(value, 'blk', pairs)  16.5 us
    pallas_call x14, Pallas kernels, call(): pl.pallas_call(kernel, out_shape=out_shape, in_specs=[spec(k) for k in ra...  12.9 us
    ppermute x8, waiting for transfers between devices, sent(): return lax.ppermute(value, 'blk', pairs)  8.05 us
    ppermute x12, starting transfers between devices, swapped(): return lax.ppermute(value, 'blk', [(s, s ^ distance) for s in range(count)])  6.24 us
    unnamed x12, local copies, waits for them, and re-layouts  2.18 us
  transfers between devices with their start and end apart: 20, of which 12 were waited for; matrix products, arithmetic and copies ran while one was open for 2% of the time, Pallas kernels for 11%

profile of v5, /device:TPU:0, one launch (start us, length us, event | category | flops | bytes accessed | tf_op | source)
XLA Modules:
  0.0 88.2 jit_solution(5254190462655302216)
XLA Ops:
  1.1 2.6 %collective-permute-start.2 = (bf16[384,512]{1,0:T(8,128)(2,1)}, bf16[384,512]{1,0:T(8,128)(2,1)S(1)}, u32[]{:S(2)}, u32[]{:S(2)}) collective-permute-start(bf16[384,512]{1,0:T(8,128)(2,1)} %refs_2_.3), channel_id=1, source_target_pairs={{0,4},{1,5},{2,6},{3,7},{4,8},{5,9},{6,10},{7,11},{8,12},{9,13},{1... | collective-permute-start | bytes 1179656 | tf_op jit(solution)/shard_map/ppermute | solution.py:203
  3.7 1.5 %collective-permute-start.3 = (bf16[384,512]{1,0:T(8,128)(2,1)}, bf16[384,512]{1,0:T(8,128)(2,1)S(1)}, u32[]{:S(2)}, u32[]{:S(2)}) collective-permute-start(bf16[384,512]{1,0:T(8,128)(2,1)} %refs_2_.3), channel_id=1, source_target_pairs={{0,2},{1,3},{2,4},{3,5},{4,6},{5,7},{6,8},{7,9},{8,10},{9,11},{10,... | collective-permute-start | bytes 1179656 | tf_op jit(solution)/shard_map/ppermute | solution.py:203
  5.2 4.1 %collective-permute-start.4 = (bf16[384,512]{1,0:T(8,128)(2,1)}, bf16[384,512]{1,0:T(8,128)(2,1)S(1)}, u32[]{:S(2)}, u32[]{:S(2)}) collective-permute-start(bf16[384,512]{1,0:T(8,128)(2,1)} %refs_2_.3), channel_id=1, source_target_pairs={{0,30},{1,31},{2,0},{3,1},{4,2},{5,3},{6,4},{7,5},{8,6},{9,7},{10,... | collective-permute-start | bytes 1179656 | tf_op jit(solution)/shard_map/ppermute | solution.py:203
  9.4 2.3 %collective-permute-start.5 = (bf16[384,512]{1,0:T(8,128)(2,1)}, bf16[384,512]{1,0:T(8,128)(2,1)S(1)}, u32[]{:S(2)}, u32[]{:S(2)}) collective-permute-start(bf16[384,512]{1,0:T(8,128)(2,1)} %refs_2_.3), channel_id=1, source_target_pairs={{0,28},{2,30},{4,0},{6,2},{8,4},{10,6},{12,8},{14,10},{16,12},{18,... | collective-permute-start | bytes 1179656 | tf_op jit(solution)/shard_map/ppermute | solution.py:203
  11.7 0.7 reshape_squeeze.3
  13.3 1.1 %collective-permute-done.1.mate_meta_ref = s32[120]{0:T(128)S(1)} collective-permute-done((s32[120]{0:T(128)S(1)}, s32[120]{0:T(128)S(1)}, u32[]{:S(2)}, u32[]{:S(2)}) %collective-permute-start.1) | collective-permute-done | bytes 512 | tf_op jit(solution)/shard_map/ppermute | solution.py:244
  14.4 1.5 %copy-done = bf16[1,8,7,128,128]{4,3,2,1,0:T(8,128)(2,1)S(1)} copy-done((bf16[1,8,7,128,128]{4,3,2,1,0:T(8,128)(2,1)S(1)}, bf16[1,8,7,128,128]{4,3,2,1,0:T(8,128)(2,1)}, u32[]{:S(2)}) %copy-start) | copy-done | bytes 1835032
  16.5 4.8 %shard_map.111 = (bf16[768,1920]{1,0:T(8,128)(2,1)S(1)}, bf16[1920,768]{1,0:T(8,128)(2,1)S(1)}) custom-call(s32[1]{0:T(128)} %bitcast.spot_ref, s32[40]{0:T(128)S(1)} %copy-done.5, s32[120]{0:T(128)S(1)} %reshape.22.own_meta_ref, s32[120]{0:T(128)S(1)} %collective-permute-done.1.mate_meta_ref, bf16[8,7,128,128]{3,2,1,0:T(8,128)(2,1)S(1)} %bitcast.9, ...), custom_call_target="tpu_custom_call" | custom-call | tf_op jit(solution)/shard_map/pallas_call | solution.py:16
  21.3 4.4 %collective-permute-done.2.refs_0_ = bf16[384,512]{1,0:T(8,128)(2,1)S(1)} collective-permute-done((bf16[384,512]{1,0:T(8,128)(2,1)}, bf16[384,512]{1,0:T(8,128)(2,1)S(1)}, u32[]{:S(2)}, u32[]{:S(2)}) %collective-permute-start.2) | collective-permute-done | bytes 393248 | tf_op jit(solution)/shard_map/ppermute | solution.py:203
  26.3 3.1 %collective-permute-done.5.refs_4_ = bf16[384,512]{1,0:T(8,128)(2,1)S(1)} collective-permute-done((bf16[384,512]{1,0:T(8,128)(2,1)}, bf16[384,512]{1,0:T(8,128)(2,1)S(1)}, u32[]{:S(2)}, u32[]{:S(2)}) %collective-permute-start.5) | collective-permute-done | bytes 393248 | tf_op jit(solution)/shard_map/ppermute | solution.py:203
  29.3 1.2 %shard_map.113 = f32[384,512]{1,0:T(8,128)S(1)} custom-call(bf16[768,1920]{1,0:T(8,128)(2,1)S(1)} %get-tuple-element.32.dense_ref, bf16[384,512]{1,0:T(8,128)(2,1)S(1)} %collective-permute-done.2.refs_0_, bf16[384,512]{1,0:T(8,128)(2,1)S(1)} %collective-permute-done.3.refs_1_, bf16[384,512]{1,0:T(8,128)(2,1)S(1)} %copy-done.1, ...), custom_call_target="tpu_custom_call" | custom-call | tf_op jit(solution)/shard_map/pallas_call | solution.py:16
  30.6 1.2 %shard_map.112.own_ref = f32[384,512]{1,0:T(8,128)S(1)} custom-call(bf16[768,1920]{1,0:T(8,128)(2,1)S(1)} %get-tuple-element.32.dense_ref, bf16[384,512]{1,0:T(8,128)(2,1)S(1)} %collective-permute-done.2.refs_0_, bf16[384,512]{1,0:T(8,128)(2,1)S(1)} %collective-permute-done.3.refs_1_, bf16[384,512]{1,0:T(8,128)(2,1)S(1)} %copy-done.1, ...), custom_call_target="tpu_custom_call" | custom-call | tf_op jit(solution)/shard_map/pallas_call | solution.py:16
  31.8 1.1 %collective-permute-done.6.mate_ref = f32[384,512]{1,0:T(8,128)S(1)} collective-permute-done((f32[384,512]{1,0:T(8,128)S(1)}, f32[384,512]{1,0:T(8,128)S(1)}, u32[]{:S(2)}, u32[]{:S(2)}) %collective-permute-start.6) | collective-permute-done | bytes 786464 | tf_op jit(solution)/shard_map/ppermute | solution.py:244
  32.9 1.4 %shard_map.114 = (bf16[384,512]{1,0:T(8,128)(2,1)}, bf16[384,512]{1,0:T(8,128)(2,1)S(1)}, f32[4,80,512]{2,1,0:T(8,128)S(1)}, bf16[4,80,512]{2,1,0:T(8,128)(2,1)S(1)}) custom-call(s32[1]{0:T(128)} %bitcast.spot_ref, f32[384,512]{1,0:T(8,128)S(1)} %shard_map.112.own_ref, f32[384,512]{1,0:T(8,128)S(1)} %collective-permute-done.6.mate_ref, ...), custom_call_target="tpu_custom_call" | custom-call | tf_op jit(solution)/shard_map/pallas_call | solution.py:16
  34.8 1.7 %collective-permute-done.7.got_ref = bf16[4,80,512]{2,1,0:T(8,128)(2,1)S(1)} collective-permute-done((bf16[4,80,512]{2,1,0:T(8,128)(2,1)S(1)}, bf16[4,80,512]{2,1,0:T(8,128)(2,1)S(1)}, u32[]{:S(2)}, u32[]{:S(2)}) %collective-permute-start.7) | collective-permute-done | bytes 327712 | tf_op jit(solution)/shard_map/ppermute | solution.py:244
  36.6 1.6 %collective-permute-start.9 = (bf16[2,80,512]{2,1,0:T(8,128)(2,1)S(1)}, bf16[2,80,512]{2,1,0:T(8,128)(2,1)S(1)}, u32[]{:S(2)}, u32[]{:S(2)}) collective-permute-start(bf16[2,80,512]{2,1,0:T(8,128)(2,1)S(1)} %get-tuple-element.39), channel_id=1, source_target_pairs={{0,2},{1,3},{2,0},{3,1},{4,6},{5,7},{6,4},{7,5},{8,10},{9,11},{10,... | collective-permute-start | bytes 491528 | tf_op jit(solution)/shard_map/ppermute | solution.py:244
  38.1 2.2 %shard_map.116 = (bf16[384,512]{1,0:T(8,128)(2,1)S(1)}, bf16[384,512]{1,0:T(8,128)(2,1)S(1)}, f32[384,512]{1,0:T(8,128)S(1)}, bf16[384,512]{1,0:T(8,128)(2,1)S(1)}, bf16[384,512]{1,0:T(8,128)(2,1)S(1)}) custom-call(bf16[1920,768]{1,0:T(8,128)(2,1)S(1)} %get-tuple-element.40.flipped_ref, bf16[384,512]{1,0:T(8,128)(2,1)S(1)} %get-tuple-element.37.own_ref, ...), custom_call_target="tpu_custom_call" | custom-call | tf_op jit(solution)/shard_map/pallas_call | solution.py:16
  40.3 1.8 %collective-permute-start.14 = (bf16[384,512]{1,0:T(8,128)(2,1)S(1)}, bf16[384,512]{1,0:T(8,128)(2,1)S(1)}, u32[]{:S(2)}, u32[]{:S(2)}) collective-permute-start(bf16[384,512]{1,0:T(8,128)(2,1)S(1)} %get-tuple-element.42), channel_id=1, source_target_pairs={{0,28},{1,29},{2,30},{3,31},{4,0},{5,1},{6,2},{7,3},{8,4},{9,5},{1... | collective-permute-start | bytes 1179656 | tf_op jit(solution)/shard_map/ppermute | solution.py:203
  42.1 1.4 %collective-permute-start.15 = (bf16[384,512]{1,0:T(8,128)(2,1)S(1)}, bf16[384,512]{1,0:T(8,128)(2,1)S(1)}, u32[]{:S(2)}, u32[]{:S(2)}) collective-permute-start(bf16[384,512]{1,0:T(8,128)(2,1)S(1)} %get-tuple-element.48), channel_id=1, source_target_pairs={{0,30},{1,31},{2,0},{3,1},{4,2},{5,3},{6,4},{7,5},{8,6},{9,7},{10,... | collective-permute-start | bytes 1179656 | tf_op jit(solution)/shard_map/ppermute | solution.py:203
  43.5 0.7 collective-permute-start.16
  44.2 2.2 %collective-permute-start.17 = (bf16[384,512]{1,0:T(8,128)(2,1)S(1)}, bf16[384,512]{1,0:T(8,128)(2,1)S(1)}, u32[]{:S(2)}, u32[]{:S(2)}) collective-permute-start(bf16[384,512]{1,0:T(8,128)(2,1)S(1)} %get-tuple-element.50), channel_id=1, source_target_pairs={{0,4},{2,6},{4,8},{6,10},{8,12},{10,14},{12,16},{14,18},{16,20},{1... | collective-permute-start | bytes 1179656 | tf_op jit(solution)/shard_map/ppermute | solution.py:203
  46.4 0.9 %collective-permute-start.10 = (bf16[1,80,512]{2,1,0:T(8,128)(2,1)S(1)}, bf16[1,80,512]{2,1,0:T(8,128)(2,1)S(1)}, u32[]{:S(2)}, u32[]{:S(2)}) collective-permute-start(bf16[1,80,512]{2,1,0:T(8,128)(2,1)S(1)} %get-tuple-element.45), channel_id=1, source_target_pairs={{0,4},{1,5},{2,6},{3,7},{4,0},{5,1},{6,2},{7,3},{8,12},{9,13},{10,... | collective-permute-start | bytes 245768 | tf_op jit(solution)/shard_map/ppermute | solution.py:244
  47.3 18.3 %collective-permute-done.10.got_ref = bf16[1,80,512]{2,1,0:T(8,128)(2,1)S(1)} collective-permute-done((bf16[1,80,512]{2,1,0:T(8,128)(2,1)S(1)}, bf16[1,80,512]{2,1,0:T(8,128)(2,1)S(1)}, u32[]{:S(2)}, u32[]{:S(2)}) %collective-permute-start.10) | collective-permute-done | bytes 81952 | tf_op jit(solution)/shard_map/ppermute | solution.py:244
  65.7 4.4 %collective-permute-done.11.refs_1_ = bf16[80,512]{1,0:T(8,128)(2,1)S(1)} collective-permute-done((bf16[80,512]{1,0:T(8,128)(2,1)S(1)}, bf16[80,512]{1,0:T(8,128)(2,1)S(1)}, u32[]{:S(2)}, u32[]{:S(2)}) %collective-permute-start.11) | collective-permute-done | bytes 81952 | tf_op jit(solution)/shard_map/ppermute | solution.py:244
  70.2 1.2 %collective-permute-start.12 = (bf16[80,512]{1,0:T(8,128)(2,1)S(1)}, bf16[80,512]{1,0:T(8,128)(2,1)S(1)}, u32[]{:S(2)}, u32[]{:S(2)}) collective-permute-start(bf16[80,512]{1,0:T(8,128)(2,1)S(1)} %shard_map.119.mine_ref), channel_id=1, source_target_pairs={{0,16},{1,17},{2,18},{3,19},{4,20},{5,21},{6,22},{7,23},{8,24},{9,... | collective-permute-start | bytes 245768 | tf_op jit(solution)/shard_map/ppermute | solution.py:244
  71.4 4.8 %collective-permute-done.12.other_ref = bf16[80,512]{1,0:T(8,128)(2,1)S(1)} collective-permute-done((bf16[80,512]{1,0:T(8,128)(2,1)S(1)}, bf16[80,512]{1,0:T(8,128)(2,1)S(1)}, u32[]{:S(2)}, u32[]{:S(2)}) %collective-permute-start.12) | collective-permute-done | bytes 81952 | tf_op jit(solution)/shard_map/ppermute | solution.py:244
  76.5 1.0 %shard_map.121 = bf16[384,512]{1,0:T(8,128)(2,1)} custom-call(f32[384,512]{1,0:T(8,128)S(1)} %get-tuple-element.47.refs_0_, bf16[384,512]{1,0:T(8,128)(2,1)S(1)} %collective-permute-done.14.refs_1_, bf16[384,512]{1,0:T(8,128)(2,1)S(1)} %collective-permute-done.15.refs_2_, bf16[384,512]{1,0:T(8,128)(2,1)S(1)} %collective-permute-done.16.refs_3_, ...), custom_call_target="tpu_custom_call" | custom-call | tf_op jit(solution)/shard_map/pallas_call | solution.py:16
  77.5 3.0 %collective-permute-done.13.other_ref = bf16[64,512]{1,0:T(8,128)(2,1)S(1)} collective-permute-done((bf16[64,512]{1,0:T(8,128)(2,1)S(1)}, bf16[64,512]{1,0:T(8,128)(2,1)S(1)}, u32[]{:S(2)}, u32[]{:S(2)}) %collective-permute-start.13) | collective-permute-done | bytes 65568 | tf_op jit(solution)/shard_map/ppermute | solution.py:244
  80.5 1.0 %collective-permute-start.18 = (bf16[128,512]{1,0:T(8,128)(2,1)S(1)}, bf16[128,512]{1,0:T(8,128)(2,1)S(1)}, u32[]{:S(2)}, u32[]{:S(2)}) collective-permute-start(bf16[128,512]{1,0:T(8,128)(2,1)S(1)} %shard_map.122.mine_ref), channel_id=1, source_target_pairs={{0,2},{1,3},{2,0},{3,1},{4,6},{5,7},{6,4},{7,5},{8,10},{9,11},{10,... | collective-permute-start | bytes 393224 | tf_op jit(solution)/shard_map/ppermute | solution.py:244
  81.5 4.0 %collective-permute-done.18.other_ref = bf16[128,512]{1,0:T(8,128)(2,1)S(1)} collective-permute-done((bf16[128,512]{1,0:T(8,128)(2,1)S(1)}, bf16[128,512]{1,0:T(8,128)(2,1)S(1)}, u32[]{:S(2)}, u32[]{:S(2)}) %collective-permute-start.18) | collective-permute-done | bytes 131104 | tf_op jit(solution)/shard_map/ppermute | solution.py:244
  86.2 0.9 %collective-permute-done.19.other_ref = bf16[256,512]{1,0:T(8,128)(2,1)S(1)} collective-permute-done((bf16[256,512]{1,0:T(8,128)(2,1)S(1)}, bf16[256,512]{1,0:T(8,128)(2,1)S(1)}, u32[]{:S(2)}, u32[]{:S(2)}) %collective-permute-start.19) | collective-permute-done | bytes 262176 | tf_op jit(solution)/shard_map/ppermute | solution.py:244
  87.1 1.0 %shard_map.124 = f32[512,512]{1,0:T(8,128)} custom-call(s32[1]{0:T(128)} %bitcast.spot_ref, bf16[256,512]{1,0:T(8,128)(2,1)S(1)} %shard_map.123.mine_ref, bf16[256,512]{1,0:T(8,128)(2,1)S(1)} %collective-permute-done.19.other_ref), custom_call_target="tpu_custom_call" | custom-call | tf_op jit(solution)/shard_map/pallas_call | solution.py:16
  (39 shorter events, 4.5 us)
Async XLA Ops:
  0.6 11.1 %collective-permute-start = (bf16[8,7,128,128]{3,2,1,0:T(8,128)(2,1)}, bf16[8,7,128,128]{3,2,1,0:T(8,128)(2,1)S(1)}, u32[]{:S(2)}, u32[]{:S(2)}) collective-permute-start(bf16[8,7,128,128]{3,2,1,0:T(8,128)(2,1)} %bitcast.8), channel_id=1, source_target_pairs={{0,1},{1,0},{2,3},{3,2},{4,5},{5,4},{6,7},{7,6},{8,9},{9,8},{10,11... | collective-permute-start | bytes 5505032 | tf_op jit(solution)/shard_map/ppermute | solution.py:244
  1.1 24.5 %collective-permute-start.2 = (bf16[384,512]{1,0:T(8,128)(2,1)}, bf16[384,512]{1,0:T(8,128)(2,1)S(1)}, u32[]{:S(2)}, u32[]{:S(2)}) collective-permute-start(bf16[384,512]{1,0:T(8,128)(2,1)} %refs_2_.3), channel_id=1, source_target_pairs={{0,4},{1,5},{2,6},{3,7},{4,8},{5,9},{6,10},{7,11},{8,12},{9,13},{1... | collective-permute-start | bytes 1179656 | tf_op jit(solution)/shard_map/ppermute | solution.py:203
  3.7 22.5 %collective-permute-start.3 = (bf16[384,512]{1,0:T(8,128)(2,1)}, bf16[384,512]{1,0:T(8,128)(2,1)S(1)}, u32[]{:S(2)}, u32[]{:S(2)}) collective-permute-start(bf16[384,512]{1,0:T(8,128)(2,1)} %refs_2_.3), channel_id=1, source_target_pairs={{0,2},{1,3},{2,4},{3,5},{4,6},{5,7},{6,8},{7,9},{8,10},{9,11},{10,... | collective-permute-start | bytes 1179656 | tf_op jit(solution)/shard_map/ppermute | solution.py:203
  5.2 21.1 %collective-permute-start.4 = (bf16[384,512]{1,0:T(8,128)(2,1)}, bf16[384,512]{1,0:T(8,128)(2,1)S(1)}, u32[]{:S(2)}, u32[]{:S(2)}) collective-permute-start(bf16[384,512]{1,0:T(8,128)(2,1)} %refs_2_.3), channel_id=1, source_target_pairs={{0,30},{1,31},{2,0},{3,1},{4,2},{5,3},{6,4},{7,5},{8,6},{9,7},{10,... | collective-permute-start | bytes 1179656 | tf_op jit(solution)/shard_map/ppermute | solution.py:203
  9.4 20.0 %collective-permute-start.5 = (bf16[384,512]{1,0:T(8,128)(2,1)}, bf16[384,512]{1,0:T(8,128)(2,1)S(1)}, u32[]{:S(2)}, u32[]{:S(2)}) collective-permute-start(bf16[384,512]{1,0:T(8,128)(2,1)} %refs_2_.3), channel_id=1, source_target_pairs={{0,28},{2,30},{4,0},{6,2},{8,4},{10,6},{12,8},{14,10},{16,12},{18,... | collective-permute-start | bytes 1179656 | tf_op jit(solution)/shard_map/ppermute | solution.py:203
  13.2 1.1 %collective-permute-start.1 = (s32[120]{0:T(128)S(1)}, s32[120]{0:T(128)S(1)}, u32[]{:S(2)}, u32[]{:S(2)}) collective-permute-start(s32[120]{0:T(128)S(1)} %reshape.22.own_meta_ref), channel_id=1, source_target_pairs={{0,1},{1,0},{2,3},{3,2},{4,5},{5,4},{6,7},{7,6},{8,9},{9,8},{10,11... | collective-permute-start | bytes 1448 | tf_op jit(solution)/shard_map/ppermute | solution.py:244
  14.4 1.5 %copy-start = (bf16[1,8,7,128,128]{4,3,2,1,0:T(8,128)(2,1)S(1)}, bf16[1,8,7,128,128]{4,3,2,1,0:T(8,128)(2,1)}, u32[]{:S(2)}) copy-start(bf16[1,8,7,128,128]{4,3,2,1,0:T(8,128)(2,1)} %param.11) | copy-start | bytes 5505028
  15.9 0.7 copy-start.5
  16.5 12.8 %copy-start.1 = (bf16[384,512]{1,0:T(8,128)(2,1)S(1)}, bf16[384,512]{1,0:T(8,128)(2,1)}, u32[]{:S(2)}) copy-start(bf16[384,512]{1,0:T(8,128)(2,1)} %refs_2_.3) | copy-start | bytes 1179652
  30.5 2.4 %copy-start.2 = (bf16[512,512]{1,0:T(8,128)(2,1)S(1)}, bf16[512,512]{1,0:T(8,128)(2,1)}, u32[]{:S(2)}) copy-start(bf16[512,512]{1,0:T(8,128)(2,1)} %weight_ref.1) | copy-start | bytes 1572868
  30.5 2.4 %copy-start.3 = (bf16[384,512]{1,0:T(8,128)(2,1)S(1)}, bf16[384,512]{1,0:T(8,128)(2,1)}, u32[]{:S(2)}) copy-start(bf16[384,512]{1,0:T(8,128)(2,1)} %grad_out_ref.1) | copy-start | bytes 1179652
  30.5 2.4 %copy-start.4 = (f32[512]{0:T(512)S(1)}, f32[512]{0:T(512)}, u32[]{:S(2)}) copy-start(f32[512]{0:T(512)} %param.13) | copy-start | bytes 6148
  30.6 2.4 %collective-permute-start.6 = (f32[384,512]{1,0:T(8,128)S(1)}, f32[384,512]{1,0:T(8,128)S(1)}, u32[]{:S(2)}, u32[]{:S(2)}) collective-permute-start(f32[384,512]{1,0:T(8,128)S(1)} %shard_map.113), channel_id=1, source_target_pairs={{0,1},{1,0},{2,3},{3,2},{4,5},{5,4},{6,7},{7,6},{8,9},{9,8},{10,11... | collective-permute-start | bytes 2359304 | tf_op jit(solution)/shard_map/ppermute | solution.py:244
  34.3 2.3 %collective-permute-start.8 = (bf16[384,512]{1,0:T(8,128)(2,1)S(1)}, bf16[384,512]{1,0:T(8,128)(2,1)S(1)}, u32[]{:S(2)}, u32[]{:S(2)}) collective-permute-start(bf16[384,512]{1,0:T(8,128)(2,1)S(1)} %get-tuple-element.37.own_ref), channel_id=1, source_target_pairs={{0,1},{1,0},{2,3},{3,2},{4,5},{5,4},{6,7},{7,6},{8,9},{9,8},{10,11... | collective-permute-start | bytes 1179656 | tf_op jit(solution)/shard_map/ppermute | solution.py:244
  34.4 2.1 %collective-permute-start.7 = (bf16[4,80,512]{2,1,0:T(8,128)(2,1)S(1)}, bf16[4,80,512]{2,1,0:T(8,128)(2,1)S(1)}, u32[]{:S(2)}, u32[]{:S(2)}) collective-permute-start(bf16[4,80,512]{2,1,0:T(8,128)(2,1)S(1)} %get-tuple-element.35), channel_id=1, source_target_pairs={{0,1},{1,0},{2,3},{3,2},{4,5},{5,4},{6,7},{7,6},{8,9},{9,8},{10,11... | collective-permute-start | bytes 983048 | tf_op jit(solution)/shard_map/ppermute | solution.py:244
  36.6 9.8 %collective-permute-start.9 = (bf16[2,80,512]{2,1,0:T(8,128)(2,1)S(1)}, bf16[2,80,512]{2,1,0:T(8,128)(2,1)S(1)}, u32[]{:S(2)}, u32[]{:S(2)}) collective-permute-start(bf16[2,80,512]{2,1,0:T(8,128)(2,1)S(1)} %get-tuple-element.39), channel_id=1, source_target_pairs={{0,2},{1,3},{2,0},{3,1},{4,6},{5,7},{6,4},{7,5},{8,10},{9,11},{10,... | collective-permute-start | bytes 491528 | tf_op jit(solution)/shard_map/ppermute | solution.py:244
  40.3 36.2 %collective-permute-start.14 = (bf16[384,512]{1,0:T(8,128)(2,1)S(1)}, bf16[384,512]{1,0:T(8,128)(2,1)S(1)}, u32[]{:S(2)}, u32[]{:S(2)}) collective-permute-start(bf16[384,512]{1,0:T(8,128)(2,1)S(1)} %get-tuple-element.42), channel_id=1, source_target_pairs={{0,28},{1,29},{2,30},{3,31},{4,0},{5,1},{6,2},{7,3},{8,4},{9,5},{1... | collective-permute-start | bytes 1179656 | tf_op jit(solution)/shard_map/ppermute | solution.py:203
  42.1 34.4 %collective-permute-start.15 = (bf16[384,512]{1,0:T(8,128)(2,1)S(1)}, bf16[384,512]{1,0:T(8,128)(2,1)S(1)}, u32[]{:S(2)}, u32[]{:S(2)}) collective-permute-start(bf16[384,512]{1,0:T(8,128)(2,1)S(1)} %get-tuple-element.48), channel_id=1, source_target_pairs={{0,30},{1,31},{2,0},{3,1},{4,2},{5,3},{6,4},{7,5},{8,6},{9,7},{10,... | collective-permute-start | bytes 1179656 | tf_op jit(solution)/shard_map/ppermute | solution.py:203
  43.5 33.0 %collective-permute-start.16 = (bf16[384,512]{1,0:T(8,128)(2,1)S(1)}, bf16[384,512]{1,0:T(8,128)(2,1)S(1)}, u32[]{:S(2)}, u32[]{:S(2)}) collective-permute-start(bf16[384,512]{1,0:T(8,128)(2,1)S(1)} %get-tuple-element.49), channel_id=1, source_target_pairs={{0,2},{1,3},{2,4},{3,5},{4,6},{5,7},{6,8},{7,9},{8,10},{9,11},{10,... | collective-permute-start | bytes 1179656 | tf_op jit(solution)/shard_map/ppermute | solution.py:203
  44.2 32.3 %collective-permute-start.17 = (bf16[384,512]{1,0:T(8,128)(2,1)S(1)}, bf16[384,512]{1,0:T(8,128)(2,1)S(1)}, u32[]{:S(2)}, u32[]{:S(2)}) collective-permute-start(bf16[384,512]{1,0:T(8,128)(2,1)S(1)} %get-tuple-element.50), channel_id=1, source_target_pairs={{0,4},{2,6},{4,8},{6,10},{8,12},{10,14},{12,16},{14,18},{16,20},{1... | collective-permute-start | bytes 1179656 | tf_op jit(solution)/shard_map/ppermute | solution.py:203
  46.4 19.2 %collective-permute-start.10 = (bf16[1,80,512]{2,1,0:T(8,128)(2,1)S(1)}, bf16[1,80,512]{2,1,0:T(8,128)(2,1)S(1)}, u32[]{:S(2)}, u32[]{:S(2)}) collective-permute-start(bf16[1,80,512]{2,1,0:T(8,128)(2,1)S(1)} %get-tuple-element.45), channel_id=1, source_target_pairs={{0,4},{1,5},{2,6},{3,7},{4,0},{5,1},{6,2},{7,3},{8,12},{9,13},{10,... | collective-permute-start | bytes 245768 | tf_op jit(solution)/shard_map/ppermute | solution.py:244
  65.7 4.5 %collective-permute-start.11 = (bf16[80,512]{1,0:T(8,128)(2,1)S(1)}, bf16[80,512]{1,0:T(8,128)(2,1)S(1)}, u32[]{:S(2)}, u32[]{:S(2)}) collective-permute-start(bf16[80,512]{1,0:T(8,128)(2,1)S(1)} %bitcast.10), channel_id=1, source_target_pairs={{0,8},{1,9},{2,10},{3,11},{4,12},{5,13},{6,14},{7,15},{8,0},{9,1},... | collective-permute-start | bytes 245768 | tf_op jit(solution)/shard_map/ppermute | solution.py:244
  70.2 5.9 %collective-permute-start.12 = (bf16[80,512]{1,0:T(8,128)(2,1)S(1)}, bf16[80,512]{1,0:T(8,128)(2,1)S(1)}, u32[]{:S(2)}, u32[]{:S(2)}) collective-permute-start(bf16[80,512]{1,0:T(8,128)(2,1)S(1)} %shard_map.119.mine_ref), channel_id=1, source_target_pairs={{0,16},{1,17},{2,18},{3,19},{4,20},{5,21},{6,22},{7,23},{8,24},{9,... | collective-permute-start | bytes 245768 | tf_op jit(solution)/shard_map/ppermute | solution.py:244
  76.1 4.3 %collective-permute-start.13 = (bf16[64,512]{1,0:T(8,128)(2,1)S(1)}, bf16[64,512]{1,0:T(8,128)(2,1)S(1)}, u32[]{:S(2)}, u32[]{:S(2)}) collective-permute-start(bf16[64,512]{1,0:T(8,128)(2,1)S(1)} %get-tuple-element.46.mine_ref), channel_id=1, source_target_pairs={{0,4},{1,5},{2,6},{3,7},{4,0},{5,1},{6,2},{7,3},{8,12},{9,13},{10,... | collective-permute-start | bytes 196616 | tf_op jit(solution)/shard_map/ppermute | solution.py:244
  80.5 5.0 %collective-permute-start.18 = (bf16[128,512]{1,0:T(8,128)(2,1)S(1)}, bf16[128,512]{1,0:T(8,128)(2,1)S(1)}, u32[]{:S(2)}, u32[]{:S(2)}) collective-permute-start(bf16[128,512]{1,0:T(8,128)(2,1)S(1)} %shard_map.122.mine_ref), channel_id=1, source_target_pairs={{0,2},{1,3},{2,0},{3,1},{4,6},{5,7},{6,4},{7,5},{8,10},{9,11},{10,... | collective-permute-start | bytes 393224 | tf_op jit(solution)/shard_map/ppermute | solution.py:244
  85.5 1.6 %collective-permute-start.19 = (bf16[256,512]{1,0:T(8,128)(2,1)S(1)}, bf16[256,512]{1,0:T(8,128)(2,1)S(1)}, u32[]{:S(2)}, u32[]{:S(2)}) collective-permute-start(bf16[256,512]{1,0:T(8,128)(2,1)S(1)} %shard_map.123.mine_ref), channel_id=1, source_target_pairs={{0,1},{1,0},{2,3},{3,2},{4,5},{5,4},{6,7},{7,6},{8,9},{9,8},{10,11... | collective-permute-start | bytes 786440 | tf_op jit(solution)/shard_map/ppermute | solution.py:244

commit v6 on v5

--- a/solution.py
+++ b/solution.py
@@ -23,13 +23,11 @@
     )(*ins)
 
 
-def dense_tiles(spot, own_meta, mate_meta, own_values, mate_values, rows_dev, table):
+def dense_tiles(spot, own_meta, mate_meta, own_values, mate_values, rows_dev, positions):
     window, slots, tile, _ = own_values.shape
     tile_rows = rows_dev // tile
-    positions = len(table[0])
-
-    def kernel(spot_ref, table_ref, own_meta_ref, mate_meta_ref, own_ref, mate_ref, dense_ref, flipped_ref):
-        spot_now = spot_ref[0]
+
+    def kernel(spot_ref, own_meta_ref, mate_meta_ref, own_ref, mate_ref, dense_ref, flipped_ref):
         dense_ref[...] = jnp.zeros_like(dense_ref)
         flipped_ref[...] = jnp.zeros_like(flipped_ref)
 
@@ -42,8 +40,7 @@
                 @pl.when(k < meta_ref[base + 2 * slots])
                 def _():
                     row = pl.multiple_of((meta_ref[base + 2 * k] + first_row) * tile, tile)
-                    column = table_ref[spot_now * positions + i + shift]
-                    col = pl.multiple_of((column * tile_rows + meta_ref[base + 2 * k + 1]) * tile, tile)
+                    col = pl.multiple_of(((i + shift) * tile_rows + meta_ref[base + 2 * k + 1]) * tile, tile)
                     values = values_ref[j, k]
                     dense_ref[pl.ds(row, tile), pl.ds(col, tile)] = values
                     flipped_ref[pl.ds(col, tile), pl.ds(row, tile)] = values.T
@@ -53,14 +50,14 @@
             lax.fori_loop(0, (window // 2) * slots, slot, 0)
 
         place(own_meta_ref, own_ref, 0, 0, 0)
-        place(mate_meta_ref, mate_ref, 1, 1 - spot_now % 2, tile_rows)
+        place(mate_meta_ref, mate_ref, 1, 1 - spot_ref[0] % 2, tile_rows)
 
     wide = positions * rows_dev
     return call(
         kernel,
         [((2 * rows_dev, wide), BF16), ((wide, 2 * rows_dev), BF16)],
-        [spot, jnp.asarray(table, jnp.int32).reshape(-1), own_meta, mate_meta, own_values, mate_values],
-        smem=4,
+        [spot, own_meta, mate_meta, own_values, mate_values],
+        smem=3,
     )
 
 
@@ -137,25 +134,31 @@
     return call(kernel, outs, [spot, keep, got], smem=1)
 
 
-def summed_terms(*terms):
-    def kernel(*refs):
-        total = refs[0][...].astype(F32)
-        for ref in refs[1:-1]:
-            total = total + ref[...].astype(F32)
+def summed_terms(spot, terms, masks=None):
+    masks = masks or [None] * len(terms)
+
+    def kernel(spot_ref, *refs):
+        total = None
+        for ref, mask in zip(refs, masks):
+            value = ref[...].astype(F32)
+            if mask is not None:
+                value = jnp.where((mask >> spot_ref[0]) % 2 == 1, value, 0.0)
+            total = value if total is None else total + value
         refs[-1][...] = total.astype(BF16)
 
-    return call(kernel, [(terms[0].shape, BF16)], list(terms))[0]
-
-
-def joined(spot, bit, mine, other):
-    rows, hidden = mine.shape
-
-    def kernel(spot_ref, mine_ref, other_ref, out_ref):
-        side = (spot_ref[0] >> bit) % 2
-        out_ref[pl.ds(pl.multiple_of(side * rows, rows), rows)] = mine_ref[...].astype(out_ref.dtype)
-        out_ref[pl.ds(pl.multiple_of((1 - side) * rows, rows), rows)] = other_ref[...].astype(out_ref.dtype)
-
-    return call(kernel, [((2 * rows, hidden), F32 if bit == 0 else BF16)], [spot, mine, other], smem=1)[0]
+    return call(kernel, [(terms[0].shape, BF16)], [spot, *terms], smem=1)[0]
+
+
+def joined(spot, bits, pieces, dtype):
+    rows, hidden = pieces[0].shape
+    low, high = bits
+
+    def kernel(spot_ref, *refs):
+        side = (spot_ref[0] >> low) % (1 << (high - low))
+        for other, ref in enumerate(refs[:-1]):
+            refs[-1][pl.ds(pl.multiple_of((side ^ other) * rows, rows), rows)] = ref[...].astype(dtype)
+
+    return call(kernel, [((len(pieces) * rows, hidden), dtype)], [spot, *pieces], smem=1)[0]
 
 
 def finished(mine, other, piece):
@@ -169,13 +172,20 @@
     return call(kernel, [((piece, hidden), BF16), ((8, hidden), F32)], [mine, other])
 
 
-def scattered_sums(flipped, own, mate, columns, dtypes):
+def scattered_sums(flipped, own, mate, columns, dtypes, spot=None, lookup=None):
     rows_dev, hidden = own.shape
-
-    def kernel(flipped_ref, own_ref, mate_ref, *out_refs):
-        out_refs = list(out_refs)
+    extra = [] if lookup is None else [spot, jnp.asarray(lookup, jnp.int32).reshape(-1)]
+
+    def kernel(*refs):
+        refs = list(refs)
+        picks = [refs.pop(0) for _ in extra]
+        flipped_ref, own_ref, mate_ref, *out_refs = refs
         for column, kinds in zip(columns, dtypes):
-            part = pl.ds(column * rows_dev, rows_dev)
+            if picks:
+                column = picks[1][picks[0][0] * len(lookup[0]) + column]
+                part = pl.ds(pl.multiple_of(column * rows_dev, rows_dev), rows_dev)
+            else:
+                part = pl.ds(column * rows_dev, rows_dev)
             total = jnp.dot(flipped_ref[part, :rows_dev], own_ref[...], preferred_element_type=F32)
             total += jnp.dot(flipped_ref[part, rows_dev:], mate_ref[...], preferred_element_type=F32)
             for kind in kinds:
@@ -184,8 +194,9 @@
     return call(
         kernel,
         [((rows_dev, hidden), kind) for kinds in dtypes for kind in kinds],
-        [flipped, own, mate],
+        [*extra, flipped, own, mate],
         flops=4 * rows_dev * rows_dev * hidden * len(columns),
+        smem=len(extra),
     )
 
 
@@ -194,9 +205,8 @@
 
 
 class Direct:
-    def __init__(self, count, reach):
-        self.count, self.reach, self.positions = count, reach, 2 * reach + 1
-        self.table = [list(range(self.positions))] * 8
+    def __init__(self, count, reach, spot):
+        self.count, self.reach, self.positions, self.spot = count, reach, 2 * reach + 1, spot
 
     def sent(self, value, chips, kept=lambda s: True):
         pairs = [(s, (s + 2 * chips) % self.count) for s in range(self.count) if kept(s)]
@@ -210,7 +220,6 @@
             else self.sent(features, self.reach - m, lambda s: m < last or s % 2 == 0)
             for m in range(self.positions)
         ]
-        return self.sources[0]
 
     def sums(self, dense, rows_dev):
         columns = range(self.positions)
@@ -219,15 +228,71 @@
         ]
 
     def scatter(self, flipped, own, mate):
+        self.flipped, self.own, self.mate = flipped, own, mate
+
+    def step(self, k, token):
+        if k != 1:
+            return []
+        _, mate = after(token, self.mate)
         kinds = [[F32 if m == self.reach else BF16] for m in range(self.positions)]
-        terms = scattered_sums(flipped, own, mate, range(self.positions), kinds)
+        terms = scattered_sums(self.flipped, self.own, mate, range(self.positions), kinds)
         last = self.positions - 1
-        arrived = [
-            self.sent(terms[m], m - self.reach, lambda s: m < last or s % 2 == 0)
-            for m in range(self.positions)
-            if m != self.reach
+        self.arriving = [
+            term if m == self.reach else self.sent(term, m - self.reach, lambda s: m < last or s % 2 == 0)
+            for m, term in enumerate(terms)
         ]
-        return terms[0], terms[0], [terms[self.reach], *arrived]
+        return terms[:1]
+
+    def finish(self):
+        return summed_terms(self.spot, self.arriving)
+
+
+class Relayed(Direct):
+    EVEN, MIDDLE, ENDS, ODD_LOW = 0b01010101, 0b00111100, 0b11000011, 0b00001010
+    LOOKUP = [
+        [2, 4, 3, 0, 1], [2, 3, 4, 0, 1],
+        [2, 4, 1, 0, 3], [2, 1, 4, 0, 3],
+        [2, 0, 3, 4, 1], [2, 3, 0, 4, 1],
+        [2, 0, 1, 4, 3], [2, 1, 0, 4, 3],
+    ]
+
+    def routed(self, value, steps):
+        pairs = [(s, (s + steps[s % 8]) % self.count) for s in range(self.count) if s % 8 in steps]
+        return lax.ppermute(value, "blk", pairs)
+
+    def step(self, k, token):
+        x = {spot: (spot ^ 2) - spot for spot in range(8)}
+        y = {spot: (spot ^ 4) - spot for spot in range(8)}
+        straight = {spot: (y if spot % 2 else x)[spot] for spot in range(8)}
+        across = {spot: (x if spot % 2 else y)[spot] for spot in range(8)}
+        take = lambda mate, *args: scattered_sums(self.flipped, self.own, mate, *args, self.spot, self.LOOKUP)
+        if k == 1:
+            _, mate = after(token, self.mate)
+            to_last, self.to_plane, self.plane_rest = take(mate, (4, 3), [[BF16], [BF16, F32]])
+            self.from_last = self.routed(to_last, straight)
+            return [to_last]
+        if k == 2:
+            _, mate = after(token, self.mate)
+            _, to_plane = after(token, self.to_plane)
+            self.from_plane = self.routed(to_plane, {1: -8, 3: -8})
+            self.kept, self.to_across, self.to_straight = take(mate, (0, 1, 2), [[F32]] * 3)
+            return [self.from_last, self.kept]
+        if k == 3:
+            _, rest = after(token, self.plane_rest)
+            out = summed_terms(self.spot, [rest, self.from_last], [self.EVEN, self.MIDDLE])
+            self.from_planes = self.routed(out, {0: -8, 2: -8, 4: 8, 6: 8, 5: -8, 3: 8})
+            return [out, self.from_plane]
+        if k == 4:
+            _, rest = after(token, self.to_straight)
+            out = summed_terms(self.spot, [rest, self.from_plane], [None, self.ODD_LOW])
+            second = self.routed(out, straight)
+            out = summed_terms(
+                self.spot,
+                [self.to_across, self.from_planes, self.from_last],
+                [None, self.EVEN | 0b00101000, self.ENDS],
+            )
+            self.arriving = [self.kept, second, self.routed(out, across)]
+        return []
 
 
 def local(features, tile_list, tile_count, tile_values, weight, bias, grad_out):
@@ -238,7 +303,7 @@
     rows_dev, hidden = features.shape
     pieces = 8
     spot = (me % pieces).astype(jnp.int32).reshape(1)
-    route = Direct(count, reach)
+    route = (Relayed if reach == 2 else Direct)(count, reach, spot)
 
     def swapped(value, distance):
         return lax.ppermute(value, "blk", [(s, s ^ distance) for s in range(count)])
@@ -247,30 +312,33 @@
     mate_values, tile_list, tile_count = after(swapped(tile_values[0], 1), tile_list, tile_count)
     meta = jnp.concatenate([tile_list[0].reshape(window, -1), tile_count[0][:, None]], axis=1).reshape(-1)
     mate_meta = swapped(meta, 1)
-    dense, flipped = dense_tiles(spot, meta, mate_meta, tile_values[0], mate_values, rows_dev, route.table)
+    dense, flipped = dense_tiles(spot, meta, mate_meta, tile_values[0], mate_values, rows_dev, route.positions)
     mate_sum, own_sum = route.sums(dense, rows_dev)
     output, grad_agg, keep, give = layer(spot, own_sum, swapped(mate_sum, 1), weight, bias, grad_out, pieces)
 
     mate_grad, got = swapped(grad_agg, 1), swapped(give, 1)
-    keep, give = folded(spot, 1, keep, got)
-    mate_grad, give = after(mate_grad, give)
-    sent_first, sent_last, arriving = route.scatter(flipped, grad_agg, mate_grad)
-    got = swapped(give, 2)
-    got, _ = after(got, sent_first)
+    route.scatter(flipped, grad_agg, mate_grad)
+
+    def exchanged(k, value, distance):
+        other = swapped(value, distance)
+        return after(other, *route.step(k, value))[0]
+
     keep, give = folded(spot, 2, keep, got)
-    total = folded(spot, 2, keep, swapped(give, 4), last=True)[0][0]
-    step = pieces
-    while 2 * step < count:
-        total = summed_terms(total, swapped(total, step))
-        step *= 2
-    total, bias_sum = finished(total, swapped(total, step), hidden // pieces)
-    grad_features = summed_terms(*arriving)
-    for bit in (2, 1, 0):
-        other = swapped(total, 1 << bit)
-        if bit == 2:
-            other, grad_features = after(other, grad_features)
-        total = joined(spot, bit, total, other)
-    return (output, grad_features, total, bias_sum[0])
+    keep, give = folded(spot, 1, keep, exchanged(0, give, 4))
+    total = folded(spot, 1, keep, exchanged(1, give, 2), last=True)[0][0]
+    step, k = pieces, 2
+    while step < count:
+        other = exchanged(k, total, step)
+        step, k = 2 * step, k + 1
+        if step < count:
+            total = summed_terms(spot, [total, other])
+        else:
+            total, bias_sum = finished(total, other, hidden // pieces)
+    gathered = [total] + [swapped(total, 2 * d) for d in range(1, pieces // 2)]
+    route.step(4, total)
+    half = joined(spot, (1, 3), gathered, BF16)
+    grad_weight = joined(spot, (0, 1), [half, swapped(half, 1)], F32)
+    return (output, route.finish(), grad_weight, bias_sum[0])
 
 
 def solution(mesh):

time: 88.5 us -> 85.9 us (0.971)
  waiting for transfers between devices: 47.4 us -> 40.6 us
  starting transfers between devices: 22.8 us -> 26.4 us
  Pallas kernels: 12.9 us -> 14.1 us
    ppermute x0 -> x5, starting transfers between devices: none -> 10.4 us  [routed(): return lax.ppermute(value, 'blk', pairs)]
    ppermute x12 -> x13, waiting for transfers between devices: 39.3 us -> 31.6 us  [swapped(): return lax.ppermute(value, 'blk', [(s, s ^ distance) for s in range(count)])]
    ppermute x8 -> x4, starting transfers between devices: 16.5 us -> 10.5 us  [sent(): return lax.ppermute(value, 'blk', pairs)]
    pallas_call x14 -> x17, Pallas kernels: 12.9 us -> 14.1 us  [call(): pl.pallas_call(kernel, out_shape=out_shape, in_specs=[spec(k) for k in ra...]
    ppermute x8 -> x4, waiting for transfers between devices: 8.05 us -> 9.04 us  [sent(): return lax.ppermute(value, 'blk', pairs)]
    ppermute x12 -> x13, starting transfers between devices: 6.24 us -> 5.48 us  [swapped(): return lax.ppermute(value, 'blk', [(s, s ^ distance) for s in range(count)])]
  transfers between devices with their start and end apart: 20 -> 22, of which waited for: 12 -> 13; matrix products, arithmetic and copies ran while one was open for 2% -> 2% of each run, Pallas kernels for 11% -> 11%
where the time goes in v6:
time: 85.9 us; the launch traced here: 85.7 us
  waiting for transfers between devices  40.6 us (47%)
  starting transfers between devices  26.4 us (31%)
  Pallas kernels  14.1 us (16%)
  local copies, waits for them, and re-layouts  2.98 us (3%)
  between operations  0.88 us (1%)
    ppermute x13, waiting for transfers between devices, swapped(): return lax.ppermute(value, 'blk', [(s, s ^ distance) for s in range(count)])  31.6 us
    pallas_call x17, Pallas kernels, call(): pl.pallas_call(kernel, out_shape=out_shape, in_specs=[spec(k) for k in ra...  14.1 us
    ppermute x4, starting transfers between devices, sent(): return lax.ppermute(value, 'blk', pairs)  10.5 us
    ppermute x5, starting transfers between devices, routed(): return lax.ppermute(value, 'blk', pairs)  10.4 us
    ppermute x4, waiting for transfers between devices, sent(): return lax.ppermute(value, 'blk', pairs)  9.04 us
    ppermute x13, starting transfers between devices, swapped(): return lax.ppermute(value, 'blk', [(s, s ^ distance) for s in range(count)])  5.48 us
  transfers between devices with their start and end apart: 22, of which 13 were waited for; matrix products, arithmetic and copies ran while one was open for 2% of the time, Pallas kernels for 11%

profile of v6, /device:TPU:0, one launch (start us, length us, event | category | flops | bytes accessed | tf_op | source)
XLA Modules:
  0.0 85.7 jit_solution(1315328962494468215)
XLA Ops:
  1.1 2.6 %collective-permute-start.2 = (bf16[384,512]{1,0:T(8,128)(2,1)}, bf16[384,512]{1,0:T(8,128)(2,1)S(1)}, u32[]{:S(2)}, u32[]{:S(2)}) collective-permute-start(bf16[384,512]{1,0:T(8,128)(2,1)} %refs_2_.3), channel_id=1, source_target_pairs={{0,4},{1,5},{2,6},{3,7},{4,8},{5,9},{6,10},{7,11},{8,12},{9,13},{1... | collective-permute-start | bytes 1179656 | tf_op jit(solution)/shard_map/ppermute | solution.py:213
  3.7 1.5 %collective-permute-start.3 = (bf16[384,512]{1,0:T(8,128)(2,1)}, bf16[384,512]{1,0:T(8,128)(2,1)S(1)}, u32[]{:S(2)}, u32[]{:S(2)}) collective-permute-start(bf16[384,512]{1,0:T(8,128)(2,1)} %refs_2_.3), channel_id=1, source_target_pairs={{0,2},{1,3},{2,4},{3,5},{4,6},{5,7},{6,8},{7,9},{8,10},{9,11},{10,... | collective-permute-start | bytes 1179656 | tf_op jit(solution)/shard_map/ppermute | solution.py:213
  5.2 4.1 %collective-permute-start.4 = (bf16[384,512]{1,0:T(8,128)(2,1)}, bf16[384,512]{1,0:T(8,128)(2,1)S(1)}, u32[]{:S(2)}, u32[]{:S(2)}) collective-permute-start(bf16[384,512]{1,0:T(8,128)(2,1)} %refs_2_.3), channel_id=1, source_target_pairs={{0,30},{1,31},{2,0},{3,1},{4,2},{5,3},{6,4},{7,5},{8,6},{9,7},{10,... | collective-permute-start | bytes 1179656 | tf_op jit(solution)/shard_map/ppermute | solution.py:213
  9.4 2.3 %collective-permute-start.5 = (bf16[384,512]{1,0:T(8,128)(2,1)}, bf16[384,512]{1,0:T(8,128)(2,1)S(1)}, u32[]{:S(2)}, u32[]{:S(2)}) collective-permute-start(bf16[384,512]{1,0:T(8,128)(2,1)} %refs_2_.3), channel_id=1, source_target_pairs={{0,28},{2,30},{4,0},{6,2},{8,4},{10,6},{12,8},{14,10},{16,12},{18,... | collective-permute-start | bytes 1179656 | tf_op jit(solution)/shard_map/ppermute | solution.py:213
  11.7 0.7 reshape_squeeze.3
  13.3 1.1 %collective-permute-done.1.mate_meta_ref = s32[120]{0:T(128)S(1)} collective-permute-done((s32[120]{0:T(128)S(1)}, s32[120]{0:T(128)S(1)}, u32[]{:S(2)}, u32[]{:S(2)}) %collective-permute-start.1) | collective-permute-done | bytes 512 | tf_op jit(solution)/shard_map/ppermute | solution.py:309
  14.4 1.5 %copy-done = bf16[1,8,7,128,128]{4,3,2,1,0:T(8,128)(2,1)S(1)} copy-done((bf16[1,8,7,128,128]{4,3,2,1,0:T(8,128)(2,1)S(1)}, bf16[1,8,7,128,128]{4,3,2,1,0:T(8,128)(2,1)}, u32[]{:S(2)}) %copy-start) | copy-done | bytes 1835032
  15.9 4.4 %shard_map.120 = (bf16[768,1920]{1,0:T(8,128)(2,1)S(1)}, bf16[1920,768]{1,0:T(8,128)(2,1)S(1)}) custom-call(s32[1]{0:T(128)} %bitcast.spot_ref.refs_0_, s32[120]{0:T(128)S(1)} %reshape.24.own_meta_ref, s32[120]{0:T(128)S(1)} %collective-permute-done.1.mate_meta_ref, bf16[8,7,128,128]{3,2,1,0:T(8,128)(2,1)S(1)} %bitcast.9, ...), custom_call_target="tpu_custom_call" | custom-call | tf_op jit(solution)/shard_map/pallas_call | solution.py:16
  20.3 5.4 %collective-permute-done.2.refs_0_ = bf16[384,512]{1,0:T(8,128)(2,1)S(1)} collective-permute-done((bf16[384,512]{1,0:T(8,128)(2,1)}, bf16[384,512]{1,0:T(8,128)(2,1)S(1)}, u32[]{:S(2)}, u32[]{:S(2)}) %collective-permute-start.2) | collective-permute-done | bytes 393248 | tf_op jit(solution)/shard_map/ppermute | solution.py:213
  26.3 3.1 %collective-permute-done.5.refs_4_ = bf16[384,512]{1,0:T(8,128)(2,1)S(1)} collective-permute-done((bf16[384,512]{1,0:T(8,128)(2,1)}, bf16[384,512]{1,0:T(8,128)(2,1)S(1)}, u32[]{:S(2)}, u32[]{:S(2)}) %collective-permute-start.5) | collective-permute-done | bytes 393248 | tf_op jit(solution)/shard_map/ppermute | solution.py:213
  29.3 1.2 %shard_map.122 = f32[384,512]{1,0:T(8,128)S(1)} custom-call(bf16[768,1920]{1,0:T(8,128)(2,1)S(1)} %get-tuple-element.36.dense_ref, bf16[384,512]{1,0:T(8,128)(2,1)S(1)} %collective-permute-done.2.refs_0_, bf16[384,512]{1,0:T(8,128)(2,1)S(1)} %collective-permute-done.3.refs_1_, bf16[384,512]{1,0:T(8,128)(2,1)S(1)} %copy-done.1, ...), custom_call_target="tpu_custom_call" | custom-call | tf_op jit(solution)/shard_map/pallas_call | solution.py:16
  30.6 1.2 %shard_map.121.own_ref = f32[384,512]{1,0:T(8,128)S(1)} custom-call(bf16[768,1920]{1,0:T(8,128)(2,1)S(1)} %get-tuple-element.36.dense_ref, bf16[384,512]{1,0:T(8,128)(2,1)S(1)} %collective-permute-done.2.refs_0_, bf16[384,512]{1,0:T(8,128)(2,1)S(1)} %collective-permute-done.3.refs_1_, bf16[384,512]{1,0:T(8,128)(2,1)S(1)} %copy-done.1, ...), custom_call_target="tpu_custom_call" | custom-call | tf_op jit(solution)/shard_map/pallas_call | solution.py:16
  31.8 1.1 %collective-permute-done.6.mate_ref = f32[384,512]{1,0:T(8,128)S(1)} collective-permute-done((f32[384,512]{1,0:T(8,128)S(1)}, f32[384,512]{1,0:T(8,128)S(1)}, u32[]{:S(2)}, u32[]{:S(2)}) %collective-permute-start.6) | collective-permute-done | bytes 786464 | tf_op jit(solution)/shard_map/ppermute | solution.py:309
  32.9 1.4 %shard_map.123 = (bf16[384,512]{1,0:T(8,128)(2,1)}, bf16[384,512]{1,0:T(8,128)(2,1)S(1)}, f32[4,80,512]{2,1,0:T(8,128)S(1)}, bf16[4,80,512]{2,1,0:T(8,128)(2,1)S(1)}) custom-call(s32[1]{0:T(128)} %bitcast.spot_ref.refs_0_, f32[384,512]{1,0:T(8,128)S(1)} %shard_map.121.own_ref, f32[384,512]{1,0:T(8,128)S(1)} %collective-permute-done.6.mate_ref, ...), custom_call_target="tpu_custom_call" | custom-call | tf_op jit(solution)/shard_map/pallas_call | solution.py:16
  34.8 1.1 %collective-permute-done.7.got_ref = bf16[4,80,512]{2,1,0:T(8,128)(2,1)S(1)} collective-permute-done((bf16[4,80,512]{2,1,0:T(8,128)(2,1)S(1)}, bf16[4,80,512]{2,1,0:T(8,128)(2,1)S(1)}, u32[]{:S(2)}, u32[]{:S(2)}) %collective-permute-start.7) | collective-permute-done | bytes 327712 | tf_op jit(solution)/shard_map/ppermute | solution.py:309
  36.1 6.2 %collective-permute-done.8.got_ref = bf16[2,80,512]{2,1,0:T(8,128)(2,1)S(1)} collective-permute-done((bf16[2,80,512]{2,1,0:T(8,128)(2,1)S(1)}, bf16[2,80,512]{2,1,0:T(8,128)(2,1)S(1)}, u32[]{:S(2)}, u32[]{:S(2)}) %collective-permute-start.8) | collective-permute-done | bytes 163872 | tf_op jit(solution)/shard_map/ppermute | solution.py:309
  42.4 1.5 %shard_map.126 = (bf16[384,512]{1,0:T(8,128)(2,1)S(1)}, bf16[384,512]{1,0:T(8,128)(2,1)S(1)}, f32[384,512]{1,0:T(8,128)S(1)}) custom-call(s32[1]{0:T(128)} %bitcast.spot_ref.refs_0_, s32[40]{0:T(128)S(1)} %copy-done.5, bf16[1920,768]{1,0:T(8,128)(2,1)S(1)} %get-tuple-element.38.refs_2_, bf16[384,512]{1,0:T(8,128)(2,1)S(1)} %get-tuple-element.39.refs_3_, ...), custom_call_target="tpu_custom_call" | custom-call | tf_op jit(solution)/shard_map/pallas_call | solution.py:16
  43.9 1.6 %collective-permute-start.12 = (bf16[384,512]{1,0:T(8,128)(2,1)S(1)}, bf16[384,512]{1,0:T(8,128)(2,1)S(1)}, u32[]{:S(2)}, u32[]{:S(2)}) collective-permute-start(bf16[384,512]{1,0:T(8,128)(2,1)S(1)} %get-tuple-element.47), channel_id=1, source_target_pairs={{0,2},{1,5},{2,0},{3,7},{4,6},{5,1},{6,4},{7,3},{8,10},{9,13},{10,... | collective-permute-start | bytes 1179656 | tf_op jit(solution)/shard_map/ppermute | solution.py:261
  46.0 6.6 %collective-permute-done.9.got_ref = bf16[1,80,512]{2,1,0:T(8,128)(2,1)S(1)} collective-permute-done((bf16[1,80,512]{2,1,0:T(8,128)(2,1)S(1)}, bf16[1,80,512]{2,1,0:T(8,128)(2,1)S(1)}, u32[]{:S(2)}, u32[]{:S(2)}) %collective-permute-start.9) | collective-permute-done | bytes 81952 | tf_op jit(solution)/shard_map/ppermute | solution.py:309
  52.7 1.9 %shard_map.128 = (f32[384,512]{1,0:T(8,128)S(1)}, f32[384,512]{1,0:T(8,128)S(1)}, f32[384,512]{1,0:T(8,128)S(1)}) custom-call(s32[1]{0:T(128)} %bitcast.spot_ref.refs_0_, s32[40]{0:T(128)S(1)} %copy-done.5, bf16[1920,768]{1,0:T(8,128)(2,1)S(1)} %get-tuple-element.38.refs_2_, bf16[384,512]{1,0:T(8,128)(2,1)S(1)} %get-tuple-element.39.refs_3_, ...), custom_call_target="tpu_custom_call" | custom-call | tf_op jit(solution)/shard_map/pallas_call | solution.py:16
  55.3 2.8 %collective-permute-done.11.refs_1_ = bf16[80,512]{1,0:T(8,128)(2,1)S(1)} collective-permute-done((bf16[80,512]{1,0:T(8,128)(2,1)S(1)}, bf16[80,512]{1,0:T(8,128)(2,1)S(1)}, u32[]{:S(2)}, u32[]{:S(2)}) %collective-permute-start.11) | collective-permute-done | bytes 81952 | tf_op jit(solution)/shard_map/ppermute | solution.py:309
  58.2 6.8 %collective-permute-start.16 = (bf16[384,512]{1,0:T(8,128)(2,1)S(1)}, bf16[384,512]{1,0:T(8,128)(2,1)S(1)}, u32[]{:S(2)}, u32[]{:S(2)}) collective-permute-start(bf16[384,512]{1,0:T(8,128)(2,1)S(1)} %shard_map.130), channel_id=1, source_target_pairs={{0,24},{2,26},{3,11},{4,12},{5,29},{6,14},{8,0},{10,2},{11,19},{12... | collective-permute-start | bytes 1179656 | tf_op jit(solution)/shard_map/ppermute | solution.py:261
  65.1 6.1 %collective-permute-done.13.other_ref = bf16[80,512]{1,0:T(8,128)(2,1)S(1)} collective-permute-done((bf16[80,512]{1,0:T(8,128)(2,1)S(1)}, bf16[80,512]{1,0:T(8,128)(2,1)S(1)}, u32[]{:S(2)}, u32[]{:S(2)}) %collective-permute-start.13) | collective-permute-done | bytes 81952 | tf_op jit(solution)/shard_map/ppermute | solution.py:309
  71.3 1.3 %collective-permute-start.15 = (bf16[384,512]{1,0:T(8,128)(2,1)S(1)}, bf16[384,512]{1,0:T(8,128)(2,1)S(1)}, u32[]{:S(2)}, u32[]{:S(2)}) collective-permute-start(bf16[384,512]{1,0:T(8,128)(2,1)S(1)} %shard_map.132), channel_id=1, source_target_pairs={{0,2},{1,5},{2,0},{3,7},{4,6},{5,1},{6,4},{7,3},{8,10},{9,13},{10,... | collective-permute-start | bytes 1179656 | tf_op jit(solution)/shard_map/ppermute | solution.py:261
  72.9 0.8 collective-permute-start.18
  73.8 1.9 %collective-permute-start.19 = (bf16[64,512]{1,0:T(8,128)(2,1)S(1)}, bf16[64,512]{1,0:T(8,128)(2,1)S(1)}, u32[]{:S(2)}, u32[]{:S(2)}) collective-permute-start(bf16[64,512]{1,0:T(8,128)(2,1)S(1)} %get-tuple-element.57.refs_0_), channel_id=1, source_target_pairs={{0,4},{1,5},{2,6},{3,7},{4,0},{5,1},{6,2},{7,3},{8,12},{9,13},{10,... | collective-permute-start | bytes 196616 | tf_op jit(solution)/shard_map/ppermute | solution.py:309
  75.7 0.8 collective-permute-start.20
  76.5 3.4 %collective-permute-done.18.refs_1_ = bf16[64,512]{1,0:T(8,128)(2,1)S(1)} collective-permute-done((bf16[64,512]{1,0:T(8,128)(2,1)S(1)}, bf16[64,512]{1,0:T(8,128)(2,1)S(1)}, u32[]{:S(2)}, u32[]{:S(2)}) %collective-permute-start.18) | collective-permute-done | bytes 65568 | tf_op jit(solution)/shard_map/ppermute | solution.py:309
  79.9 2.2 %collective-permute-done.19.refs_2_ = bf16[64,512]{1,0:T(8,128)(2,1)S(1)} collective-permute-done((bf16[64,512]{1,0:T(8,128)(2,1)S(1)}, bf16[64,512]{1,0:T(8,128)(2,1)S(1)}, u32[]{:S(2)}, u32[]{:S(2)}) %collective-permute-start.19) | collective-permute-done | bytes 65568 | tf_op jit(solution)/shard_map/ppermute | solution.py:309
  82.8 0.9 %collective-permute-done.21.refs_1_ = bf16[256,512]{1,0:T(8,128)(2,1)S(1)} collective-permute-done((bf16[256,512]{1,0:T(8,128)(2,1)S(1)}, bf16[256,512]{1,0:T(8,128)(2,1)S(1)}, u32[]{:S(2)}, u32[]{:S(2)}) %collective-permute-start.21) | collective-permute-done | bytes 262176 | tf_op jit(solution)/shard_map/ppermute | solution.py:309
  83.7 1.0 %shard_map.136 = f32[512,512]{1,0:T(8,128)} custom-call(s32[1]{0:T(128)} %bitcast.spot_ref.refs_0_, bf16[256,512]{1,0:T(8,128)(2,1)S(1)} %shard_map.135.refs_0_, bf16[256,512]{1,0:T(8,128)(2,1)S(1)} %collective-permute-done.21.refs_1_), custom_call_target="tpu_custom_call" | custom-call | tf_op jit(solution)/shard_map/pallas_call | solution.py:16
  84.8 0.9 %shard_map.134 = bf16[384,512]{1,0:T(8,128)(2,1)} custom-call(s32[1]{0:T(128)} %bitcast.spot_ref.refs_0_, f32[384,512]{1,0:T(8,128)S(1)} %get-tuple-element.50.refs_0_, bf16[384,512]{1,0:T(8,128)(2,1)S(1)} %collective-permute-done.15.refs_1_, bf16[384,512]{1,0:T(8,128)(2,1)S(1)} %collective-permute-done.17.refs_2_), custom_call_target="tpu_custom_call" | custom-call | tf_op jit(solution)/shard_map/pallas_call | solution.py:16
  (46 shorter events, 5.3 us)
Async XLA Ops:
  0.6 11.1 %collective-permute-start = (bf16[8,7,128,128]{3,2,1,0:T(8,128)(2,1)}, bf16[8,7,128,128]{3,2,1,0:T(8,128)(2,1)S(1)}, u32[]{:S(2)}, u32[]{:S(2)}) collective-permute-start(bf16[8,7,128,128]{3,2,1,0:T(8,128)(2,1)} %bitcast.8), channel_id=1, source_target_pairs={{0,1},{1,0},{2,3},{3,2},{4,5},{5,4},{6,7},{7,6},{8,9},{9,8},{10,11... | collective-permute-start | bytes 5505032 | tf_op jit(solution)/shard_map/ppermute | solution.py:309
  1.1 24.5 %collective-permute-start.2 = (bf16[384,512]{1,0:T(8,128)(2,1)}, bf16[384,512]{1,0:T(8,128)(2,1)S(1)}, u32[]{:S(2)}, u32[]{:S(2)}) collective-permute-start(bf16[384,512]{1,0:T(8,128)(2,1)} %refs_2_.3), channel_id=1, source_target_pairs={{0,4},{1,5},{2,6},{3,7},{4,8},{5,9},{6,10},{7,11},{8,12},{9,13},{1... | collective-permute-start | bytes 1179656 | tf_op jit(solution)/shard_map/ppermute | solution.py:213
  3.7 22.5 %collective-permute-start.3 = (bf16[384,512]{1,0:T(8,128)(2,1)}, bf16[384,512]{1,0:T(8,128)(2,1)S(1)}, u32[]{:S(2)}, u32[]{:S(2)}) collective-permute-start(bf16[384,512]{1,0:T(8,128)(2,1)} %refs_2_.3), channel_id=1, source_target_pairs={{0,2},{1,3},{2,4},{3,5},{4,6},{5,7},{6,8},{7,9},{8,10},{9,11},{10,... | collective-permute-start | bytes 1179656 | tf_op jit(solution)/shard_map/ppermute | solution.py:213
  5.2 21.1 %collective-permute-start.4 = (bf16[384,512]{1,0:T(8,128)(2,1)}, bf16[384,512]{1,0:T(8,128)(2,1)S(1)}, u32[]{:S(2)}, u32[]{:S(2)}) collective-permute-start(bf16[384,512]{1,0:T(8,128)(2,1)} %refs_2_.3), channel_id=1, source_target_pairs={{0,30},{1,31},{2,0},{3,1},{4,2},{5,3},{6,4},{7,5},{8,6},{9,7},{10,... | collective-permute-start | bytes 1179656 | tf_op jit(solution)/shard_map/ppermute | solution.py:213
  9.4 20.0 %collective-permute-start.5 = (bf16[384,512]{1,0:T(8,128)(2,1)}, bf16[384,512]{1,0:T(8,128)(2,1)S(1)}, u32[]{:S(2)}, u32[]{:S(2)}) collective-permute-start(bf16[384,512]{1,0:T(8,128)(2,1)} %refs_2_.3), channel_id=1, source_target_pairs={{0,28},{2,30},{4,0},{6,2},{8,4},{10,6},{12,8},{14,10},{16,12},{18,... | collective-permute-start | bytes 1179656 | tf_op jit(solution)/shard_map/ppermute | solution.py:213
  13.2 1.1 %collective-permute-start.1 = (s32[120]{0:T(128)S(1)}, s32[120]{0:T(128)S(1)}, u32[]{:S(2)}, u32[]{:S(2)}) collective-permute-start(s32[120]{0:T(128)S(1)} %reshape.24.own_meta_ref), channel_id=1, source_target_pairs={{0,1},{1,0},{2,3},{3,2},{4,5},{5,4},{6,7},{7,6},{8,9},{9,8},{10,11... | collective-permute-start | bytes 1448 | tf_op jit(solution)/shard_map/ppermute | solution.py:309
  14.4 1.5 %copy-start = (bf16[1,8,7,128,128]{4,3,2,1,0:T(8,128)(2,1)S(1)}, bf16[1,8,7,128,128]{4,3,2,1,0:T(8,128)(2,1)}, u32[]{:S(2)}) copy-start(bf16[1,8,7,128,128]{4,3,2,1,0:T(8,128)(2,1)} %param.12) | copy-start | bytes 5505028
  15.9 13.5 %copy-start.1 = (bf16[384,512]{1,0:T(8,128)(2,1)S(1)}, bf16[384,512]{1,0:T(8,128)(2,1)}, u32[]{:S(2)}) copy-start(bf16[384,512]{1,0:T(8,128)(2,1)} %refs_2_.3) | copy-start | bytes 1179652
  30.5 2.4 %copy-start.2 = (bf16[512,512]{1,0:T(8,128)(2,1)S(1)}, bf16[512,512]{1,0:T(8,128)(2,1)}, u32[]{:S(2)}) copy-start(bf16[512,512]{1,0:T(8,128)(2,1)} %weight_ref.1) | copy-start | bytes 1572868
  30.5 2.4 %copy-start.3 = (bf16[384,512]{1,0:T(8,128)(2,1)S(1)}, bf16[384,512]{1,0:T(8,128)(2,1)}, u32[]{:S(2)}) copy-start(bf16[384,512]{1,0:T(8,128)(2,1)} %grad_out_ref.1) | copy-start | bytes 1179652
  30.5 2.4 %copy-start.4 = (f32[512]{0:T(512)S(1)}, f32[512]{0:T(512)}, u32[]{:S(2)}) copy-start(f32[512]{0:T(512)} %param.14) | copy-start | bytes 6148
  30.5 2.4 %collective-permute-start.6 = (f32[384,512]{1,0:T(8,128)S(1)}, f32[384,512]{1,0:T(8,128)S(1)}, u32[]{:S(2)}, u32[]{:S(2)}) collective-permute-start(f32[384,512]{1,0:T(8,128)S(1)} %shard_map.122), channel_id=1, source_target_pairs={{0,1},{1,0},{2,3},{3,2},{4,5},{5,4},{6,7},{7,6},{8,9},{9,8},{10,11... | collective-permute-start | bytes 2359304 | tf_op jit(solution)/shard_map/ppermute | solution.py:309
  31.8 10.6 %copy-start.5 = (s32[40]{0:T(128)S(1)}, s32[40]{0:T(128)}, u32[]{:S(2)}) copy-start(s32[40]{0:T(128)} %constant.23.refs_1_) | copy-start | bytes 484
  34.3 1.6 %collective-permute-start.7 = (bf16[4,80,512]{2,1,0:T(8,128)(2,1)S(1)}, bf16[4,80,512]{2,1,0:T(8,128)(2,1)S(1)}, u32[]{:S(2)}, u32[]{:S(2)}) collective-permute-start(bf16[4,80,512]{2,1,0:T(8,128)(2,1)S(1)} %get-tuple-element.41), channel_id=1, source_target_pairs={{0,1},{1,0},{2,3},{3,2},{4,5},{5,4},{6,7},{7,6},{8,9},{9,8},{10,11... | collective-permute-start | bytes 983048 | tf_op jit(solution)/shard_map/ppermute | solution.py:309
  34.4 7.9 %collective-permute-start.10 = (bf16[384,512]{1,0:T(8,128)(2,1)S(1)}, bf16[384,512]{1,0:T(8,128)(2,1)S(1)}, u32[]{:S(2)}, u32[]{:S(2)}) collective-permute-start(bf16[384,512]{1,0:T(8,128)(2,1)S(1)} %get-tuple-element.39.refs_3_), channel_id=1, source_target_pairs={{0,1},{1,0},{2,3},{3,2},{4,5},{5,4},{6,7},{7,6},{8,9},{9,8},{10,11... | collective-permute-start | bytes 1179656 | tf_op jit(solution)/shard_map/ppermute | solution.py:309
  36.0 6.3 %collective-permute-start.8 = (bf16[2,80,512]{2,1,0:T(8,128)(2,1)S(1)}, bf16[2,80,512]{2,1,0:T(8,128)(2,1)S(1)}, u32[]{:S(2)}, u32[]{:S(2)}) collective-permute-start(bf16[2,80,512]{2,1,0:T(8,128)(2,1)S(1)} %get-tuple-element.43), channel_id=1, source_target_pairs={{0,4},{1,5},{2,6},{3,7},{4,0},{5,1},{6,2},{7,3},{8,12},{9,13},{10,... | collective-permute-start | bytes 491528 | tf_op jit(solution)/shard_map/ppermute | solution.py:309
  43.9 14.2 %collective-permute-start.12 = (bf16[384,512]{1,0:T(8,128)(2,1)S(1)}, bf16[384,512]{1,0:T(8,128)(2,1)S(1)}, u32[]{:S(2)}, u32[]{:S(2)}) collective-permute-start(bf16[384,512]{1,0:T(8,128)(2,1)S(1)} %get-tuple-element.47), channel_id=1, source_target_pairs={{0,2},{1,5},{2,0},{3,7},{4,6},{5,1},{6,4},{7,3},{8,10},{9,13},{10,... | collective-permute-start | bytes 1179656 | tf_op jit(solution)/shard_map/ppermute | solution.py:261
  45.4 7.2 %collective-permute-start.9 = (bf16[1,80,512]{2,1,0:T(8,128)(2,1)S(1)}, bf16[1,80,512]{2,1,0:T(8,128)(2,1)S(1)}, u32[]{:S(2)}, u32[]{:S(2)}) collective-permute-start(bf16[1,80,512]{2,1,0:T(8,128)(2,1)S(1)} %get-tuple-element.45), channel_id=1, source_target_pairs={{0,2},{1,3},{2,0},{3,1},{4,6},{5,7},{6,4},{7,5},{8,10},{9,11},{10,... | collective-permute-start | bytes 245768 | tf_op jit(solution)/shard_map/ppermute | solution.py:309
  52.6 5.4 %collective-permute-start.11 = (bf16[80,512]{1,0:T(8,128)(2,1)S(1)}, bf16[80,512]{1,0:T(8,128)(2,1)S(1)}, u32[]{:S(2)}, u32[]{:S(2)}) collective-permute-start(bf16[80,512]{1,0:T(8,128)(2,1)S(1)} %bitcast.10), channel_id=1, source_target_pairs={{0,8},{1,9},{2,10},{3,11},{4,12},{5,13},{6,14},{7,15},{8,0},{9,1},... | collective-permute-start | bytes 245768 | tf_op jit(solution)/shard_map/ppermute | solution.py:309
  54.6 16.6 %collective-permute-start.14 = (bf16[384,512]{1,0:T(8,128)(2,1)S(1)}, bf16[384,512]{1,0:T(8,128)(2,1)S(1)}, u32[]{:S(2)}, u32[]{:S(2)}) collective-permute-start(bf16[384,512]{1,0:T(8,128)(2,1)S(1)} %get-tuple-element.55), channel_id=1, source_target_pairs={{1,25},{3,27},{9,1},{11,3},{17,9},{19,11},{25,17},{27,19}} | collective-permute-start | bytes 1179656 | tf_op jit(solution)/shard_map/ppermute | solution.py:261
  58.2 14.4 %collective-permute-start.16 = (bf16[384,512]{1,0:T(8,128)(2,1)S(1)}, bf16[384,512]{1,0:T(8,128)(2,1)S(1)}, u32[]{:S(2)}, u32[]{:S(2)}) collective-permute-start(bf16[384,512]{1,0:T(8,128)(2,1)S(1)} %shard_map.130), channel_id=1, source_target_pairs={{0,24},{2,26},{3,11},{4,12},{5,29},{6,14},{8,0},{10,2},{11,19},{12... | collective-permute-start | bytes 1179656 | tf_op jit(solution)/shard_map/ppermute | solution.py:261
  65.0 6.2 %collective-permute-start.13 = (bf16[80,512]{1,0:T(8,128)(2,1)S(1)}, bf16[80,512]{1,0:T(8,128)(2,1)S(1)}, u32[]{:S(2)}, u32[]{:S(2)}) collective-permute-start(bf16[80,512]{1,0:T(8,128)(2,1)S(1)} %shard_map.129.mine_ref), channel_id=1, source_target_pairs={{0,16},{1,17},{2,18},{3,19},{4,20},{5,21},{6,22},{7,23},{8,24},{9,... | collective-permute-start | bytes 245768 | tf_op jit(solution)/shard_map/ppermute | solution.py:309
  71.3 13.5 %collective-permute-start.15 = (bf16[384,512]{1,0:T(8,128)(2,1)S(1)}, bf16[384,512]{1,0:T(8,128)(2,1)S(1)}, u32[]{:S(2)}, u32[]{:S(2)}) collective-permute-start(bf16[384,512]{1,0:T(8,128)(2,1)S(1)} %shard_map.132), channel_id=1, source_target_pairs={{0,2},{1,5},{2,0},{3,7},{4,6},{5,1},{6,4},{7,3},{8,10},{9,13},{10,... | collective-permute-start | bytes 1179656 | tf_op jit(solution)/shard_map/ppermute | solution.py:261
  72.9 11.9 %collective-permute-start.17 = (bf16[384,512]{1,0:T(8,128)(2,1)S(1)}, bf16[384,512]{1,0:T(8,128)(2,1)S(1)}, u32[]{:S(2)}, u32[]{:S(2)}) collective-permute-start(bf16[384,512]{1,0:T(8,128)(2,1)S(1)} %shard_map.133), channel_id=1, source_target_pairs={{0,4},{1,3},{2,6},{3,1},{4,0},{5,7},{6,2},{7,5},{8,12},{9,11},{10,... | collective-permute-start | bytes 1179656 | tf_op jit(solution)/shard_map/ppermute | solution.py:261
  72.9 6.9 %collective-permute-start.18 = (bf16[64,512]{1,0:T(8,128)(2,1)S(1)}, bf16[64,512]{1,0:T(8,128)(2,1)S(1)}, u32[]{:S(2)}, u32[]{:S(2)}) collective-permute-start(bf16[64,512]{1,0:T(8,128)(2,1)S(1)} %get-tuple-element.57.refs_0_), channel_id=1, source_target_pairs={{0,2},{1,3},{2,0},{3,1},{4,6},{5,7},{6,4},{7,5},{8,10},{9,11},{10,... | collective-permute-start | bytes 196616 | tf_op jit(solution)/shard_map/ppermute | solution.py:309
  73.8 8.4 %collective-permute-start.19 = (bf16[64,512]{1,0:T(8,128)(2,1)S(1)}, bf16[64,512]{1,0:T(8,128)(2,1)S(1)}, u32[]{:S(2)}, u32[]{:S(2)}) collective-permute-start(bf16[64,512]{1,0:T(8,128)(2,1)S(1)} %get-tuple-element.57.refs_0_), channel_id=1, source_target_pairs={{0,4},{1,5},{2,6},{3,7},{4,0},{5,1},{6,2},{7,3},{8,12},{9,13},{10,... | collective-permute-start | bytes 196616 | tf_op jit(solution)/shard_map/ppermute | solution.py:309
  75.7 6.4 %collective-permute-start.20 = (bf16[64,512]{1,0:T(8,128)(2,1)S(1)}, bf16[64,512]{1,0:T(8,128)(2,1)S(1)}, u32[]{:S(2)}, u32[]{:S(2)}) collective-permute-start(bf16[64,512]{1,0:T(8,128)(2,1)S(1)} %get-tuple-element.57.refs_0_), channel_id=1, source_target_pairs={{0,6},{1,7},{2,4},{3,5},{4,2},{5,3},{6,0},{7,1},{8,14},{9,15},{10,... | collective-permute-start | bytes 196616 | tf_op jit(solution)/shard_map/ppermute | solution.py:309
  82.1 1.6 %collective-permute-start.21 = (bf16[256,512]{1,0:T(8,128)(2,1)S(1)}, bf16[256,512]{1,0:T(8,128)(2,1)S(1)}, u32[]{:S(2)}, u32[]{:S(2)}) collective-permute-start(bf16[256,512]{1,0:T(8,128)(2,1)S(1)} %shard_map.135.refs_0_), channel_id=1, source_target_pairs={{0,1},{1,0},{2,3},{3,2},{4,5},{5,4},{6,7},{7,6},{8,9},{9,8},{10,11... | collective-permute-start | bytes 786440 | tf_op jit(solution)/shard_map/ppermute | solution.py:309

commit v7 on v6

--- a/solution.py
+++ b/solution.py
@@ -61,9 +61,9 @@
     )
 
 
-def gathered_sums(dense, columns, rows, sources, start=None):
+def gathered_sums(dense, columns, first, sources, start=None):
     rows_dev, hidden = sources[0].shape
-    first, last = rows
+    last = 2 * rows_dev
 
     def kernel(dense_ref, *refs):
         refs, out_ref = list(refs[:-1]), refs[-1]
@@ -82,12 +82,12 @@
 
 
 def layer(spot, own_sum, mate_sum, weight, bias, grad_out, pieces):
-    rows_dev, hidden = own_sum.shape
+    rows_dev, hidden = mate_sum.shape
     piece = hidden // pieces
     half = (pieces // 2, piece + BIAS_ROWS, hidden)
 
     def kernel(spot_ref, own_ref, mate_ref, weight_ref, bias_ref, grad_out_ref, out_ref, ga_ref, keep_ref, give_ref):
-        agg = (own_ref[...] + mate_ref[...]).astype(BF16)
+        agg = (own_ref[:rows_dev] + mate_ref[...]).astype(BF16)
         pre = jnp.dot(agg, weight_ref[...], preferred_element_type=F32) + bias_ref[...]
         sig = jax.nn.sigmoid(pre)
         out_ref[...] = (pre * sig).astype(BF16)
@@ -115,23 +115,28 @@
     )
 
 
-def folded(spot, bit, keep, got, last=False):
+def folded(spot, keep, got, last=False):
     count, rows, hidden = keep.shape
-    left = count if last else count // 2
+    left = count // 2
 
     def kernel(spot_ref, keep_ref, got_ref, *out_refs):
-        mine = (spot_ref[0] >> bit) % 2
+        odd = spot_ref[0] % 2
+        first_side, second_side = (spot_ref[0] >> 1) % 2, (spot_ref[0] >> 2) % 2
+        mine = odd * second_side + (1 - odd) * first_side if last else odd * first_side + (1 - odd) * second_side
         for p in range(left):
-            if last:
-                out_refs[0][p] = (keep_ref[p] + got_ref[p].astype(F32)).astype(BF16)
-                continue
             for ref, side in zip(out_refs, (mine, 1 - mine)):
-                q = side * left + p
+                q = side if last else odd * (2 * p + side) + (1 - odd) * (2 * side + p)
                 ref[p] = (keep_ref[q] + got_ref[q].astype(F32)).astype(ref.dtype)
 
     shape = (left, rows, hidden)
-    outs = [(shape, BF16)] if last else [(shape, F32), (shape, BF16)]
-    return call(kernel, outs, [spot, keep, got], smem=1)
+    return call(kernel, [(shape, F32), (shape, BF16)], [spot, keep, got], smem=1)
+
+
+def rounded_sum(keep, got):
+    def kernel(keep_ref, got_ref, out_ref):
+        out_ref[...] = (keep_ref[0] + got_ref[0].astype(F32)).astype(BF16)
+
+    return call(kernel, [(keep.shape[1:], BF16)], [keep, got])[0]
 
 
 def summed_terms(spot, terms, masks=None):
@@ -149,16 +154,34 @@
     return call(kernel, [(terms[0].shape, BF16)], [spot, *terms], smem=1)[0]
 
 
-def joined(spot, bits, pieces, dtype):
-    rows, hidden = pieces[0].shape
-    low, high = bits
-
-    def kernel(spot_ref, *refs):
-        side = (spot_ref[0] >> low) % (1 << (high - low))
-        for other, ref in enumerate(refs[:-1]):
-            refs[-1][pl.ds(pl.multiple_of((side ^ other) * rows, rows), rows)] = ref[...].astype(dtype)
-
-    return call(kernel, [((len(pieces) * rows, hidden), dtype)], [spot, *pieces], smem=1)[0]
+def joined_pieces(spot, mine, other, last=False):
+    rows, hidden = mine.shape[-2:]
+
+    def kernel(spot_ref, mine_ref, other_ref, out_ref):
+        odd = spot_ref[0] % 2
+        first_side, second_side = (spot_ref[0] >> 1) % 2, (spot_ref[0] >> 2) % 2
+        own = odd * first_side + (1 - odd) * second_side if last else odd * second_side + (1 - odd) * first_side
+        for ref, side in ((mine_ref, own), (other_ref, 1 - own)):
+            if not last:
+                out_ref[side] = ref[...]
+                continue
+            for p in range(2):
+                q = odd * (2 * p + side) + (1 - odd) * (2 * side + p)
+                out_ref[pl.ds(pl.multiple_of(q * rows, rows), rows)] = ref[p]
+
+    shape = (4 * rows, hidden) if last else (2, rows, hidden)
+    return call(kernel, [(shape, BF16)], [spot, mine, other], smem=1)[0]
+
+
+def whole_weight(spot, mine, other):
+    rows, hidden = mine.shape
+
+    def kernel(spot_ref, mine_ref, other_ref, out_ref):
+        core = spot_ref[0] % 2
+        out_ref[pl.ds(pl.multiple_of(core * rows, rows), rows)] = mine_ref[...].astype(F32)
+        out_ref[pl.ds(pl.multiple_of((1 - core) * rows, rows), rows)] = other_ref[...].astype(F32)
+
+    return call(kernel, [((2 * rows, hidden), F32)], [spot, mine, other], smem=1)[0]
 
 
 def finished(mine, other, piece):
@@ -222,10 +245,9 @@
         ]
 
     def sums(self, dense, rows_dev):
-        columns = range(self.positions)
-        return [
-            gathered_sums(dense, columns, (side * rows_dev, (side + 1) * rows_dev), self.sources) for side in (1, 0)
-        ]
+        last = self.positions - 1
+        start = gathered_sums(dense, range(last), 0, self.sources[:last])
+        return gathered_sums(dense, [last], rows_dev, self.sources[last:], start), start
 
     def scatter(self, flipped, own, mate):
         self.flipped, self.own, self.mate = flipped, own, mate
@@ -266,32 +288,35 @@
         straight = {spot: (y if spot % 2 else x)[spot] for spot in range(8)}
         across = {spot: (x if spot % 2 else y)[spot] for spot in range(8)}
         take = lambda mate, *args: scattered_sums(self.flipped, self.own, mate, *args, self.spot, self.LOOKUP)
-        if k == 1:
+        if k == 0:
             _, mate = after(token, self.mate)
             to_last, self.to_plane, self.plane_rest = take(mate, (4, 3), [[BF16], [BF16, F32]])
             self.from_last = self.routed(to_last, straight)
             return [to_last]
+        if k == 1:
+            _, mate = after(token, self.mate)
+            self.kept, self.to_across, self.to_straight = take(mate, (0, 1, 2), [[F32]] * 3)
+            return [self.kept]
         if k == 2:
-            _, mate = after(token, self.mate)
             _, to_plane = after(token, self.to_plane)
             self.from_plane = self.routed(to_plane, {1: -8, 3: -8})
-            self.kept, self.to_across, self.to_straight = take(mate, (0, 1, 2), [[F32]] * 3)
-            return [self.from_last, self.kept]
+            return [self.from_last]
         if k == 3:
             _, rest = after(token, self.plane_rest)
             out = summed_terms(self.spot, [rest, self.from_last], [self.EVEN, self.MIDDLE])
             self.from_planes = self.routed(out, {0: -8, 2: -8, 4: 8, 6: 8, 5: -8, 3: 8})
-            return [out, self.from_plane]
+            second = summed_terms(self.spot, [self.to_straight, self.from_plane], [None, self.ODD_LOW])
+            self.second = self.routed(second, straight)
+            return [out, second]
         if k == 4:
-            _, rest = after(token, self.to_straight)
-            out = summed_terms(self.spot, [rest, self.from_plane], [None, self.ODD_LOW])
-            second = self.routed(out, straight)
+            _, rest = after(token, self.to_across)
             out = summed_terms(
                 self.spot,
-                [self.to_across, self.from_planes, self.from_last],
+                [rest, self.from_planes, self.from_last],
                 [None, self.EVEN | 0b00101000, self.ENDS],
             )
-            self.arriving = [self.kept, second, self.routed(out, across)]
+            self.arriving = [self.kept, self.second, self.routed(out, across)]
+            return [out]
         return []
 
 
@@ -319,26 +344,27 @@
     mate_grad, got = swapped(grad_agg, 1), swapped(give, 1)
     route.scatter(flipped, grad_agg, mate_grad)
 
-    def exchanged(k, value, distance):
-        other = swapped(value, distance)
+    def exchanged(k, value, even, odd):
+        pairs = [(s, s ^ (odd if s % 2 else even)) for s in range(count)]
+        other = lax.ppermute(value, "blk", pairs)
         return after(other, *route.step(k, value))[0]
 
-    keep, give = folded(spot, 2, keep, got)
-    keep, give = folded(spot, 1, keep, exchanged(0, give, 4))
-    total = folded(spot, 1, keep, exchanged(1, give, 2), last=True)[0][0]
+    keep, give = folded(spot, keep, got)
+    keep, give = folded(spot, keep, exchanged(0, give, 4, 2), last=True)
+    total = rounded_sum(keep, exchanged(1, give, 2, 4))
     step, k = pieces, 2
     while step < count:
-        other = exchanged(k, total, step)
+        other = exchanged(k, total, step, step)
         step, k = 2 * step, k + 1
         if step < count:
             total = summed_terms(spot, [total, other])
         else:
             total, bias_sum = finished(total, other, hidden // pieces)
-    gathered = [total] + [swapped(total, 2 * d) for d in range(1, pieces // 2)]
-    route.step(4, total)
-    half = joined(spot, (1, 3), gathered, BF16)
-    grad_weight = joined(spot, (0, 1), [half, swapped(half, 1)], F32)
-    return (output, route.finish(), grad_weight, bias_sum[0])
+    pair = joined_pieces(spot, total, exchanged(4, total, 2, 4))
+    half = joined_pieces(spot, pair, exchanged(5, pair, 4, 2), last=True)
+    grad_features = route.finish()
+    mate_half, grad_features = after(swapped(half, 1), grad_features)
+    return (output, grad_features, whole_weight(spot, half, mate_half), bias_sum[0])
 
 
 def solution(mesh):

time: 85.9 us -> 86.7 us (level)
    ppermute x13 -> x6, waiting for transfers between devices: 31.6 us -> 5.06 us  [swapped(): return lax.ppermute(value, 'blk', [(s, s ^ distance) for s in range(count)])]
    ppermute x0 -> x6, waiting for transfers between devices: none -> 25.4 us  [exchanged(): other = lax.ppermute(value, 'blk', pairs)]
    ppermute x0 -> x6, starting transfers between devices: none -> 7.97 us  [exchanged(): other = lax.ppermute(value, 'blk', pairs)]
    ppermute x13 -> x6, starting transfers between devices: 5.48 us -> 1.18 us  [swapped(): return lax.ppermute(value, 'blk', [(s, s ^ distance) for s in range(count)])]
    ppermute x5, waiting for transfers between devices: 0.01 us -> 3.52 us  [routed(): return lax.ppermute(value, 'blk', pairs)]
    ppermute x5, starting transfers between devices: 10.4 us -> 7.12 us  [routed(): return lax.ppermute(value, 'blk', pairs)]
    ppermute x4, waiting for transfers between devices: 9.04 us -> 7.36 us  [sent(): return lax.ppermute(value, 'blk', pairs)]
    pallas_call x17 -> x18, Pallas kernels: 14.1 us -> 13.8 us  [call(): pl.pallas_call(kernel, out_shape=out_shape, in_specs=[spec(k) for k in ra...]
  transfers between devices with their start and end apart: 22 -> 21, of which waited for: 13 -> 14; matrix products, arithmetic and copies ran while one was open for 2% -> 2% of each run, Pallas kernels for 11% -> 11%
where the time goes in v7:
time: 86.7 us; the launch traced here: 86.5 us
  waiting for transfers between devices  41.4 us (48%)
  starting transfers between devices  26.8 us (31%)
  Pallas kernels  13.8 us (16%)
  local copies, waits for them, and re-layouts  2.98 us (3%)
    ppermute x6, waiting for transfers between devices, exchanged(): other = lax.ppermute(value, 'blk', pairs)  25.4 us
    pallas_call x18, Pallas kernels, call(): pl.pallas_call(kernel, out_shape=out_shape, in_specs=[spec(k) for k in ra...  13.8 us
    ppermute x4, starting transfers between devices, sent(): return lax.ppermute(value, 'blk', pairs)  10.5 us
    ppermute x6, starting transfers between devices, exchanged(): other = lax.ppermute(value, 'blk', pairs)  7.97 us
    ppermute x4, waiting for transfers between devices, sent(): return lax.ppermute(value, 'blk', pairs)  7.36 us
    ppermute x5, starting transfers between devices, routed(): return lax.ppermute(value, 'blk', pairs)  7.12 us
    ppermute x6, waiting for transfers between devices, swapped(): return lax.ppermute(value, 'blk', [(s, s ^ distance) for s in range(count)])  5.06 us
    ppermute x5, waiting for transfers between devices, routed(): return lax.ppermute(value, 'blk', pairs)  3.52 us
  transfers between devices with their start and end apart: 21, of which 14 were waited for; matrix products, arithmetic and copies ran while one was open for 2% of the time, Pallas kernels for 11%

profile of v7, /device:TPU:0, one launch (start us, length us, event | category | flops | bytes accessed | tf_op | source)
XLA Modules:
  0.0 86.5 jit_solution(8330868603262985981)
XLA Ops:
  1.1 2.6 %collective-permute-start.2 = (bf16[384,512]{1,0:T(8,128)(2,1)}, bf16[384,512]{1,0:T(8,128)(2,1)S(1)}, u32[]{:S(2)}, u32[]{:S(2)}) collective-permute-start(bf16[384,512]{1,0:T(8,128)(2,1)} %refs_2_.1), channel_id=1, source_target_pairs={{0,4},{1,5},{2,6},{3,7},{4,8},{5,9},{6,10},{7,11},{8,12},{9,13},{1... | collective-permute-start | bytes 1179656 | tf_op jit(solution)/shard_map/ppermute | solution.py:236
  3.7 1.5 %collective-permute-start.3 = (bf16[384,512]{1,0:T(8,128)(2,1)}, bf16[384,512]{1,0:T(8,128)(2,1)S(1)}, u32[]{:S(2)}, u32[]{:S(2)}) collective-permute-start(bf16[384,512]{1,0:T(8,128)(2,1)} %refs_2_.1), channel_id=1, source_target_pairs={{0,2},{1,3},{2,4},{3,5},{4,6},{5,7},{6,8},{7,9},{8,10},{9,11},{10,... | collective-permute-start | bytes 1179656 | tf_op jit(solution)/shard_map/ppermute | solution.py:236
  5.2 4.1 %collective-permute-start.4 = (bf16[384,512]{1,0:T(8,128)(2,1)}, bf16[384,512]{1,0:T(8,128)(2,1)S(1)}, u32[]{:S(2)}, u32[]{:S(2)}) collective-permute-start(bf16[384,512]{1,0:T(8,128)(2,1)} %refs_2_.1), channel_id=1, source_target_pairs={{0,30},{1,31},{2,0},{3,1},{4,2},{5,3},{6,4},{7,5},{8,6},{9,7},{10,... | collective-permute-start | bytes 1179656 | tf_op jit(solution)/shard_map/ppermute | solution.py:236
  9.4 2.3 %collective-permute-start.5 = (bf16[384,512]{1,0:T(8,128)(2,1)}, bf16[384,512]{1,0:T(8,128)(2,1)S(1)}, u32[]{:S(2)}, u32[]{:S(2)}) collective-permute-start(bf16[384,512]{1,0:T(8,128)(2,1)} %refs_2_.1), channel_id=1, source_target_pairs={{0,28},{2,30},{4,0},{6,2},{8,4},{10,6},{12,8},{14,10},{16,12},{18,... | collective-permute-start | bytes 1179656 | tf_op jit(solution)/shard_map/ppermute | solution.py:236
  11.7 0.7 reshape_squeeze.3
  12.4 0.7 pad_add_fusion
  13.3 1.1 %collective-permute-done.1.mate_meta_ref = s32[120]{0:T(128)S(1)} collective-permute-done((s32[120]{0:T(128)S(1)}, s32[120]{0:T(128)S(1)}, u32[]{:S(2)}, u32[]{:S(2)}) %collective-permute-start.1) | collective-permute-done | bytes 512 | tf_op jit(solution)/shard_map/ppermute | solution.py:334
  14.4 1.5 %copy-done = bf16[1,8,7,128,128]{4,3,2,1,0:T(8,128)(2,1)S(1)} copy-done((bf16[1,8,7,128,128]{4,3,2,1,0:T(8,128)(2,1)S(1)}, bf16[1,8,7,128,128]{4,3,2,1,0:T(8,128)(2,1)}, u32[]{:S(2)}) %copy-start) | copy-done | bytes 1835032
  15.9 4.3 %shard_map.120 = (bf16[768,1920]{1,0:T(8,128)(2,1)S(1)}, bf16[1920,768]{1,0:T(8,128)(2,1)S(1)}) custom-call(s32[1]{0:T(128)} %bitcast.spot_ref.refs_0_, s32[120]{0:T(128)S(1)} %reshape.24.own_meta_ref, s32[120]{0:T(128)S(1)} %collective-permute-done.1.mate_meta_ref, bf16[8,7,128,128]{3,2,1,0:T(8,128)(2,1)S(1)} %bitcast.8, ...), custom_call_target="tpu_custom_call" | custom-call | tf_op jit(solution)/shard_map/pallas_call | solution.py:16
  20.2 5.5 %collective-permute-done.2.refs_0_ = bf16[384,512]{1,0:T(8,128)(2,1)S(1)} collective-permute-done((bf16[384,512]{1,0:T(8,128)(2,1)}, bf16[384,512]{1,0:T(8,128)(2,1)S(1)}, u32[]{:S(2)}, u32[]{:S(2)}) %collective-permute-start.2) | collective-permute-done | bytes 393248 | tf_op jit(solution)/shard_map/ppermute | solution.py:236
  26.3 1.8 %shard_map.121.refs_0_.own_ref = f32[768,512]{1,0:T(8,128)S(1)} custom-call(bf16[768,1920]{1,0:T(8,128)(2,1)S(1)} %get-tuple-element.40.dense_ref, bf16[384,512]{1,0:T(8,128)(2,1)S(1)} %collective-permute-done.2.refs_0_, bf16[384,512]{1,0:T(8,128)(2,1)S(1)} %collective-permute-done.3.refs_1_, bf16[384,512]{1,0:T(8,128)(2,1)S(1)} %copy-done.2, ...), custom_call_target="tpu_custom_call" | custom-call | tf_op jit(solution)/shard_map/pallas_call | solution.py:16
  28.1 1.2 %collective-permute-done.5.refs_1_ = bf16[384,512]{1,0:T(8,128)(2,1)S(1)} collective-permute-done((bf16[384,512]{1,0:T(8,128)(2,1)}, bf16[384,512]{1,0:T(8,128)(2,1)S(1)}, u32[]{:S(2)}, u32[]{:S(2)}) %collective-permute-start.5) | collective-permute-done | bytes 393248 | tf_op jit(solution)/shard_map/ppermute | solution.py:236
  29.8 2.3 %collective-permute-done.6.mate_ref = f32[384,512]{1,0:T(8,128)S(1)} collective-permute-done((f32[384,512]{1,0:T(8,128)S(1)}, f32[384,512]{1,0:T(8,128)S(1)}, u32[]{:S(2)}, u32[]{:S(2)}) %collective-permute-start.6) | collective-permute-done | bytes 786464 | tf_op jit(solution)/shard_map/ppermute | solution.py:334
  32.1 1.4 %shard_map.123 = (bf16[384,512]{1,0:T(8,128)(2,1)}, bf16[384,512]{1,0:T(8,128)(2,1)S(1)}, f32[4,80,512]{2,1,0:T(8,128)S(1)}, bf16[4,80,512]{2,1,0:T(8,128)(2,1)S(1)}) custom-call(s32[1]{0:T(128)} %bitcast.spot_ref.refs_0_, f32[768,512]{1,0:T(8,128)S(1)} %shard_map.121.refs_0_.own_ref, f32[384,512]{1,0:T(8,128)S(1)} %collective-permute-done.6.mate_ref, ...), custom_call_target="tpu_custom_call" | custom-call | tf_op jit(solution)/shard_map/pallas_call | solution.py:16
  34.0 1.7 %collective-permute-done.7.got_ref = bf16[4,80,512]{2,1,0:T(8,128)(2,1)S(1)} collective-permute-done((bf16[4,80,512]{2,1,0:T(8,128)(2,1)S(1)}, bf16[4,80,512]{2,1,0:T(8,128)(2,1)S(1)}, u32[]{:S(2)}, u32[]{:S(2)}) %collective-permute-start.7) | collective-permute-done | bytes 327712 | tf_op jit(solution)/shard_map/ppermute | solution.py:334
  35.8 1.5 %shard_map.125 = (bf16[384,512]{1,0:T(8,128)(2,1)S(1)}, bf16[384,512]{1,0:T(8,128)(2,1)S(1)}, f32[384,512]{1,0:T(8,128)S(1)}) custom-call(s32[1]{0:T(128)} %bitcast.spot_ref.refs_0_, s32[40]{0:T(128)S(1)} %copy-done.5, bf16[1920,768]{1,0:T(8,128)(2,1)S(1)} %get-tuple-element.46.refs_2_, bf16[384,512]{1,0:T(8,128)(2,1)S(1)} %get-tuple-element.47.refs_3_, ...), custom_call_target="tpu_custom_call" | custom-call | tf_op jit(solution)/shard_map/pallas_call | solution.py:16
  37.3 1.6 %collective-permute-start.12 = (bf16[384,512]{1,0:T(8,128)(2,1)S(1)}, bf16[384,512]{1,0:T(8,128)(2,1)S(1)}, u32[]{:S(2)}, u32[]{:S(2)}) collective-permute-start(bf16[384,512]{1,0:T(8,128)(2,1)S(1)} %get-tuple-element.49), channel_id=1, source_target_pairs={{0,2},{1,5},{2,0},{3,7},{4,6},{5,1},{6,4},{7,3},{8,10},{9,13},{10,... | collective-permute-start | bytes 1179656 | tf_op jit(solution)/shard_map/ppermute | solution.py:283
  39.4 6.6 %collective-permute-done.8.got_ref = bf16[2,80,512]{2,1,0:T(8,128)(2,1)S(1)} collective-permute-done((bf16[2,80,512]{2,1,0:T(8,128)(2,1)S(1)}, bf16[2,80,512]{2,1,0:T(8,128)(2,1)S(1)}, u32[]{:S(2)}, u32[]{:S(2)}) %collective-permute-start.8) | collective-permute-done | bytes 163872 | tf_op jit(solution)/shard_map/ppermute | solution.py:349
  46.6 1.9 %shard_map.127 = (f32[384,512]{1,0:T(8,128)S(1)}, f32[384,512]{1,0:T(8,128)S(1)}, f32[384,512]{1,0:T(8,128)S(1)}) custom-call(s32[1]{0:T(128)} %bitcast.spot_ref.refs_0_, s32[40]{0:T(128)S(1)} %copy-done.5, bf16[1920,768]{1,0:T(8,128)(2,1)S(1)} %get-tuple-element.46.refs_2_, bf16[384,512]{1,0:T(8,128)(2,1)S(1)} %get-tuple-element.47.refs_3_, ...), custom_call_target="tpu_custom_call" | custom-call | tf_op jit(solution)/shard_map/pallas_call | solution.py:16
  48.5 2.0 %collective-permute-done.10.got_ref = bf16[1,80,512]{2,1,0:T(8,128)(2,1)S(1)} collective-permute-done((bf16[1,80,512]{2,1,0:T(8,128)(2,1)S(1)}, bf16[1,80,512]{2,1,0:T(8,128)(2,1)S(1)}, u32[]{:S(2)}, u32[]{:S(2)}) %collective-permute-start.10) | collective-permute-done | bytes 81952 | tf_op jit(solution)/shard_map/ppermute | solution.py:349
  50.7 0.7 collective-permute-start.14
  51.4 4.5 %collective-permute-done.11.refs_1_ = bf16[80,512]{1,0:T(8,128)(2,1)S(1)} collective-permute-done((bf16[80,512]{1,0:T(8,128)(2,1)S(1)}, bf16[80,512]{1,0:T(8,128)(2,1)S(1)}, u32[]{:S(2)}, u32[]{:S(2)}) %collective-permute-start.11) | collective-permute-done | bytes 81952 | tf_op jit(solution)/shard_map/ppermute | solution.py:349
  56.1 2.8 %collective-permute-start.16 = (bf16[384,512]{1,0:T(8,128)(2,1)S(1)}, bf16[384,512]{1,0:T(8,128)(2,1)S(1)}, u32[]{:S(2)}, u32[]{:S(2)}) collective-permute-start(bf16[384,512]{1,0:T(8,128)(2,1)S(1)} %shard_map.130), channel_id=1, source_target_pairs={{0,24},{2,26},{3,11},{4,12},{5,29},{6,14},{8,0},{10,2},{11,19},{12... | collective-permute-start | bytes 1179656 | tf_op jit(solution)/shard_map/ppermute | solution.py:283
  59.2 6.7 %collective-permute-done.13.other_ref = bf16[80,512]{1,0:T(8,128)(2,1)S(1)} collective-permute-done((bf16[80,512]{1,0:T(8,128)(2,1)S(1)}, bf16[80,512]{1,0:T(8,128)(2,1)S(1)}, u32[]{:S(2)}, u32[]{:S(2)}) %collective-permute-start.13) | collective-permute-done | bytes 81952 | tf_op jit(solution)/shard_map/ppermute | solution.py:349
  65.9 6.4 %collective-permute-start.15 = (bf16[64,512]{1,0:T(8,128)(2,1)S(1)}, bf16[64,512]{1,0:T(8,128)(2,1)S(1)}, u32[]{:S(2)}, u32[]{:S(2)}) collective-permute-start(bf16[64,512]{1,0:T(8,128)(2,1)S(1)} %get-tuple-element.63.mine_ref), channel_id=1, source_target_pairs={{0,2},{1,5},{2,0},{3,7},{4,6},{5,1},{6,4},{7,3},{8,10},{9,13},{10,... | collective-permute-start | bytes 196616 | tf_op jit(solution)/shard_map/ppermute | solution.py:349
  72.6 2.7 %collective-permute-done.15.other_ref = bf16[64,512]{1,0:T(8,128)(2,1)S(1)} collective-permute-done((bf16[64,512]{1,0:T(8,128)(2,1)S(1)}, bf16[64,512]{1,0:T(8,128)(2,1)S(1)}, u32[]{:S(2)}, u32[]{:S(2)}) %collective-permute-start.15) | collective-permute-done | bytes 65568 | tf_op jit(solution)/shard_map/ppermute | solution.py:349
  75.4 2.0 %collective-permute-start.20 = (bf16[384,512]{1,0:T(8,128)(2,1)S(1)}, bf16[384,512]{1,0:T(8,128)(2,1)S(1)}, u32[]{:S(2)}, u32[]{:S(2)}) collective-permute-start(bf16[384,512]{1,0:T(8,128)(2,1)S(1)} %shard_map.133), channel_id=1, source_target_pairs={{0,4},{1,3},{2,6},{3,1},{4,0},{5,7},{6,2},{7,5},{8,12},{9,11},{10,... | collective-permute-start | bytes 1179656 | tf_op jit(solution)/shard_map/ppermute | solution.py:283
  77.4 2.9 %collective-permute-done.17.other_ref = bf16[2,64,512]{2,1,0:T(8,128)(2,1)S(1)} collective-permute-done((bf16[2,64,512]{2,1,0:T(8,128)(2,1)S(1)}, bf16[2,64,512]{2,1,0:T(8,128)(2,1)S(1)}, u32[]{:S(2)}, u32[]{:S(2)}) %collective-permute-start.17) | collective-permute-done | bytes 131104 | tf_op jit(solution)/shard_map/ppermute | solution.py:349
  81.0 2.5 %collective-permute-done.19.refs_1_ = bf16[384,512]{1,0:T(8,128)(2,1)S(1)} collective-permute-done((bf16[384,512]{1,0:T(8,128)(2,1)S(1)}, bf16[384,512]{1,0:T(8,128)(2,1)S(1)}, u32[]{:S(2)}, u32[]{:S(2)}) %collective-permute-start.19) | collective-permute-done | bytes 393248 | tf_op jit(solution)/shard_map/ppermute | solution.py:283
  83.5 1.0 %collective-permute-done.20.refs_2_ = bf16[384,512]{1,0:T(8,128)(2,1)S(1)} collective-permute-done((bf16[384,512]{1,0:T(8,128)(2,1)S(1)}, bf16[384,512]{1,0:T(8,128)(2,1)S(1)}, u32[]{:S(2)}, u32[]{:S(2)}) %collective-permute-start.20) | collective-permute-done | bytes 393248 | tf_op jit(solution)/shard_map/ppermute | solution.py:283
  84.5 0.9 %shard_map.136 = bf16[384,512]{1,0:T(8,128)(2,1)} custom-call(s32[1]{0:T(128)} %bitcast.spot_ref.refs_0_, f32[384,512]{1,0:T(8,128)S(1)} %get-tuple-element.54.refs_0_, bf16[384,512]{1,0:T(8,128)(2,1)S(1)} %collective-permute-done.19.refs_1_, bf16[384,512]{1,0:T(8,128)(2,1)S(1)} %collective-permute-done.20.refs_2_), custom_call_target="tpu_custom_call" | custom-call | tf_op jit(solution)/shard_map/pallas_call | solution.py:16
  85.4 1.0 %shard_map.137 = f32[512,512]{1,0:T(8,128)} custom-call(s32[1]{0:T(128)} %bitcast.spot_ref.refs_0_, bf16[256,512]{1,0:T(8,128)(2,1)S(1)} %shard_map.135.mine_ref, bf16[256,512]{1,0:T(8,128)(2,1)S(1)} %collective-permute-done.18.other_ref), custom_call_target="tpu_custom_call" | custom-call | tf_op jit(solution)/shard_map/pallas_call | solution.py:16
  (45 shorter events, 5.2 us)
Async XLA Ops:
  0.6 11.1 %collective-permute-start = (bf16[8,7,128,128]{3,2,1,0:T(8,128)(2,1)}, bf16[8,7,128,128]{3,2,1,0:T(8,128)(2,1)S(1)}, u32[]{:S(2)}, u32[]{:S(2)}) collective-permute-start(bf16[8,7,128,128]{3,2,1,0:T(8,128)(2,1)} %bitcast.7), channel_id=1, source_target_pairs={{0,1},{1,0},{2,3},{3,2},{4,5},{5,4},{6,7},{7,6},{8,9},{9,8},{10,11... | collective-permute-start | bytes 5505032 | tf_op jit(solution)/shard_map/ppermute | solution.py:334
  1.1 24.5 %collective-permute-start.2 = (bf16[384,512]{1,0:T(8,128)(2,1)}, bf16[384,512]{1,0:T(8,128)(2,1)S(1)}, u32[]{:S(2)}, u32[]{:S(2)}) collective-permute-start(bf16[384,512]{1,0:T(8,128)(2,1)} %refs_2_.1), channel_id=1, source_target_pairs={{0,4},{1,5},{2,6},{3,7},{4,8},{5,9},{6,10},{7,11},{8,12},{9,13},{1... | collective-permute-start | bytes 1179656 | tf_op jit(solution)/shard_map/ppermute | solution.py:236
  3.7 22.5 %collective-permute-start.3 = (bf16[384,512]{1,0:T(8,128)(2,1)}, bf16[384,512]{1,0:T(8,128)(2,1)S(1)}, u32[]{:S(2)}, u32[]{:S(2)}) collective-permute-start(bf16[384,512]{1,0:T(8,128)(2,1)} %refs_2_.1), channel_id=1, source_target_pairs={{0,2},{1,3},{2,4},{3,5},{4,6},{5,7},{6,8},{7,9},{8,10},{9,11},{10,... | collective-permute-start | bytes 1179656 | tf_op jit(solution)/shard_map/ppermute | solution.py:236
  5.2 21.1 %collective-permute-start.4 = (bf16[384,512]{1,0:T(8,128)(2,1)}, bf16[384,512]{1,0:T(8,128)(2,1)S(1)}, u32[]{:S(2)}, u32[]{:S(2)}) collective-permute-start(bf16[384,512]{1,0:T(8,128)(2,1)} %refs_2_.1), channel_id=1, source_target_pairs={{0,30},{1,31},{2,0},{3,1},{4,2},{5,3},{6,4},{7,5},{8,6},{9,7},{10,... | collective-permute-start | bytes 1179656 | tf_op jit(solution)/shard_map/ppermute | solution.py:236
  9.4 20.0 %collective-permute-start.5 = (bf16[384,512]{1,0:T(8,128)(2,1)}, bf16[384,512]{1,0:T(8,128)(2,1)S(1)}, u32[]{:S(2)}, u32[]{:S(2)}) collective-permute-start(bf16[384,512]{1,0:T(8,128)(2,1)} %refs_2_.1), channel_id=1, source_target_pairs={{0,28},{2,30},{4,0},{6,2},{8,4},{10,6},{12,8},{14,10},{16,12},{18,... | collective-permute-start | bytes 1179656 | tf_op jit(solution)/shard_map/ppermute | solution.py:236
  13.2 1.1 %collective-permute-start.1 = (s32[120]{0:T(128)S(1)}, s32[120]{0:T(128)S(1)}, u32[]{:S(2)}, u32[]{:S(2)}) collective-permute-start(s32[120]{0:T(128)S(1)} %reshape.24.own_meta_ref), channel_id=1, source_target_pairs={{0,1},{1,0},{2,3},{3,2},{4,5},{5,4},{6,7},{7,6},{8,9},{9,8},{10,11... | collective-permute-start | bytes 1448 | tf_op jit(solution)/shard_map/ppermute | solution.py:334
  14.4 1.5 %copy-start = (bf16[1,8,7,128,128]{4,3,2,1,0:T(8,128)(2,1)S(1)}, bf16[1,8,7,128,128]{4,3,2,1,0:T(8,128)(2,1)}, u32[]{:S(2)}) copy-start(bf16[1,8,7,128,128]{4,3,2,1,0:T(8,128)(2,1)} %param.12) | copy-start | bytes 5505028
  15.9 10.4 %copy-start.2 = (bf16[384,512]{1,0:T(8,128)(2,1)S(1)}, bf16[384,512]{1,0:T(8,128)(2,1)}, u32[]{:S(2)}) copy-start(bf16[384,512]{1,0:T(8,128)(2,1)} %refs_2_.1) | copy-start | bytes 1179652
  28.1 4.0 %copy-start.1 = (bf16[512,512]{1,0:T(8,128)(2,1)S(1)}, bf16[512,512]{1,0:T(8,128)(2,1)}, u32[]{:S(2)}) copy-start(bf16[512,512]{1,0:T(8,128)(2,1)} %weight_ref.1) | copy-start | bytes 1572868
  28.1 4.0 %copy-start.3 = (bf16[384,512]{1,0:T(8,128)(2,1)S(1)}, bf16[384,512]{1,0:T(8,128)(2,1)}, u32[]{:S(2)}) copy-start(bf16[384,512]{1,0:T(8,128)(2,1)} %grad_out_ref.1) | copy-start | bytes 1179652
  28.1 4.0 %copy-start.4 = (f32[512]{0:T(512)S(1)}, f32[512]{0:T(512)}, u32[]{:S(2)}) copy-start(f32[512]{0:T(512)} %param.14) | copy-start | bytes 6148
  29.7 2.4 %collective-permute-start.6 = (f32[384,512]{1,0:T(8,128)S(1)}, f32[384,512]{1,0:T(8,128)S(1)}, u32[]{:S(2)}, u32[]{:S(2)}) collective-permute-start(f32[384,512]{1,0:T(8,128)S(1)} %shard_map.122), channel_id=1, source_target_pairs={{0,1},{1,0},{2,3},{3,2},{4,5},{5,4},{6,7},{7,6},{8,9},{9,8},{10,11... | collective-permute-start | bytes 2359304 | tf_op jit(solution)/shard_map/ppermute | solution.py:334
  32.1 3.7 %copy-start.5 = (s32[40]{0:T(128)S(1)}, s32[40]{0:T(128)}, u32[]{:S(2)}) copy-start(s32[40]{0:T(128)} %constant.23.refs_1_) | copy-start | bytes 484
  33.5 2.3 %collective-permute-start.9 = (bf16[384,512]{1,0:T(8,128)(2,1)S(1)}, bf16[384,512]{1,0:T(8,128)(2,1)S(1)}, u32[]{:S(2)}, u32[]{:S(2)}) collective-permute-start(bf16[384,512]{1,0:T(8,128)(2,1)S(1)} %get-tuple-element.47.refs_3_), channel_id=1, source_target_pairs={{0,1},{1,0},{2,3},{3,2},{4,5},{5,4},{6,7},{7,6},{8,9},{9,8},{10,11... | collective-permute-start | bytes 1179656 | tf_op jit(solution)/shard_map/ppermute | solution.py:334
  33.6 2.1 %collective-permute-start.7 = (bf16[4,80,512]{2,1,0:T(8,128)(2,1)S(1)}, bf16[4,80,512]{2,1,0:T(8,128)(2,1)S(1)}, u32[]{:S(2)}, u32[]{:S(2)}) collective-permute-start(bf16[4,80,512]{2,1,0:T(8,128)(2,1)S(1)} %get-tuple-element.43), channel_id=1, source_target_pairs={{0,1},{1,0},{2,3},{3,2},{4,5},{5,4},{6,7},{7,6},{8,9},{9,8},{10,11... | collective-permute-start | bytes 983048 | tf_op jit(solution)/shard_map/ppermute | solution.py:334
  37.3 18.6 %collective-permute-start.12 = (bf16[384,512]{1,0:T(8,128)(2,1)S(1)}, bf16[384,512]{1,0:T(8,128)(2,1)S(1)}, u32[]{:S(2)}, u32[]{:S(2)}) collective-permute-start(bf16[384,512]{1,0:T(8,128)(2,1)S(1)} %get-tuple-element.49), channel_id=1, source_target_pairs={{0,2},{1,5},{2,0},{3,7},{4,6},{5,1},{6,4},{7,3},{8,10},{9,13},{10,... | collective-permute-start | bytes 1179656 | tf_op jit(solution)/shard_map/ppermute | solution.py:283
  38.9 7.1 %collective-permute-start.8 = (bf16[2,80,512]{2,1,0:T(8,128)(2,1)S(1)}, bf16[2,80,512]{2,1,0:T(8,128)(2,1)S(1)}, u32[]{:S(2)}, u32[]{:S(2)}) collective-permute-start(bf16[2,80,512]{2,1,0:T(8,128)(2,1)S(1)} %get-tuple-element.45), channel_id=1, source_target_pairs={{0,4},{1,3},{2,6},{3,1},{4,0},{5,7},{6,2},{7,5},{8,12},{9,11},{10,... | collective-permute-start | bytes 491528 | tf_op jit(solution)/shard_map/ppermute | solution.py:349
  46.0 4.5 %collective-permute-start.10 = (bf16[1,80,512]{2,1,0:T(8,128)(2,1)S(1)}, bf16[1,80,512]{2,1,0:T(8,128)(2,1)S(1)}, u32[]{:S(2)}, u32[]{:S(2)}) collective-permute-start(bf16[1,80,512]{2,1,0:T(8,128)(2,1)S(1)} %get-tuple-element.52), channel_id=1, source_target_pairs={{0,2},{1,5},{2,0},{3,7},{4,6},{5,1},{6,4},{7,3},{8,10},{9,13},{10,... | collective-permute-start | bytes 245768 | tf_op jit(solution)/shard_map/ppermute | solution.py:349
  50.6 5.4 %collective-permute-start.11 = (bf16[80,512]{1,0:T(8,128)(2,1)S(1)}, bf16[80,512]{1,0:T(8,128)(2,1)S(1)}, u32[]{:S(2)}, u32[]{:S(2)}) collective-permute-start(bf16[80,512]{1,0:T(8,128)(2,1)S(1)} %shard_map.128.refs_0_), channel_id=1, source_target_pairs={{0,8},{1,9},{2,10},{3,11},{4,12},{5,13},{6,14},{7,15},{8,0},{9,1},... | collective-permute-start | bytes 245768 | tf_op jit(solution)/shard_map/ppermute | solution.py:349
  50.7 8.3 %collective-permute-start.14 = (bf16[384,512]{1,0:T(8,128)(2,1)S(1)}, bf16[384,512]{1,0:T(8,128)(2,1)S(1)}, u32[]{:S(2)}, u32[]{:S(2)}) collective-permute-start(bf16[384,512]{1,0:T(8,128)(2,1)S(1)} %get-tuple-element.61), channel_id=1, source_target_pairs={{1,25},{3,27},{9,1},{11,3},{17,9},{19,11},{25,17},{27,19}} | collective-permute-start | bytes 1179656 | tf_op jit(solution)/shard_map/ppermute | solution.py:283
  56.1 16.4 %collective-permute-start.16 = (bf16[384,512]{1,0:T(8,128)(2,1)S(1)}, bf16[384,512]{1,0:T(8,128)(2,1)S(1)}, u32[]{:S(2)}, u32[]{:S(2)}) collective-permute-start(bf16[384,512]{1,0:T(8,128)(2,1)S(1)} %shard_map.130), channel_id=1, source_target_pairs={{0,24},{2,26},{3,11},{4,12},{5,29},{6,14},{8,0},{10,2},{11,19},{12... | collective-permute-start | bytes 1179656 | tf_op jit(solution)/shard_map/ppermute | solution.py:283
  58.9 7.0 %collective-permute-start.13 = (bf16[80,512]{1,0:T(8,128)(2,1)S(1)}, bf16[80,512]{1,0:T(8,128)(2,1)S(1)}, u32[]{:S(2)}, u32[]{:S(2)}) collective-permute-start(bf16[80,512]{1,0:T(8,128)(2,1)S(1)} %shard_map.129.mine_ref), channel_id=1, source_target_pairs={{0,16},{1,17},{2,18},{3,19},{4,20},{5,21},{6,22},{7,23},{8,24},{9,... | collective-permute-start | bytes 245768 | tf_op jit(solution)/shard_map/ppermute | solution.py:349
  65.9 9.4 %collective-permute-start.15 = (bf16[64,512]{1,0:T(8,128)(2,1)S(1)}, bf16[64,512]{1,0:T(8,128)(2,1)S(1)}, u32[]{:S(2)}, u32[]{:S(2)}) collective-permute-start(bf16[64,512]{1,0:T(8,128)(2,1)S(1)} %get-tuple-element.63.mine_ref), channel_id=1, source_target_pairs={{0,2},{1,5},{2,0},{3,7},{4,6},{5,1},{6,4},{7,3},{8,10},{9,13},{10,... | collective-permute-start | bytes 196616 | tf_op jit(solution)/shard_map/ppermute | solution.py:349
  72.4 11.2 %collective-permute-start.19 = (bf16[384,512]{1,0:T(8,128)(2,1)S(1)}, bf16[384,512]{1,0:T(8,128)(2,1)S(1)}, u32[]{:S(2)}, u32[]{:S(2)}) collective-permute-start(bf16[384,512]{1,0:T(8,128)(2,1)S(1)} %shard_map.131), channel_id=1, source_target_pairs={{0,2},{1,5},{2,0},{3,7},{4,6},{5,1},{6,4},{7,3},{8,10},{9,13},{10,... | collective-permute-start | bytes 1179656 | tf_op jit(solution)/shard_map/ppermute | solution.py:283
  75.3 5.0 %collective-permute-start.17 = (bf16[2,64,512]{2,1,0:T(8,128)(2,1)S(1)}, bf16[2,64,512]{2,1,0:T(8,128)(2,1)S(1)}, u32[]{:S(2)}, u32[]{:S(2)}) collective-permute-start(bf16[2,64,512]{2,1,0:T(8,128)(2,1)S(1)} %shard_map.134.mine_ref), channel_id=1, source_target_pairs={{0,4},{1,3},{2,6},{3,1},{4,0},{5,7},{6,2},{7,5},{8,12},{9,11},{10,... | collective-permute-start | bytes 393224 | tf_op jit(solution)/shard_map/ppermute | solution.py:349
  75.4 9.2 %collective-permute-start.20 = (bf16[384,512]{1,0:T(8,128)(2,1)S(1)}, bf16[384,512]{1,0:T(8,128)(2,1)S(1)}, u32[]{:S(2)}, u32[]{:S(2)}) collective-permute-start(bf16[384,512]{1,0:T(8,128)(2,1)S(1)} %shard_map.133), channel_id=1, source_target_pairs={{0,4},{1,3},{2,6},{3,1},{4,0},{5,7},{6,2},{7,5},{8,12},{9,11},{10,... | collective-permute-start | bytes 1179656 | tf_op jit(solution)/shard_map/ppermute | solution.py:283
  80.4 5.1 %collective-permute-start.18 = (bf16[256,512]{1,0:T(8,128)(2,1)S(1)}, bf16[256,512]{1,0:T(8,128)(2,1)S(1)}, u32[]{:S(2)}, u32[]{:S(2)}) collective-permute-start(bf16[256,512]{1,0:T(8,128)(2,1)S(1)} %shard_map.135.mine_ref), channel_id=1, source_target_pairs={{0,1},{1,0},{2,3},{3,2},{4,5},{5,4},{6,7},{7,6},{8,9},{9,8},{10,11... | collective-permute-start | bytes 786440 | tf_op jit(solution)/shard_map/ppermute | solution.py:334

commit v8 on v7

--- a/solution.py
+++ b/solution.py
@@ -290,25 +290,21 @@
         take = lambda mate, *args: scattered_sums(self.flipped, self.own, mate, *args, self.spot, self.LOOKUP)
         if k == 0:
             _, mate = after(token, self.mate)
-            to_last, self.to_plane, self.plane_rest = take(mate, (4, 3), [[BF16], [BF16, F32]])
+            self.to_last, self.to_plane, self.plane_rest = take(mate, (4, 3), [[BF16], [BF16, F32]])
+            self.kept, self.to_across, self.to_straight = take(mate, (0, 1, 2), [[F32]] * 3)
+            return [self.to_last, self.kept]
+        if k == 2:
+            _, to_last, to_plane = after(token, self.to_last, self.to_plane)
             self.from_last = self.routed(to_last, straight)
-            return [to_last]
-        if k == 1:
-            _, mate = after(token, self.mate)
-            self.kept, self.to_across, self.to_straight = take(mate, (0, 1, 2), [[F32]] * 3)
-            return [self.kept]
-        if k == 2:
-            _, to_plane = after(token, self.to_plane)
             self.from_plane = self.routed(to_plane, {1: -8, 3: -8})
-            return [self.from_last]
-        if k == 3:
-            _, rest = after(token, self.plane_rest)
-            out = summed_terms(self.spot, [rest, self.from_last], [self.EVEN, self.MIDDLE])
+        if k == 4:
+            _, rest, plane_rest = after(token, self.to_straight, self.plane_rest)
+            out = summed_terms(self.spot, [plane_rest, self.from_last], [self.EVEN, self.MIDDLE])
             self.from_planes = self.routed(out, {0: -8, 2: -8, 4: 8, 6: 8, 5: -8, 3: 8})
-            second = summed_terms(self.spot, [self.to_straight, self.from_plane], [None, self.ODD_LOW])
+            second = summed_terms(self.spot, [rest, self.from_plane], [None, self.ODD_LOW])
             self.second = self.routed(second, straight)
-            return [out, second]
-        if k == 4:
+            return [second]
+        if k == 5:
             _, rest = after(token, self.to_across)
             out = summed_terms(
                 self.spot,

time: 86.7 us -> 81.9 us (0.945)
  waiting for transfers between devices: 41.4 us -> 36.2 us
    ppermute x6, waiting for transfers between devices: 25.4 us -> 20.3 us  [exchanged(): other = lax.ppermute(value, 'blk', pairs)]
    ppermute x5, starting transfers between devices: 7.12 us -> 11.6 us  [routed(): return lax.ppermute(value, 'blk', pairs)]
    ppermute x6, starting transfers between devices: 7.97 us -> 4.11 us  [exchanged(): other = lax.ppermute(value, 'blk', pairs)]
  transfers between devices with their start and end apart: 21 -> 21, of which waited for: 14 -> 14; matrix products, arithmetic and copies ran while one was open for 2% -> 3% of each run, Pallas kernels for 11% -> 13%
where the time goes in v8:
time: 81.9 us; the launch traced here: 81.6 us
  waiting for transfers between devices  36.2 us (44%)
  starting transfers between devices  27.4 us (33%)
  Pallas kernels  13.5 us (16%)
  local copies, waits for them, and re-layouts  2.98 us (4%)
  between operations  0.85 us (1%)
    ppermute x6, waiting for transfers between devices, exchanged(): other = lax.ppermute(value, 'blk', pairs)  20.3 us
    pallas_call x18, Pallas kernels, call(): pl.pallas_call(kernel, out_shape=out_shape, in_specs=[spec(k) for k in ra...  13.5 us
    ppermute x5, starting transfers between devices, routed(): return lax.ppermute(value, 'blk', pairs)  11.6 us
    ppermute x4, starting transfers between devices, sent(): return lax.ppermute(value, 'blk', pairs)  10.5 us
    ppermute x4, waiting for transfers between devices, sent(): return lax.ppermute(value, 'blk', pairs)  7.68 us
    ppermute x6, waiting for transfers between devices, swapped(): return lax.ppermute(value, 'blk', [(s, s ^ distance) for s in range(count)])  4.5 us
    ppermute x6, starting transfers between devices, exchanged(): other = lax.ppermute(value, 'blk', pairs)  4.11 us
    ppermute x5, waiting for transfers between devices, routed(): return lax.ppermute(value, 'blk', pairs)  3.73 us
  transfers between devices with their start and end apart: 21, of which 14 were waited for; matrix products, arithmetic and copies ran while one was open for 3% of the time, Pallas kernels for 13%

profile of v8, /device:TPU:0, one launch (start us, length us, event | category | flops | bytes accessed | tf_op | source)
XLA Modules:
  0.0 81.6 jit_solution(15579271202054948314)
XLA Ops:
  1.1 2.6 %collective-permute-start.2 = (bf16[384,512]{1,0:T(8,128)(2,1)}, bf16[384,512]{1,0:T(8,128)(2,1)S(1)}, u32[]{:S(2)}, u32[]{:S(2)}) collective-permute-start(bf16[384,512]{1,0:T(8,128)(2,1)} %refs_2_.1), channel_id=1, source_target_pairs={{0,4},{1,5},{2,6},{3,7},{4,8},{5,9},{6,10},{7,11},{8,12},{9,13},{1... | collective-permute-start | bytes 1179656 | tf_op jit(solution)/shard_map/ppermute | solution.py:236
  3.7 1.5 %collective-permute-start.3 = (bf16[384,512]{1,0:T(8,128)(2,1)}, bf16[384,512]{1,0:T(8,128)(2,1)S(1)}, u32[]{:S(2)}, u32[]{:S(2)}) collective-permute-start(bf16[384,512]{1,0:T(8,128)(2,1)} %refs_2_.1), channel_id=1, source_target_pairs={{0,2},{1,3},{2,4},{3,5},{4,6},{5,7},{6,8},{7,9},{8,10},{9,11},{10,... | collective-permute-start | bytes 1179656 | tf_op jit(solution)/shard_map/ppermute | solution.py:236
  5.2 4.1 %collective-permute-start.4 = (bf16[384,512]{1,0:T(8,128)(2,1)}, bf16[384,512]{1,0:T(8,128)(2,1)S(1)}, u32[]{:S(2)}, u32[]{:S(2)}) collective-permute-start(bf16[384,512]{1,0:T(8,128)(2,1)} %refs_2_.1), channel_id=1, source_target_pairs={{0,30},{1,31},{2,0},{3,1},{4,2},{5,3},{6,4},{7,5},{8,6},{9,7},{10,... | collective-permute-start | bytes 1179656 | tf_op jit(solution)/shard_map/ppermute | solution.py:236
  9.4 2.3 %collective-permute-start.5 = (bf16[384,512]{1,0:T(8,128)(2,1)}, bf16[384,512]{1,0:T(8,128)(2,1)S(1)}, u32[]{:S(2)}, u32[]{:S(2)}) collective-permute-start(bf16[384,512]{1,0:T(8,128)(2,1)} %refs_2_.1), channel_id=1, source_target_pairs={{0,28},{2,30},{4,0},{6,2},{8,4},{10,6},{12,8},{14,10},{16,12},{18,... | collective-permute-start | bytes 1179656 | tf_op jit(solution)/shard_map/ppermute | solution.py:236
  11.7 0.7 reshape_squeeze.3
  13.3 1.1 %collective-permute-done.1.mate_meta_ref = s32[120]{0:T(128)S(1)} collective-permute-done((s32[120]{0:T(128)S(1)}, s32[120]{0:T(128)S(1)}, u32[]{:S(2)}, u32[]{:S(2)}) %collective-permute-start.1) | collective-permute-done | bytes 512 | tf_op jit(solution)/shard_map/ppermute | solution.py:330
  14.4 1.5 %copy-done = bf16[1,8,7,128,128]{4,3,2,1,0:T(8,128)(2,1)S(1)} copy-done((bf16[1,8,7,128,128]{4,3,2,1,0:T(8,128)(2,1)S(1)}, bf16[1,8,7,128,128]{4,3,2,1,0:T(8,128)(2,1)}, u32[]{:S(2)}) %copy-start) | copy-done | bytes 1835032
  15.9 4.0 %shard_map.120 = (bf16[768,1920]{1,0:T(8,128)(2,1)S(1)}, bf16[1920,768]{1,0:T(8,128)(2,1)S(1)}) custom-call(s32[1]{0:T(128)} %bitcast.spot_ref.refs_0_, s32[120]{0:T(128)S(1)} %reshape.24.own_meta_ref, s32[120]{0:T(128)S(1)} %collective-permute-done.1.mate_meta_ref, bf16[8,7,128,128]{3,2,1,0:T(8,128)(2,1)S(1)} %bitcast.8, ...), custom_call_target="tpu_custom_call" | custom-call | tf_op jit(solution)/shard_map/pallas_call | solution.py:16
  19.8 5.8 %collective-permute-done.2.refs_0_ = bf16[384,512]{1,0:T(8,128)(2,1)S(1)} collective-permute-done((bf16[384,512]{1,0:T(8,128)(2,1)}, bf16[384,512]{1,0:T(8,128)(2,1)S(1)}, u32[]{:S(2)}, u32[]{:S(2)}) %collective-permute-start.2) | collective-permute-done | bytes 393248 | tf_op jit(solution)/shard_map/ppermute | solution.py:236
  26.3 1.8 %shard_map.121.refs_0_.own_ref = f32[768,512]{1,0:T(8,128)S(1)} custom-call(bf16[768,1920]{1,0:T(8,128)(2,1)S(1)} %get-tuple-element.39.dense_ref, bf16[384,512]{1,0:T(8,128)(2,1)S(1)} %collective-permute-done.2.refs_0_, bf16[384,512]{1,0:T(8,128)(2,1)S(1)} %collective-permute-done.3.refs_1_, bf16[384,512]{1,0:T(8,128)(2,1)S(1)} %copy-done.2, ...), custom_call_target="tpu_custom_call" | custom-call | tf_op jit(solution)/shard_map/pallas_call | solution.py:16
  28.1 1.2 %collective-permute-done.5.refs_1_ = bf16[384,512]{1,0:T(8,128)(2,1)S(1)} collective-permute-done((bf16[384,512]{1,0:T(8,128)(2,1)}, bf16[384,512]{1,0:T(8,128)(2,1)S(1)}, u32[]{:S(2)}, u32[]{:S(2)}) %collective-permute-start.5) | collective-permute-done | bytes 393248 | tf_op jit(solution)/shard_map/ppermute | solution.py:236
  29.8 2.3 %collective-permute-done.6.mate_ref = f32[384,512]{1,0:T(8,128)S(1)} collective-permute-done((f32[384,512]{1,0:T(8,128)S(1)}, f32[384,512]{1,0:T(8,128)S(1)}, u32[]{:S(2)}, u32[]{:S(2)}) %collective-permute-start.6) | collective-permute-done | bytes 786464 | tf_op jit(solution)/shard_map/ppermute | solution.py:330
  32.1 1.4 %shard_map.123 = (bf16[384,512]{1,0:T(8,128)(2,1)}, bf16[384,512]{1,0:T(8,128)(2,1)S(1)}, f32[4,80,512]{2,1,0:T(8,128)S(1)}, bf16[4,80,512]{2,1,0:T(8,128)(2,1)S(1)}) custom-call(s32[1]{0:T(128)} %bitcast.spot_ref.refs_0_, f32[768,512]{1,0:T(8,128)S(1)} %shard_map.121.refs_0_.own_ref, f32[384,512]{1,0:T(8,128)S(1)} %collective-permute-done.6.mate_ref, ...), custom_call_target="tpu_custom_call" | custom-call | tf_op jit(solution)/shard_map/pallas_call | solution.py:16
  34.0 1.1 %collective-permute-done.7.got_ref = bf16[4,80,512]{2,1,0:T(8,128)(2,1)S(1)} collective-permute-done((bf16[4,80,512]{2,1,0:T(8,128)(2,1)S(1)}, bf16[4,80,512]{2,1,0:T(8,128)(2,1)S(1)}, u32[]{:S(2)}, u32[]{:S(2)}) %collective-permute-start.7) | collective-permute-done | bytes 327712 | tf_op jit(solution)/shard_map/ppermute | solution.py:330
  35.8 1.9 %shard_map.126 = (f32[384,512]{1,0:T(8,128)S(1)}, f32[384,512]{1,0:T(8,128)S(1)}, f32[384,512]{1,0:T(8,128)S(1)}) custom-call(s32[1]{0:T(128)} %bitcast.spot_ref.refs_0_, s32[40]{0:T(128)S(1)} %copy-done.5, bf16[1920,768]{1,0:T(8,128)(2,1)S(1)} %get-tuple-element.45.refs_2_, bf16[384,512]{1,0:T(8,128)(2,1)S(1)} %get-tuple-element.46.refs_3_, ...), custom_call_target="tpu_custom_call" | custom-call | tf_op jit(solution)/shard_map/pallas_call | solution.py:16
  37.7 1.5 %shard_map.125 = (bf16[384,512]{1,0:T(8,128)(2,1)S(1)}, bf16[384,512]{1,0:T(8,128)(2,1)S(1)}, f32[384,512]{1,0:T(8,128)S(1)}) custom-call(s32[1]{0:T(128)} %bitcast.spot_ref.refs_0_, s32[40]{0:T(128)S(1)} %copy-done.5, bf16[1920,768]{1,0:T(8,128)(2,1)S(1)} %get-tuple-element.45.refs_2_, bf16[384,512]{1,0:T(8,128)(2,1)S(1)} %get-tuple-element.46.refs_3_, ...), custom_call_target="tpu_custom_call" | custom-call | tf_op jit(solution)/shard_map/pallas_call | solution.py:16
  39.2 1.3 %collective-permute-done.8.got_ref = bf16[2,80,512]{2,1,0:T(8,128)(2,1)S(1)} collective-permute-done((bf16[2,80,512]{2,1,0:T(8,128)(2,1)S(1)}, bf16[2,80,512]{2,1,0:T(8,128)(2,1)S(1)}, u32[]{:S(2)}, u32[]{:S(2)}) %collective-permute-start.8) | collective-permute-done | bytes 163872 | tf_op jit(solution)/shard_map/ppermute | solution.py:345
  40.6 1.6 %collective-permute-start.10 = (bf16[1,80,512]{2,1,0:T(8,128)(2,1)S(1)}, bf16[1,80,512]{2,1,0:T(8,128)(2,1)S(1)}, u32[]{:S(2)}, u32[]{:S(2)}) collective-permute-start(bf16[1,80,512]{2,1,0:T(8,128)(2,1)S(1)} %get-tuple-element.52), channel_id=1, source_target_pairs={{0,2},{1,5},{2,0},{3,7},{4,6},{5,1},{6,4},{7,3},{8,10},{9,13},{10,... | collective-permute-start | bytes 245768 | tf_op jit(solution)/shard_map/ppermute | solution.py:345
  42.2 3.0 %collective-permute-done.10.got_ref = bf16[1,80,512]{2,1,0:T(8,128)(2,1)S(1)} collective-permute-done((bf16[1,80,512]{2,1,0:T(8,128)(2,1)S(1)}, bf16[1,80,512]{2,1,0:T(8,128)(2,1)S(1)}, u32[]{:S(2)}, u32[]{:S(2)}) %collective-permute-start.10) | collective-permute-done | bytes 81952 | tf_op jit(solution)/shard_map/ppermute | solution.py:345
  45.2 1.6 %collective-permute-start.16 = (bf16[384,512]{1,0:T(8,128)(2,1)S(1)}, bf16[384,512]{1,0:T(8,128)(2,1)S(1)}, u32[]{:S(2)}, u32[]{:S(2)}) collective-permute-start(bf16[384,512]{1,0:T(8,128)(2,1)S(1)} %get-tuple-element.63), channel_id=1, source_target_pairs={{0,2},{1,5},{2,0},{3,7},{4,6},{5,1},{6,4},{7,3},{8,10},{9,13},{10,... | collective-permute-start | bytes 1179656 | tf_op jit(solution)/shard_map/ppermute | solution.py:283
  47.0 5.1 %collective-permute-done.11.refs_1_ = bf16[80,512]{1,0:T(8,128)(2,1)S(1)} collective-permute-done((bf16[80,512]{1,0:T(8,128)(2,1)S(1)}, bf16[80,512]{1,0:T(8,128)(2,1)S(1)}, u32[]{:S(2)}, u32[]{:S(2)}) %collective-permute-start.11) | collective-permute-done | bytes 81952 | tf_op jit(solution)/shard_map/ppermute | solution.py:345
  52.5 0.7 collective-permute-start.14
  53.2 5.6 %collective-permute-done.12.other_ref = bf16[80,512]{1,0:T(8,128)(2,1)S(1)} collective-permute-done((bf16[80,512]{1,0:T(8,128)(2,1)S(1)}, bf16[80,512]{1,0:T(8,128)(2,1)S(1)}, u32[]{:S(2)}, u32[]{:S(2)}) %collective-permute-start.12) | collective-permute-done | bytes 81952 | tf_op jit(solution)/shard_map/ppermute | solution.py:345
  59.0 6.5 %collective-permute-start.17 = (bf16[384,512]{1,0:T(8,128)(2,1)S(1)}, bf16[384,512]{1,0:T(8,128)(2,1)S(1)}, u32[]{:S(2)}, u32[]{:S(2)}) collective-permute-start(bf16[384,512]{1,0:T(8,128)(2,1)S(1)} %shard_map.133), channel_id=1, source_target_pairs={{0,24},{2,26},{3,11},{4,12},{5,29},{6,14},{8,0},{10,2},{11,19},{12... | collective-permute-start | bytes 1179656 | tf_op jit(solution)/shard_map/ppermute | solution.py:283
  65.5 1.1 %collective-permute-start.13 = (bf16[64,512]{1,0:T(8,128)(2,1)S(1)}, bf16[64,512]{1,0:T(8,128)(2,1)S(1)}, u32[]{:S(2)}, u32[]{:S(2)}) collective-permute-start(bf16[64,512]{1,0:T(8,128)(2,1)S(1)} %get-tuple-element.53.mine_ref), channel_id=1, source_target_pairs={{0,2},{1,5},{2,0},{3,7},{4,6},{5,1},{6,4},{7,3},{8,10},{9,13},{10,... | collective-permute-start | bytes 196616 | tf_op jit(solution)/shard_map/ppermute | solution.py:345
  66.7 1.0 %collective-permute-start.19 = (bf16[384,512]{1,0:T(8,128)(2,1)S(1)}, bf16[384,512]{1,0:T(8,128)(2,1)S(1)}, u32[]{:S(2)}, u32[]{:S(2)}) collective-permute-start(bf16[384,512]{1,0:T(8,128)(2,1)S(1)} %shard_map.131), channel_id=1, source_target_pairs={{0,2},{1,5},{2,0},{3,7},{4,6},{5,1},{6,4},{7,3},{8,10},{9,13},{10,... | collective-permute-start | bytes 1179656 | tf_op jit(solution)/shard_map/ppermute | solution.py:283
  67.7 2.7 %collective-permute-done.13.other_ref = bf16[64,512]{1,0:T(8,128)(2,1)S(1)} collective-permute-done((bf16[64,512]{1,0:T(8,128)(2,1)S(1)}, bf16[64,512]{1,0:T(8,128)(2,1)S(1)}, u32[]{:S(2)}, u32[]{:S(2)}) %collective-permute-start.13) | collective-permute-done | bytes 65568 | tf_op jit(solution)/shard_map/ppermute | solution.py:345
  70.9 1.9 %collective-permute-start.20 = (bf16[384,512]{1,0:T(8,128)(2,1)S(1)}, bf16[384,512]{1,0:T(8,128)(2,1)S(1)}, u32[]{:S(2)}, u32[]{:S(2)}) collective-permute-start(bf16[384,512]{1,0:T(8,128)(2,1)S(1)} %shard_map.134), channel_id=1, source_target_pairs={{0,4},{1,3},{2,6},{3,1},{4,0},{5,7},{6,2},{7,5},{8,12},{9,11},{10,... | collective-permute-start | bytes 1179656 | tf_op jit(solution)/shard_map/ppermute | solution.py:283
  72.8 2.7 %collective-permute-done.15.other_ref = bf16[2,64,512]{2,1,0:T(8,128)(2,1)S(1)} collective-permute-done((bf16[2,64,512]{2,1,0:T(8,128)(2,1)S(1)}, bf16[2,64,512]{2,1,0:T(8,128)(2,1)S(1)}, u32[]{:S(2)}, u32[]{:S(2)}) %collective-permute-start.15) | collective-permute-done | bytes 131104 | tf_op jit(solution)/shard_map/ppermute | solution.py:345
  76.2 3.5 %collective-permute-done.20.refs_2_ = bf16[384,512]{1,0:T(8,128)(2,1)S(1)} collective-permute-done((bf16[384,512]{1,0:T(8,128)(2,1)S(1)}, bf16[384,512]{1,0:T(8,128)(2,1)S(1)}, u32[]{:S(2)}, u32[]{:S(2)}) %collective-permute-start.20) | collective-permute-done | bytes 393248 | tf_op jit(solution)/shard_map/ppermute | solution.py:283
  79.7 0.9 %shard_map.136 = bf16[384,512]{1,0:T(8,128)(2,1)} custom-call(s32[1]{0:T(128)} %bitcast.spot_ref.refs_0_, f32[384,512]{1,0:T(8,128)S(1)} %get-tuple-element.49.refs_0_, bf16[384,512]{1,0:T(8,128)(2,1)S(1)} %collective-permute-done.19.refs_1_, bf16[384,512]{1,0:T(8,128)(2,1)S(1)} %collective-permute-done.20.refs_2_), custom_call_target="tpu_custom_call" | custom-call | tf_op jit(solution)/shard_map/pallas_call | solution.py:16
  80.6 1.0 %shard_map.137 = f32[512,512]{1,0:T(8,128)} custom-call(s32[1]{0:T(128)} %bitcast.spot_ref.refs_0_, bf16[256,512]{1,0:T(8,128)(2,1)S(1)} %shard_map.135.mine_ref, bf16[256,512]{1,0:T(8,128)(2,1)S(1)} %collective-permute-done.18.other_ref), custom_call_target="tpu_custom_call" | custom-call | tf_op jit(solution)/shard_map/pallas_call | solution.py:16
  (45 shorter events, 5.8 us)
Async XLA Ops:
  0.6 11.1 %collective-permute-start = (bf16[8,7,128,128]{3,2,1,0:T(8,128)(2,1)}, bf16[8,7,128,128]{3,2,1,0:T(8,128)(2,1)S(1)}, u32[]{:S(2)}, u32[]{:S(2)}) collective-permute-start(bf16[8,7,128,128]{3,2,1,0:T(8,128)(2,1)} %bitcast.7), channel_id=1, source_target_pairs={{0,1},{1,0},{2,3},{3,2},{4,5},{5,4},{6,7},{7,6},{8,9},{9,8},{10,11... | collective-permute-start | bytes 5505032 | tf_op jit(solution)/shard_map/ppermute | solution.py:330
  1.1 24.5 %collective-permute-start.2 = (bf16[384,512]{1,0:T(8,128)(2,1)}, bf16[384,512]{1,0:T(8,128)(2,1)S(1)}, u32[]{:S(2)}, u32[]{:S(2)}) collective-permute-start(bf16[384,512]{1,0:T(8,128)(2,1)} %refs_2_.1), channel_id=1, source_target_pairs={{0,4},{1,5},{2,6},{3,7},{4,8},{5,9},{6,10},{7,11},{8,12},{9,13},{1... | collective-permute-start | bytes 1179656 | tf_op jit(solution)/shard_map/ppermute | solution.py:236
  3.7 22.5 %collective-permute-start.3 = (bf16[384,512]{1,0:T(8,128)(2,1)}, bf16[384,512]{1,0:T(8,128)(2,1)S(1)}, u32[]{:S(2)}, u32[]{:S(2)}) collective-permute-start(bf16[384,512]{1,0:T(8,128)(2,1)} %refs_2_.1), channel_id=1, source_target_pairs={{0,2},{1,3},{2,4},{3,5},{4,6},{5,7},{6,8},{7,9},{8,10},{9,11},{10,... | collective-permute-start | bytes 1179656 | tf_op jit(solution)/shard_map/ppermute | solution.py:236
  5.2 21.1 %collective-permute-start.4 = (bf16[384,512]{1,0:T(8,128)(2,1)}, bf16[384,512]{1,0:T(8,128)(2,1)S(1)}, u32[]{:S(2)}, u32[]{:S(2)}) collective-permute-start(bf16[384,512]{1,0:T(8,128)(2,1)} %refs_2_.1), channel_id=1, source_target_pairs={{0,30},{1,31},{2,0},{3,1},{4,2},{5,3},{6,4},{7,5},{8,6},{9,7},{10,... | collective-permute-start | bytes 1179656 | tf_op jit(solution)/shard_map/ppermute | solution.py:236
  9.4 20.0 %collective-permute-start.5 = (bf16[384,512]{1,0:T(8,128)(2,1)}, bf16[384,512]{1,0:T(8,128)(2,1)S(1)}, u32[]{:S(2)}, u32[]{:S(2)}) collective-permute-start(bf16[384,512]{1,0:T(8,128)(2,1)} %refs_2_.1), channel_id=1, source_target_pairs={{0,28},{2,30},{4,0},{6,2},{8,4},{10,6},{12,8},{14,10},{16,12},{18,... | collective-permute-start | bytes 1179656 | tf_op jit(solution)/shard_map/ppermute | solution.py:236
  13.2 1.1 %collective-permute-start.1 = (s32[120]{0:T(128)S(1)}, s32[120]{0:T(128)S(1)}, u32[]{:S(2)}, u32[]{:S(2)}) collective-permute-start(s32[120]{0:T(128)S(1)} %reshape.24.own_meta_ref), channel_id=1, source_target_pairs={{0,1},{1,0},{2,3},{3,2},{4,5},{5,4},{6,7},{7,6},{8,9},{9,8},{10,11... | collective-permute-start | bytes 1448 | tf_op jit(solution)/shard_map/ppermute | solution.py:330
  14.4 1.5 %copy-start = (bf16[1,8,7,128,128]{4,3,2,1,0:T(8,128)(2,1)S(1)}, bf16[1,8,7,128,128]{4,3,2,1,0:T(8,128)(2,1)}, u32[]{:S(2)}) copy-start(bf16[1,8,7,128,128]{4,3,2,1,0:T(8,128)(2,1)} %param.12) | copy-start | bytes 5505028
  15.9 10.4 %copy-start.2 = (bf16[384,512]{1,0:T(8,128)(2,1)S(1)}, bf16[384,512]{1,0:T(8,128)(2,1)}, u32[]{:S(2)}) copy-start(bf16[384,512]{1,0:T(8,128)(2,1)} %refs_2_.1) | copy-start | bytes 1179652
  28.1 4.0 %copy-start.1 = (bf16[512,512]{1,0:T(8,128)(2,1)S(1)}, bf16[512,512]{1,0:T(8,128)(2,1)}, u32[]{:S(2)}) copy-start(bf16[512,512]{1,0:T(8,128)(2,1)} %weight_ref.1) | copy-start | bytes 1572868
  28.1 4.0 %copy-start.3 = (bf16[384,512]{1,0:T(8,128)(2,1)S(1)}, bf16[384,512]{1,0:T(8,128)(2,1)}, u32[]{:S(2)}) copy-start(bf16[384,512]{1,0:T(8,128)(2,1)} %grad_out_ref.1) | copy-start | bytes 1179652
  28.1 4.0 %copy-start.4 = (f32[512]{0:T(512)S(1)}, f32[512]{0:T(512)}, u32[]{:S(2)}) copy-start(f32[512]{0:T(512)} %param.14) | copy-start | bytes 6148
  29.7 2.4 %collective-permute-start.6 = (f32[384,512]{1,0:T(8,128)S(1)}, f32[384,512]{1,0:T(8,128)S(1)}, u32[]{:S(2)}, u32[]{:S(2)}) collective-permute-start(f32[384,512]{1,0:T(8,128)S(1)} %shard_map.122), channel_id=1, source_target_pairs={{0,1},{1,0},{2,3},{3,2},{4,5},{5,4},{6,7},{7,6},{8,9},{9,8},{10,11... | collective-permute-start | bytes 2359304 | tf_op jit(solution)/shard_map/ppermute | solution.py:330
  32.1 3.7 %copy-start.5 = (s32[40]{0:T(128)S(1)}, s32[40]{0:T(128)}, u32[]{:S(2)}) copy-start(s32[40]{0:T(128)} %constant.23.refs_1_) | copy-start | bytes 484
  33.5 1.6 %collective-permute-start.7 = (bf16[4,80,512]{2,1,0:T(8,128)(2,1)S(1)}, bf16[4,80,512]{2,1,0:T(8,128)(2,1)S(1)}, u32[]{:S(2)}, u32[]{:S(2)}) collective-permute-start(bf16[4,80,512]{2,1,0:T(8,128)(2,1)S(1)} %get-tuple-element.42), channel_id=1, source_target_pairs={{0,1},{1,0},{2,3},{3,2},{4,5},{5,4},{6,7},{7,6},{8,9},{9,8},{10,11... | collective-permute-start | bytes 983048 | tf_op jit(solution)/shard_map/ppermute | solution.py:330
  33.6 2.2 %collective-permute-start.9 = (bf16[384,512]{1,0:T(8,128)(2,1)S(1)}, bf16[384,512]{1,0:T(8,128)(2,1)S(1)}, u32[]{:S(2)}, u32[]{:S(2)}) collective-permute-start(bf16[384,512]{1,0:T(8,128)(2,1)S(1)} %get-tuple-element.46.refs_3_), channel_id=1, source_target_pairs={{0,1},{1,0},{2,3},{3,2},{4,5},{5,4},{6,7},{7,6},{8,9},{9,8},{10,11... | collective-permute-start | bytes 1179656 | tf_op jit(solution)/shard_map/ppermute | solution.py:330
  35.2 5.4 %collective-permute-start.8 = (bf16[2,80,512]{2,1,0:T(8,128)(2,1)S(1)}, bf16[2,80,512]{2,1,0:T(8,128)(2,1)S(1)}, u32[]{:S(2)}, u32[]{:S(2)}) collective-permute-start(bf16[2,80,512]{2,1,0:T(8,128)(2,1)S(1)} %get-tuple-element.44), channel_id=1, source_target_pairs={{0,4},{1,3},{2,6},{3,1},{4,0},{5,7},{6,2},{7,5},{8,12},{9,11},{10,... | collective-permute-start | bytes 491528 | tf_op jit(solution)/shard_map/ppermute | solution.py:345
  40.6 4.5 %collective-permute-start.10 = (bf16[1,80,512]{2,1,0:T(8,128)(2,1)S(1)}, bf16[1,80,512]{2,1,0:T(8,128)(2,1)S(1)}, u32[]{:S(2)}, u32[]{:S(2)}) collective-permute-start(bf16[1,80,512]{2,1,0:T(8,128)(2,1)S(1)} %get-tuple-element.52), channel_id=1, source_target_pairs={{0,2},{1,5},{2,0},{3,7},{4,6},{5,1},{6,4},{7,3},{8,10},{9,13},{10,... | collective-permute-start | bytes 245768 | tf_op jit(solution)/shard_map/ppermute | solution.py:345
  45.2 13.7 %collective-permute-start.16 = (bf16[384,512]{1,0:T(8,128)(2,1)S(1)}, bf16[384,512]{1,0:T(8,128)(2,1)S(1)}, u32[]{:S(2)}, u32[]{:S(2)}) collective-permute-start(bf16[384,512]{1,0:T(8,128)(2,1)S(1)} %get-tuple-element.63), channel_id=1, source_target_pairs={{0,2},{1,5},{2,0},{3,7},{4,6},{5,1},{6,4},{7,3},{8,10},{9,13},{10,... | collective-permute-start | bytes 1179656 | tf_op jit(solution)/shard_map/ppermute | solution.py:283
  46.7 5.3 %collective-permute-start.11 = (bf16[80,512]{1,0:T(8,128)(2,1)S(1)}, bf16[80,512]{1,0:T(8,128)(2,1)S(1)}, u32[]{:S(2)}, u32[]{:S(2)}) collective-permute-start(bf16[80,512]{1,0:T(8,128)(2,1)S(1)} %shard_map.128.refs_0_), channel_id=1, source_target_pairs={{0,8},{1,9},{2,10},{3,11},{4,12},{5,13},{6,14},{7,15},{8,0},{9,1},... | collective-permute-start | bytes 245768 | tf_op jit(solution)/shard_map/ppermute | solution.py:345
  52.1 6.7 %collective-permute-start.12 = (bf16[80,512]{1,0:T(8,128)(2,1)S(1)}, bf16[80,512]{1,0:T(8,128)(2,1)S(1)}, u32[]{:S(2)}, u32[]{:S(2)}) collective-permute-start(bf16[80,512]{1,0:T(8,128)(2,1)S(1)} %shard_map.129.mine_ref), channel_id=1, source_target_pairs={{0,16},{1,17},{2,18},{3,19},{4,20},{5,21},{6,22},{7,23},{8,24},{9,... | collective-permute-start | bytes 245768 | tf_op jit(solution)/shard_map/ppermute | solution.py:345
  52.5 14.1 %collective-permute-start.14 = (bf16[384,512]{1,0:T(8,128)(2,1)S(1)}, bf16[384,512]{1,0:T(8,128)(2,1)S(1)}, u32[]{:S(2)}, u32[]{:S(2)}) collective-permute-start(bf16[384,512]{1,0:T(8,128)(2,1)S(1)} %get-tuple-element.58), channel_id=1, source_target_pairs={{1,25},{3,27},{9,1},{11,3},{17,9},{19,11},{25,17},{27,19}} | collective-permute-start | bytes 1179656 | tf_op jit(solution)/shard_map/ppermute | solution.py:283
  59.0 11.8 %collective-permute-start.17 = (bf16[384,512]{1,0:T(8,128)(2,1)S(1)}, bf16[384,512]{1,0:T(8,128)(2,1)S(1)}, u32[]{:S(2)}, u32[]{:S(2)}) collective-permute-start(bf16[384,512]{1,0:T(8,128)(2,1)S(1)} %shard_map.133), channel_id=1, source_target_pairs={{0,24},{2,26},{3,11},{4,12},{5,29},{6,14},{8,0},{10,2},{11,19},{12... | collective-permute-start | bytes 1179656 | tf_op jit(solution)/shard_map/ppermute | solution.py:283
  65.5 5.0 %collective-permute-start.13 = (bf16[64,512]{1,0:T(8,128)(2,1)S(1)}, bf16[64,512]{1,0:T(8,128)(2,1)S(1)}, u32[]{:S(2)}, u32[]{:S(2)}) collective-permute-start(bf16[64,512]{1,0:T(8,128)(2,1)S(1)} %get-tuple-element.53.mine_ref), channel_id=1, source_target_pairs={{0,2},{1,5},{2,0},{3,7},{4,6},{5,1},{6,4},{7,3},{8,10},{9,13},{10,... | collective-permute-start | bytes 196616 | tf_op jit(solution)/shard_map/ppermute | solution.py:345
  66.7 9.5 %collective-permute-start.19 = (bf16[384,512]{1,0:T(8,128)(2,1)S(1)}, bf16[384,512]{1,0:T(8,128)(2,1)S(1)}, u32[]{:S(2)}, u32[]{:S(2)}) collective-permute-start(bf16[384,512]{1,0:T(8,128)(2,1)S(1)} %shard_map.131), channel_id=1, source_target_pairs={{0,2},{1,5},{2,0},{3,7},{4,6},{5,1},{6,4},{7,3},{8,10},{9,13},{10,... | collective-permute-start | bytes 1179656 | tf_op jit(solution)/shard_map/ppermute | solution.py:283
  70.4 5.0 %collective-permute-start.15 = (bf16[2,64,512]{2,1,0:T(8,128)(2,1)S(1)}, bf16[2,64,512]{2,1,0:T(8,128)(2,1)S(1)}, u32[]{:S(2)}, u32[]{:S(2)}) collective-permute-start(bf16[2,64,512]{2,1,0:T(8,128)(2,1)S(1)} %shard_map.132.mine_ref), channel_id=1, source_target_pairs={{0,4},{1,3},{2,6},{3,1},{4,0},{5,7},{6,2},{7,5},{8,12},{9,11},{10,... | collective-permute-start | bytes 393224 | tf_op jit(solution)/shard_map/ppermute | solution.py:345
  70.9 8.8 %collective-permute-start.20 = (bf16[384,512]{1,0:T(8,128)(2,1)S(1)}, bf16[384,512]{1,0:T(8,128)(2,1)S(1)}, u32[]{:S(2)}, u32[]{:S(2)}) collective-permute-start(bf16[384,512]{1,0:T(8,128)(2,1)S(1)} %shard_map.134), channel_id=1, source_target_pairs={{0,4},{1,3},{2,6},{3,1},{4,0},{5,7},{6,2},{7,5},{8,12},{9,11},{10,... | collective-permute-start | bytes 1179656 | tf_op jit(solution)/shard_map/ppermute | solution.py:283
  75.5 5.0 %collective-permute-start.18 = (bf16[256,512]{1,0:T(8,128)(2,1)S(1)}, bf16[256,512]{1,0:T(8,128)(2,1)S(1)}, u32[]{:S(2)}, u32[]{:S(2)}) collective-permute-start(bf16[256,512]{1,0:T(8,128)(2,1)S(1)} %shard_map.135.mine_ref), channel_id=1, source_target_pairs={{0,1},{1,0},{2,3},{3,2},{4,5},{5,4},{6,7},{7,6},{8,9},{9,8},{10,11... | collective-permute-start | bytes 786440 | tf_op jit(solution)/shard_map/ppermute | solution.py:330

commit v9 on v8

--- a/solution.py
+++ b/solution.py
@@ -115,28 +115,20 @@
     )
 
 
-def folded(spot, keep, got, last=False):
+def folded(spot, keep, got):
     count, rows, hidden = keep.shape
-    left = count // 2
-
-    def kernel(spot_ref, keep_ref, got_ref, *out_refs):
-        odd = spot_ref[0] % 2
-        first_side, second_side = (spot_ref[0] >> 1) % 2, (spot_ref[0] >> 2) % 2
-        mine = odd * second_side + (1 - odd) * first_side if last else odd * first_side + (1 - odd) * second_side
-        for p in range(left):
-            for ref, side in zip(out_refs, (mine, 1 - mine)):
-                q = side if last else odd * (2 * p + side) + (1 - odd) * (2 * side + p)
-                ref[p] = (keep_ref[q] + got_ref[q].astype(F32)).astype(ref.dtype)
-
-    shape = (left, rows, hidden)
-    return call(kernel, [(shape, F32), (shape, BF16)], [spot, keep, got], smem=1)
-
-
-def rounded_sum(keep, got):
-    def kernel(keep_ref, got_ref, out_ref):
-        out_ref[...] = (keep_ref[0] + got_ref[0].astype(F32)).astype(BF16)
-
-    return call(kernel, [(keep.shape[1:], BF16)], [keep, got])[0]
+
+    def kernel(spot_ref, keep_ref, got_ref, own_ref, *out_refs):
+        for other in range(count):
+            q = (spot_ref[0] >> 1) ^ other
+            value = keep_ref[q] + got_ref[q].astype(F32)
+            if other == 0:
+                own_ref[...] = value
+            else:
+                out_refs[other - 1][...] = value.astype(BF16)
+
+    shape = (rows, hidden)
+    return call(kernel, [(shape, F32)] + [(shape, BF16)] * (count - 1), [spot, keep, got], smem=1)
 
 
 def summed_terms(spot, terms, masks=None):
@@ -154,23 +146,16 @@
     return call(kernel, [(terms[0].shape, BF16)], [spot, *terms], smem=1)[0]
 
 
-def joined_pieces(spot, mine, other, last=False):
-    rows, hidden = mine.shape[-2:]
-
-    def kernel(spot_ref, mine_ref, other_ref, out_ref):
-        odd = spot_ref[0] % 2
-        first_side, second_side = (spot_ref[0] >> 1) % 2, (spot_ref[0] >> 2) % 2
-        own = odd * first_side + (1 - odd) * second_side if last else odd * second_side + (1 - odd) * first_side
-        for ref, side in ((mine_ref, own), (other_ref, 1 - own)):
-            if not last:
-                out_ref[side] = ref[...]
-                continue
-            for p in range(2):
-                q = odd * (2 * p + side) + (1 - odd) * (2 * side + p)
-                out_ref[pl.ds(pl.multiple_of(q * rows, rows), rows)] = ref[p]
-
-    shape = (4 * rows, hidden) if last else (2, rows, hidden)
-    return call(kernel, [(shape, BF16)], [spot, mine, other], smem=1)[0]
+def joined_pieces(spot, pieces):
+    rows, hidden = pieces[0].shape
+    count = len(pieces)
+
+    def kernel(spot_ref, *refs):
+        for other, ref in enumerate(refs[:-1]):
+            q = (spot_ref[0] >> 1) ^ other
+            refs[-1][pl.ds(pl.multiple_of(q * rows, rows), rows)] = ref[...]
+
+    return call(kernel, [((count * rows, hidden), BF16)], [spot, *pieces], smem=1)[0]
 
 
 def whole_weight(spot, mine, other):
@@ -184,15 +169,18 @@
     return call(kernel, [((2 * rows, hidden), F32)], [spot, mine, other], smem=1)[0]
 
 
-def finished(mine, other, piece):
-    hidden = mine.shape[1]
-
-    def kernel(mine_ref, other_ref, weight_ref, bias_ref):
-        total = mine_ref[...].astype(F32) + other_ref[...].astype(F32)
-        weight_ref[...] = total[:piece].astype(BF16)
-        bias_ref[...] = total[piece : piece + 8]
-
-    return call(kernel, [((piece, hidden), BF16), ((8, hidden), F32)], [mine, other])
+def finished(values, piece):
+    hidden = values[0].shape[1]
+
+    def kernel(*refs):
+        parts = [ref[...].astype(F32) for ref in refs[:-2]]
+        while len(parts) > 1:
+            parts = [parts[k] + parts[k + 1] for k in range(0, len(parts), 2)]
+        refs[-2][...] = parts[0][:piece].astype(BF16)
+        refs[-1][...] = parts[0][piece:]
+
+    rows = values[0].shape[0]
+    return call(kernel, [((piece, hidden), BF16), ((rows - piece, hidden), F32)], list(values))
 
 
 def scattered_sums(flipped, own, mate, columns, dtypes, spot=None, lookup=None):
@@ -265,7 +253,7 @@
         ]
         return terms[:1]
 
-    def finish(self):
+    def finish(self, token):
         return summed_terms(self.spot, self.arriving)
 
 
@@ -286,34 +274,32 @@
         x = {spot: (spot ^ 2) - spot for spot in range(8)}
         y = {spot: (spot ^ 4) - spot for spot in range(8)}
         straight = {spot: (y if spot % 2 else x)[spot] for spot in range(8)}
-        across = {spot: (x if spot % 2 else y)[spot] for spot in range(8)}
+        self.across = {spot: (x if spot % 2 else y)[spot] for spot in range(8)}
         take = lambda mate, *args: scattered_sums(self.flipped, self.own, mate, *args, self.spot, self.LOOKUP)
         if k == 0:
             _, mate = after(token, self.mate)
             self.to_last, self.to_plane, self.plane_rest = take(mate, (4, 3), [[BF16], [BF16, F32]])
             self.kept, self.to_across, self.to_straight = take(mate, (0, 1, 2), [[F32]] * 3)
-            return [self.to_last, self.kept]
-        if k == 2:
-            _, to_last, to_plane = after(token, self.to_last, self.to_plane)
+            self.from_plane = self.routed(self.to_plane, {1: -8, 3: -8})
+            return [self.to_last, self.kept, self.from_plane]
+        if k == 1:
+            _, to_last, rest = after(token, self.to_last, self.to_straight)
             self.from_last = self.routed(to_last, straight)
-            self.from_plane = self.routed(to_plane, {1: -8, 3: -8})
-        if k == 4:
-            _, rest, plane_rest = after(token, self.to_straight, self.plane_rest)
-            out = summed_terms(self.spot, [plane_rest, self.from_last], [self.EVEN, self.MIDDLE])
-            self.from_planes = self.routed(out, {0: -8, 2: -8, 4: 8, 6: 8, 5: -8, 3: 8})
             second = summed_terms(self.spot, [rest, self.from_plane], [None, self.ODD_LOW])
             self.second = self.routed(second, straight)
             return [second]
-        if k == 5:
-            _, rest = after(token, self.to_across)
-            out = summed_terms(
-                self.spot,
-                [rest, self.from_planes, self.from_last],
-                [None, self.EVEN | 0b00101000, self.ENDS],
-            )
-            self.arriving = [self.kept, self.second, self.routed(out, across)]
-            return [out]
+        if k == 2:
+            _, plane_rest = after(token, self.plane_rest)
+            out = summed_terms(self.spot, [plane_rest, self.from_last], [self.EVEN, self.MIDDLE])
+            self.from_planes = self.routed(out, {0: -8, 2: -8, 4: 8, 6: 8, 5: -8, 3: 8})
         return []
+
+    def finish(self, token):
+        _, rest = after(token, self.to_across)
+        out = summed_terms(
+            self.spot, [rest, self.from_planes, self.from_last], [None, self.EVEN | 0b00101000, self.ENDS]
+        )
+        return summed_terms(self.spot, [self.kept, self.second, self.routed(out, self.across)])
 
 
 def local(features, tile_list, tile_count, tile_values, weight, bias, grad_out):
@@ -340,25 +326,24 @@
     mate_grad, got = swapped(grad_agg, 1), swapped(give, 1)
     route.scatter(flipped, grad_agg, mate_grad)
 
-    def exchanged(k, value, even, odd):
-        pairs = [(s, s ^ (odd if s % 2 else even)) for s in range(count)]
-        other = lax.ppermute(value, "blk", pairs)
-        return after(other, *route.step(k, value))[0]
-
-    keep, give = folded(spot, keep, got)
-    keep, give = folded(spot, keep, exchanged(0, give, 4, 2), last=True)
-    total = rounded_sum(keep, exchanged(1, give, 2, 4))
-    step, k = pieces, 2
+    def exchanged(k, values, distances):
+        others = [swapped(value, distance) for value, distance in zip(values, distances)]
+        return after(others, *route.step(k, values[0]))[0]
+
+    in_plane = [2 * d for d in range(1, pieces // 2)]
+    own, *give = folded(spot, keep, got)
+    total = summed_terms(spot, [own, *exchanged(0, give, in_plane)])
+    step, k = pieces, 1
     while step < count:
-        other = exchanged(k, total, step, step)
-        step, k = 2 * step, k + 1
+        group = min(4, count // step)
+        across = [step * d for d in range(1, group)]
+        values = [total, *exchanged(k, [total] * (group - 1), across)]
+        step, k = step * group, k + 1
         if step < count:
-            total = summed_terms(spot, [total, other])
-        else:
-            total, bias_sum = finished(total, other, hidden // pieces)
-    pair = joined_pieces(spot, total, exchanged(4, total, 2, 4))
-    half = joined_pieces(spot, pair, exchanged(5, pair, 4, 2), last=True)
-    grad_features = route.finish()
+            total = summed_terms(spot, values)
+    total, bias_sum = finished(values, hidden // pieces)
+    half = joined_pieces(spot, [total, *exchanged(k, [total] * len(in_plane), in_plane)])
+    grad_features = route.finish(half)
     mate_half, grad_features = after(swapped(half, 1), grad_features)
     return (output, grad_features, whole_weight(spot, half, mate_half), bias_sum[0])
 

time: 81.9 us -> 80.1 us (0.978)
  waiting for transfers between devices: 36.2 us -> 29 us
  starting transfers between devices: 27.4 us -> 32.6 us
    ppermute x6 -> x0, waiting for transfers between devices: 20.3 us -> none  [exchanged(): other = lax.ppermute(value, 'blk', pairs)]
    ppermute x6 -> x15, waiting for transfers between devices: 4.5 us -> 16.4 us  [swapped(): return lax.ppermute(value, 'blk', [(s, s ^ distance) for s in range(count)])]
    ppermute x6 -> x15, starting transfers between devices: 1.18 us -> 12.6 us  [swapped(): return lax.ppermute(value, 'blk', [(s, s ^ distance) for s in range(count)])]
    ppermute x6 -> x0, starting transfers between devices: 4.11 us -> none  [exchanged(): other = lax.ppermute(value, 'blk', pairs)]
    ppermute x5, starting transfers between devices: 11.6 us -> 9.52 us  [routed(): return lax.ppermute(value, 'blk', pairs)]
    ppermute x5, waiting for transfers between devices: 3.73 us -> 5.18 us  [routed(): return lax.ppermute(value, 'blk', pairs)]
    pallas_call x18 -> x15, Pallas kernels: 13.5 us -> 13.7 us  [call(): pl.pallas_call(kernel, out_shape=out_shape, in_specs=[spec(k) for k in ra...]
  transfers between devices with their start and end apart: 21 -> 24, of which waited for: 14 -> 14; matrix products, arithmetic and copies ran while one was open for 3% -> 3% of each run, Pallas kernels for 13% -> 12%
where the time goes in v9:
time: 80.1 us; the launch traced here: 79.8 us
  starting transfers between devices  32.6 us (41%)
  waiting for transfers between devices  29 us (36%)
  Pallas kernels  13.7 us (17%)
  local copies, waits for them, and re-layouts  2.98 us (4%)
  between operations  0.85 us (1%)
    ppermute x15, waiting for transfers between devices, swapped(): return lax.ppermute(value, 'blk', [(s, s ^ distance) for s in range(count)])  16.4 us
    pallas_call x15, Pallas kernels, call(): pl.pallas_call(kernel, out_shape=out_shape, in_specs=[spec(k) for k in ra...  13.7 us
    ppermute x15, starting transfers between devices, swapped(): return lax.ppermute(value, 'blk', [(s, s ^ distance) for s in range(count)])  12.6 us
    ppermute x4, starting transfers between devices, sent(): return lax.ppermute(value, 'blk', pairs)  10.5 us
    ppermute x5, starting transfers between devices, routed(): return lax.ppermute(value, 'blk', pairs)  9.52 us
    ppermute x4, waiting for transfers between devices, sent(): return lax.ppermute(value, 'blk', pairs)  7.36 us
    ppermute x5, waiting for transfers between devices, routed(): return lax.ppermute(value, 'blk', pairs)  5.18 us
  transfers between devices with their start and end apart: 24, of which 14 were waited for; matrix products, arithmetic and copies ran while one was open for 3% of the time, Pallas kernels for 12%

profile of v9, /device:TPU:0, one launch (start us, length us, event | category | flops | bytes accessed | tf_op | source)
XLA Modules:
  0.0 79.8 jit_solution(13162656450575472363)
XLA Ops:
  1.1 2.6 %collective-permute-start.2 = (bf16[384,512]{1,0:T(8,128)(2,1)}, bf16[384,512]{1,0:T(8,128)(2,1)S(1)}, u32[]{:S(2)}, u32[]{:S(2)}) collective-permute-start(bf16[384,512]{1,0:T(8,128)(2,1)} %refs_2_.1), channel_id=1, source_target_pairs={{0,4},{1,5},{2,6},{3,7},{4,8},{5,9},{6,10},{7,11},{8,12},{9,13},{1... | collective-permute-start | bytes 1179656 | tf_op jit(solution)/shard_map/ppermute | solution.py:224
  3.7 1.5 %collective-permute-start.3 = (bf16[384,512]{1,0:T(8,128)(2,1)}, bf16[384,512]{1,0:T(8,128)(2,1)S(1)}, u32[]{:S(2)}, u32[]{:S(2)}) collective-permute-start(bf16[384,512]{1,0:T(8,128)(2,1)} %refs_2_.1), channel_id=1, source_target_pairs={{0,2},{1,3},{2,4},{3,5},{4,6},{5,7},{6,8},{7,9},{8,10},{9,11},{10,... | collective-permute-start | bytes 1179656 | tf_op jit(solution)/shard_map/ppermute | solution.py:224
  5.2 4.1 %collective-permute-start.4 = (bf16[384,512]{1,0:T(8,128)(2,1)}, bf16[384,512]{1,0:T(8,128)(2,1)S(1)}, u32[]{:S(2)}, u32[]{:S(2)}) collective-permute-start(bf16[384,512]{1,0:T(8,128)(2,1)} %refs_2_.1), channel_id=1, source_target_pairs={{0,30},{1,31},{2,0},{3,1},{4,2},{5,3},{6,4},{7,5},{8,6},{9,7},{10,... | collective-permute-start | bytes 1179656 | tf_op jit(solution)/shard_map/ppermute | solution.py:224
  9.4 2.3 %collective-permute-start.5 = (bf16[384,512]{1,0:T(8,128)(2,1)}, bf16[384,512]{1,0:T(8,128)(2,1)S(1)}, u32[]{:S(2)}, u32[]{:S(2)}) collective-permute-start(bf16[384,512]{1,0:T(8,128)(2,1)} %refs_2_.1), channel_id=1, source_target_pairs={{0,28},{2,30},{4,0},{6,2},{8,4},{10,6},{12,8},{14,10},{16,12},{18,... | collective-permute-start | bytes 1179656 | tf_op jit(solution)/shard_map/ppermute | solution.py:224
  13.3 1.1 %collective-permute-done.1.mate_meta_ref = s32[120]{0:T(128)S(1)} collective-permute-done((s32[120]{0:T(128)S(1)}, s32[120]{0:T(128)S(1)}, u32[]{:S(2)}, u32[]{:S(2)}) %collective-permute-start.1) | collective-permute-done | bytes 512 | tf_op jit(solution)/shard_map/ppermute | solution.py:316
  14.4 1.5 %copy-done = bf16[1,8,7,128,128]{4,3,2,1,0:T(8,128)(2,1)S(1)} copy-done((bf16[1,8,7,128,128]{4,3,2,1,0:T(8,128)(2,1)S(1)}, bf16[1,8,7,128,128]{4,3,2,1,0:T(8,128)(2,1)}, u32[]{:S(2)}) %copy-start) | copy-done | bytes 1835032
  15.9 4.3 %shard_map.120 = (bf16[768,1920]{1,0:T(8,128)(2,1)S(1)}, bf16[1920,768]{1,0:T(8,128)(2,1)S(1)}) custom-call(s32[1]{0:T(128)} %bitcast.spot_ref.refs_0_, s32[120]{0:T(128)S(1)} %reshape.24.own_meta_ref, s32[120]{0:T(128)S(1)} %collective-permute-done.1.mate_meta_ref, bf16[8,7,128,128]{3,2,1,0:T(8,128)(2,1)S(1)} %bitcast.8, ...), custom_call_target="tpu_custom_call" | custom-call | tf_op jit(solution)/shard_map/pallas_call | solution.py:16
  20.2 5.5 %collective-permute-done.2.refs_0_ = bf16[384,512]{1,0:T(8,128)(2,1)S(1)} collective-permute-done((bf16[384,512]{1,0:T(8,128)(2,1)}, bf16[384,512]{1,0:T(8,128)(2,1)S(1)}, u32[]{:S(2)}, u32[]{:S(2)}) %collective-permute-start.2) | collective-permute-done | bytes 393248 | tf_op jit(solution)/shard_map/ppermute | solution.py:224
  26.3 1.8 %shard_map.121.refs_0_.own_ref = f32[768,512]{1,0:T(8,128)S(1)} custom-call(bf16[768,1920]{1,0:T(8,128)(2,1)S(1)} %get-tuple-element.44.dense_ref, bf16[384,512]{1,0:T(8,128)(2,1)S(1)} %collective-permute-done.2.refs_0_, bf16[384,512]{1,0:T(8,128)(2,1)S(1)} %collective-permute-done.3.refs_1_, bf16[384,512]{1,0:T(8,128)(2,1)S(1)} %copy-done.2, ...), custom_call_target="tpu_custom_call" | custom-call | tf_op jit(solution)/shard_map/pallas_call | solution.py:16
  28.1 1.2 %collective-permute-done.5.refs_1_ = bf16[384,512]{1,0:T(8,128)(2,1)S(1)} collective-permute-done((bf16[384,512]{1,0:T(8,128)(2,1)}, bf16[384,512]{1,0:T(8,128)(2,1)S(1)}, u32[]{:S(2)}, u32[]{:S(2)}) %collective-permute-start.5) | collective-permute-done | bytes 393248 | tf_op jit(solution)/shard_map/ppermute | solution.py:224
  29.8 2.3 %collective-permute-done.6.mate_ref = f32[384,512]{1,0:T(8,128)S(1)} collective-permute-done((f32[384,512]{1,0:T(8,128)S(1)}, f32[384,512]{1,0:T(8,128)S(1)}, u32[]{:S(2)}, u32[]{:S(2)}) %collective-permute-start.6) | collective-permute-done | bytes 786464 | tf_op jit(solution)/shard_map/ppermute | solution.py:316
  32.1 1.4 %shard_map.123 = (bf16[384,512]{1,0:T(8,128)(2,1)}, bf16[384,512]{1,0:T(8,128)(2,1)S(1)}, f32[4,80,512]{2,1,0:T(8,128)S(1)}, bf16[4,80,512]{2,1,0:T(8,128)(2,1)S(1)}) custom-call(s32[1]{0:T(128)} %bitcast.spot_ref.refs_0_, f32[768,512]{1,0:T(8,128)S(1)} %shard_map.121.refs_0_.own_ref, f32[384,512]{1,0:T(8,128)S(1)} %collective-permute-done.6.mate_ref, ...), custom_call_target="tpu_custom_call" | custom-call | tf_op jit(solution)/shard_map/pallas_call | solution.py:16
  34.0 1.7 %collective-permute-done.7.got_ref = bf16[4,80,512]{2,1,0:T(8,128)(2,1)S(1)} collective-permute-done((bf16[4,80,512]{2,1,0:T(8,128)(2,1)S(1)}, bf16[4,80,512]{2,1,0:T(8,128)(2,1)S(1)}, u32[]{:S(2)}, u32[]{:S(2)}) %collective-permute-start.7) | collective-permute-done | bytes 327712 | tf_op jit(solution)/shard_map/ppermute | solution.py:316
  35.8 1.5 %shard_map.125 = (bf16[384,512]{1,0:T(8,128)(2,1)S(1)}, bf16[384,512]{1,0:T(8,128)(2,1)S(1)}, f32[384,512]{1,0:T(8,128)S(1)}) custom-call(s32[1]{0:T(128)} %bitcast.spot_ref.refs_0_, s32[40]{0:T(128)S(1)} %copy-done.5, bf16[1920,768]{1,0:T(8,128)(2,1)S(1)} %get-tuple-element.52.refs_2_, bf16[384,512]{1,0:T(8,128)(2,1)S(1)} %get-tuple-element.53.refs_3_, ...), custom_call_target="tpu_custom_call" | custom-call | tf_op jit(solution)/shard_map/pallas_call | solution.py:16
  38.0 1.6 %collective-permute-start.8 = (bf16[80,512]{1,0:T(8,128)(2,1)S(1)}, bf16[80,512]{1,0:T(8,128)(2,1)S(1)}, u32[]{:S(2)}, u32[]{:S(2)}) collective-permute-start(bf16[80,512]{1,0:T(8,128)(2,1)S(1)} %get-tuple-element.49), channel_id=1, source_target_pairs={{0,2},{1,3},{2,0},{3,1},{4,6},{5,7},{6,4},{7,5},{8,10},{9,11},{10,... | collective-permute-start | bytes 245768 | tf_op jit(solution)/shard_map/ppermute | solution.py:316
  40.0 1.5 %collective-permute-start.9 = (bf16[80,512]{1,0:T(8,128)(2,1)S(1)}, bf16[80,512]{1,0:T(8,128)(2,1)S(1)}, u32[]{:S(2)}, u32[]{:S(2)}) collective-permute-start(bf16[80,512]{1,0:T(8,128)(2,1)S(1)} %get-tuple-element.50), channel_id=1, source_target_pairs={{0,4},{1,5},{2,6},{3,7},{4,0},{5,1},{6,2},{7,3},{8,12},{9,13},{10,... | collective-permute-start | bytes 245768 | tf_op jit(solution)/shard_map/ppermute | solution.py:316
  41.5 1.9 %shard_map.126 = (f32[384,512]{1,0:T(8,128)S(1)}, f32[384,512]{1,0:T(8,128)S(1)}, f32[384,512]{1,0:T(8,128)S(1)}) custom-call(s32[1]{0:T(128)} %bitcast.spot_ref.refs_0_, s32[40]{0:T(128)S(1)} %copy-done.5, bf16[1920,768]{1,0:T(8,128)(2,1)S(1)} %get-tuple-element.52.refs_2_, bf16[384,512]{1,0:T(8,128)(2,1)S(1)} %get-tuple-element.53.refs_3_, ...), custom_call_target="tpu_custom_call" | custom-call | tf_op jit(solution)/shard_map/pallas_call | solution.py:16
  43.4 1.5 %collective-permute-done.10.refs_3_ = bf16[80,512]{1,0:T(8,128)(2,1)S(1)} collective-permute-done((bf16[80,512]{1,0:T(8,128)(2,1)S(1)}, bf16[80,512]{1,0:T(8,128)(2,1)S(1)}, u32[]{:S(2)}, u32[]{:S(2)}) %collective-permute-start.10) | collective-permute-done | bytes 81952 | tf_op jit(solution)/shard_map/ppermute | solution.py:316
  45.0 1.6 %collective-permute-done.9.refs_2_ = bf16[80,512]{1,0:T(8,128)(2,1)S(1)} collective-permute-done((bf16[80,512]{1,0:T(8,128)(2,1)S(1)}, bf16[80,512]{1,0:T(8,128)(2,1)S(1)}, u32[]{:S(2)}, u32[]{:S(2)}) %collective-permute-start.9) | collective-permute-done | bytes 81952 | tf_op jit(solution)/shard_map/ppermute | solution.py:316
  47.4 1.8 %collective-permute-start.13 = (bf16[80,512]{1,0:T(8,128)(2,1)S(1)}, bf16[80,512]{1,0:T(8,128)(2,1)S(1)}, u32[]{:S(2)}, u32[]{:S(2)}) collective-permute-start(bf16[80,512]{1,0:T(8,128)(2,1)S(1)} %shard_map.127.refs_0_), channel_id=1, source_target_pairs={{0,8},{1,9},{2,10},{3,11},{4,12},{5,13},{6,14},{7,15},{8,0},{9,1},... | collective-permute-start | bytes 245768 | tf_op jit(solution)/shard_map/ppermute | solution.py:316
  49.2 2.0 %collective-permute-start.14 = (bf16[80,512]{1,0:T(8,128)(2,1)S(1)}, bf16[80,512]{1,0:T(8,128)(2,1)S(1)}, u32[]{:S(2)}, u32[]{:S(2)}) collective-permute-start(bf16[80,512]{1,0:T(8,128)(2,1)S(1)} %shard_map.127.refs_0_), channel_id=1, source_target_pairs={{0,16},{1,17},{2,18},{3,19},{4,20},{5,21},{6,22},{7,23},{8,24},{9,... | collective-permute-start | bytes 245768 | tf_op jit(solution)/shard_map/ppermute | solution.py:316
  51.9 1.2 %collective-permute-done.13.refs_1_ = bf16[80,512]{1,0:T(8,128)(2,1)S(1)} collective-permute-done((bf16[80,512]{1,0:T(8,128)(2,1)S(1)}, bf16[80,512]{1,0:T(8,128)(2,1)S(1)}, u32[]{:S(2)}, u32[]{:S(2)}) %collective-permute-start.13) | collective-permute-done | bytes 81952 | tf_op jit(solution)/shard_map/ppermute | solution.py:316
  53.1 4.7 %collective-permute-done.14.refs_2_ = bf16[80,512]{1,0:T(8,128)(2,1)S(1)} collective-permute-done((bf16[80,512]{1,0:T(8,128)(2,1)S(1)}, bf16[80,512]{1,0:T(8,128)(2,1)S(1)}, u32[]{:S(2)}, u32[]{:S(2)}) %collective-permute-start.14) | collective-permute-done | bytes 81952 | tf_op jit(solution)/shard_map/ppermute | solution.py:316
  58.0 4.0 %collective-permute-start.22 = (bf16[384,512]{1,0:T(8,128)(2,1)S(1)}, bf16[384,512]{1,0:T(8,128)(2,1)S(1)}, u32[]{:S(2)}, u32[]{:S(2)}) collective-permute-start(bf16[384,512]{1,0:T(8,128)(2,1)S(1)} %shard_map.131), channel_id=1, source_target_pairs={{0,24},{2,26},{3,11},{4,12},{5,29},{6,14},{8,0},{10,2},{11,19},{12... | collective-permute-start | bytes 1179656 | tf_op jit(solution)/shard_map/ppermute | solution.py:271
  62.0 1.5 %collective-permute-start.16 = (bf16[64,512]{1,0:T(8,128)(2,1)S(1)}, bf16[64,512]{1,0:T(8,128)(2,1)S(1)}, u32[]{:S(2)}, u32[]{:S(2)}) collective-permute-start(bf16[64,512]{1,0:T(8,128)(2,1)S(1)} %get-tuple-element.66.refs_0_), channel_id=1, source_target_pairs={{0,2},{1,3},{2,0},{3,1},{4,6},{5,7},{6,4},{7,5},{8,10},{9,11},{10,... | collective-permute-start | bytes 196616 | tf_op jit(solution)/shard_map/ppermute | solution.py:316
  64.0 1.5 %collective-permute-start.18 = (bf16[64,512]{1,0:T(8,128)(2,1)S(1)}, bf16[64,512]{1,0:T(8,128)(2,1)S(1)}, u32[]{:S(2)}, u32[]{:S(2)}) collective-permute-start(bf16[64,512]{1,0:T(8,128)(2,1)S(1)} %get-tuple-element.66.refs_0_), channel_id=1, source_target_pairs={{0,6},{1,7},{2,4},{3,5},{4,2},{5,3},{6,0},{7,1},{8,14},{9,15},{10,... | collective-permute-start | bytes 196616 | tf_op jit(solution)/shard_map/ppermute | solution.py:316
  65.5 1.5 %collective-permute-start.20 = (bf16[384,512]{1,0:T(8,128)(2,1)S(1)}, bf16[384,512]{1,0:T(8,128)(2,1)S(1)}, u32[]{:S(2)}, u32[]{:S(2)}) collective-permute-start(bf16[384,512]{1,0:T(8,128)(2,1)S(1)} %shard_map.128), channel_id=1, source_target_pairs={{0,2},{1,5},{2,0},{3,7},{4,6},{5,1},{6,4},{7,3},{8,10},{9,13},{10,... | collective-permute-start | bytes 1179656 | tf_op jit(solution)/shard_map/ppermute | solution.py:271
  67.0 1.5 %collective-permute-done.17.refs_2_ = bf16[64,512]{1,0:T(8,128)(2,1)S(1)} collective-permute-done((bf16[64,512]{1,0:T(8,128)(2,1)S(1)}, bf16[64,512]{1,0:T(8,128)(2,1)S(1)}, u32[]{:S(2)}, u32[]{:S(2)}) %collective-permute-start.17) | collective-permute-done | bytes 65568 | tf_op jit(solution)/shard_map/ppermute | solution.py:316
  69.5 2.7 %collective-permute-start.23 = (bf16[384,512]{1,0:T(8,128)(2,1)S(1)}, bf16[384,512]{1,0:T(8,128)(2,1)S(1)}, u32[]{:S(2)}, u32[]{:S(2)}) collective-permute-start(bf16[384,512]{1,0:T(8,128)(2,1)S(1)} %shard_map.132), channel_id=1, source_target_pairs={{0,4},{1,3},{2,6},{3,1},{4,0},{5,7},{6,2},{7,5},{8,12},{9,11},{10,... | collective-permute-start | bytes 1179656 | tf_op jit(solution)/shard_map/ppermute | solution.py:271
  72.7 4.4 %collective-permute-done.20.refs_1_ = bf16[384,512]{1,0:T(8,128)(2,1)S(1)} collective-permute-done((bf16[384,512]{1,0:T(8,128)(2,1)S(1)}, bf16[384,512]{1,0:T(8,128)(2,1)S(1)}, u32[]{:S(2)}, u32[]{:S(2)}) %collective-permute-start.20) | collective-permute-done | bytes 393248 | tf_op jit(solution)/shard_map/ppermute | solution.py:271
  77.9 0.9 %shard_map.133 = bf16[384,512]{1,0:T(8,128)(2,1)} custom-call(s32[1]{0:T(128)} %bitcast.spot_ref.refs_0_, f32[384,512]{1,0:T(8,128)S(1)} %get-tuple-element.56.refs_0_, bf16[384,512]{1,0:T(8,128)(2,1)S(1)} %collective-permute-done.20.refs_1_, bf16[384,512]{1,0:T(8,128)(2,1)S(1)} %collective-permute-done.23.refs_2_), custom_call_target="tpu_custom_call" | custom-call | tf_op jit(solution)/shard_map/pallas_call | solution.py:16
  78.8 1.0 %shard_map.134 = f32[512,512]{1,0:T(8,128)} custom-call(s32[1]{0:T(128)} %bitcast.spot_ref.refs_0_, bf16[256,512]{1,0:T(8,128)(2,1)S(1)} %shard_map.130.mine_ref, bf16[256,512]{1,0:T(8,128)(2,1)S(1)} %collective-permute-done.19.other_ref), custom_call_target="tpu_custom_call" | custom-call | tf_op jit(solution)/shard_map/pallas_call | solution.py:16
  (48 shorter events, 9.3 us)
Async XLA Ops:
  0.6 11.1 %collective-permute-start = (bf16[8,7,128,128]{3,2,1,0:T(8,128)(2,1)}, bf16[8,7,128,128]{3,2,1,0:T(8,128)(2,1)S(1)}, u32[]{:S(2)}, u32[]{:S(2)}) collective-permute-start(bf16[8,7,128,128]{3,2,1,0:T(8,128)(2,1)} %bitcast.7), channel_id=1, source_target_pairs={{0,1},{1,0},{2,3},{3,2},{4,5},{5,4},{6,7},{7,6},{8,9},{9,8},{10,11... | collective-permute-start | bytes 5505032 | tf_op jit(solution)/shard_map/ppermute | solution.py:316
  1.1 24.5 %collective-permute-start.2 = (bf16[384,512]{1,0:T(8,128)(2,1)}, bf16[384,512]{1,0:T(8,128)(2,1)S(1)}, u32[]{:S(2)}, u32[]{:S(2)}) collective-permute-start(bf16[384,512]{1,0:T(8,128)(2,1)} %refs_2_.1), channel_id=1, source_target_pairs={{0,4},{1,5},{2,6},{3,7},{4,8},{5,9},{6,10},{7,11},{8,12},{9,13},{1... | collective-permute-start | bytes 1179656 | tf_op jit(solution)/shard_map/ppermute | solution.py:224
  3.7 22.5 %collective-permute-start.3 = (bf16[384,512]{1,0:T(8,128)(2,1)}, bf16[384,512]{1,0:T(8,128)(2,1)S(1)}, u32[]{:S(2)}, u32[]{:S(2)}) collective-permute-start(bf16[384,512]{1,0:T(8,128)(2,1)} %refs_2_.1), channel_id=1, source_target_pairs={{0,2},{1,3},{2,4},{3,5},{4,6},{5,7},{6,8},{7,9},{8,10},{9,11},{10,... | collective-permute-start | bytes 1179656 | tf_op jit(solution)/shard_map/ppermute | solution.py:224
  5.2 21.1 %collective-permute-start.4 = (bf16[384,512]{1,0:T(8,128)(2,1)}, bf16[384,512]{1,0:T(8,128)(2,1)S(1)}, u32[]{:S(2)}, u32[]{:S(2)}) collective-permute-start(bf16[384,512]{1,0:T(8,128)(2,1)} %refs_2_.1), channel_id=1, source_target_pairs={{0,30},{1,31},{2,0},{3,1},{4,2},{5,3},{6,4},{7,5},{8,6},{9,7},{10,... | collective-permute-start | bytes 1179656 | tf_op jit(solution)/shard_map/ppermute | solution.py:224
  9.4 20.0 %collective-permute-start.5 = (bf16[384,512]{1,0:T(8,128)(2,1)}, bf16[384,512]{1,0:T(8,128)(2,1)S(1)}, u32[]{:S(2)}, u32[]{:S(2)}) collective-permute-start(bf16[384,512]{1,0:T(8,128)(2,1)} %refs_2_.1), channel_id=1, source_target_pairs={{0,28},{2,30},{4,0},{6,2},{8,4},{10,6},{12,8},{14,10},{16,12},{18,... | collective-permute-start | bytes 1179656 | tf_op jit(solution)/shard_map/ppermute | solution.py:224
  13.2 1.1 %collective-permute-start.1 = (s32[120]{0:T(128)S(1)}, s32[120]{0:T(128)S(1)}, u32[]{:S(2)}, u32[]{:S(2)}) collective-permute-start(s32[120]{0:T(128)S(1)} %reshape.24.own_meta_ref), channel_id=1, source_target_pairs={{0,1},{1,0},{2,3},{3,2},{4,5},{5,4},{6,7},{7,6},{8,9},{9,8},{10,11... | collective-permute-start | bytes 1448 | tf_op jit(solution)/shard_map/ppermute | solution.py:316
  14.4 1.5 %copy-start = (bf16[1,8,7,128,128]{4,3,2,1,0:T(8,128)(2,1)S(1)}, bf16[1,8,7,128,128]{4,3,2,1,0:T(8,128)(2,1)}, u32[]{:S(2)}) copy-start(bf16[1,8,7,128,128]{4,3,2,1,0:T(8,128)(2,1)} %param.12) | copy-start | bytes 5505028
  15.9 10.4 %copy-start.2 = (bf16[384,512]{1,0:T(8,128)(2,1)S(1)}, bf16[384,512]{1,0:T(8,128)(2,1)}, u32[]{:S(2)}) copy-start(bf16[384,512]{1,0:T(8,128)(2,1)} %refs_2_.1) | copy-start | bytes 1179652
  28.1 4.0 %copy-start.1 = (bf16[512,512]{1,0:T(8,128)(2,1)S(1)}, bf16[512,512]{1,0:T(8,128)(2,1)}, u32[]{:S(2)}) copy-start(bf16[512,512]{1,0:T(8,128)(2,1)} %weight_ref.1) | copy-start | bytes 1572868
  28.1 4.0 %copy-start.3 = (bf16[384,512]{1,0:T(8,128)(2,1)S(1)}, bf16[384,512]{1,0:T(8,128)(2,1)}, u32[]{:S(2)}) copy-start(bf16[384,512]{1,0:T(8,128)(2,1)} %grad_out_ref.1) | copy-start | bytes 1179652
  28.1 4.0 %copy-start.4 = (f32[512]{0:T(512)S(1)}, f32[512]{0:T(512)}, u32[]{:S(2)}) copy-start(f32[512]{0:T(512)} %param.14) | copy-start | bytes 6148
  29.7 2.4 %collective-permute-start.6 = (f32[384,512]{1,0:T(8,128)S(1)}, f32[384,512]{1,0:T(8,128)S(1)}, u32[]{:S(2)}, u32[]{:S(2)}) collective-permute-start(f32[384,512]{1,0:T(8,128)S(1)} %shard_map.122), channel_id=1, source_target_pairs={{0,1},{1,0},{2,3},{3,2},{4,5},{5,4},{6,7},{7,6},{8,9},{9,8},{10,11... | collective-permute-start | bytes 2359304 | tf_op jit(solution)/shard_map/ppermute | solution.py:316
  32.1 3.7 %copy-start.5 = (s32[40]{0:T(128)S(1)}, s32[40]{0:T(128)}, u32[]{:S(2)}) copy-start(s32[40]{0:T(128)} %constant.23.refs_1_) | copy-start | bytes 484
  33.5 2.3 %collective-permute-start.11 = (bf16[384,512]{1,0:T(8,128)(2,1)S(1)}, bf16[384,512]{1,0:T(8,128)(2,1)S(1)}, u32[]{:S(2)}, u32[]{:S(2)}) collective-permute-start(bf16[384,512]{1,0:T(8,128)(2,1)S(1)} %get-tuple-element.53.refs_3_), channel_id=1, source_target_pairs={{0,1},{1,0},{2,3},{3,2},{4,5},{5,4},{6,7},{7,6},{8,9},{9,8},{10,11... | collective-permute-start | bytes 1179656 | tf_op jit(solution)/shard_map/ppermute | solution.py:316
  33.6 2.1 %collective-permute-start.7 = (bf16[4,80,512]{2,1,0:T(8,128)(2,1)S(1)}, bf16[4,80,512]{2,1,0:T(8,128)(2,1)S(1)}, u32[]{:S(2)}, u32[]{:S(2)}) collective-permute-start(bf16[4,80,512]{2,1,0:T(8,128)(2,1)S(1)} %get-tuple-element.47), channel_id=1, source_target_pairs={{0,1},{1,0},{2,3},{3,2},{4,5},{5,4},{6,7},{7,6},{8,9},{9,8},{10,11... | collective-permute-start | bytes 983048 | tf_op jit(solution)/shard_map/ppermute | solution.py:316
  37.3 9.3 %collective-permute-start.12 = (bf16[384,512]{1,0:T(8,128)(2,1)S(1)}, bf16[384,512]{1,0:T(8,128)(2,1)S(1)}, u32[]{:S(2)}, u32[]{:S(2)}) collective-permute-start(bf16[384,512]{1,0:T(8,128)(2,1)S(1)} %get-tuple-element.57), channel_id=1, source_target_pairs={{1,25},{3,27},{9,1},{11,3},{17,9},{19,11},{25,17},{27,19}} | collective-permute-start | bytes 1179656 | tf_op jit(solution)/shard_map/ppermute | solution.py:271
  38.0 7.0 %collective-permute-start.8 = (bf16[80,512]{1,0:T(8,128)(2,1)S(1)}, bf16[80,512]{1,0:T(8,128)(2,1)S(1)}, u32[]{:S(2)}, u32[]{:S(2)}) collective-permute-start(bf16[80,512]{1,0:T(8,128)(2,1)S(1)} %get-tuple-element.49), channel_id=1, source_target_pairs={{0,2},{1,3},{2,0},{3,1},{4,6},{5,7},{6,4},{7,5},{8,10},{9,11},{10,... | collective-permute-start | bytes 245768 | tf_op jit(solution)/shard_map/ppermute | solution.py:316
  39.5 5.4 %collective-permute-start.10 = (bf16[80,512]{1,0:T(8,128)(2,1)S(1)}, bf16[80,512]{1,0:T(8,128)(2,1)S(1)}, u32[]{:S(2)}, u32[]{:S(2)}) collective-permute-start(bf16[80,512]{1,0:T(8,128)(2,1)S(1)} %get-tuple-element.51), channel_id=1, source_target_pairs={{0,6},{1,7},{2,4},{3,5},{4,2},{5,3},{6,0},{7,1},{8,14},{9,15},{10,... | collective-permute-start | bytes 245768 | tf_op jit(solution)/shard_map/ppermute | solution.py:316
  40.0 6.6 %collective-permute-start.9 = (bf16[80,512]{1,0:T(8,128)(2,1)S(1)}, bf16[80,512]{1,0:T(8,128)(2,1)S(1)}, u32[]{:S(2)}, u32[]{:S(2)}) collective-permute-start(bf16[80,512]{1,0:T(8,128)(2,1)S(1)} %get-tuple-element.50), channel_id=1, source_target_pairs={{0,4},{1,5},{2,6},{3,7},{4,0},{5,1},{6,2},{7,3},{8,12},{9,13},{10,... | collective-permute-start | bytes 245768 | tf_op jit(solution)/shard_map/ppermute | solution.py:316
  46.7 11.2 %collective-permute-start.21 = (bf16[384,512]{1,0:T(8,128)(2,1)S(1)}, bf16[384,512]{1,0:T(8,128)(2,1)S(1)}, u32[]{:S(2)}, u32[]{:S(2)}) collective-permute-start(bf16[384,512]{1,0:T(8,128)(2,1)S(1)} %get-tuple-element.74), channel_id=1, source_target_pairs={{0,2},{1,5},{2,0},{3,7},{4,6},{5,1},{6,4},{7,3},{8,10},{9,13},{10,... | collective-permute-start | bytes 1179656 | tf_op jit(solution)/shard_map/ppermute | solution.py:271
  47.4 5.7 %collective-permute-start.13 = (bf16[80,512]{1,0:T(8,128)(2,1)S(1)}, bf16[80,512]{1,0:T(8,128)(2,1)S(1)}, u32[]{:S(2)}, u32[]{:S(2)}) collective-permute-start(bf16[80,512]{1,0:T(8,128)(2,1)S(1)} %shard_map.127.refs_0_), channel_id=1, source_target_pairs={{0,8},{1,9},{2,10},{3,11},{4,12},{5,13},{6,14},{7,15},{8,0},{9,1},... | collective-permute-start | bytes 245768 | tf_op jit(solution)/shard_map/ppermute | solution.py:316
  49.2 8.6 %collective-permute-start.14 = (bf16[80,512]{1,0:T(8,128)(2,1)S(1)}, bf16[80,512]{1,0:T(8,128)(2,1)S(1)}, u32[]{:S(2)}, u32[]{:S(2)}) collective-permute-start(bf16[80,512]{1,0:T(8,128)(2,1)S(1)} %shard_map.127.refs_0_), channel_id=1, source_target_pairs={{0,16},{1,17},{2,18},{3,19},{4,20},{5,21},{6,22},{7,23},{8,24},{9,... | collective-permute-start | bytes 245768 | tf_op jit(solution)/shard_map/ppermute | solution.py:316
  51.2 6.5 %collective-permute-start.15 = (bf16[80,512]{1,0:T(8,128)(2,1)S(1)}, bf16[80,512]{1,0:T(8,128)(2,1)S(1)}, u32[]{:S(2)}, u32[]{:S(2)}) collective-permute-start(bf16[80,512]{1,0:T(8,128)(2,1)S(1)} %shard_map.127.refs_0_), channel_id=1, source_target_pairs={{0,24},{1,25},{2,26},{3,27},{4,28},{5,29},{6,30},{7,31},{8,16},{9,... | collective-permute-start | bytes 245768 | tf_op jit(solution)/shard_map/ppermute | solution.py:316
  58.0 11.3 %collective-permute-start.22 = (bf16[384,512]{1,0:T(8,128)(2,1)S(1)}, bf16[384,512]{1,0:T(8,128)(2,1)S(1)}, u32[]{:S(2)}, u32[]{:S(2)}) collective-permute-start(bf16[384,512]{1,0:T(8,128)(2,1)S(1)} %shard_map.131), channel_id=1, source_target_pairs={{0,24},{2,26},{3,11},{4,12},{5,29},{6,14},{8,0},{10,2},{11,19},{12... | collective-permute-start | bytes 1179656 | tf_op jit(solution)/shard_map/ppermute | solution.py:271
  62.0 5.0 %collective-permute-start.16 = (bf16[64,512]{1,0:T(8,128)(2,1)S(1)}, bf16[64,512]{1,0:T(8,128)(2,1)S(1)}, u32[]{:S(2)}, u32[]{:S(2)}) collective-permute-start(bf16[64,512]{1,0:T(8,128)(2,1)S(1)} %get-tuple-element.66.refs_0_), channel_id=1, source_target_pairs={{0,2},{1,3},{2,0},{3,1},{4,6},{5,7},{6,4},{7,5},{8,10},{9,11},{10,... | collective-permute-start | bytes 196616 | tf_op jit(solution)/shard_map/ppermute | solution.py:316
  63.5 5.0 %collective-permute-start.17 = (bf16[64,512]{1,0:T(8,128)(2,1)S(1)}, bf16[64,512]{1,0:T(8,128)(2,1)S(1)}, u32[]{:S(2)}, u32[]{:S(2)}) collective-permute-start(bf16[64,512]{1,0:T(8,128)(2,1)S(1)} %get-tuple-element.66.refs_0_), channel_id=1, source_target_pairs={{0,4},{1,5},{2,6},{3,7},{4,0},{5,1},{6,2},{7,3},{8,12},{9,13},{10,... | collective-permute-start | bytes 196616 | tf_op jit(solution)/shard_map/ppermute | solution.py:316
  64.0 5.3 %collective-permute-start.18 = (bf16[64,512]{1,0:T(8,128)(2,1)S(1)}, bf16[64,512]{1,0:T(8,128)(2,1)S(1)}, u32[]{:S(2)}, u32[]{:S(2)}) collective-permute-start(bf16[64,512]{1,0:T(8,128)(2,1)S(1)} %get-tuple-element.66.refs_0_), channel_id=1, source_target_pairs={{0,6},{1,7},{2,4},{3,5},{4,2},{5,3},{6,0},{7,1},{8,14},{9,15},{10,... | collective-permute-start | bytes 196616 | tf_op jit(solution)/shard_map/ppermute | solution.py:316
  65.5 11.7 %collective-permute-start.20 = (bf16[384,512]{1,0:T(8,128)(2,1)S(1)}, bf16[384,512]{1,0:T(8,128)(2,1)S(1)}, u32[]{:S(2)}, u32[]{:S(2)}) collective-permute-start(bf16[384,512]{1,0:T(8,128)(2,1)S(1)} %shard_map.128), channel_id=1, source_target_pairs={{0,2},{1,5},{2,0},{3,7},{4,6},{5,1},{6,4},{7,3},{8,10},{9,13},{10,... | collective-permute-start | bytes 1179656 | tf_op jit(solution)/shard_map/ppermute | solution.py:271
  69.5 8.4 %collective-permute-start.23 = (bf16[384,512]{1,0:T(8,128)(2,1)S(1)}, bf16[384,512]{1,0:T(8,128)(2,1)S(1)}, u32[]{:S(2)}, u32[]{:S(2)}) collective-permute-start(bf16[384,512]{1,0:T(8,128)(2,1)S(1)} %shard_map.132), channel_id=1, source_target_pairs={{0,4},{1,3},{2,6},{3,1},{4,0},{5,7},{6,2},{7,5},{8,12},{9,11},{10,... | collective-permute-start | bytes 1179656 | tf_op jit(solution)/shard_map/ppermute | solution.py:271
  72.1 6.7 %collective-permute-start.19 = (bf16[256,512]{1,0:T(8,128)(2,1)S(1)}, bf16[256,512]{1,0:T(8,128)(2,1)S(1)}, u32[]{:S(2)}, u32[]{:S(2)}) collective-permute-start(bf16[256,512]{1,0:T(8,128)(2,1)S(1)} %shard_map.130.mine_ref), channel_id=1, source_target_pairs={{0,1},{1,0},{2,3},{3,2},{4,5},{5,4},{6,7},{7,6},{8,9},{9,8},{10,11... | collective-permute-start | bytes 786440 | tf_op jit(solution)/shard_map/ppermute | solution.py:316

commit v10 on v9

--- a/solution.py
+++ b/solution.py
@@ -9,7 +9,7 @@
 BIAS_ROWS = 16
 
 
-def call(kernel, outs, ins, flops=0, smem=0):
+def call(kernel, outs, ins, smem=0, cost=0):
     spec = lambda k: pl.BlockSpec(memory_space=pltpu.SMEM if k < smem else pltpu.VMEM)
     out_shape = [jax.ShapeDtypeStruct(s, d) for s, d in outs]
     moved = sum(a.size * a.dtype.itemsize for a in list(ins) + out_shape)
@@ -19,7 +19,7 @@
         in_specs=[spec(k) for k in range(len(ins))],
         out_specs=[pl.BlockSpec(memory_space=pltpu.VMEM)] * len(outs),
         compiler_params=pltpu.CompilerParams(vmem_limit_bytes=moved + moved // 4 + 4 * 1024 * 1024),
-        cost_estimate=pl.CostEstimate(flops=0, bytes_accessed=0, transcendentals=0),
+        cost_estimate=pl.CostEstimate(flops=int(cost * 1e9), bytes_accessed=0, transcendentals=0),
     )(*ins)
 
 
@@ -77,7 +77,6 @@
         kernel,
         [((last - first, hidden), F32)],
         [dense, *([] if start is None else [start]), *sources],
-        flops=2 * (last - first) * rows_dev * hidden * len(sources),
     )[0]
 
 
@@ -110,7 +109,6 @@
         kernel,
         [(shape, BF16), (shape, BF16), (half, F32), (half, BF16)],
         [spot, own_sum, mate_sum, weight, bias.reshape(1, hidden), grad_out],
-        flops=6 * rows_dev * hidden * hidden,
         smem=1,
     )
 
@@ -131,7 +129,7 @@
     return call(kernel, [(shape, F32)] + [(shape, BF16)] * (count - 1), [spot, keep, got], smem=1)
 
 
-def summed_terms(spot, terms, masks=None):
+def summed_terms(spot, terms, masks=None, cost=10):
     masks = masks or [None] * len(terms)
 
     def kernel(spot_ref, *refs):
@@ -143,7 +141,7 @@
             total = value if total is None else total + value
         refs[-1][...] = total.astype(BF16)
 
-    return call(kernel, [(terms[0].shape, BF16)], [spot, *terms], smem=1)[0]
+    return call(kernel, [(terms[0].shape, BF16)], [spot, *terms], smem=1, cost=cost)[0]
 
 
 def joined_pieces(spot, pieces):
@@ -155,7 +153,7 @@
             q = (spot_ref[0] >> 1) ^ other
             refs[-1][pl.ds(pl.multiple_of(q * rows, rows), rows)] = ref[...]
 
-    return call(kernel, [((count * rows, hidden), BF16)], [spot, *pieces], smem=1)[0]
+    return call(kernel, [((count * rows, hidden), BF16)], [spot, *pieces], smem=1, cost=10)[0]
 
 
 def whole_weight(spot, mine, other):
@@ -180,7 +178,7 @@
         refs[-1][...] = parts[0][piece:]
 
     rows = values[0].shape[0]
-    return call(kernel, [((piece, hidden), BF16), ((rows - piece, hidden), F32)], list(values))
+    return call(kernel, [((piece, hidden), BF16), ((rows - piece, hidden), F32)], list(values), cost=10)
 
 
 def scattered_sums(flipped, own, mate, columns, dtypes, spot=None, lookup=None):
@@ -206,7 +204,7 @@
         kernel,
         [((rows_dev, hidden), kind) for kinds in dtypes for kind in kinds],
         [*extra, flipped, own, mate],
-        flops=4 * rows_dev * rows_dev * hidden * len(columns),
+        cost=10,
         smem=len(extra),
     )
 
@@ -253,7 +251,7 @@
         ]
         return terms[:1]
 
-    def finish(self, token):
+    def finish(self):
         return summed_terms(self.spot, self.arriving)
 
 
@@ -274,32 +272,30 @@
         x = {spot: (spot ^ 2) - spot for spot in range(8)}
         y = {spot: (spot ^ 4) - spot for spot in range(8)}
         straight = {spot: (y if spot % 2 else x)[spot] for spot in range(8)}
-        self.across = {spot: (x if spot % 2 else y)[spot] for spot in range(8)}
+        across = {spot: (x if spot % 2 else y)[spot] for spot in range(8)}
         take = lambda mate, *args: scattered_sums(self.flipped, self.own, mate, *args, self.spot, self.LOOKUP)
         if k == 0:
             _, mate = after(token, self.mate)
             self.to_last, self.to_plane, self.plane_rest = take(mate, (4, 3), [[BF16], [BF16, F32]])
             self.kept, self.to_across, self.to_straight = take(mate, (0, 1, 2), [[F32]] * 3)
             self.from_plane = self.routed(self.to_plane, {1: -8, 3: -8})
-            return [self.to_last, self.kept, self.from_plane]
+            self.from_last = self.routed(self.to_last, straight)
+            return [self.kept, self.from_plane]
         if k == 1:
-            _, to_last, rest = after(token, self.to_last, self.to_straight)
-            self.from_last = self.routed(to_last, straight)
+            _, rest, plane_rest = after(token, self.to_straight, self.plane_rest)
+            out = summed_terms(self.spot, [plane_rest, self.from_last], [self.EVEN, self.MIDDLE])
+            self.from_planes = self.routed(out, {0: -8, 2: -8, 4: 8, 6: 8, 5: -8, 3: 8})
             second = summed_terms(self.spot, [rest, self.from_plane], [None, self.ODD_LOW])
             self.second = self.routed(second, straight)
-            return [second]
+            return [second, out]
         if k == 2:
-            _, plane_rest = after(token, self.plane_rest)
-            out = summed_terms(self.spot, [plane_rest, self.from_last], [self.EVEN, self.MIDDLE])
-            self.from_planes = self.routed(out, {0: -8, 2: -8, 4: 8, 6: 8, 5: -8, 3: 8})
+            _, rest = after(token, self.to_across)
+            out = summed_terms(
+                self.spot, [rest, self.from_planes, self.from_last], [None, self.EVEN | 0b00101000, self.ENDS]
+            )
+            self.arriving = [self.kept, self.second, self.routed(out, across)]
+            return [out, self.second]
         return []
-
-    def finish(self, token):
-        _, rest = after(token, self.to_across)
-        out = summed_terms(
-            self.spot, [rest, self.from_planes, self.from_last], [None, self.EVEN | 0b00101000, self.ENDS]
-        )
-        return summed_terms(self.spot, [self.kept, self.second, self.routed(out, self.across)])
 
 
 def local(features, tile_list, tile_count, tile_values, weight, bias, grad_out):
@@ -343,7 +339,7 @@
             total = summed_terms(spot, values)
     total, bias_sum = finished(values, hidden // pieces)
     half = joined_pieces(spot, [total, *exchanged(k, [total] * len(in_plane), in_plane)])
-    grad_features = route.finish(half)
+    grad_features = route.finish()
     mate_half, grad_features = after(swapped(half, 1), grad_features)
     return (output, grad_features, whole_weight(spot, half, mate_half), bias_sum[0])
 

time: 80.1 us -> 76.1 us (0.950)
  the two profiles are of different devices: /device:TPU:0 before, /device:TPU:10 now
where the time goes in v10:
time: 76.1 us; the launch traced here: 75.8 us
  waiting for transfers between devices  33 us (43%)
  starting transfers between devices  24.9 us (33%)
  Pallas kernels  13.4 us (18%)
  local copies, waits for them, and re-layouts  2.98 us (4%)
  between operations  0.89 us (1%)
    ppermute x5, waiting for transfers between devices, routed(): return lax.ppermute(value, 'blk', pairs)  19.4 us
    pallas_call x15, Pallas kernels, call(): pl.pallas_call(kernel, out_shape=out_shape, in_specs=[spec(k) for k in ra...  13.4 us
    ppermute x15, starting transfers between devices, swapped(): return lax.ppermute(value, 'blk', [(s, s ^ distance) for s in range(count)])  12.1 us
    ppermute x4, waiting for transfers between devices, sent(): return lax.ppermute(value, 'blk', pairs)  8.51 us
    ppermute x4, starting transfers between devices, sent(): return lax.ppermute(value, 'blk', pairs)  6.9 us
    ppermute x5, starting transfers between devices, routed(): return lax.ppermute(value, 'blk', pairs)  5.88 us
    ppermute x15, waiting for transfers between devices, swapped(): return lax.ppermute(value, 'blk', [(s, s ^ distance) for s in range(count)])  5.08 us
    unnamed x12, local copies, waits for them, and re-layouts  1.53 us
  transfers between devices with their start and end apart: 24, of which 7 were waited for; matrix products, arithmetic and copies ran while one was open for 3% of the time, Pallas kernels for 14%

profile of v10, /device:TPU:10, one launch (start us, length us, event | category | flops | bytes accessed | tf_op | source)
XLA Modules:
  0.0 75.8 jit_solution(11216092979572868737)
XLA Ops:
  0.7 1.6 %collective-permute-start.2 = (bf16[384,512]{1,0:T(8,128)(2,1)}, bf16[384,512]{1,0:T(8,128)(2,1)S(1)}, u32[]{:S(2)}, u32[]{:S(2)}) collective-permute-start(bf16[384,512]{1,0:T(8,128)(2,1)} %refs_2_.1), channel_id=1, source_target_pairs={{0,4},{1,5},{2,6},{3,7},{4,8},{5,9},{6,10},{7,11},{8,12},{9,13},{1... | collective-permute-start | bytes 1179656 | tf_op jit(solution)/shard_map/ppermute | solution.py:222
  2.3 1.5 %collective-permute-start.3 = (bf16[384,512]{1,0:T(8,128)(2,1)}, bf16[384,512]{1,0:T(8,128)(2,1)S(1)}, u32[]{:S(2)}, u32[]{:S(2)}) collective-permute-start(bf16[384,512]{1,0:T(8,128)(2,1)} %refs_2_.1), channel_id=1, source_target_pairs={{0,2},{1,3},{2,4},{3,5},{4,6},{5,7},{6,8},{7,9},{8,10},{9,11},{10,... | collective-permute-start | bytes 1179656 | tf_op jit(solution)/shard_map/ppermute | solution.py:222
  3.8 0.5 collective-permute-start.4
  4.3 3.3 %collective-permute-start.5 = (bf16[384,512]{1,0:T(8,128)(2,1)}, bf16[384,512]{1,0:T(8,128)(2,1)S(1)}, u32[]{:S(2)}, u32[]{:S(2)}) collective-permute-start(bf16[384,512]{1,0:T(8,128)(2,1)} %refs_2_.1), channel_id=1, source_target_pairs={{0,28},{2,30},{4,0},{6,2},{8,4},{10,6},{12,8},{14,10},{16,12},{18,... | collective-permute-start | bytes 1179656 | tf_op jit(solution)/shard_map/ppermute | solution.py:222
  7.6 0.7 reshape_squeeze.3
  8.3 0.7 pad_add_fusion
  9.2 1.1 %collective-permute-done.1.mate_meta_ref = s32[120]{0:T(128)S(1)} collective-permute-done((s32[120]{0:T(128)S(1)}, s32[120]{0:T(128)S(1)}, u32[]{:S(2)}, u32[]{:S(2)}) %collective-permute-start.1) | collective-permute-done | bytes 512 | tf_op jit(solution)/shard_map/ppermute | solution.py:312
  10.3 1.5 %copy-done = bf16[1,8,7,128,128]{4,3,2,1,0:T(8,128)(2,1)S(1)} copy-done((bf16[1,8,7,128,128]{4,3,2,1,0:T(8,128)(2,1)S(1)}, bf16[1,8,7,128,128]{4,3,2,1,0:T(8,128)(2,1)}, u32[]{:S(2)}) %copy-start) | copy-done | bytes 1835032
  11.8 3.9 %shard_map.120 = (bf16[768,1920]{1,0:T(8,128)(2,1)S(1)}, bf16[1920,768]{1,0:T(8,128)(2,1)S(1)}) custom-call(s32[1]{0:T(128)} %bitcast.spot_ref.refs_0_, s32[120]{0:T(128)S(1)} %reshape.24.own_meta_ref, s32[120]{0:T(128)S(1)} %collective-permute-done.1.mate_meta_ref, bf16[8,7,128,128]{3,2,1,0:T(8,128)(2,1)S(1)} %bitcast.8, ...), custom_call_target="tpu_custom_call" | custom-call | tf_op jit(solution)/shard_map/pallas_call | solution.py:16
  15.7 8.5 %collective-permute-done.2.refs_0_ = bf16[384,512]{1,0:T(8,128)(2,1)S(1)} collective-permute-done((bf16[384,512]{1,0:T(8,128)(2,1)}, bf16[384,512]{1,0:T(8,128)(2,1)S(1)}, u32[]{:S(2)}, u32[]{:S(2)}) %collective-permute-start.2) | collective-permute-done | bytes 393248 | tf_op jit(solution)/shard_map/ppermute | solution.py:222
  24.2 1.8 %shard_map.121.refs_0_.own_ref = f32[768,512]{1,0:T(8,128)S(1)} custom-call(bf16[768,1920]{1,0:T(8,128)(2,1)S(1)} %get-tuple-element.43.dense_ref, bf16[384,512]{1,0:T(8,128)(2,1)S(1)} %collective-permute-done.2.refs_0_, bf16[384,512]{1,0:T(8,128)(2,1)S(1)} %collective-permute-done.3.refs_1_, bf16[384,512]{1,0:T(8,128)(2,1)S(1)} %copy-done.2, ...), custom_call_target="tpu_custom_call" | custom-call | tf_op jit(solution)/shard_map/pallas_call | solution.py:16
  26.5 2.3 %collective-permute-done.6.mate_ref = f32[384,512]{1,0:T(8,128)S(1)} collective-permute-done((f32[384,512]{1,0:T(8,128)S(1)}, f32[384,512]{1,0:T(8,128)S(1)}, u32[]{:S(2)}, u32[]{:S(2)}) %collective-permute-start.6) | collective-permute-done | bytes 786464 | tf_op jit(solution)/shard_map/ppermute | solution.py:312
  28.8 1.4 %shard_map.123 = (bf16[384,512]{1,0:T(8,128)(2,1)}, bf16[384,512]{1,0:T(8,128)(2,1)S(1)}, f32[4,80,512]{2,1,0:T(8,128)S(1)}, bf16[4,80,512]{2,1,0:T(8,128)(2,1)S(1)}) custom-call(s32[1]{0:T(128)} %bitcast.spot_ref.refs_0_, f32[768,512]{1,0:T(8,128)S(1)} %shard_map.121.refs_0_.own_ref, f32[384,512]{1,0:T(8,128)S(1)} %collective-permute-done.6.mate_ref, ...), custom_call_target="tpu_custom_call" | custom-call | tf_op jit(solution)/shard_map/pallas_call | solution.py:16
  30.7 1.7 %collective-permute-done.7.got_ref = bf16[4,80,512]{2,1,0:T(8,128)(2,1)S(1)} collective-permute-done((bf16[4,80,512]{2,1,0:T(8,128)(2,1)S(1)}, bf16[4,80,512]{2,1,0:T(8,128)(2,1)S(1)}, u32[]{:S(2)}, u32[]{:S(2)}) %collective-permute-start.7) | collective-permute-done | bytes 327712 | tf_op jit(solution)/shard_map/ppermute | solution.py:312
  32.5 2.4 %collective-permute-start.10 = (bf16[80,512]{1,0:T(8,128)(2,1)S(1)}, bf16[80,512]{1,0:T(8,128)(2,1)S(1)}, u32[]{:S(2)}, u32[]{:S(2)}) collective-permute-start(bf16[80,512]{1,0:T(8,128)(2,1)S(1)} %get-tuple-element.50), channel_id=1, source_target_pairs={{0,6},{1,7},{2,4},{3,5},{4,2},{5,3},{6,0},{7,1},{8,14},{9,15},{10,... | collective-permute-start | bytes 245768 | tf_op jit(solution)/shard_map/ppermute | solution.py:312
  34.9 1.5 %collective-permute-start.8 = (bf16[80,512]{1,0:T(8,128)(2,1)S(1)}, bf16[80,512]{1,0:T(8,128)(2,1)S(1)}, u32[]{:S(2)}, u32[]{:S(2)}) collective-permute-start(bf16[80,512]{1,0:T(8,128)(2,1)S(1)} %get-tuple-element.48), channel_id=1, source_target_pairs={{0,2},{1,3},{2,0},{3,1},{4,6},{5,7},{6,4},{7,5},{8,10},{9,11},{10,... | collective-permute-start | bytes 245768 | tf_op jit(solution)/shard_map/ppermute | solution.py:312
  36.4 1.5 %shard_map.126 = (bf16[384,512]{1,0:T(8,128)(2,1)S(1)}, bf16[384,512]{1,0:T(8,128)(2,1)S(1)}, f32[384,512]{1,0:T(8,128)S(1)}) custom-call(s32[1]{0:T(128)} %bitcast.spot_ref.refs_0_, s32[40]{0:T(128)S(1)} %copy-done.5, bf16[1920,768]{1,0:T(8,128)(2,1)S(1)} %get-tuple-element.51.refs_2_, bf16[384,512]{1,0:T(8,128)(2,1)S(1)} %get-tuple-element.52.refs_3_, ...), custom_call_target="tpu_custom_call" | custom-call | flops 10000000000 | tf_op jit(solution)/shard_map/pallas_call | solution.py:16
  37.9 0.7 collective-permute-start.12
  38.6 1.9 %shard_map.125 = (f32[384,512]{1,0:T(8,128)S(1)}, f32[384,512]{1,0:T(8,128)S(1)}, f32[384,512]{1,0:T(8,128)S(1)}) custom-call(s32[1]{0:T(128)} %bitcast.spot_ref.refs_0_, s32[40]{0:T(128)S(1)} %copy-done.5, bf16[1920,768]{1,0:T(8,128)(2,1)S(1)} %get-tuple-element.51.refs_2_, bf16[384,512]{1,0:T(8,128)(2,1)S(1)} %get-tuple-element.52.refs_3_, ...), custom_call_target="tpu_custom_call" | custom-call | flops 10000000000 | tf_op jit(solution)/shard_map/pallas_call | solution.py:16
  40.5 0.7 collective-permute-start.16
  41.3 1.9 %collective-permute-start.13 = (bf16[80,512]{1,0:T(8,128)(2,1)S(1)}, bf16[80,512]{1,0:T(8,128)(2,1)S(1)}, u32[]{:S(2)}, u32[]{:S(2)}) collective-permute-start(bf16[80,512]{1,0:T(8,128)(2,1)S(1)} %shard_map.127.refs_0_), channel_id=1, source_target_pairs={{0,8},{1,9},{2,10},{3,11},{4,12},{5,13},{6,14},{7,15},{8,0},{9,1},... | collective-permute-start | bytes 245768 | tf_op jit(solution)/shard_map/ppermute | solution.py:312
  43.2 1.2 %collective-permute-start.14 = (bf16[80,512]{1,0:T(8,128)(2,1)S(1)}, bf16[80,512]{1,0:T(8,128)(2,1)S(1)}, u32[]{:S(2)}, u32[]{:S(2)}) collective-permute-start(bf16[80,512]{1,0:T(8,128)(2,1)S(1)} %shard_map.127.refs_0_), channel_id=1, source_target_pairs={{0,16},{1,17},{2,18},{3,19},{4,20},{5,21},{6,22},{7,23},{8,24},{9,... | collective-permute-start | bytes 245768 | tf_op jit(solution)/shard_map/ppermute | solution.py:312
  44.8 3.5 %collective-permute-done.16.refs_1_.refs_2_ = bf16[384,512]{1,0:T(8,128)(2,1)S(1)} collective-permute-done((bf16[384,512]{1,0:T(8,128)(2,1)S(1)}, bf16[384,512]{1,0:T(8,128)(2,1)S(1)}, u32[]{:S(2)}, u32[]{:S(2)}) %collective-permute-start.16) | collective-permute-done | bytes 393248 | tf_op jit(solution)/shard_map/ppermute | solution.py:269
  48.5 3.8 %collective-permute-start.20 = (bf16[384,512]{1,0:T(8,128)(2,1)S(1)}, bf16[384,512]{1,0:T(8,128)(2,1)S(1)}, u32[]{:S(2)}, u32[]{:S(2)}) collective-permute-start(bf16[384,512]{1,0:T(8,128)(2,1)S(1)} %shard_map.129), channel_id=1, source_target_pairs={{0,24},{2,26},{3,11},{4,12},{5,29},{6,14},{8,0},{10,2},{11,19},{12... | collective-permute-start | bytes 1179656 | tf_op jit(solution)/shard_map/ppermute | solution.py:269
  52.4 0.6 collective-permute-start.21
  53.1 1.6 %collective-permute-start.17 = (bf16[64,512]{1,0:T(8,128)(2,1)S(1)}, bf16[64,512]{1,0:T(8,128)(2,1)S(1)}, u32[]{:S(2)}, u32[]{:S(2)}) collective-permute-start(bf16[64,512]{1,0:T(8,128)(2,1)S(1)} %get-tuple-element.67.refs_0_), channel_id=1, source_target_pairs={{0,2},{1,3},{2,0},{3,1},{4,6},{5,7},{6,4},{7,5},{8,10},{9,11},{10,... | collective-permute-start | bytes 196616 | tf_op jit(solution)/shard_map/ppermute | solution.py:312
  54.6 2.3 %collective-permute-start.18 = (bf16[64,512]{1,0:T(8,128)(2,1)S(1)}, bf16[64,512]{1,0:T(8,128)(2,1)S(1)}, u32[]{:S(2)}, u32[]{:S(2)}) collective-permute-start(bf16[64,512]{1,0:T(8,128)(2,1)S(1)} %get-tuple-element.67.refs_0_), channel_id=1, source_target_pairs={{0,4},{1,5},{2,6},{3,7},{4,0},{5,1},{6,2},{7,3},{8,12},{9,13},{10,... | collective-permute-start | bytes 196616 | tf_op jit(solution)/shard_map/ppermute | solution.py:312
  56.9 0.6 slice.3
  57.5 8.4 %collective-permute-done.20.refs_1_ = bf16[384,512]{1,0:T(8,128)(2,1)S(1)} collective-permute-done((bf16[384,512]{1,0:T(8,128)(2,1)S(1)}, bf16[384,512]{1,0:T(8,128)(2,1)S(1)}, u32[]{:S(2)}, u32[]{:S(2)}) %collective-permute-start.20) | collective-permute-done | bytes 393248 | tf_op jit(solution)/shard_map/ppermute | solution.py:269
  66.3 7.5 %collective-permute-done.23.refs_2_ = bf16[384,512]{1,0:T(8,128)(2,1)S(1)} collective-permute-done((bf16[384,512]{1,0:T(8,128)(2,1)S(1)}, bf16[384,512]{1,0:T(8,128)(2,1)S(1)}, u32[]{:S(2)}, u32[]{:S(2)}) %collective-permute-start.23) | collective-permute-done | bytes 393248 | tf_op jit(solution)/shard_map/ppermute | solution.py:269
  73.9 0.9 %shard_map.133 = bf16[384,512]{1,0:T(8,128)(2,1)} custom-call(s32[1]{0:T(128)} %bitcast.spot_ref.refs_0_, f32[384,512]{1,0:T(8,128)S(1)} %get-tuple-element.54.refs_0_, bf16[384,512]{1,0:T(8,128)(2,1)S(1)} %collective-permute-done.21.refs_1_, bf16[384,512]{1,0:T(8,128)(2,1)S(1)} %collective-permute-done.23.refs_2_), custom_call_target="tpu_custom_call" | custom-call | flops 10000000000 | tf_op jit(solution)/shard_map/pallas_call | solution.py:16
  74.8 1.0 %shard_map.134 = f32[512,512]{1,0:T(8,128)} custom-call(s32[1]{0:T(128)} %bitcast.spot_ref.refs_0_, bf16[256,512]{1,0:T(8,128)(2,1)S(1)} %shard_map.132.mine_ref, bf16[256,512]{1,0:T(8,128)(2,1)S(1)} %collective-permute-done.22.other_ref), custom_call_target="tpu_custom_call" | custom-call | tf_op jit(solution)/shard_map/pallas_call | solution.py:16
  (48 shorter events, 2.5 us)
Async XLA Ops:
  0.6 7.0 %collective-permute-start = (bf16[8,7,128,128]{3,2,1,0:T(8,128)(2,1)}, bf16[8,7,128,128]{3,2,1,0:T(8,128)(2,1)S(1)}, u32[]{:S(2)}, u32[]{:S(2)}) collective-permute-start(bf16[8,7,128,128]{3,2,1,0:T(8,128)(2,1)} %bitcast.7), channel_id=1, source_target_pairs={{0,1},{1,0},{2,3},{3,2},{4,5},{5,4},{6,7},{7,6},{8,9},{9,8},{10,11... | collective-permute-start | bytes 5505032 | tf_op jit(solution)/shard_map/ppermute | solution.py:312
  0.7 23.5 %collective-permute-start.2 = (bf16[384,512]{1,0:T(8,128)(2,1)}, bf16[384,512]{1,0:T(8,128)(2,1)S(1)}, u32[]{:S(2)}, u32[]{:S(2)}) collective-permute-start(bf16[384,512]{1,0:T(8,128)(2,1)} %refs_2_.1), channel_id=1, source_target_pairs={{0,4},{1,5},{2,6},{3,7},{4,8},{5,9},{6,10},{7,11},{8,12},{9,13},{1... | collective-permute-start | bytes 1179656 | tf_op jit(solution)/shard_map/ppermute | solution.py:222
  2.3 21.9 %collective-permute-start.3 = (bf16[384,512]{1,0:T(8,128)(2,1)}, bf16[384,512]{1,0:T(8,128)(2,1)S(1)}, u32[]{:S(2)}, u32[]{:S(2)}) collective-permute-start(bf16[384,512]{1,0:T(8,128)(2,1)} %refs_2_.1), channel_id=1, source_target_pairs={{0,2},{1,3},{2,4},{3,5},{4,6},{5,7},{6,8},{7,9},{8,10},{9,11},{10,... | collective-permute-start | bytes 1179656 | tf_op jit(solution)/shard_map/ppermute | solution.py:222
  3.8 20.5 %collective-permute-start.4 = (bf16[384,512]{1,0:T(8,128)(2,1)}, bf16[384,512]{1,0:T(8,128)(2,1)S(1)}, u32[]{:S(2)}, u32[]{:S(2)}) collective-permute-start(bf16[384,512]{1,0:T(8,128)(2,1)} %refs_2_.1), channel_id=1, source_target_pairs={{0,30},{1,31},{2,0},{3,1},{4,2},{5,3},{6,4},{7,5},{8,6},{9,7},{10,... | collective-permute-start | bytes 1179656 | tf_op jit(solution)/shard_map/ppermute | solution.py:222
  4.3 21.7 %collective-permute-start.5 = (bf16[384,512]{1,0:T(8,128)(2,1)}, bf16[384,512]{1,0:T(8,128)(2,1)S(1)}, u32[]{:S(2)}, u32[]{:S(2)}) collective-permute-start(bf16[384,512]{1,0:T(8,128)(2,1)} %refs_2_.1), channel_id=1, source_target_pairs={{0,28},{2,30},{4,0},{6,2},{8,4},{10,6},{12,8},{14,10},{16,12},{18,... | collective-permute-start | bytes 1179656 | tf_op jit(solution)/shard_map/ppermute | solution.py:222
  9.2 1.1 %collective-permute-start.1 = (s32[120]{0:T(128)S(1)}, s32[120]{0:T(128)S(1)}, u32[]{:S(2)}, u32[]{:S(2)}) collective-permute-start(s32[120]{0:T(128)S(1)} %reshape.24.own_meta_ref), channel_id=1, source_target_pairs={{0,1},{1,0},{2,3},{3,2},{4,5},{5,4},{6,7},{7,6},{8,9},{9,8},{10,11... | collective-permute-start | bytes 1448 | tf_op jit(solution)/shard_map/ppermute | solution.py:312
  10.3 1.5 %copy-start = (bf16[1,8,7,128,128]{4,3,2,1,0:T(8,128)(2,1)S(1)}, bf16[1,8,7,128,128]{4,3,2,1,0:T(8,128)(2,1)}, u32[]{:S(2)}) copy-start(bf16[1,8,7,128,128]{4,3,2,1,0:T(8,128)(2,1)} %param.12) | copy-start | bytes 5505028
  11.8 12.4 %copy-start.2 = (bf16[384,512]{1,0:T(8,128)(2,1)S(1)}, bf16[384,512]{1,0:T(8,128)(2,1)}, u32[]{:S(2)}) copy-start(bf16[384,512]{1,0:T(8,128)(2,1)} %refs_2_.1) | copy-start | bytes 1179652
  26.0 2.8 %copy-start.1 = (bf16[512,512]{1,0:T(8,128)(2,1)S(1)}, bf16[512,512]{1,0:T(8,128)(2,1)}, u32[]{:S(2)}) copy-start(bf16[512,512]{1,0:T(8,128)(2,1)} %weight_ref.1) | copy-start | bytes 1572868
  26.0 2.8 %copy-start.3 = (bf16[384,512]{1,0:T(8,128)(2,1)S(1)}, bf16[384,512]{1,0:T(8,128)(2,1)}, u32[]{:S(2)}) copy-start(bf16[384,512]{1,0:T(8,128)(2,1)} %grad_out_ref.1) | copy-start | bytes 1179652
  26.0 2.7 %copy-start.4 = (f32[512]{0:T(512)S(1)}, f32[512]{0:T(512)}, u32[]{:S(2)}) copy-start(f32[512]{0:T(512)} %param.14) | copy-start | bytes 6148
  26.4 2.4 %collective-permute-start.6 = (f32[384,512]{1,0:T(8,128)S(1)}, f32[384,512]{1,0:T(8,128)S(1)}, u32[]{:S(2)}, u32[]{:S(2)}) collective-permute-start(f32[384,512]{1,0:T(8,128)S(1)} %shard_map.122), channel_id=1, source_target_pairs={{0,1},{1,0},{2,3},{3,2},{4,5},{5,4},{6,7},{7,6},{8,9},{9,8},{10,11... | collective-permute-start | bytes 2359304 | tf_op jit(solution)/shard_map/ppermute | solution.py:312
  28.8 7.6 %copy-start.5 = (s32[40]{0:T(128)S(1)}, s32[40]{0:T(128)}, u32[]{:S(2)}) copy-start(s32[40]{0:T(128)} %constant.23.refs_1_) | copy-start | bytes 484
  30.2 6.2 %collective-permute-start.11 = (bf16[384,512]{1,0:T(8,128)(2,1)S(1)}, bf16[384,512]{1,0:T(8,128)(2,1)S(1)}, u32[]{:S(2)}, u32[]{:S(2)}) collective-permute-start(bf16[384,512]{1,0:T(8,128)(2,1)S(1)} %get-tuple-element.52.refs_3_), channel_id=1, source_target_pairs={{0,1},{1,0},{2,3},{3,2},{4,5},{5,4},{6,7},{7,6},{8,9},{9,8},{10,11... | collective-permute-start | bytes 1179656 | tf_op jit(solution)/shard_map/ppermute | solution.py:312
  30.3 2.1 %collective-permute-start.7 = (bf16[4,80,512]{2,1,0:T(8,128)(2,1)S(1)}, bf16[4,80,512]{2,1,0:T(8,128)(2,1)S(1)}, u32[]{:S(2)}, u32[]{:S(2)}) collective-permute-start(bf16[4,80,512]{2,1,0:T(8,128)(2,1)S(1)} %get-tuple-element.46), channel_id=1, source_target_pairs={{0,1},{1,0},{2,3},{3,2},{4,5},{5,4},{6,7},{7,6},{8,9},{9,8},{10,11... | collective-permute-start | bytes 983048 | tf_op jit(solution)/shard_map/ppermute | solution.py:312
  32.5 8.7 %collective-permute-start.10 = (bf16[80,512]{1,0:T(8,128)(2,1)S(1)}, bf16[80,512]{1,0:T(8,128)(2,1)S(1)}, u32[]{:S(2)}, u32[]{:S(2)}) collective-permute-start(bf16[80,512]{1,0:T(8,128)(2,1)S(1)} %get-tuple-element.50), channel_id=1, source_target_pairs={{0,6},{1,7},{2,4},{3,5},{4,2},{5,3},{6,0},{7,1},{8,14},{9,15},{10,... | collective-permute-start | bytes 245768 | tf_op jit(solution)/shard_map/ppermute | solution.py:312
  34.9 6.3 %collective-permute-start.8 = (bf16[80,512]{1,0:T(8,128)(2,1)S(1)}, bf16[80,512]{1,0:T(8,128)(2,1)S(1)}, u32[]{:S(2)}, u32[]{:S(2)}) collective-permute-start(bf16[80,512]{1,0:T(8,128)(2,1)S(1)} %get-tuple-element.48), channel_id=1, source_target_pairs={{0,2},{1,3},{2,0},{3,1},{4,6},{5,7},{6,4},{7,5},{8,10},{9,11},{10,... | collective-permute-start | bytes 245768 | tf_op jit(solution)/shard_map/ppermute | solution.py:312
  36.4 4.9 %collective-permute-start.9 = (bf16[80,512]{1,0:T(8,128)(2,1)S(1)}, bf16[80,512]{1,0:T(8,128)(2,1)S(1)}, u32[]{:S(2)}, u32[]{:S(2)}) collective-permute-start(bf16[80,512]{1,0:T(8,128)(2,1)S(1)} %get-tuple-element.49), channel_id=1, source_target_pairs={{0,4},{1,5},{2,6},{3,7},{4,0},{5,1},{6,2},{7,3},{8,12},{9,13},{10,... | collective-permute-start | bytes 245768 | tf_op jit(solution)/shard_map/ppermute | solution.py:312
  37.9 3.3 %collective-permute-start.12 = (bf16[384,512]{1,0:T(8,128)(2,1)S(1)}, bf16[384,512]{1,0:T(8,128)(2,1)S(1)}, u32[]{:S(2)}, u32[]{:S(2)}) collective-permute-start(bf16[384,512]{1,0:T(8,128)(2,1)S(1)} %get-tuple-element.55), channel_id=1, source_target_pairs={{1,25},{3,27},{9,1},{11,3},{17,9},{19,11},{25,17},{27,19}} | collective-permute-start | bytes 1179656 | tf_op jit(solution)/shard_map/ppermute | solution.py:269
  40.5 7.8 %collective-permute-start.16 = (bf16[384,512]{1,0:T(8,128)(2,1)S(1)}, bf16[384,512]{1,0:T(8,128)(2,1)S(1)}, u32[]{:S(2)}, u32[]{:S(2)}) collective-permute-start(bf16[384,512]{1,0:T(8,128)(2,1)S(1)} %get-tuple-element.63), channel_id=1, source_target_pairs={{0,2},{1,5},{2,0},{3,7},{4,6},{5,1},{6,4},{7,3},{8,10},{9,13},{10,... | collective-permute-start | bytes 1179656 | tf_op jit(solution)/shard_map/ppermute | solution.py:269
  41.3 11.7 %collective-permute-start.13 = (bf16[80,512]{1,0:T(8,128)(2,1)S(1)}, bf16[80,512]{1,0:T(8,128)(2,1)S(1)}, u32[]{:S(2)}, u32[]{:S(2)}) collective-permute-start(bf16[80,512]{1,0:T(8,128)(2,1)S(1)} %shard_map.127.refs_0_), channel_id=1, source_target_pairs={{0,8},{1,9},{2,10},{3,11},{4,12},{5,13},{6,14},{7,15},{8,0},{9,1},... | collective-permute-start | bytes 245768 | tf_op jit(solution)/shard_map/ppermute | solution.py:312
  43.2 9.8 %collective-permute-start.14 = (bf16[80,512]{1,0:T(8,128)(2,1)S(1)}, bf16[80,512]{1,0:T(8,128)(2,1)S(1)}, u32[]{:S(2)}, u32[]{:S(2)}) collective-permute-start(bf16[80,512]{1,0:T(8,128)(2,1)S(1)} %shard_map.127.refs_0_), channel_id=1, source_target_pairs={{0,16},{1,17},{2,18},{3,19},{4,20},{5,21},{6,22},{7,23},{8,24},{9,... | collective-permute-start | bytes 245768 | tf_op jit(solution)/shard_map/ppermute | solution.py:312
  44.4 8.6 %collective-permute-start.15 = (bf16[80,512]{1,0:T(8,128)(2,1)S(1)}, bf16[80,512]{1,0:T(8,128)(2,1)S(1)}, u32[]{:S(2)}, u32[]{:S(2)}) collective-permute-start(bf16[80,512]{1,0:T(8,128)(2,1)S(1)} %shard_map.127.refs_0_), channel_id=1, source_target_pairs={{0,24},{1,25},{2,26},{3,27},{4,28},{5,29},{6,30},{7,31},{8,16},{9,... | collective-permute-start | bytes 245768 | tf_op jit(solution)/shard_map/ppermute | solution.py:312
  48.5 17.4 %collective-permute-start.20 = (bf16[384,512]{1,0:T(8,128)(2,1)S(1)}, bf16[384,512]{1,0:T(8,128)(2,1)S(1)}, u32[]{:S(2)}, u32[]{:S(2)}) collective-permute-start(bf16[384,512]{1,0:T(8,128)(2,1)S(1)} %shard_map.129), channel_id=1, source_target_pairs={{0,24},{2,26},{3,11},{4,12},{5,29},{6,14},{8,0},{10,2},{11,19},{12... | collective-permute-start | bytes 1179656 | tf_op jit(solution)/shard_map/ppermute | solution.py:269
  52.4 13.7 %collective-permute-start.21 = (bf16[384,512]{1,0:T(8,128)(2,1)S(1)}, bf16[384,512]{1,0:T(8,128)(2,1)S(1)}, u32[]{:S(2)}, u32[]{:S(2)}) collective-permute-start(bf16[384,512]{1,0:T(8,128)(2,1)S(1)} %shard_map.128), channel_id=1, source_target_pairs={{0,2},{1,5},{2,0},{3,7},{4,6},{5,1},{6,4},{7,3},{8,10},{9,13},{10,... | collective-permute-start | bytes 1179656 | tf_op jit(solution)/shard_map/ppermute | solution.py:269
  53.1 13.0 %collective-permute-start.17 = (bf16[64,512]{1,0:T(8,128)(2,1)S(1)}, bf16[64,512]{1,0:T(8,128)(2,1)S(1)}, u32[]{:S(2)}, u32[]{:S(2)}) collective-permute-start(bf16[64,512]{1,0:T(8,128)(2,1)S(1)} %get-tuple-element.67.refs_0_), channel_id=1, source_target_pairs={{0,2},{1,3},{2,0},{3,1},{4,6},{5,7},{6,4},{7,5},{8,10},{9,11},{10,... | collective-permute-start | bytes 196616 | tf_op jit(solution)/shard_map/ppermute | solution.py:312
  54.6 11.5 %collective-permute-start.18 = (bf16[64,512]{1,0:T(8,128)(2,1)S(1)}, bf16[64,512]{1,0:T(8,128)(2,1)S(1)}, u32[]{:S(2)}, u32[]{:S(2)}) collective-permute-start(bf16[64,512]{1,0:T(8,128)(2,1)S(1)} %get-tuple-element.67.refs_0_), channel_id=1, source_target_pairs={{0,4},{1,5},{2,6},{3,7},{4,0},{5,1},{6,2},{7,3},{8,12},{9,13},{10,... | collective-permute-start | bytes 196616 | tf_op jit(solution)/shard_map/ppermute | solution.py:312
  56.9 9.2 %collective-permute-start.19 = (bf16[64,512]{1,0:T(8,128)(2,1)S(1)}, bf16[64,512]{1,0:T(8,128)(2,1)S(1)}, u32[]{:S(2)}, u32[]{:S(2)}) collective-permute-start(bf16[64,512]{1,0:T(8,128)(2,1)S(1)} %get-tuple-element.67.refs_0_), channel_id=1, source_target_pairs={{0,6},{1,7},{2,4},{3,5},{4,2},{5,3},{6,0},{7,1},{8,14},{9,15},{10,... | collective-permute-start | bytes 196616 | tf_op jit(solution)/shard_map/ppermute | solution.py:312
  66.0 7.8 %collective-permute-start.23 = (bf16[384,512]{1,0:T(8,128)(2,1)S(1)}, bf16[384,512]{1,0:T(8,128)(2,1)S(1)}, u32[]{:S(2)}, u32[]{:S(2)}) collective-permute-start(bf16[384,512]{1,0:T(8,128)(2,1)S(1)} %shard_map.131), channel_id=1, source_target_pairs={{0,4},{1,3},{2,6},{3,1},{4,0},{5,7},{6,2},{7,5},{8,12},{9,11},{10,... | collective-permute-start | bytes 1179656 | tf_op jit(solution)/shard_map/ppermute | solution.py:269
  66.2 8.6 %collective-permute-start.22 = (bf16[256,512]{1,0:T(8,128)(2,1)S(1)}, bf16[256,512]{1,0:T(8,128)(2,1)S(1)}, u32[]{:S(2)}, u32[]{:S(2)}) collective-permute-start(bf16[256,512]{1,0:T(8,128)(2,1)S(1)} %shard_map.132.mine_ref), channel_id=1, source_target_pairs={{0,1},{1,0},{2,3},{3,2},{4,5},{5,4},{6,7},{7,6},{8,9},{9,8},{10,11... | collective-permute-start | bytes 786440 | tf_op jit(solution)/shard_map/ppermute | solution.py:312

commit v11 on v10

--- a/solution.py
+++ b/solution.py
@@ -175,10 +175,9 @@
         while len(parts) > 1:
             parts = [parts[k] + parts[k + 1] for k in range(0, len(parts), 2)]
         refs[-2][...] = parts[0][:piece].astype(BF16)
-        refs[-1][...] = parts[0][piece:]
-
-    rows = values[0].shape[0]
-    return call(kernel, [((piece, hidden), BF16), ((rows - piece, hidden), F32)], list(values), cost=10)
+        refs[-1][...] = parts[0][piece : piece + 1]
+
+    return call(kernel, [((piece, hidden), BF16), ((1, hidden), F32)], list(values), cost=10)
 
 
 def scattered_sums(flipped, own, mate, columns, dtypes, spot=None, lookup=None):
@@ -251,12 +250,12 @@
         ]
         return terms[:1]
 
-    def finish(self):
+    def finish(self, token):
         return summed_terms(self.spot, self.arriving)
 
 
 class Relayed(Direct):
-    EVEN, MIDDLE, ENDS, ODD_LOW = 0b01010101, 0b00111100, 0b11000011, 0b00001010
+    EVEN, MIDDLE, ENDS = 0b01010101, 0b00111100, 0b11000011
     LOOKUP = [
         [2, 4, 3, 0, 1], [2, 3, 4, 0, 1],
         [2, 4, 1, 0, 3], [2, 1, 4, 0, 3],
@@ -277,15 +276,17 @@
         if k == 0:
             _, mate = after(token, self.mate)
             self.to_last, self.to_plane, self.plane_rest = take(mate, (4, 3), [[BF16], [BF16, F32]])
-            self.kept, self.to_across, self.to_straight = take(mate, (0, 1, 2), [[F32]] * 3)
-            self.from_plane = self.routed(self.to_plane, {1: -8, 3: -8})
+            self.from_plane = self.routed(self.to_plane, {1: -8, 3: 4})
             self.from_last = self.routed(self.to_last, straight)
-            return [self.kept, self.from_plane]
+            return [self.to_last]
         if k == 1:
-            _, rest, plane_rest = after(token, self.to_straight, self.plane_rest)
-            out = summed_terms(self.spot, [plane_rest, self.from_last], [self.EVEN, self.MIDDLE])
-            self.from_planes = self.routed(out, {0: -8, 2: -8, 4: 8, 6: 8, 5: -8, 3: 8})
-            second = summed_terms(self.spot, [rest, self.from_plane], [None, self.ODD_LOW])
+            _, mate, plane_rest = after(token, self.mate, self.plane_rest)
+            self.kept, self.to_across, to_straight = take(mate, (0, 1, 2), [[F32]] * 3)
+            out = summed_terms(
+                self.spot, [plane_rest, self.from_last, self.from_plane], [self.EVEN, self.MIDDLE, 0b10000000]
+            )
+            self.from_planes = self.routed(out, {0: -8, 2: -8, 4: 8, 6: 8, 5: -8, 3: 8, 7: -8})
+            second = summed_terms(self.spot, [to_straight, self.from_plane], [None, 0b00000010])
             self.second = self.routed(second, straight)
             return [second, out]
         if k == 2:
@@ -293,9 +294,14 @@
             out = summed_terms(
                 self.spot, [rest, self.from_planes, self.from_last], [None, self.EVEN | 0b00101000, self.ENDS]
             )
-            self.arriving = [self.kept, self.second, self.routed(out, across)]
+            self.first = self.routed(out, across)
             return [out, self.second]
         return []
+
+    def finish(self, token):
+        _, kept = after(token, self.kept)
+        terms = [kept, self.second, self.first, self.from_planes]
+        return summed_terms(self.spot, terms, [None, None, None, 0b10000000])
 
 
 def local(features, tile_list, tile_count, tile_values, weight, bias, grad_out):
@@ -339,9 +345,8 @@
             total = summed_terms(spot, values)
     total, bias_sum = finished(values, hidden // pieces)
     half = joined_pieces(spot, [total, *exchanged(k, [total] * len(in_plane), in_plane)])
-    grad_features = route.finish()
-    mate_half, grad_features = after(swapped(half, 1), grad_features)
-    return (output, grad_features, whole_weight(spot, half, mate_half), bias_sum[0])
+    grad_weight = whole_weight(spot, half, swapped(half, 1))
+    return (output, route.finish(grad_weight), grad_weight, bias_sum.reshape(hidden))
 
 
 def solution(mesh):

time: 76.1 us -> 79 us (1.038)
  the two profiles are of different devices: /device:TPU:10 before, /device:TPU:19 now
where the time goes in v11:
time: 79 us; the launch traced here: 78.8 us
  starting transfers between devices  33.2 us (42%)
  waiting for transfers between devices  28 us (35%)
  Pallas kernels  13.6 us (17%)
  local copies, waits for them, and re-layouts  2.39 us (3%)
  between operations  0.87 us (1%)
    ppermute x15, starting transfers between devices, swapped(): return lax.ppermute(value, 'blk', [(s, s ^ distance) for s in range(count)])  22.8 us
    pallas_call x15, Pallas kernels, call(): pl.pallas_call(kernel, out_shape=out_shape, in_specs=[spec(k) for k in ra...  13.6 us
    ppermute x5, waiting for transfers between devices, routed(): return lax.ppermute(value, 'blk', pairs)  13.2 us
    ppermute x4, waiting for transfers between devices, sent(): return lax.ppermute(value, 'blk', pairs)  8.41 us
    ppermute x5, starting transfers between devices, routed(): return lax.ppermute(value, 'blk', pairs)  7.02 us
    ppermute x15, waiting for transfers between devices, swapped(): return lax.ppermute(value, 'blk', [(s, s ^ distance) for s in range(count)])  6.35 us
    ppermute x4, starting transfers between devices, sent(): return lax.ppermute(value, 'blk', pairs)  3.38 us
  transfers between devices with their start and end apart: 24, of which 10 were waited for; matrix products, arithmetic and copies ran while one was open for 2% of the time, Pallas kernels for 14%

profile of v11, /device:TPU:19, one launch (start us, length us, event | category | flops | bytes accessed | tf_op | source)
XLA Modules:
  0.0 78.8 jit_solution(14912261147967685572)
XLA Ops:
  0.6 0.7 collective-permute-start
  1.4 1.2 %collective-permute-start.2 = (bf16[384,512]{1,0:T(8,128)(2,1)}, bf16[384,512]{1,0:T(8,128)(2,1)S(1)}, u32[]{:S(2)}, u32[]{:S(2)}) collective-permute-start(bf16[384,512]{1,0:T(8,128)(2,1)} %refs_2_.1), channel_id=1, source_target_pairs={{0,4},{1,5},{2,6},{3,7},{4,8},{5,9},{6,10},{7,11},{8,12},{9,13},{1... | collective-permute-start | bytes 1179656 | tf_op jit(solution)/shard_map/ppermute | solution.py:221
  2.6 1.2 %collective-permute-start.3 = (bf16[384,512]{1,0:T(8,128)(2,1)}, bf16[384,512]{1,0:T(8,128)(2,1)S(1)}, u32[]{:S(2)}, u32[]{:S(2)}) collective-permute-start(bf16[384,512]{1,0:T(8,128)(2,1)} %refs_2_.1), channel_id=1, source_target_pairs={{0,2},{1,3},{2,4},{3,5},{4,6},{5,7},{6,8},{7,9},{8,10},{9,11},{10,... | collective-permute-start | bytes 1179656 | tf_op jit(solution)/shard_map/ppermute | solution.py:221
  4.1 0.7 collective-permute-start.5
  5.0 0.7 reshape_squeeze.3
  6.5 3.3 %collective-permute-start.1 = (s32[120]{0:T(128)S(1)}, s32[120]{0:T(128)S(1)}, u32[]{:S(2)}, u32[]{:S(2)}) collective-permute-start(s32[120]{0:T(128)S(1)} %reshape.27.own_meta_ref), channel_id=1, source_target_pairs={{0,1},{1,0},{2,3},{3,2},{4,5},{5,4},{6,7},{7,6},{8,9},{9,8},{10,11... | collective-permute-start | bytes 1448 | tf_op jit(solution)/shard_map/ppermute | solution.py:318
  9.8 0.8 %collective-permute-done.1.mate_meta_ref = s32[120]{0:T(128)S(1)} collective-permute-done((s32[120]{0:T(128)S(1)}, s32[120]{0:T(128)S(1)}, u32[]{:S(2)}, u32[]{:S(2)}) %collective-permute-start.1) | collective-permute-done | bytes 512 | tf_op jit(solution)/shard_map/ppermute | solution.py:318
  10.7 1.5 %copy-done = bf16[1,8,7,128,128]{4,3,2,1,0:T(8,128)(2,1)S(1)} copy-done((bf16[1,8,7,128,128]{4,3,2,1,0:T(8,128)(2,1)S(1)}, bf16[1,8,7,128,128]{4,3,2,1,0:T(8,128)(2,1)}, u32[]{:S(2)}) %copy-start) | copy-done | bytes 1835032
  12.2 3.5 %shard_map.120 = (bf16[768,1920]{1,0:T(8,128)(2,1)S(1)}, bf16[1920,768]{1,0:T(8,128)(2,1)S(1)}) custom-call(s32[1]{0:T(128)} %bitcast.spot_ref.refs_0_, s32[120]{0:T(128)S(1)} %reshape.27.own_meta_ref, s32[120]{0:T(128)S(1)} %collective-permute-done.1.mate_meta_ref, bf16[8,7,128,128]{3,2,1,0:T(8,128)(2,1)S(1)} %bitcast.8, ...), custom_call_target="tpu_custom_call" | custom-call | tf_op jit(solution)/shard_map/pallas_call | solution.py:16
  15.6 8.4 %collective-permute-done.2.refs_0_ = bf16[384,512]{1,0:T(8,128)(2,1)S(1)} collective-permute-done((bf16[384,512]{1,0:T(8,128)(2,1)}, bf16[384,512]{1,0:T(8,128)(2,1)S(1)}, u32[]{:S(2)}, u32[]{:S(2)}) %collective-permute-start.2) | collective-permute-done | bytes 393248 | tf_op jit(solution)/shard_map/ppermute | solution.py:221
  24.0 1.8 %shard_map.121.refs_0_.own_ref = f32[768,512]{1,0:T(8,128)S(1)} custom-call(bf16[768,1920]{1,0:T(8,128)(2,1)S(1)} %get-tuple-element.42.dense_ref, bf16[384,512]{1,0:T(8,128)(2,1)S(1)} %collective-permute-done.2.refs_0_, bf16[384,512]{1,0:T(8,128)(2,1)S(1)} %collective-permute-done.3.refs_1_, bf16[384,512]{1,0:T(8,128)(2,1)S(1)} %copy-done.2, ...), custom_call_target="tpu_custom_call" | custom-call | tf_op jit(solution)/shard_map/pallas_call | solution.py:16
  26.2 0.9 %collective-permute-start.6 = (f32[384,512]{1,0:T(8,128)S(1)}, f32[384,512]{1,0:T(8,128)S(1)}, u32[]{:S(2)}, u32[]{:S(2)}) collective-permute-start(f32[384,512]{1,0:T(8,128)S(1)} %shard_map.122), channel_id=1, source_target_pairs={{0,1},{1,0},{2,3},{3,2},{4,5},{5,4},{6,7},{7,6},{8,9},{9,8},{10,11... | collective-permute-start | bytes 2359304 | tf_op jit(solution)/shard_map/ppermute | solution.py:318
  27.2 1.9 %collective-permute-done.6.mate_ref = f32[384,512]{1,0:T(8,128)S(1)} collective-permute-done((f32[384,512]{1,0:T(8,128)S(1)}, f32[384,512]{1,0:T(8,128)S(1)}, u32[]{:S(2)}, u32[]{:S(2)}) %collective-permute-start.6) | collective-permute-done | bytes 786464 | tf_op jit(solution)/shard_map/ppermute | solution.py:318
  29.1 1.4 %shard_map.123 = (bf16[384,512]{1,0:T(8,128)(2,1)}, bf16[384,512]{1,0:T(8,128)(2,1)S(1)}, f32[4,80,512]{2,1,0:T(8,128)S(1)}, bf16[4,80,512]{2,1,0:T(8,128)(2,1)S(1)}) custom-call(s32[1]{0:T(128)} %bitcast.spot_ref.refs_0_, f32[768,512]{1,0:T(8,128)S(1)} %shard_map.121.refs_0_.own_ref, f32[384,512]{1,0:T(8,128)S(1)} %collective-permute-done.6.mate_ref, ...), custom_call_target="tpu_custom_call" | custom-call | tf_op jit(solution)/shard_map/pallas_call | solution.py:16
  31.0 1.7 %collective-permute-done.7.got_ref = bf16[4,80,512]{2,1,0:T(8,128)(2,1)S(1)} collective-permute-done((bf16[4,80,512]{2,1,0:T(8,128)(2,1)S(1)}, bf16[4,80,512]{2,1,0:T(8,128)(2,1)S(1)}, u32[]{:S(2)}, u32[]{:S(2)}) %collective-permute-start.7) | collective-permute-done | bytes 327712 | tf_op jit(solution)/shard_map/ppermute | solution.py:318
  32.8 2.1 %collective-permute-start.10 = (bf16[80,512]{1,0:T(8,128)(2,1)S(1)}, bf16[80,512]{1,0:T(8,128)(2,1)S(1)}, u32[]{:S(2)}, u32[]{:S(2)}) collective-permute-start(bf16[80,512]{1,0:T(8,128)(2,1)S(1)} %get-tuple-element.49), channel_id=1, source_target_pairs={{0,6},{1,7},{2,4},{3,5},{4,2},{5,3},{6,0},{7,1},{8,14},{9,15},{10,... | collective-permute-start | bytes 245768 | tf_op jit(solution)/shard_map/ppermute | solution.py:318
  34.9 1.2 %collective-permute-start.8 = (bf16[80,512]{1,0:T(8,128)(2,1)S(1)}, bf16[80,512]{1,0:T(8,128)(2,1)S(1)}, u32[]{:S(2)}, u32[]{:S(2)}) collective-permute-start(bf16[80,512]{1,0:T(8,128)(2,1)S(1)} %get-tuple-element.47), channel_id=1, source_target_pairs={{0,2},{1,3},{2,0},{3,1},{4,6},{5,7},{6,4},{7,5},{8,10},{9,11},{10,... | collective-permute-start | bytes 245768 | tf_op jit(solution)/shard_map/ppermute | solution.py:318
  36.1 1.5 %shard_map.125 = (bf16[384,512]{1,0:T(8,128)(2,1)S(1)}, bf16[384,512]{1,0:T(8,128)(2,1)S(1)}, f32[384,512]{1,0:T(8,128)S(1)}) custom-call(s32[1]{0:T(128)} %bitcast.spot_ref.refs_0_, s32[40]{0:T(128)S(1)} %copy-done.5, bf16[1920,768]{1,0:T(8,128)(2,1)S(1)} %get-tuple-element.50.refs_2_, bf16[384,512]{1,0:T(8,128)(2,1)S(1)} %get-tuple-element.51.refs_3_, ...), custom_call_target="tpu_custom_call" | custom-call | flops 10000000000 | tf_op jit(solution)/shard_map/pallas_call | solution.py:16
  37.6 3.4 %collective-permute-start.15 = (bf16[384,512]{1,0:T(8,128)(2,1)S(1)}, bf16[384,512]{1,0:T(8,128)(2,1)S(1)}, u32[]{:S(2)}, u32[]{:S(2)}) collective-permute-start(bf16[384,512]{1,0:T(8,128)(2,1)S(1)} %get-tuple-element.60), channel_id=1, source_target_pairs={{1,25},{3,7},{9,1},{11,15},{17,9},{19,23},{25,17},{27,31}} | collective-permute-start | bytes 1179656 | tf_op jit(solution)/shard_map/ppermute | solution.py:268
  41.2 1.4 %collective-permute-start.12 = (bf16[80,512]{1,0:T(8,128)(2,1)S(1)}, bf16[80,512]{1,0:T(8,128)(2,1)S(1)}, u32[]{:S(2)}, u32[]{:S(2)}) collective-permute-start(bf16[80,512]{1,0:T(8,128)(2,1)S(1)} %shard_map.126.refs_0_), channel_id=1, source_target_pairs={{0,8},{1,9},{2,10},{3,11},{4,12},{5,13},{6,14},{7,15},{8,0},{9,1},... | collective-permute-start | bytes 245768 | tf_op jit(solution)/shard_map/ppermute | solution.py:318
  42.6 1.3 %collective-permute-start.14 = (bf16[80,512]{1,0:T(8,128)(2,1)S(1)}, bf16[80,512]{1,0:T(8,128)(2,1)S(1)}, u32[]{:S(2)}, u32[]{:S(2)}) collective-permute-start(bf16[80,512]{1,0:T(8,128)(2,1)S(1)} %shard_map.126.refs_0_), channel_id=1, source_target_pairs={{0,24},{1,25},{2,26},{3,27},{4,28},{5,29},{6,30},{7,31},{8,16},{9,... | collective-permute-start | bytes 245768 | tf_op jit(solution)/shard_map/ppermute | solution.py:318
  43.9 1.9 %shard_map.127 = (f32[384,512]{1,0:T(8,128)S(1)}, f32[384,512]{1,0:T(8,128)S(1)}, f32[384,512]{1,0:T(8,128)S(1)}) custom-call(s32[1]{0:T(128)} %bitcast.spot_ref.refs_0_, s32[40]{0:T(128)S(1)} %copy-done.5, bf16[1920,768]{1,0:T(8,128)(2,1)S(1)} %get-tuple-element.50.refs_2_, bf16[384,512]{1,0:T(8,128)(2,1)S(1)} %get-tuple-element.51.refs_3_, ...), custom_call_target="tpu_custom_call" | custom-call | flops 10000000000 | tf_op jit(solution)/shard_map/pallas_call | solution.py:16
  45.8 4.1 %collective-permute-done.16.refs_1_.refs_2_ = bf16[384,512]{1,0:T(8,128)(2,1)S(1)} collective-permute-done((bf16[384,512]{1,0:T(8,128)(2,1)S(1)}, bf16[384,512]{1,0:T(8,128)(2,1)S(1)}, u32[]{:S(2)}, u32[]{:S(2)}) %collective-permute-start.16) | collective-permute-done | bytes 393248 | tf_op jit(solution)/shard_map/ppermute | solution.py:268
  50.1 3.2 %collective-permute-start.20 = (bf16[384,512]{1,0:T(8,128)(2,1)S(1)}, bf16[384,512]{1,0:T(8,128)(2,1)S(1)}, u32[]{:S(2)}, u32[]{:S(2)}) collective-permute-start(bf16[384,512]{1,0:T(8,128)(2,1)S(1)} %shard_map.129), channel_id=1, source_target_pairs={{0,24},{2,26},{3,11},{4,12},{5,29},{6,14},{7,31},{8,0},{10,2},{11,... | collective-permute-start | bytes 1179656 | tf_op jit(solution)/shard_map/ppermute | solution.py:268
  54.1 5.8 %collective-permute-start.17 = (bf16[64,512]{1,0:T(8,128)(2,1)S(1)}, bf16[64,512]{1,0:T(8,128)(2,1)S(1)}, u32[]{:S(2)}, u32[]{:S(2)}) collective-permute-start(bf16[64,512]{1,0:T(8,128)(2,1)S(1)} %get-tuple-element.65.refs_0_), channel_id=1, source_target_pairs={{0,2},{1,3},{2,0},{3,1},{4,6},{5,7},{6,4},{7,5},{8,10},{9,11},{10,... | collective-permute-start | bytes 196616 | tf_op jit(solution)/shard_map/ppermute | solution.py:318
  59.9 1.2 %collective-permute-start.19 = (bf16[64,512]{1,0:T(8,128)(2,1)S(1)}, bf16[64,512]{1,0:T(8,128)(2,1)S(1)}, u32[]{:S(2)}, u32[]{:S(2)}) collective-permute-start(bf16[64,512]{1,0:T(8,128)(2,1)S(1)} %get-tuple-element.65.refs_0_), channel_id=1, source_target_pairs={{0,6},{1,7},{2,4},{3,5},{4,2},{5,3},{6,0},{7,1},{8,14},{9,15},{10,... | collective-permute-start | bytes 196616 | tf_op jit(solution)/shard_map/ppermute | solution.py:318
  61.3 1.8 %collective-permute-done.20.refs_1_.refs_3_ = bf16[384,512]{1,0:T(8,128)(2,1)S(1)} collective-permute-done((bf16[384,512]{1,0:T(8,128)(2,1)S(1)}, bf16[384,512]{1,0:T(8,128)(2,1)S(1)}, u32[]{:S(2)}, u32[]{:S(2)}) %collective-permute-start.20) | collective-permute-done | bytes 393248 | tf_op jit(solution)/shard_map/ppermute | solution.py:268
  63.9 7.3 %collective-permute-done.21.refs_1_ = bf16[384,512]{1,0:T(8,128)(2,1)S(1)} collective-permute-done((bf16[384,512]{1,0:T(8,128)(2,1)S(1)}, bf16[384,512]{1,0:T(8,128)(2,1)S(1)}, u32[]{:S(2)}, u32[]{:S(2)}) %collective-permute-start.21) | collective-permute-done | bytes 393248 | tf_op jit(solution)/shard_map/ppermute | solution.py:268
  71.3 4.3 %collective-permute-start.22 = (bf16[256,512]{1,0:T(8,128)(2,1)S(1)}, bf16[256,512]{1,0:T(8,128)(2,1)S(1)}, u32[]{:S(2)}, u32[]{:S(2)}) collective-permute-start(bf16[256,512]{1,0:T(8,128)(2,1)S(1)} %shard_map.132.mine_ref), channel_id=1, source_target_pairs={{0,1},{1,0},{2,3},{3,2},{4,5},{5,4},{6,7},{7,6},{8,9},{9,8},{10,11... | collective-permute-start | bytes 786440 | tf_op jit(solution)/shard_map/ppermute | solution.py:318
  75.6 1.2 %collective-permute-done.22.other_ref = bf16[256,512]{1,0:T(8,128)(2,1)S(1)} collective-permute-done((bf16[256,512]{1,0:T(8,128)(2,1)S(1)}, bf16[256,512]{1,0:T(8,128)(2,1)S(1)}, u32[]{:S(2)}, u32[]{:S(2)}) %collective-permute-start.22) | collective-permute-done | bytes 262176 | tf_op jit(solution)/shard_map/ppermute | solution.py:318
  76.8 1.0 %shard_map.133 = f32[512,512]{1,0:T(8,128)} custom-call(s32[1]{0:T(128)} %bitcast.spot_ref.refs_0_, bf16[256,512]{1,0:T(8,128)(2,1)S(1)} %shard_map.132.mine_ref, bf16[256,512]{1,0:T(8,128)(2,1)S(1)} %collective-permute-done.22.other_ref), custom_call_target="tpu_custom_call" | custom-call | tf_op jit(solution)/shard_map/pallas_call | solution.py:16
  77.8 1.0 %shard_map.134 = bf16[384,512]{1,0:T(8,128)(2,1)} custom-call(s32[1]{0:T(128)} %bitcast.spot_ref.refs_0_, f32[384,512]{1,0:T(8,128)S(1)} %get-tuple-element.72.refs_0_, bf16[384,512]{1,0:T(8,128)(2,1)S(1)} %collective-permute-done.21.refs_1_, bf16[384,512]{1,0:T(8,128)(2,1)S(1)} %collective-permute-done.23.refs_2_, ...), custom_call_target="tpu_custom_call" | custom-call | flops 10000000000 | tf_op jit(solution)/shard_map/pallas_call | solution.py:16
  (47 shorter events, 4.4 us)
Async XLA Ops:
  0.6 4.4 %collective-permute-start = (bf16[8,7,128,128]{3,2,1,0:T(8,128)(2,1)}, bf16[8,7,128,128]{3,2,1,0:T(8,128)(2,1)S(1)}, u32[]{:S(2)}, u32[]{:S(2)}) collective-permute-start(bf16[8,7,128,128]{3,2,1,0:T(8,128)(2,1)} %bitcast.7), channel_id=1, source_target_pairs={{0,1},{1,0},{2,3},{3,2},{4,5},{5,4},{6,7},{7,6},{8,9},{9,8},{10,11... | collective-permute-start | bytes 5505032 | tf_op jit(solution)/shard_map/ppermute | solution.py:318
  1.4 22.7 %collective-permute-start.2 = (bf16[384,512]{1,0:T(8,128)(2,1)}, bf16[384,512]{1,0:T(8,128)(2,1)S(1)}, u32[]{:S(2)}, u32[]{:S(2)}) collective-permute-start(bf16[384,512]{1,0:T(8,128)(2,1)} %refs_2_.1), channel_id=1, source_target_pairs={{0,4},{1,5},{2,6},{3,7},{4,8},{5,9},{6,10},{7,11},{8,12},{9,13},{1... | collective-permute-start | bytes 1179656 | tf_op jit(solution)/shard_map/ppermute | solution.py:221
  2.6 21.4 %collective-permute-start.3 = (bf16[384,512]{1,0:T(8,128)(2,1)}, bf16[384,512]{1,0:T(8,128)(2,1)S(1)}, u32[]{:S(2)}, u32[]{:S(2)}) collective-permute-start(bf16[384,512]{1,0:T(8,128)(2,1)} %refs_2_.1), channel_id=1, source_target_pairs={{0,2},{1,3},{2,4},{3,5},{4,6},{5,7},{6,8},{7,9},{8,10},{9,11},{10,... | collective-permute-start | bytes 1179656 | tf_op jit(solution)/shard_map/ppermute | solution.py:221
  3.8 20.2 %collective-permute-start.4 = (bf16[384,512]{1,0:T(8,128)(2,1)}, bf16[384,512]{1,0:T(8,128)(2,1)S(1)}, u32[]{:S(2)}, u32[]{:S(2)}) collective-permute-start(bf16[384,512]{1,0:T(8,128)(2,1)} %refs_2_.1), channel_id=1, source_target_pairs={{0,30},{1,31},{2,0},{3,1},{4,2},{5,3},{6,4},{7,5},{8,6},{9,7},{10,... | collective-permute-start | bytes 1179656 | tf_op jit(solution)/shard_map/ppermute | solution.py:221
  4.1 21.8 %collective-permute-start.5 = (bf16[384,512]{1,0:T(8,128)(2,1)}, bf16[384,512]{1,0:T(8,128)(2,1)S(1)}, u32[]{:S(2)}, u32[]{:S(2)}) collective-permute-start(bf16[384,512]{1,0:T(8,128)(2,1)} %refs_2_.1), channel_id=1, source_target_pairs={{0,28},{2,30},{4,0},{6,2},{8,4},{10,6},{12,8},{14,10},{16,12},{18,... | collective-permute-start | bytes 1179656 | tf_op jit(solution)/shard_map/ppermute | solution.py:221
  6.5 4.1 %collective-permute-start.1 = (s32[120]{0:T(128)S(1)}, s32[120]{0:T(128)S(1)}, u32[]{:S(2)}, u32[]{:S(2)}) collective-permute-start(s32[120]{0:T(128)S(1)} %reshape.27.own_meta_ref), channel_id=1, source_target_pairs={{0,1},{1,0},{2,3},{3,2},{4,5},{5,4},{6,7},{7,6},{8,9},{9,8},{10,11... | collective-permute-start | bytes 1448 | tf_op jit(solution)/shard_map/ppermute | solution.py:318
  10.7 1.5 %copy-start = (bf16[1,8,7,128,128]{4,3,2,1,0:T(8,128)(2,1)S(1)}, bf16[1,8,7,128,128]{4,3,2,1,0:T(8,128)(2,1)}, u32[]{:S(2)}) copy-start(bf16[1,8,7,128,128]{4,3,2,1,0:T(8,128)(2,1)} %param.12) | copy-start | bytes 5505028
  12.2 11.9 %copy-start.2 = (bf16[384,512]{1,0:T(8,128)(2,1)S(1)}, bf16[384,512]{1,0:T(8,128)(2,1)}, u32[]{:S(2)}) copy-start(bf16[384,512]{1,0:T(8,128)(2,1)} %refs_2_.1) | copy-start | bytes 1179652
  25.8 3.3 %copy-start.1 = (bf16[512,512]{1,0:T(8,128)(2,1)S(1)}, bf16[512,512]{1,0:T(8,128)(2,1)}, u32[]{:S(2)}) copy-start(bf16[512,512]{1,0:T(8,128)(2,1)} %weight_ref.1) | copy-start | bytes 1572868
  25.8 3.2 %copy-start.3 = (bf16[384,512]{1,0:T(8,128)(2,1)S(1)}, bf16[384,512]{1,0:T(8,128)(2,1)}, u32[]{:S(2)}) copy-start(bf16[384,512]{1,0:T(8,128)(2,1)} %grad_out_ref.1) | copy-start | bytes 1179652
  25.9 3.2 %copy-start.4 = (f32[512]{0:T(512)S(1)}, f32[512]{0:T(512)}, u32[]{:S(2)}) copy-start(f32[512]{0:T(512)} %param.14) | copy-start | bytes 6148
  26.2 2.8 %collective-permute-start.6 = (f32[384,512]{1,0:T(8,128)S(1)}, f32[384,512]{1,0:T(8,128)S(1)}, u32[]{:S(2)}, u32[]{:S(2)}) collective-permute-start(f32[384,512]{1,0:T(8,128)S(1)} %shard_map.122), channel_id=1, source_target_pairs={{0,1},{1,0},{2,3},{3,2},{4,5},{5,4},{6,7},{7,6},{8,9},{9,8},{10,11... | collective-permute-start | bytes 2359304 | tf_op jit(solution)/shard_map/ppermute | solution.py:318
  29.1 7.0 %copy-start.5 = (s32[40]{0:T(128)S(1)}, s32[40]{0:T(128)}, u32[]{:S(2)}) copy-start(s32[40]{0:T(128)} %constant.23.refs_1_) | copy-start | bytes 484
  30.5 5.6 %collective-permute-start.11 = (bf16[384,512]{1,0:T(8,128)(2,1)S(1)}, bf16[384,512]{1,0:T(8,128)(2,1)S(1)}, u32[]{:S(2)}, u32[]{:S(2)}) collective-permute-start(bf16[384,512]{1,0:T(8,128)(2,1)S(1)} %get-tuple-element.51.refs_3_), channel_id=1, source_target_pairs={{0,1},{1,0},{2,3},{3,2},{4,5},{5,4},{6,7},{7,6},{8,9},{9,8},{10,11... | collective-permute-start | bytes 1179656 | tf_op jit(solution)/shard_map/ppermute | solution.py:318
  30.9 1.8 %collective-permute-start.7 = (bf16[4,80,512]{2,1,0:T(8,128)(2,1)S(1)}, bf16[4,80,512]{2,1,0:T(8,128)(2,1)S(1)}, u32[]{:S(2)}, u32[]{:S(2)}) collective-permute-start(bf16[4,80,512]{2,1,0:T(8,128)(2,1)S(1)} %get-tuple-element.45), channel_id=1, source_target_pairs={{0,1},{1,0},{2,3},{3,2},{4,5},{5,4},{6,7},{7,6},{8,9},{9,8},{10,11... | collective-permute-start | bytes 983048 | tf_op jit(solution)/shard_map/ppermute | solution.py:318
  32.8 8.4 %collective-permute-start.10 = (bf16[80,512]{1,0:T(8,128)(2,1)S(1)}, bf16[80,512]{1,0:T(8,128)(2,1)S(1)}, u32[]{:S(2)}, u32[]{:S(2)}) collective-permute-start(bf16[80,512]{1,0:T(8,128)(2,1)S(1)} %get-tuple-element.49), channel_id=1, source_target_pairs={{0,6},{1,7},{2,4},{3,5},{4,2},{5,3},{6,0},{7,1},{8,14},{9,15},{10,... | collective-permute-start | bytes 245768 | tf_op jit(solution)/shard_map/ppermute | solution.py:318
  34.9 6.2 %collective-permute-start.8 = (bf16[80,512]{1,0:T(8,128)(2,1)S(1)}, bf16[80,512]{1,0:T(8,128)(2,1)S(1)}, u32[]{:S(2)}, u32[]{:S(2)}) collective-permute-start(bf16[80,512]{1,0:T(8,128)(2,1)S(1)} %get-tuple-element.47), channel_id=1, source_target_pairs={{0,2},{1,3},{2,0},{3,1},{4,6},{5,7},{6,4},{7,5},{8,10},{9,11},{10,... | collective-permute-start | bytes 245768 | tf_op jit(solution)/shard_map/ppermute | solution.py:318
  36.1 5.0 %collective-permute-start.9 = (bf16[80,512]{1,0:T(8,128)(2,1)S(1)}, bf16[80,512]{1,0:T(8,128)(2,1)S(1)}, u32[]{:S(2)}, u32[]{:S(2)}) collective-permute-start(bf16[80,512]{1,0:T(8,128)(2,1)S(1)} %get-tuple-element.48), channel_id=1, source_target_pairs={{0,4},{1,5},{2,6},{3,7},{4,0},{5,1},{6,2},{7,3},{8,12},{9,13},{10,... | collective-permute-start | bytes 245768 | tf_op jit(solution)/shard_map/ppermute | solution.py:318
  37.6 8.2 %collective-permute-start.15 = (bf16[384,512]{1,0:T(8,128)(2,1)S(1)}, bf16[384,512]{1,0:T(8,128)(2,1)S(1)}, u32[]{:S(2)}, u32[]{:S(2)}) collective-permute-start(bf16[384,512]{1,0:T(8,128)(2,1)S(1)} %get-tuple-element.60), channel_id=1, source_target_pairs={{1,25},{3,7},{9,1},{11,15},{17,9},{19,23},{25,17},{27,31}} | collective-permute-start | bytes 1179656 | tf_op jit(solution)/shard_map/ppermute | solution.py:268
  41.0 8.9 %collective-permute-start.16 = (bf16[384,512]{1,0:T(8,128)(2,1)S(1)}, bf16[384,512]{1,0:T(8,128)(2,1)S(1)}, u32[]{:S(2)}, u32[]{:S(2)}) collective-permute-start(bf16[384,512]{1,0:T(8,128)(2,1)S(1)} %get-tuple-element.53), channel_id=1, source_target_pairs={{0,2},{1,5},{2,0},{3,7},{4,6},{5,1},{6,4},{7,3},{8,10},{9,13},{10,... | collective-permute-start | bytes 1179656 | tf_op jit(solution)/shard_map/ppermute | solution.py:268
  41.2 12.2 %collective-permute-start.12 = (bf16[80,512]{1,0:T(8,128)(2,1)S(1)}, bf16[80,512]{1,0:T(8,128)(2,1)S(1)}, u32[]{:S(2)}, u32[]{:S(2)}) collective-permute-start(bf16[80,512]{1,0:T(8,128)(2,1)S(1)} %shard_map.126.refs_0_), channel_id=1, source_target_pairs={{0,8},{1,9},{2,10},{3,11},{4,12},{5,13},{6,14},{7,15},{8,0},{9,1},... | collective-permute-start | bytes 245768 | tf_op jit(solution)/shard_map/ppermute | solution.py:318
  42.6 10.9 %collective-permute-start.13 = (bf16[80,512]{1,0:T(8,128)(2,1)S(1)}, bf16[80,512]{1,0:T(8,128)(2,1)S(1)}, u32[]{:S(2)}, u32[]{:S(2)}) collective-permute-start(bf16[80,512]{1,0:T(8,128)(2,1)S(1)} %shard_map.126.refs_0_), channel_id=1, source_target_pairs={{0,16},{1,17},{2,18},{3,19},{4,20},{5,21},{6,22},{7,23},{8,24},{9,... | collective-permute-start | bytes 245768 | tf_op jit(solution)/shard_map/ppermute | solution.py:318
  42.6 10.8 %collective-permute-start.14 = (bf16[80,512]{1,0:T(8,128)(2,1)S(1)}, bf16[80,512]{1,0:T(8,128)(2,1)S(1)}, u32[]{:S(2)}, u32[]{:S(2)}) collective-permute-start(bf16[80,512]{1,0:T(8,128)(2,1)S(1)} %shard_map.126.refs_0_), channel_id=1, source_target_pairs={{0,24},{1,25},{2,26},{3,27},{4,28},{5,29},{6,30},{7,31},{8,16},{9,... | collective-permute-start | bytes 245768 | tf_op jit(solution)/shard_map/ppermute | solution.py:318
  50.1 13.0 %collective-permute-start.20 = (bf16[384,512]{1,0:T(8,128)(2,1)S(1)}, bf16[384,512]{1,0:T(8,128)(2,1)S(1)}, u32[]{:S(2)}, u32[]{:S(2)}) collective-permute-start(bf16[384,512]{1,0:T(8,128)(2,1)S(1)} %shard_map.129), channel_id=1, source_target_pairs={{0,24},{2,26},{3,11},{4,12},{5,29},{6,14},{7,31},{8,0},{10,2},{11,... | collective-permute-start | bytes 1179656 | tf_op jit(solution)/shard_map/ppermute | solution.py:268
  54.1 9.4 %collective-permute-start.17 = (bf16[64,512]{1,0:T(8,128)(2,1)S(1)}, bf16[64,512]{1,0:T(8,128)(2,1)S(1)}, u32[]{:S(2)}, u32[]{:S(2)}) collective-permute-start(bf16[64,512]{1,0:T(8,128)(2,1)S(1)} %get-tuple-element.65.refs_0_), channel_id=1, source_target_pairs={{0,2},{1,3},{2,0},{3,1},{4,6},{5,7},{6,4},{7,5},{8,10},{9,11},{10,... | collective-permute-start | bytes 196616 | tf_op jit(solution)/shard_map/ppermute | solution.py:318
  59.9 3.5 %collective-permute-start.18 = (bf16[64,512]{1,0:T(8,128)(2,1)S(1)}, bf16[64,512]{1,0:T(8,128)(2,1)S(1)}, u32[]{:S(2)}, u32[]{:S(2)}) collective-permute-start(bf16[64,512]{1,0:T(8,128)(2,1)S(1)} %get-tuple-element.65.refs_0_), channel_id=1, source_target_pairs={{0,4},{1,5},{2,6},{3,7},{4,0},{5,1},{6,2},{7,3},{8,12},{9,13},{10,... | collective-permute-start | bytes 196616 | tf_op jit(solution)/shard_map/ppermute | solution.py:318
  59.9 4.1 %collective-permute-start.19 = (bf16[64,512]{1,0:T(8,128)(2,1)S(1)}, bf16[64,512]{1,0:T(8,128)(2,1)S(1)}, u32[]{:S(2)}, u32[]{:S(2)}) collective-permute-start(bf16[64,512]{1,0:T(8,128)(2,1)S(1)} %get-tuple-element.65.refs_0_), channel_id=1, source_target_pairs={{0,6},{1,7},{2,4},{3,5},{4,2},{5,3},{6,0},{7,1},{8,14},{9,15},{10,... | collective-permute-start | bytes 196616 | tf_op jit(solution)/shard_map/ppermute | solution.py:318
  61.1 10.2 %collective-permute-start.21 = (bf16[384,512]{1,0:T(8,128)(2,1)S(1)}, bf16[384,512]{1,0:T(8,128)(2,1)S(1)}, u32[]{:S(2)}, u32[]{:S(2)}) collective-permute-start(bf16[384,512]{1,0:T(8,128)(2,1)S(1)} %shard_map.128), channel_id=1, source_target_pairs={{0,2},{1,5},{2,0},{3,7},{4,6},{5,1},{6,4},{7,3},{8,10},{9,13},{10,... | collective-permute-start | bytes 1179656 | tf_op jit(solution)/shard_map/ppermute | solution.py:268
  63.3 14.5 %collective-permute-start.23 = (bf16[384,512]{1,0:T(8,128)(2,1)S(1)}, bf16[384,512]{1,0:T(8,128)(2,1)S(1)}, u32[]{:S(2)}, u32[]{:S(2)}) collective-permute-start(bf16[384,512]{1,0:T(8,128)(2,1)S(1)} %shard_map.131), channel_id=1, source_target_pairs={{0,4},{1,3},{2,6},{3,1},{4,0},{5,7},{6,2},{7,5},{8,12},{9,11},{10,... | collective-permute-start | bytes 1179656 | tf_op jit(solution)/shard_map/ppermute | solution.py:268
  71.3 5.4 %collective-permute-start.22 = (bf16[256,512]{1,0:T(8,128)(2,1)S(1)}, bf16[256,512]{1,0:T(8,128)(2,1)S(1)}, u32[]{:S(2)}, u32[]{:S(2)}) collective-permute-start(bf16[256,512]{1,0:T(8,128)(2,1)S(1)} %shard_map.132.mine_ref), channel_id=1, source_target_pairs={{0,1},{1,0},{2,3},{3,2},{4,5},{5,4},{6,7},{7,6},{8,9},{9,8},{10,11... | collective-permute-start | bytes 786440 | tf_op jit(solution)/shard_map/ppermute | solution.py:318

commit v12 on v11

--- a/solution.py
+++ b/solution.py
@@ -290,12 +290,12 @@
             self.second = self.routed(second, straight)
             return [second, out]
         if k == 2:
-            _, rest = after(token, self.to_across)
+            _, rest, _ = after(token, self.to_across, self.second)
             out = summed_terms(
                 self.spot, [rest, self.from_planes, self.from_last], [None, self.EVEN | 0b00101000, self.ENDS]
             )
             self.first = self.routed(out, across)
-            return [out, self.second]
+            return [out]
         return []
 
     def finish(self, token):

time: 79 us -> 73.8 us (0.934)
  the two profiles are of different devices: /device:TPU:19 before, /device:TPU:0 now
where the time goes in v12:
time: 73.8 us; the launch traced here: 73.6 us
  starting transfers between devices  37 us (50%)
  waiting for transfers between devices  18.2 us (25%)
  Pallas kernels  14.4 us (20%)
  local copies, waits for them, and re-layouts  2.4 us (3%)
  between operations  0.86 us (1%)
    pallas_call x15, Pallas kernels, call(): pl.pallas_call(kernel, out_shape=out_shape, in_specs=[spec(k) for k in ra...  14.4 us
    ppermute x5, starting transfers between devices, routed(): return lax.ppermute(value, 'blk', pairs)  13.8 us
    ppermute x15, starting transfers between devices, swapped(): return lax.ppermute(value, 'blk', [(s, s ^ distance) for s in range(count)])  12.7 us
    ppermute x4, starting transfers between devices, sent(): return lax.ppermute(value, 'blk', pairs)  10.5 us
    ppermute x4, waiting for transfers between devices, sent(): return lax.ppermute(value, 'blk', pairs)  7.42 us
    ppermute x15, waiting for transfers between devices, swapped(): return lax.ppermute(value, 'blk', [(s, s ^ distance) for s in range(count)])  6.6 us
    ppermute x5, waiting for transfers between devices, routed(): return lax.ppermute(value, 'blk', pairs)  4.23 us
    unnamed x12, local copies, waits for them, and re-layouts  1.53 us
  transfers between devices with their start and end apart: 24, of which 9 were waited for; matrix products, arithmetic and copies ran while one was open for 2% of the time, Pallas kernels for 16%

profile of v12, /device:TPU:0, one launch (start us, length us, event | category | flops | bytes accessed | tf_op | source)
XLA Modules:
  0.0 73.6 jit_solution(6045001743076861340)
XLA Ops:
  1.1 2.6 %collective-permute-start.2 = (bf16[384,512]{1,0:T(8,128)(2,1)}, bf16[384,512]{1,0:T(8,128)(2,1)S(1)}, u32[]{:S(2)}, u32[]{:S(2)}) collective-permute-start(bf16[384,512]{1,0:T(8,128)(2,1)} %refs_2_.1), channel_id=1, source_target_pairs={{0,4},{1,5},{2,6},{3,7},{4,8},{5,9},{6,10},{7,11},{8,12},{9,13},{1... | collective-permute-start | bytes 1179656 | tf_op jit(solution)/shard_map/ppermute | solution.py:221
  3.7 1.5 %collective-permute-start.3 = (bf16[384,512]{1,0:T(8,128)(2,1)}, bf16[384,512]{1,0:T(8,128)(2,1)S(1)}, u32[]{:S(2)}, u32[]{:S(2)}) collective-permute-start(bf16[384,512]{1,0:T(8,128)(2,1)} %refs_2_.1), channel_id=1, source_target_pairs={{0,2},{1,3},{2,4},{3,5},{4,6},{5,7},{6,8},{7,9},{8,10},{9,11},{10,... | collective-permute-start | bytes 1179656 | tf_op jit(solution)/shard_map/ppermute | solution.py:221
  5.2 4.1 %collective-permute-start.4 = (bf16[384,512]{1,0:T(8,128)(2,1)}, bf16[384,512]{1,0:T(8,128)(2,1)S(1)}, u32[]{:S(2)}, u32[]{:S(2)}) collective-permute-start(bf16[384,512]{1,0:T(8,128)(2,1)} %refs_2_.1), channel_id=1, source_target_pairs={{0,30},{1,31},{2,0},{3,1},{4,2},{5,3},{6,4},{7,5},{8,6},{9,7},{10,... | collective-permute-start | bytes 1179656 | tf_op jit(solution)/shard_map/ppermute | solution.py:221
  9.4 2.3 %collective-permute-start.5 = (bf16[384,512]{1,0:T(8,128)(2,1)}, bf16[384,512]{1,0:T(8,128)(2,1)S(1)}, u32[]{:S(2)}, u32[]{:S(2)}) collective-permute-start(bf16[384,512]{1,0:T(8,128)(2,1)} %refs_2_.1), channel_id=1, source_target_pairs={{0,28},{2,30},{4,0},{6,2},{8,4},{10,6},{12,8},{14,10},{16,12},{18,... | collective-permute-start | bytes 1179656 | tf_op jit(solution)/shard_map/ppermute | solution.py:221
  11.7 0.7 reshape_squeeze.3
  13.3 1.1 %collective-permute-done.1.mate_meta_ref = s32[120]{0:T(128)S(1)} collective-permute-done((s32[120]{0:T(128)S(1)}, s32[120]{0:T(128)S(1)}, u32[]{:S(2)}, u32[]{:S(2)}) %collective-permute-start.1) | collective-permute-done | bytes 512 | tf_op jit(solution)/shard_map/ppermute | solution.py:318
  14.4 1.5 %copy-done = bf16[1,8,7,128,128]{4,3,2,1,0:T(8,128)(2,1)S(1)} copy-done((bf16[1,8,7,128,128]{4,3,2,1,0:T(8,128)(2,1)S(1)}, bf16[1,8,7,128,128]{4,3,2,1,0:T(8,128)(2,1)}, u32[]{:S(2)}) %copy-start) | copy-done | bytes 1835032
  15.9 4.2 %shard_map.120 = (bf16[768,1920]{1,0:T(8,128)(2,1)S(1)}, bf16[1920,768]{1,0:T(8,128)(2,1)S(1)}) custom-call(s32[1]{0:T(128)} %bitcast.spot_ref.refs_0_, s32[120]{0:T(128)S(1)} %reshape.27.own_meta_ref, s32[120]{0:T(128)S(1)} %collective-permute-done.1.mate_meta_ref, bf16[8,7,128,128]{3,2,1,0:T(8,128)(2,1)S(1)} %bitcast.8, ...), custom_call_target="tpu_custom_call" | custom-call | tf_op jit(solution)/shard_map/pallas_call | solution.py:16
  20.1 5.6 %collective-permute-done.2.refs_0_ = bf16[384,512]{1,0:T(8,128)(2,1)S(1)} collective-permute-done((bf16[384,512]{1,0:T(8,128)(2,1)}, bf16[384,512]{1,0:T(8,128)(2,1)S(1)}, u32[]{:S(2)}, u32[]{:S(2)}) %collective-permute-start.2) | collective-permute-done | bytes 393248 | tf_op jit(solution)/shard_map/ppermute | solution.py:221
  26.3 1.8 %shard_map.121.refs_0_.own_ref = f32[768,512]{1,0:T(8,128)S(1)} custom-call(bf16[768,1920]{1,0:T(8,128)(2,1)S(1)} %get-tuple-element.42.dense_ref, bf16[384,512]{1,0:T(8,128)(2,1)S(1)} %collective-permute-done.2.refs_0_, bf16[384,512]{1,0:T(8,128)(2,1)S(1)} %collective-permute-done.3.refs_1_, bf16[384,512]{1,0:T(8,128)(2,1)S(1)} %copy-done.2, ...), custom_call_target="tpu_custom_call" | custom-call | tf_op jit(solution)/shard_map/pallas_call | solution.py:16
  28.1 1.2 %collective-permute-done.5.refs_1_ = bf16[384,512]{1,0:T(8,128)(2,1)S(1)} collective-permute-done((bf16[384,512]{1,0:T(8,128)(2,1)}, bf16[384,512]{1,0:T(8,128)(2,1)S(1)}, u32[]{:S(2)}, u32[]{:S(2)}) %collective-permute-start.5) | collective-permute-done | bytes 393248 | tf_op jit(solution)/shard_map/ppermute | solution.py:221
  29.8 2.3 %collective-permute-done.6.mate_ref = f32[384,512]{1,0:T(8,128)S(1)} collective-permute-done((f32[384,512]{1,0:T(8,128)S(1)}, f32[384,512]{1,0:T(8,128)S(1)}, u32[]{:S(2)}, u32[]{:S(2)}) %collective-permute-start.6) | collective-permute-done | bytes 786464 | tf_op jit(solution)/shard_map/ppermute | solution.py:318
  32.1 1.4 %shard_map.123 = (bf16[384,512]{1,0:T(8,128)(2,1)}, bf16[384,512]{1,0:T(8,128)(2,1)S(1)}, f32[4,80,512]{2,1,0:T(8,128)S(1)}, bf16[4,80,512]{2,1,0:T(8,128)(2,1)S(1)}) custom-call(s32[1]{0:T(128)} %bitcast.spot_ref.refs_0_, f32[768,512]{1,0:T(8,128)S(1)} %shard_map.121.refs_0_.own_ref, f32[384,512]{1,0:T(8,128)S(1)} %collective-permute-done.6.mate_ref, ...), custom_call_target="tpu_custom_call" | custom-call | tf_op jit(solution)/shard_map/pallas_call | solution.py:16
  34.0 1.7 %collective-permute-done.7.got_ref = bf16[4,80,512]{2,1,0:T(8,128)(2,1)S(1)} collective-permute-done((bf16[4,80,512]{2,1,0:T(8,128)(2,1)S(1)}, bf16[4,80,512]{2,1,0:T(8,128)(2,1)S(1)}, u32[]{:S(2)}, u32[]{:S(2)}) %collective-permute-start.7) | collective-permute-done | bytes 327712 | tf_op jit(solution)/shard_map/ppermute | solution.py:318
  35.7 1.5 %collective-permute-start.10 = (bf16[80,512]{1,0:T(8,128)(2,1)S(1)}, bf16[80,512]{1,0:T(8,128)(2,1)S(1)}, u32[]{:S(2)}, u32[]{:S(2)}) collective-permute-start(bf16[80,512]{1,0:T(8,128)(2,1)S(1)} %get-tuple-element.49), channel_id=1, source_target_pairs={{0,6},{1,7},{2,4},{3,5},{4,2},{5,3},{6,0},{7,1},{8,14},{9,15},{10,... | collective-permute-start | bytes 245768 | tf_op jit(solution)/shard_map/ppermute | solution.py:318
  37.8 1.5 %collective-permute-start.9 = (bf16[80,512]{1,0:T(8,128)(2,1)S(1)}, bf16[80,512]{1,0:T(8,128)(2,1)S(1)}, u32[]{:S(2)}, u32[]{:S(2)}) collective-permute-start(bf16[80,512]{1,0:T(8,128)(2,1)S(1)} %get-tuple-element.48), channel_id=1, source_target_pairs={{0,4},{1,5},{2,6},{3,7},{4,0},{5,1},{6,2},{7,3},{8,12},{9,13},{10,... | collective-permute-start | bytes 245768 | tf_op jit(solution)/shard_map/ppermute | solution.py:318
  39.3 1.5 %shard_map.125 = (bf16[384,512]{1,0:T(8,128)(2,1)S(1)}, bf16[384,512]{1,0:T(8,128)(2,1)S(1)}, f32[384,512]{1,0:T(8,128)S(1)}) custom-call(s32[1]{0:T(128)} %bitcast.spot_ref.refs_0_, s32[40]{0:T(128)S(1)} %copy-done.5, bf16[1920,768]{1,0:T(8,128)(2,1)S(1)} %get-tuple-element.50.refs_2_, bf16[384,512]{1,0:T(8,128)(2,1)S(1)} %get-tuple-element.51.refs_3_, ...), custom_call_target="tpu_custom_call" | custom-call | flops 10000000000 | tf_op jit(solution)/shard_map/pallas_call | solution.py:16
  40.8 0.7 collective-permute-start.15
  41.5 1.6 %collective-permute-start.16 = (bf16[384,512]{1,0:T(8,128)(2,1)S(1)}, bf16[384,512]{1,0:T(8,128)(2,1)S(1)}, u32[]{:S(2)}, u32[]{:S(2)}) collective-permute-start(bf16[384,512]{1,0:T(8,128)(2,1)S(1)} %get-tuple-element.53), channel_id=1, source_target_pairs={{0,2},{1,5},{2,0},{3,7},{4,6},{5,1},{6,4},{7,3},{8,10},{9,13},{10,... | collective-permute-start | bytes 1179656 | tf_op jit(solution)/shard_map/ppermute | solution.py:268
  43.1 0.8 %collective-permute-start.12 = (bf16[80,512]{1,0:T(8,128)(2,1)S(1)}, bf16[80,512]{1,0:T(8,128)(2,1)S(1)}, u32[]{:S(2)}, u32[]{:S(2)}) collective-permute-start(bf16[80,512]{1,0:T(8,128)(2,1)S(1)} %shard_map.126.refs_0_), channel_id=1, source_target_pairs={{0,8},{1,9},{2,10},{3,11},{4,12},{5,13},{6,14},{7,15},{8,0},{9,1},... | collective-permute-start | bytes 245768 | tf_op jit(solution)/shard_map/ppermute | solution.py:318
  43.9 2.2 %collective-permute-start.13 = (bf16[80,512]{1,0:T(8,128)(2,1)S(1)}, bf16[80,512]{1,0:T(8,128)(2,1)S(1)}, u32[]{:S(2)}, u32[]{:S(2)}) collective-permute-start(bf16[80,512]{1,0:T(8,128)(2,1)S(1)} %shard_map.126.refs_0_), channel_id=1, source_target_pairs={{0,16},{1,17},{2,18},{3,19},{4,20},{5,21},{6,22},{7,23},{8,24},{9,... | collective-permute-start | bytes 245768 | tf_op jit(solution)/shard_map/ppermute | solution.py:318
  46.2 1.4 %collective-permute-start.14 = (bf16[80,512]{1,0:T(8,128)(2,1)S(1)}, bf16[80,512]{1,0:T(8,128)(2,1)S(1)}, u32[]{:S(2)}, u32[]{:S(2)}) collective-permute-start(bf16[80,512]{1,0:T(8,128)(2,1)S(1)} %shard_map.126.refs_0_), channel_id=1, source_target_pairs={{0,24},{1,25},{2,26},{3,27},{4,28},{5,29},{6,30},{7,31},{8,16},{9,... | collective-permute-start | bytes 245768 | tf_op jit(solution)/shard_map/ppermute | solution.py:318
  47.6 1.9 %shard_map.127 = (f32[384,512]{1,0:T(8,128)S(1)}, f32[384,512]{1,0:T(8,128)S(1)}, f32[384,512]{1,0:T(8,128)S(1)}) custom-call(s32[1]{0:T(128)} %bitcast.spot_ref.refs_0_, s32[40]{0:T(128)S(1)} %copy-done.5, bf16[1920,768]{1,0:T(8,128)(2,1)S(1)} %get-tuple-element.50.refs_2_, bf16[384,512]{1,0:T(8,128)(2,1)S(1)} %get-tuple-element.51.refs_3_, ...), custom_call_target="tpu_custom_call" | custom-call | flops 10000000000 | tf_op jit(solution)/shard_map/pallas_call | solution.py:16
  49.6 1.4 %collective-permute-start.20 = (bf16[384,512]{1,0:T(8,128)(2,1)S(1)}, bf16[384,512]{1,0:T(8,128)(2,1)S(1)}, u32[]{:S(2)}, u32[]{:S(2)}) collective-permute-start(bf16[384,512]{1,0:T(8,128)(2,1)S(1)} %shard_map.128), channel_id=1, source_target_pairs={{0,2},{1,5},{2,0},{3,7},{4,6},{5,1},{6,4},{7,3},{8,10},{9,13},{10,... | collective-permute-start | bytes 1179656 | tf_op jit(solution)/shard_map/ppermute | solution.py:268
  51.2 4.8 %collective-permute-start.21 = (bf16[384,512]{1,0:T(8,128)(2,1)S(1)}, bf16[384,512]{1,0:T(8,128)(2,1)S(1)}, u32[]{:S(2)}, u32[]{:S(2)}) collective-permute-start(bf16[384,512]{1,0:T(8,128)(2,1)S(1)} %shard_map.129), channel_id=1, source_target_pairs={{0,24},{2,26},{3,11},{4,12},{5,29},{6,14},{7,31},{8,0},{10,2},{11,... | collective-permute-start | bytes 1179656 | tf_op jit(solution)/shard_map/ppermute | solution.py:268
  56.9 3.3 %collective-permute-start.19 = (bf16[64,512]{1,0:T(8,128)(2,1)S(1)}, bf16[64,512]{1,0:T(8,128)(2,1)S(1)}, u32[]{:S(2)}, u32[]{:S(2)}) collective-permute-start(bf16[64,512]{1,0:T(8,128)(2,1)S(1)} %get-tuple-element.65.refs_0_), channel_id=1, source_target_pairs={{0,6},{1,7},{2,4},{3,5},{4,2},{5,3},{6,0},{7,1},{8,14},{9,15},{10,... | collective-permute-start | bytes 196616 | tf_op jit(solution)/shard_map/ppermute | solution.py:318
  60.2 1.2 %collective-permute-done.21.refs_1_.refs_3_ = bf16[384,512]{1,0:T(8,128)(2,1)S(1)} collective-permute-done((bf16[384,512]{1,0:T(8,128)(2,1)S(1)}, bf16[384,512]{1,0:T(8,128)(2,1)S(1)}, u32[]{:S(2)}, u32[]{:S(2)}) %collective-permute-start.21) | collective-permute-done | bytes 393248 | tf_op jit(solution)/shard_map/ppermute | solution.py:268
  61.5 5.3 %collective-permute-start.23 = (bf16[384,512]{1,0:T(8,128)(2,1)S(1)}, bf16[384,512]{1,0:T(8,128)(2,1)S(1)}, u32[]{:S(2)}, u32[]{:S(2)}) collective-permute-start(bf16[384,512]{1,0:T(8,128)(2,1)S(1)} %shard_map.131), channel_id=1, source_target_pairs={{0,4},{1,3},{2,6},{3,1},{4,0},{5,7},{6,2},{7,5},{8,12},{9,11},{10,... | collective-permute-start | bytes 1179656 | tf_op jit(solution)/shard_map/ppermute | solution.py:268
  67.0 1.5 %collective-permute-done.22.other_ref = bf16[256,512]{1,0:T(8,128)(2,1)S(1)} collective-permute-done((bf16[256,512]{1,0:T(8,128)(2,1)S(1)}, bf16[256,512]{1,0:T(8,128)(2,1)S(1)}, u32[]{:S(2)}, u32[]{:S(2)}) %collective-permute-start.22) | collective-permute-done | bytes 262176 | tf_op jit(solution)/shard_map/ppermute | solution.py:318
  68.5 1.0 %shard_map.133 = f32[512,512]{1,0:T(8,128)} custom-call(s32[1]{0:T(128)} %bitcast.spot_ref.refs_0_, bf16[256,512]{1,0:T(8,128)(2,1)S(1)} %shard_map.132.mine_ref, bf16[256,512]{1,0:T(8,128)(2,1)S(1)} %collective-permute-done.22.other_ref), custom_call_target="tpu_custom_call" | custom-call | tf_op jit(solution)/shard_map/pallas_call | solution.py:16
  69.6 3.1 %collective-permute-done.23.refs_2_ = bf16[384,512]{1,0:T(8,128)(2,1)S(1)} collective-permute-done((bf16[384,512]{1,0:T(8,128)(2,1)S(1)}, bf16[384,512]{1,0:T(8,128)(2,1)S(1)}, u32[]{:S(2)}, u32[]{:S(2)}) %collective-permute-start.23) | collective-permute-done | bytes 393248 | tf_op jit(solution)/shard_map/ppermute | solution.py:268
  72.6 1.0 %shard_map.134 = bf16[384,512]{1,0:T(8,128)(2,1)} custom-call(s32[1]{0:T(128)} %bitcast.spot_ref.refs_0_, f32[384,512]{1,0:T(8,128)S(1)} %get-tuple-element.72.refs_0_, bf16[384,512]{1,0:T(8,128)(2,1)S(1)} %collective-permute-done.20.refs_1_, bf16[384,512]{1,0:T(8,128)(2,1)S(1)} %collective-permute-done.23.refs_2_, ...), custom_call_target="tpu_custom_call" | custom-call | flops 10000000000 | tf_op jit(solution)/shard_map/pallas_call | solution.py:16
  (47 shorter events, 5.0 us)
Async XLA Ops:
  0.6 11.1 %collective-permute-start = (bf16[8,7,128,128]{3,2,1,0:T(8,128)(2,1)}, bf16[8,7,128,128]{3,2,1,0:T(8,128)(2,1)S(1)}, u32[]{:S(2)}, u32[]{:S(2)}) collective-permute-start(bf16[8,7,128,128]{3,2,1,0:T(8,128)(2,1)} %bitcast.7), channel_id=1, source_target_pairs={{0,1},{1,0},{2,3},{3,2},{4,5},{5,4},{6,7},{7,6},{8,9},{9,8},{10,11... | collective-permute-start | bytes 5505032 | tf_op jit(solution)/shard_map/ppermute | solution.py:318
  1.1 24.5 %collective-permute-start.2 = (bf16[384,512]{1,0:T(8,128)(2,1)}, bf16[384,512]{1,0:T(8,128)(2,1)S(1)}, u32[]{:S(2)}, u32[]{:S(2)}) collective-permute-start(bf16[384,512]{1,0:T(8,128)(2,1)} %refs_2_.1), channel_id=1, source_target_pairs={{0,4},{1,5},{2,6},{3,7},{4,8},{5,9},{6,10},{7,11},{8,12},{9,13},{1... | collective-permute-start | bytes 1179656 | tf_op jit(solution)/shard_map/ppermute | solution.py:221
  3.7 22.5 %collective-permute-start.3 = (bf16[384,512]{1,0:T(8,128)(2,1)}, bf16[384,512]{1,0:T(8,128)(2,1)S(1)}, u32[]{:S(2)}, u32[]{:S(2)}) collective-permute-start(bf16[384,512]{1,0:T(8,128)(2,1)} %refs_2_.1), channel_id=1, source_target_pairs={{0,2},{1,3},{2,4},{3,5},{4,6},{5,7},{6,8},{7,9},{8,10},{9,11},{10,... | collective-permute-start | bytes 1179656 | tf_op jit(solution)/shard_map/ppermute | solution.py:221
  5.2 21.1 %collective-permute-start.4 = (bf16[384,512]{1,0:T(8,128)(2,1)}, bf16[384,512]{1,0:T(8,128)(2,1)S(1)}, u32[]{:S(2)}, u32[]{:S(2)}) collective-permute-start(bf16[384,512]{1,0:T(8,128)(2,1)} %refs_2_.1), channel_id=1, source_target_pairs={{0,30},{1,31},{2,0},{3,1},{4,2},{5,3},{6,4},{7,5},{8,6},{9,7},{10,... | collective-permute-start | bytes 1179656 | tf_op jit(solution)/shard_map/ppermute | solution.py:221
  9.4 20.0 %collective-permute-start.5 = (bf16[384,512]{1,0:T(8,128)(2,1)}, bf16[384,512]{1,0:T(8,128)(2,1)S(1)}, u32[]{:S(2)}, u32[]{:S(2)}) collective-permute-start(bf16[384,512]{1,0:T(8,128)(2,1)} %refs_2_.1), channel_id=1, source_target_pairs={{0,28},{2,30},{4,0},{6,2},{8,4},{10,6},{12,8},{14,10},{16,12},{18,... | collective-permute-start | bytes 1179656 | tf_op jit(solution)/shard_map/ppermute | solution.py:221
  13.2 1.1 %collective-permute-start.1 = (s32[120]{0:T(128)S(1)}, s32[120]{0:T(128)S(1)}, u32[]{:S(2)}, u32[]{:S(2)}) collective-permute-start(s32[120]{0:T(128)S(1)} %reshape.27.own_meta_ref), channel_id=1, source_target_pairs={{0,1},{1,0},{2,3},{3,2},{4,5},{5,4},{6,7},{7,6},{8,9},{9,8},{10,11... | collective-permute-start | bytes 1448 | tf_op jit(solution)/shard_map/ppermute | solution.py:318
  14.4 1.5 %copy-start = (bf16[1,8,7,128,128]{4,3,2,1,0:T(8,128)(2,1)S(1)}, bf16[1,8,7,128,128]{4,3,2,1,0:T(8,128)(2,1)}, u32[]{:S(2)}) copy-start(bf16[1,8,7,128,128]{4,3,2,1,0:T(8,128)(2,1)} %param.12) | copy-start | bytes 5505028
  15.9 10.4 %copy-start.2 = (bf16[384,512]{1,0:T(8,128)(2,1)S(1)}, bf16[384,512]{1,0:T(8,128)(2,1)}, u32[]{:S(2)}) copy-start(bf16[384,512]{1,0:T(8,128)(2,1)} %refs_2_.1) | copy-start | bytes 1179652
  28.1 4.0 %copy-start.1 = (bf16[512,512]{1,0:T(8,128)(2,1)S(1)}, bf16[512,512]{1,0:T(8,128)(2,1)}, u32[]{:S(2)}) copy-start(bf16[512,512]{1,0:T(8,128)(2,1)} %weight_ref.1) | copy-start | bytes 1572868
  28.1 4.0 %copy-start.3 = (bf16[384,512]{1,0:T(8,128)(2,1)S(1)}, bf16[384,512]{1,0:T(8,128)(2,1)}, u32[]{:S(2)}) copy-start(bf16[384,512]{1,0:T(8,128)(2,1)} %grad_out_ref.1) | copy-start | bytes 1179652
  28.1 4.0 %copy-start.4 = (f32[512]{0:T(512)S(1)}, f32[512]{0:T(512)}, u32[]{:S(2)}) copy-start(f32[512]{0:T(512)} %param.14) | copy-start | bytes 6148
  29.7 2.4 %collective-permute-start.6 = (f32[384,512]{1,0:T(8,128)S(1)}, f32[384,512]{1,0:T(8,128)S(1)}, u32[]{:S(2)}, u32[]{:S(2)}) collective-permute-start(f32[384,512]{1,0:T(8,128)S(1)} %shard_map.122), channel_id=1, source_target_pairs={{0,1},{1,0},{2,3},{3,2},{4,5},{5,4},{6,7},{7,6},{8,9},{9,8},{10,11... | collective-permute-start | bytes 2359304 | tf_op jit(solution)/shard_map/ppermute | solution.py:318
  32.1 7.2 %copy-start.5 = (s32[40]{0:T(128)S(1)}, s32[40]{0:T(128)}, u32[]{:S(2)}) copy-start(s32[40]{0:T(128)} %constant.23.refs_1_) | copy-start | bytes 484
  33.5 5.8 %collective-permute-start.11 = (bf16[384,512]{1,0:T(8,128)(2,1)S(1)}, bf16[384,512]{1,0:T(8,128)(2,1)S(1)}, u32[]{:S(2)}, u32[]{:S(2)}) collective-permute-start(bf16[384,512]{1,0:T(8,128)(2,1)S(1)} %get-tuple-element.51.refs_3_), channel_id=1, source_target_pairs={{0,1},{1,0},{2,3},{3,2},{4,5},{5,4},{6,7},{7,6},{8,9},{9,8},{10,11... | collective-permute-start | bytes 1179656 | tf_op jit(solution)/shard_map/ppermute | solution.py:318
  33.6 2.1 %collective-permute-start.7 = (bf16[4,80,512]{2,1,0:T(8,128)(2,1)S(1)}, bf16[4,80,512]{2,1,0:T(8,128)(2,1)S(1)}, u32[]{:S(2)}, u32[]{:S(2)}) collective-permute-start(bf16[4,80,512]{2,1,0:T(8,128)(2,1)S(1)} %get-tuple-element.45), channel_id=1, source_target_pairs={{0,1},{1,0},{2,3},{3,2},{4,5},{5,4},{6,7},{7,6},{8,9},{9,8},{10,11... | collective-permute-start | bytes 983048 | tf_op jit(solution)/shard_map/ppermute | solution.py:318
  35.7 7.3 %collective-permute-start.10 = (bf16[80,512]{1,0:T(8,128)(2,1)S(1)}, bf16[80,512]{1,0:T(8,128)(2,1)S(1)}, u32[]{:S(2)}, u32[]{:S(2)}) collective-permute-start(bf16[80,512]{1,0:T(8,128)(2,1)S(1)} %get-tuple-element.49), channel_id=1, source_target_pairs={{0,6},{1,7},{2,4},{3,5},{4,2},{5,3},{6,0},{7,1},{8,14},{9,15},{10,... | collective-permute-start | bytes 245768 | tf_op jit(solution)/shard_map/ppermute | solution.py:318
  37.3 5.8 %collective-permute-start.8 = (bf16[80,512]{1,0:T(8,128)(2,1)S(1)}, bf16[80,512]{1,0:T(8,128)(2,1)S(1)}, u32[]{:S(2)}, u32[]{:S(2)}) collective-permute-start(bf16[80,512]{1,0:T(8,128)(2,1)S(1)} %get-tuple-element.47), channel_id=1, source_target_pairs={{0,2},{1,3},{2,0},{3,1},{4,6},{5,7},{6,4},{7,5},{8,10},{9,11},{10,... | collective-permute-start | bytes 245768 | tf_op jit(solution)/shard_map/ppermute | solution.py:318
  37.8 5.3 %collective-permute-start.9 = (bf16[80,512]{1,0:T(8,128)(2,1)S(1)}, bf16[80,512]{1,0:T(8,128)(2,1)S(1)}, u32[]{:S(2)}, u32[]{:S(2)}) collective-permute-start(bf16[80,512]{1,0:T(8,128)(2,1)S(1)} %get-tuple-element.48), channel_id=1, source_target_pairs={{0,4},{1,5},{2,6},{3,7},{4,0},{5,1},{6,2},{7,3},{8,12},{9,13},{10,... | collective-permute-start | bytes 245768 | tf_op jit(solution)/shard_map/ppermute | solution.py:318
  40.8 8.7 %collective-permute-start.15 = (bf16[384,512]{1,0:T(8,128)(2,1)S(1)}, bf16[384,512]{1,0:T(8,128)(2,1)S(1)}, u32[]{:S(2)}, u32[]{:S(2)}) collective-permute-start(bf16[384,512]{1,0:T(8,128)(2,1)S(1)} %get-tuple-element.60), channel_id=1, source_target_pairs={{1,25},{3,7},{9,1},{11,15},{17,9},{19,23},{25,17},{27,31}} | collective-permute-start | bytes 1179656 | tf_op jit(solution)/shard_map/ppermute | solution.py:268
  41.5 9.5 %collective-permute-start.16 = (bf16[384,512]{1,0:T(8,128)(2,1)S(1)}, bf16[384,512]{1,0:T(8,128)(2,1)S(1)}, u32[]{:S(2)}, u32[]{:S(2)}) collective-permute-start(bf16[384,512]{1,0:T(8,128)(2,1)S(1)} %get-tuple-element.53), channel_id=1, source_target_pairs={{0,2},{1,5},{2,0},{3,7},{4,6},{5,1},{6,4},{7,3},{8,10},{9,13},{10,... | collective-permute-start | bytes 1179656 | tf_op jit(solution)/shard_map/ppermute | solution.py:268
  43.1 12.9 %collective-permute-start.12 = (bf16[80,512]{1,0:T(8,128)(2,1)S(1)}, bf16[80,512]{1,0:T(8,128)(2,1)S(1)}, u32[]{:S(2)}, u32[]{:S(2)}) collective-permute-start(bf16[80,512]{1,0:T(8,128)(2,1)S(1)} %shard_map.126.refs_0_), channel_id=1, source_target_pairs={{0,8},{1,9},{2,10},{3,11},{4,12},{5,13},{6,14},{7,15},{8,0},{9,1},... | collective-permute-start | bytes 245768 | tf_op jit(solution)/shard_map/ppermute | solution.py:318
  43.9 12.1 %collective-permute-start.13 = (bf16[80,512]{1,0:T(8,128)(2,1)S(1)}, bf16[80,512]{1,0:T(8,128)(2,1)S(1)}, u32[]{:S(2)}, u32[]{:S(2)}) collective-permute-start(bf16[80,512]{1,0:T(8,128)(2,1)S(1)} %shard_map.126.refs_0_), channel_id=1, source_target_pairs={{0,16},{1,17},{2,18},{3,19},{4,20},{5,21},{6,22},{7,23},{8,24},{9,... | collective-permute-start | bytes 245768 | tf_op jit(solution)/shard_map/ppermute | solution.py:318
  46.2 9.9 %collective-permute-start.14 = (bf16[80,512]{1,0:T(8,128)(2,1)S(1)}, bf16[80,512]{1,0:T(8,128)(2,1)S(1)}, u32[]{:S(2)}, u32[]{:S(2)}) collective-permute-start(bf16[80,512]{1,0:T(8,128)(2,1)S(1)} %shard_map.126.refs_0_), channel_id=1, source_target_pairs={{0,24},{1,25},{2,26},{3,27},{4,28},{5,29},{6,30},{7,31},{8,16},{9,... | collective-permute-start | bytes 245768 | tf_op jit(solution)/shard_map/ppermute | solution.py:318
  49.6 10.6 %collective-permute-start.20 = (bf16[384,512]{1,0:T(8,128)(2,1)S(1)}, bf16[384,512]{1,0:T(8,128)(2,1)S(1)}, u32[]{:S(2)}, u32[]{:S(2)}) collective-permute-start(bf16[384,512]{1,0:T(8,128)(2,1)S(1)} %shard_map.128), channel_id=1, source_target_pairs={{0,2},{1,5},{2,0},{3,7},{4,6},{5,1},{6,4},{7,3},{8,10},{9,13},{10,... | collective-permute-start | bytes 1179656 | tf_op jit(solution)/shard_map/ppermute | solution.py:268
  51.2 10.1 %collective-permute-start.21 = (bf16[384,512]{1,0:T(8,128)(2,1)S(1)}, bf16[384,512]{1,0:T(8,128)(2,1)S(1)}, u32[]{:S(2)}, u32[]{:S(2)}) collective-permute-start(bf16[384,512]{1,0:T(8,128)(2,1)S(1)} %shard_map.129), channel_id=1, source_target_pairs={{0,24},{2,26},{3,11},{4,12},{5,29},{6,14},{7,31},{8,0},{10,2},{11,... | collective-permute-start | bytes 1179656 | tf_op jit(solution)/shard_map/ppermute | solution.py:268
  56.7 10.2 %collective-permute-start.17 = (bf16[64,512]{1,0:T(8,128)(2,1)S(1)}, bf16[64,512]{1,0:T(8,128)(2,1)S(1)}, u32[]{:S(2)}, u32[]{:S(2)}) collective-permute-start(bf16[64,512]{1,0:T(8,128)(2,1)S(1)} %get-tuple-element.65.refs_0_), channel_id=1, source_target_pairs={{0,2},{1,3},{2,0},{3,1},{4,6},{5,7},{6,4},{7,5},{8,10},{9,11},{10,... | collective-permute-start | bytes 196616 | tf_op jit(solution)/shard_map/ppermute | solution.py:318
  56.8 10.0 %collective-permute-start.18 = (bf16[64,512]{1,0:T(8,128)(2,1)S(1)}, bf16[64,512]{1,0:T(8,128)(2,1)S(1)}, u32[]{:S(2)}, u32[]{:S(2)}) collective-permute-start(bf16[64,512]{1,0:T(8,128)(2,1)S(1)} %get-tuple-element.65.refs_0_), channel_id=1, source_target_pairs={{0,4},{1,5},{2,6},{3,7},{4,0},{5,1},{6,2},{7,3},{8,12},{9,13},{10,... | collective-permute-start | bytes 196616 | tf_op jit(solution)/shard_map/ppermute | solution.py:318
  56.9 10.0 %collective-permute-start.19 = (bf16[64,512]{1,0:T(8,128)(2,1)S(1)}, bf16[64,512]{1,0:T(8,128)(2,1)S(1)}, u32[]{:S(2)}, u32[]{:S(2)}) collective-permute-start(bf16[64,512]{1,0:T(8,128)(2,1)S(1)} %get-tuple-element.65.refs_0_), channel_id=1, source_target_pairs={{0,6},{1,7},{2,4},{3,5},{4,2},{5,3},{6,0},{7,1},{8,14},{9,15},{10,... | collective-permute-start | bytes 196616 | tf_op jit(solution)/shard_map/ppermute | solution.py:318
  61.5 11.1 %collective-permute-start.23 = (bf16[384,512]{1,0:T(8,128)(2,1)S(1)}, bf16[384,512]{1,0:T(8,128)(2,1)S(1)}, u32[]{:S(2)}, u32[]{:S(2)}) collective-permute-start(bf16[384,512]{1,0:T(8,128)(2,1)S(1)} %shard_map.131), channel_id=1, source_target_pairs={{0,4},{1,3},{2,6},{3,1},{4,0},{5,7},{6,2},{7,5},{8,12},{9,11},{10,... | collective-permute-start | bytes 1179656 | tf_op jit(solution)/shard_map/ppermute | solution.py:268
  66.9 1.6 %collective-permute-start.22 = (bf16[256,512]{1,0:T(8,128)(2,1)S(1)}, bf16[256,512]{1,0:T(8,128)(2,1)S(1)}, u32[]{:S(2)}, u32[]{:S(2)}) collective-permute-start(bf16[256,512]{1,0:T(8,128)(2,1)S(1)} %shard_map.132.mine_ref), channel_id=1, source_target_pairs={{0,1},{1,0},{2,3},{3,2},{4,5},{5,4},{6,7},{7,6},{8,9},{9,8},{10,11... | collective-permute-start | bytes 786440 | tf_op jit(solution)/shard_map/ppermute | solution.py:318

commit v13 on v12

--- a/solution.py
+++ b/solution.py
@@ -180,7 +180,7 @@
     return call(kernel, [((piece, hidden), BF16), ((1, hidden), F32)], list(values), cost=10)
 
 
-def scattered_sums(flipped, own, mate, columns, dtypes, spot=None, lookup=None):
+def scattered_sums(flipped, own, mate, columns, dtypes, spot=None, lookup=None, cost=10):
     rows_dev, hidden = own.shape
     extra = [] if lookup is None else [spot, jnp.asarray(lookup, jnp.int32).reshape(-1)]
 
@@ -203,7 +203,7 @@
         kernel,
         [((rows_dev, hidden), kind) for kinds in dtypes for kind in kinds],
         [*extra, flipped, own, mate],
-        cost=10,
+        cost=cost,
         smem=len(extra),
     )
 
@@ -272,23 +272,28 @@
         y = {spot: (spot ^ 4) - spot for spot in range(8)}
         straight = {spot: (y if spot % 2 else x)[spot] for spot in range(8)}
         across = {spot: (x if spot % 2 else y)[spot] for spot in range(8)}
-        take = lambda mate, *args: scattered_sums(self.flipped, self.own, mate, *args, self.spot, self.LOOKUP)
+        take = lambda mate, *args, cost=10: scattered_sums(
+            self.flipped, self.own, mate, *args, self.spot, self.LOOKUP, cost
+        )
         if k == 0:
             _, mate = after(token, self.mate)
-            self.to_last, self.to_plane, self.plane_rest = take(mate, (4, 3), [[BF16], [BF16, F32]])
+            self.to_last, self.to_plane, self.plane_rest, self.to_straight = take(
+                mate, (4, 3, 2), [[BF16], [BF16, F32], [F32]]
+            )
+            self.from_last = self.routed(self.to_last, straight)
             self.from_plane = self.routed(self.to_plane, {1: -8, 3: 4})
-            self.from_last = self.routed(self.to_last, straight)
             return [self.to_last]
         if k == 1:
-            _, mate, plane_rest = after(token, self.mate, self.plane_rest)
-            self.kept, self.to_across, to_straight = take(mate, (0, 1, 2), [[F32]] * 3)
+            _, plane_rest = after(token, self.plane_rest)
             out = summed_terms(
                 self.spot, [plane_rest, self.from_last, self.from_plane], [self.EVEN, self.MIDDLE, 0b10000000]
             )
             self.from_planes = self.routed(out, {0: -8, 2: -8, 4: 8, 6: 8, 5: -8, 3: 8, 7: -8})
+            out, to_straight, mate = after(out, self.to_straight, self.mate)
             second = summed_terms(self.spot, [to_straight, self.from_plane], [None, 0b00000010])
             self.second = self.routed(second, straight)
-            return [second, out]
+            self.kept, self.to_across = take(mate, (0, 1), [[F32]] * 2, cost=10)
+            return [second, self.kept]
         if k == 2:
             _, rest, _ = after(token, self.to_across, self.second)
             out = summed_terms(

time: 73.8 us -> 74.4 us (level)
  the two profiles are of different devices: /device:TPU:0 before, /device:TPU:16 now
where the time goes in v13:
time: 74.4 us; the launch traced here: 74.1 us
  waiting for transfers between devices  31 us (42%)
  starting transfers between devices  25.6 us (34%)
  Pallas kernels  13.5 us (18%)
  local copies, waits for them, and re-layouts  2.4 us (3%)
  between operations  0.85 us (1%)
    ppermute x15, waiting for transfers between devices, swapped(): return lax.ppermute(value, 'blk', [(s, s ^ distance) for s in range(count)])  18.6 us
    pallas_call x15, Pallas kernels, call(): pl.pallas_call(kernel, out_shape=out_shape, in_specs=[spec(k) for k in ra...  13.5 us
    ppermute x15, starting transfers between devices, swapped(): return lax.ppermute(value, 'blk', [(s, s ^ distance) for s in range(count)])  11.8 us
    ppermute x4, waiting for transfers between devices, sent(): return lax.ppermute(value, 'blk', pairs)  8.13 us
    ppermute x4, starting transfers between devices, sent(): return lax.ppermute(value, 'blk', pairs)  7.8 us
    ppermute x5, starting transfers between devices, routed(): return lax.ppermute(value, 'blk', pairs)  6.02 us
    ppermute x5, waiting for transfers between devices, routed(): return lax.ppermute(value, 'blk', pairs)  4.31 us
    unnamed x12, local copies, waits for them, and re-layouts  1.53 us
  transfers between devices with their start and end apart: 24, of which 12 were waited for; matrix products, arithmetic and copies ran while one was open for 2% of the time, Pallas kernels for 15%

profile of v13, /device:TPU:16, one launch (start us, length us, event | category | flops | bytes accessed | tf_op | source)
XLA Modules:
  0.0 74.1 jit_solution(9133040027145772102)
XLA Ops:
  0.7 1.6 %collective-permute-start.2 = (bf16[384,512]{1,0:T(8,128)(2,1)}, bf16[384,512]{1,0:T(8,128)(2,1)S(1)}, u32[]{:S(2)}, u32[]{:S(2)}) collective-permute-start(bf16[384,512]{1,0:T(8,128)(2,1)} %refs_2_.1), channel_id=1, source_target_pairs={{0,4},{1,5},{2,6},{3,7},{4,8},{5,9},{6,10},{7,11},{8,12},{9,13},{1... | collective-permute-start | bytes 1179656 | tf_op jit(solution)/shard_map/ppermute | solution.py:221
  2.3 1.5 %collective-permute-start.3 = (bf16[384,512]{1,0:T(8,128)(2,1)}, bf16[384,512]{1,0:T(8,128)(2,1)S(1)}, u32[]{:S(2)}, u32[]{:S(2)}) collective-permute-start(bf16[384,512]{1,0:T(8,128)(2,1)} %refs_2_.1), channel_id=1, source_target_pairs={{0,2},{1,3},{2,4},{3,5},{4,6},{5,7},{6,8},{7,9},{8,10},{9,11},{10,... | collective-permute-start | bytes 1179656 | tf_op jit(solution)/shard_map/ppermute | solution.py:221
  3.8 2.3 %collective-permute-start.4 = (bf16[384,512]{1,0:T(8,128)(2,1)}, bf16[384,512]{1,0:T(8,128)(2,1)S(1)}, u32[]{:S(2)}, u32[]{:S(2)}) collective-permute-start(bf16[384,512]{1,0:T(8,128)(2,1)} %refs_2_.1), channel_id=1, source_target_pairs={{0,30},{1,31},{2,0},{3,1},{4,2},{5,3},{6,4},{7,5},{8,6},{9,7},{10,... | collective-permute-start | bytes 1179656 | tf_op jit(solution)/shard_map/ppermute | solution.py:221
  6.1 2.4 %collective-permute-start.5 = (bf16[384,512]{1,0:T(8,128)(2,1)}, bf16[384,512]{1,0:T(8,128)(2,1)S(1)}, u32[]{:S(2)}, u32[]{:S(2)}) collective-permute-start(bf16[384,512]{1,0:T(8,128)(2,1)} %refs_2_.1), channel_id=1, source_target_pairs={{0,28},{2,30},{4,0},{6,2},{8,4},{10,6},{12,8},{14,10},{16,12},{18,... | collective-permute-start | bytes 1179656 | tf_op jit(solution)/shard_map/ppermute | solution.py:221
  8.5 0.7 reshape_squeeze.3
  10.1 1.1 %collective-permute-done.1.mate_meta_ref = s32[120]{0:T(128)S(1)} collective-permute-done((s32[120]{0:T(128)S(1)}, s32[120]{0:T(128)S(1)}, u32[]{:S(2)}, u32[]{:S(2)}) %collective-permute-start.1) | collective-permute-done | bytes 512 | tf_op jit(solution)/shard_map/ppermute | solution.py:323
  11.2 1.5 %copy-done = bf16[1,8,7,128,128]{4,3,2,1,0:T(8,128)(2,1)S(1)} copy-done((bf16[1,8,7,128,128]{4,3,2,1,0:T(8,128)(2,1)S(1)}, bf16[1,8,7,128,128]{4,3,2,1,0:T(8,128)(2,1)}, u32[]{:S(2)}) %copy-start) | copy-done | bytes 1835032
  12.7 3.4 %shard_map.120 = (bf16[768,1920]{1,0:T(8,128)(2,1)S(1)}, bf16[1920,768]{1,0:T(8,128)(2,1)S(1)}) custom-call(s32[1]{0:T(128)} %bitcast.spot_ref.refs_0_, s32[120]{0:T(128)S(1)} %reshape.27.own_meta_ref, s32[120]{0:T(128)S(1)} %collective-permute-done.1.mate_meta_ref, bf16[8,7,128,128]{3,2,1,0:T(8,128)(2,1)S(1)} %bitcast.8, ...), custom_call_target="tpu_custom_call" | custom-call | tf_op jit(solution)/shard_map/pallas_call | solution.py:16
  16.1 8.1 %collective-permute-done.2.refs_0_ = bf16[384,512]{1,0:T(8,128)(2,1)S(1)} collective-permute-done((bf16[384,512]{1,0:T(8,128)(2,1)}, bf16[384,512]{1,0:T(8,128)(2,1)S(1)}, u32[]{:S(2)}, u32[]{:S(2)}) %collective-permute-start.2) | collective-permute-done | bytes 393248 | tf_op jit(solution)/shard_map/ppermute | solution.py:221
  24.2 1.8 %shard_map.121.refs_0_.own_ref = f32[768,512]{1,0:T(8,128)S(1)} custom-call(bf16[768,1920]{1,0:T(8,128)(2,1)S(1)} %get-tuple-element.43.dense_ref, bf16[384,512]{1,0:T(8,128)(2,1)S(1)} %collective-permute-done.2.refs_0_, bf16[384,512]{1,0:T(8,128)(2,1)S(1)} %collective-permute-done.3.refs_1_, bf16[384,512]{1,0:T(8,128)(2,1)S(1)} %copy-done.2, ...), custom_call_target="tpu_custom_call" | custom-call | tf_op jit(solution)/shard_map/pallas_call | solution.py:16
  26.5 2.3 %collective-permute-done.6.mate_ref = f32[384,512]{1,0:T(8,128)S(1)} collective-permute-done((f32[384,512]{1,0:T(8,128)S(1)}, f32[384,512]{1,0:T(8,128)S(1)}, u32[]{:S(2)}, u32[]{:S(2)}) %collective-permute-start.6) | collective-permute-done | bytes 786464 | tf_op jit(solution)/shard_map/ppermute | solution.py:323
  28.8 1.4 %shard_map.123 = (bf16[384,512]{1,0:T(8,128)(2,1)}, bf16[384,512]{1,0:T(8,128)(2,1)S(1)}, f32[4,80,512]{2,1,0:T(8,128)S(1)}, bf16[4,80,512]{2,1,0:T(8,128)(2,1)S(1)}) custom-call(s32[1]{0:T(128)} %bitcast.spot_ref.refs_0_, f32[768,512]{1,0:T(8,128)S(1)} %shard_map.121.refs_0_.own_ref, f32[384,512]{1,0:T(8,128)S(1)} %collective-permute-done.6.mate_ref, ...), custom_call_target="tpu_custom_call" | custom-call | tf_op jit(solution)/shard_map/pallas_call | solution.py:16
  30.7 1.7 %collective-permute-done.7.got_ref = bf16[4,80,512]{2,1,0:T(8,128)(2,1)S(1)} collective-permute-done((bf16[4,80,512]{2,1,0:T(8,128)(2,1)S(1)}, bf16[4,80,512]{2,1,0:T(8,128)(2,1)S(1)}, u32[]{:S(2)}, u32[]{:S(2)}) %collective-permute-start.7) | collective-permute-done | bytes 327712 | tf_op jit(solution)/shard_map/ppermute | solution.py:323
  32.5 3.4 %collective-permute-start.10 = (bf16[80,512]{1,0:T(8,128)(2,1)S(1)}, bf16[80,512]{1,0:T(8,128)(2,1)S(1)}, u32[]{:S(2)}, u32[]{:S(2)}) collective-permute-start(bf16[80,512]{1,0:T(8,128)(2,1)S(1)} %get-tuple-element.50), channel_id=1, source_target_pairs={{0,6},{1,7},{2,4},{3,5},{4,2},{5,3},{6,0},{7,1},{8,14},{9,15},{10,... | collective-permute-start | bytes 245768 | tf_op jit(solution)/shard_map/ppermute | solution.py:323
  36.5 1.9 %shard_map.125 = (bf16[384,512]{1,0:T(8,128)(2,1)S(1)}, bf16[384,512]{1,0:T(8,128)(2,1)S(1)}, f32[384,512]{1,0:T(8,128)S(1)}, f32[384,512]{1,0:T(8,128)S(1)}) custom-call(s32[1]{0:T(128)} %bitcast.spot_ref.refs_0_, s32[40]{0:T(128)S(1)} %copy-done.5, bf16[1920,768]{1,0:T(8,128)(2,1)S(1)} %get-tuple-element.51.refs_2_, ...), custom_call_target="tpu_custom_call" | custom-call | flops 10000000000 | tf_op jit(solution)/shard_map/pallas_call | solution.py:16
  38.4 1.5 %collective-permute-start.15 = (bf16[384,512]{1,0:T(8,128)(2,1)S(1)}, bf16[384,512]{1,0:T(8,128)(2,1)S(1)}, u32[]{:S(2)}, u32[]{:S(2)}) collective-permute-start(bf16[384,512]{1,0:T(8,128)(2,1)S(1)} %get-tuple-element.54), channel_id=1, source_target_pairs={{0,2},{1,5},{2,0},{3,7},{4,6},{5,1},{6,4},{7,3},{8,10},{9,13},{10,... | collective-permute-start | bytes 1179656 | tf_op jit(solution)/shard_map/ppermute | solution.py:268
  39.9 0.7 collective-permute-start.16
  41.1 1.2 %collective-permute-start.12 = (bf16[80,512]{1,0:T(8,128)(2,1)S(1)}, bf16[80,512]{1,0:T(8,128)(2,1)S(1)}, u32[]{:S(2)}, u32[]{:S(2)}) collective-permute-start(bf16[80,512]{1,0:T(8,128)(2,1)S(1)} %shard_map.126.refs_0_), channel_id=1, source_target_pairs={{0,8},{1,9},{2,10},{3,11},{4,12},{5,13},{6,14},{7,15},{8,0},{9,1},... | collective-permute-start | bytes 245768 | tf_op jit(solution)/shard_map/ppermute | solution.py:323
  42.3 0.8 %collective-permute-start.13 = (bf16[80,512]{1,0:T(8,128)(2,1)S(1)}, bf16[80,512]{1,0:T(8,128)(2,1)S(1)}, u32[]{:S(2)}, u32[]{:S(2)}) collective-permute-start(bf16[80,512]{1,0:T(8,128)(2,1)S(1)} %shard_map.126.refs_0_), channel_id=1, source_target_pairs={{0,16},{1,17},{2,18},{3,19},{4,20},{5,21},{6,22},{7,23},{8,24},{9,... | collective-permute-start | bytes 245768 | tf_op jit(solution)/shard_map/ppermute | solution.py:323
  43.1 1.6 %collective-permute-start.14 = (bf16[80,512]{1,0:T(8,128)(2,1)S(1)}, bf16[80,512]{1,0:T(8,128)(2,1)S(1)}, u32[]{:S(2)}, u32[]{:S(2)}) collective-permute-start(bf16[80,512]{1,0:T(8,128)(2,1)S(1)} %shard_map.126.refs_0_), channel_id=1, source_target_pairs={{0,24},{1,25},{2,26},{3,27},{4,28},{5,29},{6,30},{7,31},{8,16},{9,... | collective-permute-start | bytes 245768 | tf_op jit(solution)/shard_map/ppermute | solution.py:323
  44.6 1.6 %collective-permute-done.15.refs_1_.refs_2_ = bf16[384,512]{1,0:T(8,128)(2,1)S(1)} collective-permute-done((bf16[384,512]{1,0:T(8,128)(2,1)S(1)}, bf16[384,512]{1,0:T(8,128)(2,1)S(1)}, u32[]{:S(2)}, u32[]{:S(2)}) %collective-permute-start.15) | collective-permute-done | bytes 393248 | tf_op jit(solution)/shard_map/ppermute | solution.py:268
  46.4 2.4 %collective-permute-start.21 = (bf16[384,512]{1,0:T(8,128)(2,1)S(1)}, bf16[384,512]{1,0:T(8,128)(2,1)S(1)}, u32[]{:S(2)}, u32[]{:S(2)}) collective-permute-start(bf16[384,512]{1,0:T(8,128)(2,1)S(1)} %shard_map.127), channel_id=1, source_target_pairs={{0,24},{2,26},{3,11},{4,12},{5,29},{6,14},{7,31},{8,0},{10,2},{11,... | collective-permute-start | bytes 1179656 | tf_op jit(solution)/shard_map/ppermute | solution.py:268
  48.8 1.5 %shard_map.129 = (f32[384,512]{1,0:T(8,128)S(1)}, f32[384,512]{1,0:T(8,128)S(1)}) custom-call(s32[1]{0:T(128)} %bitcast.spot_ref.refs_0_, s32[40]{0:T(128)S(1)} %copy-done.5, bf16[1920,768]{1,0:T(8,128)(2,1)S(1)} %get-tuple-element.51.refs_2_, bf16[384,512]{1,0:T(8,128)(2,1)S(1)} %get-tuple-element.52.refs_3_, ...), custom_call_target="tpu_custom_call" | custom-call | flops 10000000000 | tf_op jit(solution)/shard_map/pallas_call | solution.py:16
  50.4 1.5 %collective-permute-start.20 = (bf16[384,512]{1,0:T(8,128)(2,1)S(1)}, bf16[384,512]{1,0:T(8,128)(2,1)S(1)}, u32[]{:S(2)}, u32[]{:S(2)}) collective-permute-start(bf16[384,512]{1,0:T(8,128)(2,1)S(1)} %shard_map.128), channel_id=1, source_target_pairs={{0,2},{1,5},{2,0},{3,7},{4,6},{5,1},{6,4},{7,3},{8,10},{9,13},{10,... | collective-permute-start | bytes 1179656 | tf_op jit(solution)/shard_map/ppermute | solution.py:268
  51.9 9.1 %collective-permute-done.14.refs_3_ = bf16[80,512]{1,0:T(8,128)(2,1)S(1)} collective-permute-done((bf16[80,512]{1,0:T(8,128)(2,1)S(1)}, bf16[80,512]{1,0:T(8,128)(2,1)S(1)}, u32[]{:S(2)}, u32[]{:S(2)}) %collective-permute-start.14) | collective-permute-done | bytes 81952 | tf_op jit(solution)/shard_map/ppermute | solution.py:323
  61.6 3.5 %collective-permute-start.19 = (bf16[64,512]{1,0:T(8,128)(2,1)S(1)}, bf16[64,512]{1,0:T(8,128)(2,1)S(1)}, u32[]{:S(2)}, u32[]{:S(2)}) collective-permute-start(bf16[64,512]{1,0:T(8,128)(2,1)S(1)} %get-tuple-element.68.refs_0_), channel_id=1, source_target_pairs={{0,6},{1,7},{2,4},{3,5},{4,2},{5,3},{6,0},{7,1},{8,14},{9,15},{10,... | collective-permute-start | bytes 196616 | tf_op jit(solution)/shard_map/ppermute | solution.py:323
  65.4 0.9 %collective-permute-done.17.refs_1_ = bf16[64,512]{1,0:T(8,128)(2,1)S(1)} collective-permute-done((bf16[64,512]{1,0:T(8,128)(2,1)S(1)}, bf16[64,512]{1,0:T(8,128)(2,1)S(1)}, u32[]{:S(2)}, u32[]{:S(2)}) %collective-permute-start.17) | collective-permute-done | bytes 65568 | tf_op jit(solution)/shard_map/ppermute | solution.py:323
  66.6 1.2 %collective-permute-done.19.refs_3_ = bf16[64,512]{1,0:T(8,128)(2,1)S(1)} collective-permute-done((bf16[64,512]{1,0:T(8,128)(2,1)S(1)}, bf16[64,512]{1,0:T(8,128)(2,1)S(1)}, u32[]{:S(2)}, u32[]{:S(2)}) %collective-permute-start.19) | collective-permute-done | bytes 65568 | tf_op jit(solution)/shard_map/ppermute | solution.py:323
  67.9 1.5 %collective-permute-done.22.other_ref = bf16[256,512]{1,0:T(8,128)(2,1)S(1)} collective-permute-done((bf16[256,512]{1,0:T(8,128)(2,1)S(1)}, bf16[256,512]{1,0:T(8,128)(2,1)S(1)}, u32[]{:S(2)}, u32[]{:S(2)}) %collective-permute-start.22) | collective-permute-done | bytes 262176 | tf_op jit(solution)/shard_map/ppermute | solution.py:323
  69.4 1.0 %shard_map.133 = f32[512,512]{1,0:T(8,128)} custom-call(s32[1]{0:T(128)} %bitcast.spot_ref.refs_0_, bf16[256,512]{1,0:T(8,128)(2,1)S(1)} %shard_map.132.mine_ref, bf16[256,512]{1,0:T(8,128)(2,1)S(1)} %collective-permute-done.22.other_ref), custom_call_target="tpu_custom_call" | custom-call | tf_op jit(solution)/shard_map/pallas_call | solution.py:16
  70.4 2.7 %collective-permute-done.23.refs_2_ = bf16[384,512]{1,0:T(8,128)(2,1)S(1)} collective-permute-done((bf16[384,512]{1,0:T(8,128)(2,1)S(1)}, bf16[384,512]{1,0:T(8,128)(2,1)S(1)}, u32[]{:S(2)}, u32[]{:S(2)}) %collective-permute-start.23) | collective-permute-done | bytes 393248 | tf_op jit(solution)/shard_map/ppermute | solution.py:268
  73.1 1.0 %shard_map.134 = bf16[384,512]{1,0:T(8,128)(2,1)} custom-call(s32[1]{0:T(128)} %bitcast.spot_ref.refs_0_, f32[384,512]{1,0:T(8,128)S(1)} %get-tuple-element.74.refs_0_, bf16[384,512]{1,0:T(8,128)(2,1)S(1)} %collective-permute-done.20.refs_1_, bf16[384,512]{1,0:T(8,128)(2,1)S(1)} %collective-permute-done.23.refs_2_, ...), custom_call_target="tpu_custom_call" | custom-call | flops 10000000000 | tf_op jit(solution)/shard_map/pallas_call | solution.py:16
  (47 shorter events, 4.7 us)
Async XLA Ops:
  0.6 7.9 %collective-permute-start = (bf16[8,7,128,128]{3,2,1,0:T(8,128)(2,1)}, bf16[8,7,128,128]{3,2,1,0:T(8,128)(2,1)S(1)}, u32[]{:S(2)}, u32[]{:S(2)}) collective-permute-start(bf16[8,7,128,128]{3,2,1,0:T(8,128)(2,1)} %bitcast.7), channel_id=1, source_target_pairs={{0,1},{1,0},{2,3},{3,2},{4,5},{5,4},{6,7},{7,6},{8,9},{9,8},{10,11... | collective-permute-start | bytes 5505032 | tf_op jit(solution)/shard_map/ppermute | solution.py:323
  0.7 23.5 %collective-permute-start.2 = (bf16[384,512]{1,0:T(8,128)(2,1)}, bf16[384,512]{1,0:T(8,128)(2,1)S(1)}, u32[]{:S(2)}, u32[]{:S(2)}) collective-permute-start(bf16[384,512]{1,0:T(8,128)(2,1)} %refs_2_.1), channel_id=1, source_target_pairs={{0,4},{1,5},{2,6},{3,7},{4,8},{5,9},{6,10},{7,11},{8,12},{9,13},{1... | collective-permute-start | bytes 1179656 | tf_op jit(solution)/shard_map/ppermute | solution.py:221
  2.3 21.9 %collective-permute-start.3 = (bf16[384,512]{1,0:T(8,128)(2,1)}, bf16[384,512]{1,0:T(8,128)(2,1)S(1)}, u32[]{:S(2)}, u32[]{:S(2)}) collective-permute-start(bf16[384,512]{1,0:T(8,128)(2,1)} %refs_2_.1), channel_id=1, source_target_pairs={{0,2},{1,3},{2,4},{3,5},{4,6},{5,7},{6,8},{7,9},{8,10},{9,11},{10,... | collective-permute-start | bytes 1179656 | tf_op jit(solution)/shard_map/ppermute | solution.py:221
  3.8 20.5 %collective-permute-start.4 = (bf16[384,512]{1,0:T(8,128)(2,1)}, bf16[384,512]{1,0:T(8,128)(2,1)S(1)}, u32[]{:S(2)}, u32[]{:S(2)}) collective-permute-start(bf16[384,512]{1,0:T(8,128)(2,1)} %refs_2_.1), channel_id=1, source_target_pairs={{0,30},{1,31},{2,0},{3,1},{4,2},{5,3},{6,4},{7,5},{8,6},{9,7},{10,... | collective-permute-start | bytes 1179656 | tf_op jit(solution)/shard_map/ppermute | solution.py:221
  6.1 19.9 %collective-permute-start.5 = (bf16[384,512]{1,0:T(8,128)(2,1)}, bf16[384,512]{1,0:T(8,128)(2,1)S(1)}, u32[]{:S(2)}, u32[]{:S(2)}) collective-permute-start(bf16[384,512]{1,0:T(8,128)(2,1)} %refs_2_.1), channel_id=1, source_target_pairs={{0,28},{2,30},{4,0},{6,2},{8,4},{10,6},{12,8},{14,10},{16,12},{18,... | collective-permute-start | bytes 1179656 | tf_op jit(solution)/shard_map/ppermute | solution.py:221
  10.1 1.1 %collective-permute-start.1 = (s32[120]{0:T(128)S(1)}, s32[120]{0:T(128)S(1)}, u32[]{:S(2)}, u32[]{:S(2)}) collective-permute-start(s32[120]{0:T(128)S(1)} %reshape.27.own_meta_ref), channel_id=1, source_target_pairs={{0,1},{1,0},{2,3},{3,2},{4,5},{5,4},{6,7},{7,6},{8,9},{9,8},{10,11... | collective-permute-start | bytes 1448 | tf_op jit(solution)/shard_map/ppermute | solution.py:323
  11.2 1.5 %copy-start = (bf16[1,8,7,128,128]{4,3,2,1,0:T(8,128)(2,1)S(1)}, bf16[1,8,7,128,128]{4,3,2,1,0:T(8,128)(2,1)}, u32[]{:S(2)}) copy-start(bf16[1,8,7,128,128]{4,3,2,1,0:T(8,128)(2,1)} %param.12) | copy-start | bytes 5505028
  12.7 11.5 %copy-start.2 = (bf16[384,512]{1,0:T(8,128)(2,1)S(1)}, bf16[384,512]{1,0:T(8,128)(2,1)}, u32[]{:S(2)}) copy-start(bf16[384,512]{1,0:T(8,128)(2,1)} %refs_2_.1) | copy-start | bytes 1179652
  26.0 2.8 %copy-start.1 = (bf16[512,512]{1,0:T(8,128)(2,1)S(1)}, bf16[512,512]{1,0:T(8,128)(2,1)}, u32[]{:S(2)}) copy-start(bf16[512,512]{1,0:T(8,128)(2,1)} %weight_ref.1) | copy-start | bytes 1572868
  26.0 2.8 %copy-start.3 = (bf16[384,512]{1,0:T(8,128)(2,1)S(1)}, bf16[384,512]{1,0:T(8,128)(2,1)}, u32[]{:S(2)}) copy-start(bf16[384,512]{1,0:T(8,128)(2,1)} %grad_out_ref.1) | copy-start | bytes 1179652
  26.0 2.8 %copy-start.4 = (f32[512]{0:T(512)S(1)}, f32[512]{0:T(512)}, u32[]{:S(2)}) copy-start(f32[512]{0:T(512)} %param.14) | copy-start | bytes 6148
  26.4 2.4 %collective-permute-start.6 = (f32[384,512]{1,0:T(8,128)S(1)}, f32[384,512]{1,0:T(8,128)S(1)}, u32[]{:S(2)}, u32[]{:S(2)}) collective-permute-start(f32[384,512]{1,0:T(8,128)S(1)} %shard_map.122), channel_id=1, source_target_pairs={{0,1},{1,0},{2,3},{3,2},{4,5},{5,4},{6,7},{7,6},{8,9},{9,8},{10,11... | collective-permute-start | bytes 2359304 | tf_op jit(solution)/shard_map/ppermute | solution.py:323
  28.8 7.7 %copy-start.5 = (s32[40]{0:T(128)S(1)}, s32[40]{0:T(128)}, u32[]{:S(2)}) copy-start(s32[40]{0:T(128)} %constant.23.refs_1_) | copy-start | bytes 484
  30.2 6.3 %collective-permute-start.11 = (bf16[384,512]{1,0:T(8,128)(2,1)S(1)}, bf16[384,512]{1,0:T(8,128)(2,1)S(1)}, u32[]{:S(2)}, u32[]{:S(2)}) collective-permute-start(bf16[384,512]{1,0:T(8,128)(2,1)S(1)} %get-tuple-element.52.refs_3_), channel_id=1, source_target_pairs={{0,1},{1,0},{2,3},{3,2},{4,5},{5,4},{6,7},{7,6},{8,9},{9,8},{10,11... | collective-permute-start | bytes 1179656 | tf_op jit(solution)/shard_map/ppermute | solution.py:323
  30.3 2.1 %collective-permute-start.7 = (bf16[4,80,512]{2,1,0:T(8,128)(2,1)S(1)}, bf16[4,80,512]{2,1,0:T(8,128)(2,1)S(1)}, u32[]{:S(2)}, u32[]{:S(2)}) collective-permute-start(bf16[4,80,512]{2,1,0:T(8,128)(2,1)S(1)} %get-tuple-element.46), channel_id=1, source_target_pairs={{0,1},{1,0},{2,3},{3,2},{4,5},{5,4},{6,7},{7,6},{8,9},{9,8},{10,11... | collective-permute-start | bytes 983048 | tf_op jit(solution)/shard_map/ppermute | solution.py:323
  32.5 8.1 %collective-permute-start.10 = (bf16[80,512]{1,0:T(8,128)(2,1)S(1)}, bf16[80,512]{1,0:T(8,128)(2,1)S(1)}, u32[]{:S(2)}, u32[]{:S(2)}) collective-permute-start(bf16[80,512]{1,0:T(8,128)(2,1)S(1)} %get-tuple-element.50), channel_id=1, source_target_pairs={{0,6},{1,7},{2,4},{3,5},{4,2},{5,3},{6,0},{7,1},{8,14},{9,15},{10,... | collective-permute-start | bytes 245768 | tf_op jit(solution)/shard_map/ppermute | solution.py:323
  35.8 4.8 %collective-permute-start.8 = (bf16[80,512]{1,0:T(8,128)(2,1)S(1)}, bf16[80,512]{1,0:T(8,128)(2,1)S(1)}, u32[]{:S(2)}, u32[]{:S(2)}) collective-permute-start(bf16[80,512]{1,0:T(8,128)(2,1)S(1)} %get-tuple-element.48), channel_id=1, source_target_pairs={{0,2},{1,3},{2,0},{3,1},{4,6},{5,7},{6,4},{7,5},{8,10},{9,11},{10,... | collective-permute-start | bytes 245768 | tf_op jit(solution)/shard_map/ppermute | solution.py:323
  36.4 4.7 %collective-permute-start.9 = (bf16[80,512]{1,0:T(8,128)(2,1)S(1)}, bf16[80,512]{1,0:T(8,128)(2,1)S(1)}, u32[]{:S(2)}, u32[]{:S(2)}) collective-permute-start(bf16[80,512]{1,0:T(8,128)(2,1)S(1)} %get-tuple-element.49), channel_id=1, source_target_pairs={{0,4},{1,5},{2,6},{3,7},{4,0},{5,1},{6,2},{7,3},{8,12},{9,13},{10,... | collective-permute-start | bytes 245768 | tf_op jit(solution)/shard_map/ppermute | solution.py:323
  38.4 7.8 %collective-permute-start.15 = (bf16[384,512]{1,0:T(8,128)(2,1)S(1)}, bf16[384,512]{1,0:T(8,128)(2,1)S(1)}, u32[]{:S(2)}, u32[]{:S(2)}) collective-permute-start(bf16[384,512]{1,0:T(8,128)(2,1)S(1)} %get-tuple-element.54), channel_id=1, source_target_pairs={{0,2},{1,5},{2,0},{3,7},{4,6},{5,1},{6,4},{7,3},{8,10},{9,13},{10,... | collective-permute-start | bytes 1179656 | tf_op jit(solution)/shard_map/ppermute | solution.py:268
  39.9 6.4 %collective-permute-start.16 = (bf16[384,512]{1,0:T(8,128)(2,1)S(1)}, bf16[384,512]{1,0:T(8,128)(2,1)S(1)}, u32[]{:S(2)}, u32[]{:S(2)}) collective-permute-start(bf16[384,512]{1,0:T(8,128)(2,1)S(1)} %get-tuple-element.60), channel_id=1, source_target_pairs={{1,25},{3,7},{9,1},{11,15},{17,9},{19,23},{25,17},{27,31}} | collective-permute-start | bytes 1179656 | tf_op jit(solution)/shard_map/ppermute | solution.py:268
  41.1 10.8 %collective-permute-start.12 = (bf16[80,512]{1,0:T(8,128)(2,1)S(1)}, bf16[80,512]{1,0:T(8,128)(2,1)S(1)}, u32[]{:S(2)}, u32[]{:S(2)}) collective-permute-start(bf16[80,512]{1,0:T(8,128)(2,1)S(1)} %shard_map.126.refs_0_), channel_id=1, source_target_pairs={{0,8},{1,9},{2,10},{3,11},{4,12},{5,13},{6,14},{7,15},{8,0},{9,1},... | collective-permute-start | bytes 245768 | tf_op jit(solution)/shard_map/ppermute | solution.py:323
  42.3 9.6 %collective-permute-start.13 = (bf16[80,512]{1,0:T(8,128)(2,1)S(1)}, bf16[80,512]{1,0:T(8,128)(2,1)S(1)}, u32[]{:S(2)}, u32[]{:S(2)}) collective-permute-start(bf16[80,512]{1,0:T(8,128)(2,1)S(1)} %shard_map.126.refs_0_), channel_id=1, source_target_pairs={{0,16},{1,17},{2,18},{3,19},{4,20},{5,21},{6,22},{7,23},{8,24},{9,... | collective-permute-start | bytes 245768 | tf_op jit(solution)/shard_map/ppermute | solution.py:323
  43.1 18.0 %collective-permute-start.14 = (bf16[80,512]{1,0:T(8,128)(2,1)S(1)}, bf16[80,512]{1,0:T(8,128)(2,1)S(1)}, u32[]{:S(2)}, u32[]{:S(2)}) collective-permute-start(bf16[80,512]{1,0:T(8,128)(2,1)S(1)} %shard_map.126.refs_0_), channel_id=1, source_target_pairs={{0,24},{1,25},{2,26},{3,27},{4,28},{5,29},{6,30},{7,31},{8,16},{9,... | collective-permute-start | bytes 245768 | tf_op jit(solution)/shard_map/ppermute | solution.py:323
  46.4 18.7 %collective-permute-start.21 = (bf16[384,512]{1,0:T(8,128)(2,1)S(1)}, bf16[384,512]{1,0:T(8,128)(2,1)S(1)}, u32[]{:S(2)}, u32[]{:S(2)}) collective-permute-start(bf16[384,512]{1,0:T(8,128)(2,1)S(1)} %shard_map.127), channel_id=1, source_target_pairs={{0,24},{2,26},{3,11},{4,12},{5,29},{6,14},{7,31},{8,0},{10,2},{11,... | collective-permute-start | bytes 1179656 | tf_op jit(solution)/shard_map/ppermute | solution.py:268
  50.4 14.7 %collective-permute-start.20 = (bf16[384,512]{1,0:T(8,128)(2,1)S(1)}, bf16[384,512]{1,0:T(8,128)(2,1)S(1)}, u32[]{:S(2)}, u32[]{:S(2)}) collective-permute-start(bf16[384,512]{1,0:T(8,128)(2,1)S(1)} %shard_map.128), channel_id=1, source_target_pairs={{0,2},{1,5},{2,0},{3,7},{4,6},{5,1},{6,4},{7,3},{8,10},{9,13},{10,... | collective-permute-start | bytes 1179656 | tf_op jit(solution)/shard_map/ppermute | solution.py:268
  61.6 4.6 %collective-permute-start.17 = (bf16[64,512]{1,0:T(8,128)(2,1)S(1)}, bf16[64,512]{1,0:T(8,128)(2,1)S(1)}, u32[]{:S(2)}, u32[]{:S(2)}) collective-permute-start(bf16[64,512]{1,0:T(8,128)(2,1)S(1)} %get-tuple-element.68.refs_0_), channel_id=1, source_target_pairs={{0,2},{1,3},{2,0},{3,1},{4,6},{5,7},{6,4},{7,5},{8,10},{9,11},{10,... | collective-permute-start | bytes 196616 | tf_op jit(solution)/shard_map/ppermute | solution.py:323
  61.6 5.0 %collective-permute-start.18 = (bf16[64,512]{1,0:T(8,128)(2,1)S(1)}, bf16[64,512]{1,0:T(8,128)(2,1)S(1)}, u32[]{:S(2)}, u32[]{:S(2)}) collective-permute-start(bf16[64,512]{1,0:T(8,128)(2,1)S(1)} %get-tuple-element.68.refs_0_), channel_id=1, source_target_pairs={{0,4},{1,5},{2,6},{3,7},{4,0},{5,1},{6,2},{7,3},{8,12},{9,13},{10,... | collective-permute-start | bytes 196616 | tf_op jit(solution)/shard_map/ppermute | solution.py:323
  61.6 6.1 %collective-permute-start.19 = (bf16[64,512]{1,0:T(8,128)(2,1)S(1)}, bf16[64,512]{1,0:T(8,128)(2,1)S(1)}, u32[]{:S(2)}, u32[]{:S(2)}) collective-permute-start(bf16[64,512]{1,0:T(8,128)(2,1)S(1)} %get-tuple-element.68.refs_0_), channel_id=1, source_target_pairs={{0,6},{1,7},{2,4},{3,5},{4,2},{5,3},{6,0},{7,1},{8,14},{9,15},{10,... | collective-permute-start | bytes 196616 | tf_op jit(solution)/shard_map/ppermute | solution.py:323
  65.3 7.8 %collective-permute-start.23 = (bf16[384,512]{1,0:T(8,128)(2,1)S(1)}, bf16[384,512]{1,0:T(8,128)(2,1)S(1)}, u32[]{:S(2)}, u32[]{:S(2)}) collective-permute-start(bf16[384,512]{1,0:T(8,128)(2,1)S(1)} %shard_map.131), channel_id=1, source_target_pairs={{0,4},{1,3},{2,6},{3,1},{4,0},{5,7},{6,2},{7,5},{8,12},{9,11},{10,... | collective-permute-start | bytes 1179656 | tf_op jit(solution)/shard_map/ppermute | solution.py:268
  67.8 1.6 %collective-permute-start.22 = (bf16[256,512]{1,0:T(8,128)(2,1)S(1)}, bf16[256,512]{1,0:T(8,128)(2,1)S(1)}, u32[]{:S(2)}, u32[]{:S(2)}) collective-permute-start(bf16[256,512]{1,0:T(8,128)(2,1)S(1)} %shard_map.132.mine_ref), channel_id=1, source_target_pairs={{0,1},{1,0},{2,3},{3,2},{4,5},{5,4},{6,7},{7,6},{8,9},{9,8},{10,11... | collective-permute-start | bytes 786440 | tf_op jit(solution)/shard_map/ppermute | solution.py:323

commit v14 on v13

--- a/solution.py
+++ b/solution.py
@@ -281,26 +281,27 @@
                 mate, (4, 3, 2), [[BF16], [BF16, F32], [F32]]
             )
             self.from_last = self.routed(self.to_last, straight)
-            self.from_plane = self.routed(self.to_plane, {1: -8, 3: 4})
+            self.from_side = self.routed(self.to_plane, {3: 4})
             return [self.to_last]
         if k == 1:
-            _, plane_rest = after(token, self.plane_rest)
+            _, plane_rest, to_plane = after(token, self.plane_rest, self.to_plane)
+            self.from_plane = self.routed(to_plane, {1: -8})
             out = summed_terms(
-                self.spot, [plane_rest, self.from_last, self.from_plane], [self.EVEN, self.MIDDLE, 0b10000000]
+                self.spot, [plane_rest, self.from_last, self.from_side], [self.EVEN, self.MIDDLE, 0b10000000]
             )
             self.from_planes = self.routed(out, {0: -8, 2: -8, 4: 8, 6: 8, 5: -8, 3: 8, 7: -8})
-            out, to_straight, mate = after(out, self.to_straight, self.mate)
+            out, mate = after(out, self.mate)
+            self.kept, self.to_across = take(mate, (0, 1), [[F32]] * 2, cost=10)
+            return [self.kept]
+        if k == 2:
+            _, rest, to_straight = after(token, self.to_across, self.to_straight)
             second = summed_terms(self.spot, [to_straight, self.from_plane], [None, 0b00000010])
             self.second = self.routed(second, straight)
-            self.kept, self.to_across = take(mate, (0, 1), [[F32]] * 2, cost=10)
-            return [second, self.kept]
-        if k == 2:
-            _, rest, _ = after(token, self.to_across, self.second)
             out = summed_terms(
                 self.spot, [rest, self.from_planes, self.from_last], [None, self.EVEN | 0b00101000, self.ENDS]
             )
             self.first = self.routed(out, across)
-            return [out]
+            return [second, out]
         return []
 
     def finish(self, token):

time: 74.4 us -> 73.9 us (level)
  the two profiles are of different devices: /device:TPU:16 before, /device:TPU:0 now
where the time goes in v14:
time: 73.9 us; the launch traced here: 73.6 us
  starting transfers between devices  35.9 us (49%)
  waiting for transfers between devices  19.9 us (27%)
  Pallas kernels  13.9 us (19%)
  local copies, waits for them, and re-layouts  2.4 us (3%)
  between operations  0.88 us (1%)
    ppermute x15, starting transfers between devices, swapped(): return lax.ppermute(value, 'blk', [(s, s ^ distance) for s in range(count)])  14.2 us
    pallas_call x15, Pallas kernels, call(): pl.pallas_call(kernel, out_shape=out_shape, in_specs=[spec(k) for k in ra...  13.9 us
    ppermute x6, starting transfers between devices, routed(): return lax.ppermute(value, 'blk', pairs)  11.1 us
    ppermute x4, starting transfers between devices, sent(): return lax.ppermute(value, 'blk', pairs)  10.5 us
    ppermute x4, waiting for transfers between devices, sent(): return lax.ppermute(value, 'blk', pairs)  7.94 us
    ppermute x15, waiting for transfers between devices, swapped(): return lax.ppermute(value, 'blk', [(s, s ^ distance) for s in range(count)])  6.24 us
    ppermute x6, waiting for transfers between devices, routed(): return lax.ppermute(value, 'blk', pairs)  5.75 us
    unnamed x12, local copies, waits for them, and re-layouts  1.53 us
  transfers between devices with their start and end apart: 25, of which 10 were waited for; matrix products, arithmetic and copies ran while one was open for 2% of the time, Pallas kernels for 15%

profile of v14, /device:TPU:0, one launch (start us, length us, event | category | flops | bytes accessed | tf_op | source)
XLA Modules:
  0.0 73.6 jit_solution(16393253896815933033)
XLA Ops:
  1.1 2.6 %collective-permute-start.2 = (bf16[384,512]{1,0:T(8,128)(2,1)}, bf16[384,512]{1,0:T(8,128)(2,1)S(1)}, u32[]{:S(2)}, u32[]{:S(2)}) collective-permute-start(bf16[384,512]{1,0:T(8,128)(2,1)} %refs_2_.1), channel_id=1, source_target_pairs={{0,4},{1,5},{2,6},{3,7},{4,8},{5,9},{6,10},{7,11},{8,12},{9,13},{1... | collective-permute-start | bytes 1179656 | tf_op jit(solution)/shard_map/ppermute | solution.py:221
  3.7 1.5 %collective-permute-start.3 = (bf16[384,512]{1,0:T(8,128)(2,1)}, bf16[384,512]{1,0:T(8,128)(2,1)S(1)}, u32[]{:S(2)}, u32[]{:S(2)}) collective-permute-start(bf16[384,512]{1,0:T(8,128)(2,1)} %refs_2_.1), channel_id=1, source_target_pairs={{0,2},{1,3},{2,4},{3,5},{4,6},{5,7},{6,8},{7,9},{8,10},{9,11},{10,... | collective-permute-start | bytes 1179656 | tf_op jit(solution)/shard_map/ppermute | solution.py:221
  5.2 4.1 %collective-permute-start.4 = (bf16[384,512]{1,0:T(8,128)(2,1)}, bf16[384,512]{1,0:T(8,128)(2,1)S(1)}, u32[]{:S(2)}, u32[]{:S(2)}) collective-permute-start(bf16[384,512]{1,0:T(8,128)(2,1)} %refs_2_.1), channel_id=1, source_target_pairs={{0,30},{1,31},{2,0},{3,1},{4,2},{5,3},{6,4},{7,5},{8,6},{9,7},{10,... | collective-permute-start | bytes 1179656 | tf_op jit(solution)/shard_map/ppermute | solution.py:221
  9.4 2.3 %collective-permute-start.5 = (bf16[384,512]{1,0:T(8,128)(2,1)}, bf16[384,512]{1,0:T(8,128)(2,1)S(1)}, u32[]{:S(2)}, u32[]{:S(2)}) collective-permute-start(bf16[384,512]{1,0:T(8,128)(2,1)} %refs_2_.1), channel_id=1, source_target_pairs={{0,28},{2,30},{4,0},{6,2},{8,4},{10,6},{12,8},{14,10},{16,12},{18,... | collective-permute-start | bytes 1179656 | tf_op jit(solution)/shard_map/ppermute | solution.py:221
  13.3 1.1 %collective-permute-done.1.mate_meta_ref = s32[120]{0:T(128)S(1)} collective-permute-done((s32[120]{0:T(128)S(1)}, s32[120]{0:T(128)S(1)}, u32[]{:S(2)}, u32[]{:S(2)}) %collective-permute-start.1) | collective-permute-done | bytes 512 | tf_op jit(solution)/shard_map/ppermute | solution.py:324
  14.4 1.5 %copy-done = bf16[1,8,7,128,128]{4,3,2,1,0:T(8,128)(2,1)S(1)} copy-done((bf16[1,8,7,128,128]{4,3,2,1,0:T(8,128)(2,1)S(1)}, bf16[1,8,7,128,128]{4,3,2,1,0:T(8,128)(2,1)}, u32[]{:S(2)}) %copy-start) | copy-done | bytes 1835032
  15.9 3.7 %shard_map.120 = (bf16[768,1920]{1,0:T(8,128)(2,1)S(1)}, bf16[1920,768]{1,0:T(8,128)(2,1)S(1)}) custom-call(s32[1]{0:T(128)} %bitcast.spot_ref.refs_0_, s32[120]{0:T(128)S(1)} %reshape.27.own_meta_ref, s32[120]{0:T(128)S(1)} %collective-permute-done.1.mate_meta_ref, bf16[8,7,128,128]{3,2,1,0:T(8,128)(2,1)S(1)} %bitcast.8, ...), custom_call_target="tpu_custom_call" | custom-call | tf_op jit(solution)/shard_map/pallas_call | solution.py:16
  19.6 6.1 %collective-permute-done.2.refs_0_ = bf16[384,512]{1,0:T(8,128)(2,1)S(1)} collective-permute-done((bf16[384,512]{1,0:T(8,128)(2,1)}, bf16[384,512]{1,0:T(8,128)(2,1)S(1)}, u32[]{:S(2)}, u32[]{:S(2)}) %collective-permute-start.2) | collective-permute-done | bytes 393248 | tf_op jit(solution)/shard_map/ppermute | solution.py:221
  26.3 1.8 %shard_map.121.refs_0_.own_ref = f32[768,512]{1,0:T(8,128)S(1)} custom-call(bf16[768,1920]{1,0:T(8,128)(2,1)S(1)} %get-tuple-element.44.dense_ref, bf16[384,512]{1,0:T(8,128)(2,1)S(1)} %collective-permute-done.2.refs_0_, bf16[384,512]{1,0:T(8,128)(2,1)S(1)} %collective-permute-done.3.refs_1_, bf16[384,512]{1,0:T(8,128)(2,1)S(1)} %copy-done.2, ...), custom_call_target="tpu_custom_call" | custom-call | tf_op jit(solution)/shard_map/pallas_call | solution.py:16
  28.1 1.2 %collective-permute-done.5.refs_1_ = bf16[384,512]{1,0:T(8,128)(2,1)S(1)} collective-permute-done((bf16[384,512]{1,0:T(8,128)(2,1)}, bf16[384,512]{1,0:T(8,128)(2,1)S(1)}, u32[]{:S(2)}, u32[]{:S(2)}) %collective-permute-start.5) | collective-permute-done | bytes 393248 | tf_op jit(solution)/shard_map/ppermute | solution.py:221
  29.8 2.3 %collective-permute-done.6.mate_ref = f32[384,512]{1,0:T(8,128)S(1)} collective-permute-done((f32[384,512]{1,0:T(8,128)S(1)}, f32[384,512]{1,0:T(8,128)S(1)}, u32[]{:S(2)}, u32[]{:S(2)}) %collective-permute-start.6) | collective-permute-done | bytes 786464 | tf_op jit(solution)/shard_map/ppermute | solution.py:324
  32.1 1.4 %shard_map.123 = (bf16[384,512]{1,0:T(8,128)(2,1)}, bf16[384,512]{1,0:T(8,128)(2,1)S(1)}, f32[4,80,512]{2,1,0:T(8,128)S(1)}, bf16[4,80,512]{2,1,0:T(8,128)(2,1)S(1)}) custom-call(s32[1]{0:T(128)} %bitcast.spot_ref.refs_0_, f32[768,512]{1,0:T(8,128)S(1)} %shard_map.121.refs_0_.own_ref, f32[384,512]{1,0:T(8,128)S(1)} %collective-permute-done.6.mate_ref, ...), custom_call_target="tpu_custom_call" | custom-call | tf_op jit(solution)/shard_map/pallas_call | solution.py:16
  34.0 1.7 %collective-permute-done.7.got_ref = bf16[4,80,512]{2,1,0:T(8,128)(2,1)S(1)} collective-permute-done((bf16[4,80,512]{2,1,0:T(8,128)(2,1)S(1)}, bf16[4,80,512]{2,1,0:T(8,128)(2,1)S(1)}, u32[]{:S(2)}, u32[]{:S(2)}) %collective-permute-start.7) | collective-permute-done | bytes 327712 | tf_op jit(solution)/shard_map/ppermute | solution.py:324
  35.7 1.5 %collective-permute-start.10 = (bf16[80,512]{1,0:T(8,128)(2,1)S(1)}, bf16[80,512]{1,0:T(8,128)(2,1)S(1)}, u32[]{:S(2)}, u32[]{:S(2)}) collective-permute-start(bf16[80,512]{1,0:T(8,128)(2,1)S(1)} %get-tuple-element.51), channel_id=1, source_target_pairs={{0,6},{1,7},{2,4},{3,5},{4,2},{5,3},{6,0},{7,1},{8,14},{9,15},{10,... | collective-permute-start | bytes 245768 | tf_op jit(solution)/shard_map/ppermute | solution.py:324
  37.8 1.5 %collective-permute-start.9 = (bf16[80,512]{1,0:T(8,128)(2,1)S(1)}, bf16[80,512]{1,0:T(8,128)(2,1)S(1)}, u32[]{:S(2)}, u32[]{:S(2)}) collective-permute-start(bf16[80,512]{1,0:T(8,128)(2,1)S(1)} %get-tuple-element.50), channel_id=1, source_target_pairs={{0,4},{1,5},{2,6},{3,7},{4,0},{5,1},{6,2},{7,3},{8,12},{9,13},{10,... | collective-permute-start | bytes 245768 | tf_op jit(solution)/shard_map/ppermute | solution.py:324
  39.3 1.9 %shard_map.125 = (bf16[384,512]{1,0:T(8,128)(2,1)S(1)}, bf16[384,512]{1,0:T(8,128)(2,1)S(1)}, f32[384,512]{1,0:T(8,128)S(1)}, f32[384,512]{1,0:T(8,128)S(1)}) custom-call(s32[1]{0:T(128)} %bitcast.spot_ref.refs_0_, s32[40]{0:T(128)S(1)} %copy-done.5, bf16[1920,768]{1,0:T(8,128)(2,1)S(1)} %get-tuple-element.52.refs_2_, ...), custom_call_target="tpu_custom_call" | custom-call | flops 10000000000 | tf_op jit(solution)/shard_map/pallas_call | solution.py:16
  41.2 1.6 %collective-permute-start.15 = (bf16[384,512]{1,0:T(8,128)(2,1)S(1)}, bf16[384,512]{1,0:T(8,128)(2,1)S(1)}, u32[]{:S(2)}, u32[]{:S(2)}) collective-permute-start(bf16[384,512]{1,0:T(8,128)(2,1)S(1)} %get-tuple-element.55), channel_id=1, source_target_pairs={{0,2},{1,5},{2,0},{3,7},{4,6},{5,1},{6,4},{7,3},{8,10},{9,13},{10,... | collective-permute-start | bytes 1179656 | tf_op jit(solution)/shard_map/ppermute | solution.py:268
  44.2 2.1 %collective-permute-start.13 = (bf16[80,512]{1,0:T(8,128)(2,1)S(1)}, bf16[80,512]{1,0:T(8,128)(2,1)S(1)}, u32[]{:S(2)}, u32[]{:S(2)}) collective-permute-start(bf16[80,512]{1,0:T(8,128)(2,1)S(1)} %shard_map.126.refs_0_), channel_id=1, source_target_pairs={{0,16},{1,17},{2,18},{3,19},{4,20},{5,21},{6,22},{7,23},{8,24},{9,... | collective-permute-start | bytes 245768 | tf_op jit(solution)/shard_map/ppermute | solution.py:324
  46.3 1.7 %collective-permute-start.14 = (bf16[80,512]{1,0:T(8,128)(2,1)S(1)}, bf16[80,512]{1,0:T(8,128)(2,1)S(1)}, u32[]{:S(2)}, u32[]{:S(2)}) collective-permute-start(bf16[80,512]{1,0:T(8,128)(2,1)S(1)} %shard_map.126.refs_0_), channel_id=1, source_target_pairs={{0,24},{1,25},{2,26},{3,27},{4,28},{5,29},{6,30},{7,31},{8,16},{9,... | collective-permute-start | bytes 245768 | tf_op jit(solution)/shard_map/ppermute | solution.py:324
  48.0 1.1 %collective-permute-done.15.refs_1_.refs_2_ = bf16[384,512]{1,0:T(8,128)(2,1)S(1)} collective-permute-done((bf16[384,512]{1,0:T(8,128)(2,1)S(1)}, bf16[384,512]{1,0:T(8,128)(2,1)S(1)}, u32[]{:S(2)}, u32[]{:S(2)}) %collective-permute-start.15) | collective-permute-done | bytes 393248 | tf_op jit(solution)/shard_map/ppermute | solution.py:268
  50.0 4.1 %collective-permute-start.21 = (bf16[384,512]{1,0:T(8,128)(2,1)S(1)}, bf16[384,512]{1,0:T(8,128)(2,1)S(1)}, u32[]{:S(2)}, u32[]{:S(2)}) collective-permute-start(bf16[384,512]{1,0:T(8,128)(2,1)S(1)} %shard_map.127), channel_id=1, source_target_pairs={{0,24},{2,26},{3,11},{4,12},{5,29},{6,14},{7,31},{8,0},{10,2},{11,... | collective-permute-start | bytes 1179656 | tf_op jit(solution)/shard_map/ppermute | solution.py:268
  54.1 1.5 %shard_map.128 = (f32[384,512]{1,0:T(8,128)S(1)}, f32[384,512]{1,0:T(8,128)S(1)}) custom-call(s32[1]{0:T(128)} %bitcast.spot_ref.refs_0_, s32[40]{0:T(128)S(1)} %copy-done.5, bf16[1920,768]{1,0:T(8,128)(2,1)S(1)} %get-tuple-element.52.refs_2_, bf16[384,512]{1,0:T(8,128)(2,1)S(1)} %get-tuple-element.53.refs_3_, ...), custom_call_target="tpu_custom_call" | custom-call | flops 10000000000 | tf_op jit(solution)/shard_map/pallas_call | solution.py:16
  56.2 1.4 %collective-permute-start.17 = (bf16[64,512]{1,0:T(8,128)(2,1)S(1)}, bf16[64,512]{1,0:T(8,128)(2,1)S(1)}, u32[]{:S(2)}, u32[]{:S(2)}) collective-permute-start(bf16[64,512]{1,0:T(8,128)(2,1)S(1)} %get-tuple-element.67.refs_0_), channel_id=1, source_target_pairs={{0,2},{1,3},{2,0},{3,1},{4,6},{5,7},{6,4},{7,5},{8,10},{9,11},{10,... | collective-permute-start | bytes 196616 | tf_op jit(solution)/shard_map/ppermute | solution.py:324
  57.6 2.1 %collective-permute-start.19 = (bf16[64,512]{1,0:T(8,128)(2,1)S(1)}, bf16[64,512]{1,0:T(8,128)(2,1)S(1)}, u32[]{:S(2)}, u32[]{:S(2)}) collective-permute-start(bf16[64,512]{1,0:T(8,128)(2,1)S(1)} %get-tuple-element.67.refs_0_), channel_id=1, source_target_pairs={{0,6},{1,7},{2,4},{3,5},{4,2},{5,3},{6,0},{7,1},{8,14},{9,15},{10,... | collective-permute-start | bytes 196616 | tf_op jit(solution)/shard_map/ppermute | solution.py:324
  59.8 1.5 %collective-permute-start.23 = (bf16[384,512]{1,0:T(8,128)(2,1)S(1)}, bf16[384,512]{1,0:T(8,128)(2,1)S(1)}, u32[]{:S(2)}, u32[]{:S(2)}) collective-permute-start(bf16[384,512]{1,0:T(8,128)(2,1)S(1)} %shard_map.130), channel_id=1, source_target_pairs={{0,2},{1,5},{2,0},{3,7},{4,6},{5,1},{6,4},{7,3},{8,10},{9,13},{10,... | collective-permute-start | bytes 1179656 | tf_op jit(solution)/shard_map/ppermute | solution.py:268
  61.5 2.6 %collective-permute-start.24 = (bf16[384,512]{1,0:T(8,128)(2,1)S(1)}, bf16[384,512]{1,0:T(8,128)(2,1)S(1)}, u32[]{:S(2)}, u32[]{:S(2)}) collective-permute-start(bf16[384,512]{1,0:T(8,128)(2,1)S(1)} %shard_map.131), channel_id=1, source_target_pairs={{0,4},{1,3},{2,6},{3,1},{4,0},{5,7},{6,2},{7,5},{8,12},{9,11},{10,... | collective-permute-start | bytes 1179656 | tf_op jit(solution)/shard_map/ppermute | solution.py:268
  64.2 1.6 %collective-permute-start.22 = (bf16[256,512]{1,0:T(8,128)(2,1)S(1)}, bf16[256,512]{1,0:T(8,128)(2,1)S(1)}, u32[]{:S(2)}, u32[]{:S(2)}) collective-permute-start(bf16[256,512]{1,0:T(8,128)(2,1)S(1)} %shard_map.132.mine_ref), channel_id=1, source_target_pairs={{0,1},{1,0},{2,3},{3,2},{4,5},{5,4},{6,7},{7,6},{8,9},{9,8},{10,11... | collective-permute-start | bytes 786440 | tf_op jit(solution)/shard_map/ppermute | solution.py:324
  65.8 1.2 %collective-permute-done.22.other_ref = bf16[256,512]{1,0:T(8,128)(2,1)S(1)} collective-permute-done((bf16[256,512]{1,0:T(8,128)(2,1)S(1)}, bf16[256,512]{1,0:T(8,128)(2,1)S(1)}, u32[]{:S(2)}, u32[]{:S(2)}) %collective-permute-start.22) | collective-permute-done | bytes 262176 | tf_op jit(solution)/shard_map/ppermute | solution.py:324
  66.9 1.0 %shard_map.133 = f32[512,512]{1,0:T(8,128)} custom-call(s32[1]{0:T(128)} %bitcast.spot_ref.refs_0_, bf16[256,512]{1,0:T(8,128)(2,1)S(1)} %shard_map.132.mine_ref, bf16[256,512]{1,0:T(8,128)(2,1)S(1)} %collective-permute-done.22.other_ref), custom_call_target="tpu_custom_call" | custom-call | tf_op jit(solution)/shard_map/pallas_call | solution.py:16
  68.0 1.8 %collective-permute-done.23.refs_1_ = bf16[384,512]{1,0:T(8,128)(2,1)S(1)} collective-permute-done((bf16[384,512]{1,0:T(8,128)(2,1)S(1)}, bf16[384,512]{1,0:T(8,128)(2,1)S(1)}, u32[]{:S(2)}, u32[]{:S(2)}) %collective-permute-start.23) | collective-permute-done | bytes 393248 | tf_op jit(solution)/shard_map/ppermute | solution.py:268
  69.8 2.9 %collective-permute-done.24.refs_2_ = bf16[384,512]{1,0:T(8,128)(2,1)S(1)} collective-permute-done((bf16[384,512]{1,0:T(8,128)(2,1)S(1)}, bf16[384,512]{1,0:T(8,128)(2,1)S(1)}, u32[]{:S(2)}, u32[]{:S(2)}) %collective-permute-start.24) | collective-permute-done | bytes 393248 | tf_op jit(solution)/shard_map/ppermute | solution.py:268
  72.7 1.0 %shard_map.134 = bf16[384,512]{1,0:T(8,128)(2,1)} custom-call(s32[1]{0:T(128)} %bitcast.spot_ref.refs_0_, f32[384,512]{1,0:T(8,128)S(1)} %get-tuple-element.76.refs_0_, bf16[384,512]{1,0:T(8,128)(2,1)S(1)} %collective-permute-done.23.refs_1_, bf16[384,512]{1,0:T(8,128)(2,1)S(1)} %collective-permute-done.24.refs_2_, ...), custom_call_target="tpu_custom_call" | custom-call | flops 10000000000 | tf_op jit(solution)/shard_map/pallas_call | solution.py:16
  (49 shorter events, 7.4 us)
Async XLA Ops:
  0.6 11.1 %collective-permute-start = (bf16[8,7,128,128]{3,2,1,0:T(8,128)(2,1)}, bf16[8,7,128,128]{3,2,1,0:T(8,128)(2,1)S(1)}, u32[]{:S(2)}, u32[]{:S(2)}) collective-permute-start(bf16[8,7,128,128]{3,2,1,0:T(8,128)(2,1)} %bitcast.7), channel_id=1, source_target_pairs={{0,1},{1,0},{2,3},{3,2},{4,5},{5,4},{6,7},{7,6},{8,9},{9,8},{10,11... | collective-permute-start | bytes 5505032 | tf_op jit(solution)/shard_map/ppermute | solution.py:324
  1.1 24.5 %collective-permute-start.2 = (bf16[384,512]{1,0:T(8,128)(2,1)}, bf16[384,512]{1,0:T(8,128)(2,1)S(1)}, u32[]{:S(2)}, u32[]{:S(2)}) collective-permute-start(bf16[384,512]{1,0:T(8,128)(2,1)} %refs_2_.1), channel_id=1, source_target_pairs={{0,4},{1,5},{2,6},{3,7},{4,8},{5,9},{6,10},{7,11},{8,12},{9,13},{1... | collective-permute-start | bytes 1179656 | tf_op jit(solution)/shard_map/ppermute | solution.py:221
  3.7 22.5 %collective-permute-start.3 = (bf16[384,512]{1,0:T(8,128)(2,1)}, bf16[384,512]{1,0:T(8,128)(2,1)S(1)}, u32[]{:S(2)}, u32[]{:S(2)}) collective-permute-start(bf16[384,512]{1,0:T(8,128)(2,1)} %refs_2_.1), channel_id=1, source_target_pairs={{0,2},{1,3},{2,4},{3,5},{4,6},{5,7},{6,8},{7,9},{8,10},{9,11},{10,... | collective-permute-start | bytes 1179656 | tf_op jit(solution)/shard_map/ppermute | solution.py:221
  5.2 21.1 %collective-permute-start.4 = (bf16[384,512]{1,0:T(8,128)(2,1)}, bf16[384,512]{1,0:T(8,128)(2,1)S(1)}, u32[]{:S(2)}, u32[]{:S(2)}) collective-permute-start(bf16[384,512]{1,0:T(8,128)(2,1)} %refs_2_.1), channel_id=1, source_target_pairs={{0,30},{1,31},{2,0},{3,1},{4,2},{5,3},{6,4},{7,5},{8,6},{9,7},{10,... | collective-permute-start | bytes 1179656 | tf_op jit(solution)/shard_map/ppermute | solution.py:221
  9.4 20.0 %collective-permute-start.5 = (bf16[384,512]{1,0:T(8,128)(2,1)}, bf16[384,512]{1,0:T(8,128)(2,1)S(1)}, u32[]{:S(2)}, u32[]{:S(2)}) collective-permute-start(bf16[384,512]{1,0:T(8,128)(2,1)} %refs_2_.1), channel_id=1, source_target_pairs={{0,28},{2,30},{4,0},{6,2},{8,4},{10,6},{12,8},{14,10},{16,12},{18,... | collective-permute-start | bytes 1179656 | tf_op jit(solution)/shard_map/ppermute | solution.py:221
  13.2 1.1 %collective-permute-start.1 = (s32[120]{0:T(128)S(1)}, s32[120]{0:T(128)S(1)}, u32[]{:S(2)}, u32[]{:S(2)}) collective-permute-start(s32[120]{0:T(128)S(1)} %reshape.27.own_meta_ref), channel_id=1, source_target_pairs={{0,1},{1,0},{2,3},{3,2},{4,5},{5,4},{6,7},{7,6},{8,9},{9,8},{10,11... | collective-permute-start | bytes 1448 | tf_op jit(solution)/shard_map/ppermute | solution.py:324
  14.4 1.5 %copy-start = (bf16[1,8,7,128,128]{4,3,2,1,0:T(8,128)(2,1)S(1)}, bf16[1,8,7,128,128]{4,3,2,1,0:T(8,128)(2,1)}, u32[]{:S(2)}) copy-start(bf16[1,8,7,128,128]{4,3,2,1,0:T(8,128)(2,1)} %param.12) | copy-start | bytes 5505028
  15.9 10.4 %copy-start.2 = (bf16[384,512]{1,0:T(8,128)(2,1)S(1)}, bf16[384,512]{1,0:T(8,128)(2,1)}, u32[]{:S(2)}) copy-start(bf16[384,512]{1,0:T(8,128)(2,1)} %refs_2_.1) | copy-start | bytes 1179652
  28.1 4.0 %copy-start.1 = (bf16[512,512]{1,0:T(8,128)(2,1)S(1)}, bf16[512,512]{1,0:T(8,128)(2,1)}, u32[]{:S(2)}) copy-start(bf16[512,512]{1,0:T(8,128)(2,1)} %weight_ref.1) | copy-start | bytes 1572868
  28.1 4.0 %copy-start.3 = (bf16[384,512]{1,0:T(8,128)(2,1)S(1)}, bf16[384,512]{1,0:T(8,128)(2,1)}, u32[]{:S(2)}) copy-start(bf16[384,512]{1,0:T(8,128)(2,1)} %grad_out_ref.1) | copy-start | bytes 1179652
  28.1 4.0 %copy-start.4 = (f32[512]{0:T(512)S(1)}, f32[512]{0:T(512)}, u32[]{:S(2)}) copy-start(f32[512]{0:T(512)} %param.14) | copy-start | bytes 6148
  29.7 2.4 %collective-permute-start.6 = (f32[384,512]{1,0:T(8,128)S(1)}, f32[384,512]{1,0:T(8,128)S(1)}, u32[]{:S(2)}, u32[]{:S(2)}) collective-permute-start(f32[384,512]{1,0:T(8,128)S(1)} %shard_map.122), channel_id=1, source_target_pairs={{0,1},{1,0},{2,3},{3,2},{4,5},{5,4},{6,7},{7,6},{8,9},{9,8},{10,11... | collective-permute-start | bytes 2359304 | tf_op jit(solution)/shard_map/ppermute | solution.py:324
  32.1 7.2 %copy-start.5 = (s32[40]{0:T(128)S(1)}, s32[40]{0:T(128)}, u32[]{:S(2)}) copy-start(s32[40]{0:T(128)} %constant.23.refs_1_) | copy-start | bytes 484
  33.5 5.8 %collective-permute-start.11 = (bf16[384,512]{1,0:T(8,128)(2,1)S(1)}, bf16[384,512]{1,0:T(8,128)(2,1)S(1)}, u32[]{:S(2)}, u32[]{:S(2)}) collective-permute-start(bf16[384,512]{1,0:T(8,128)(2,1)S(1)} %get-tuple-element.53.refs_3_), channel_id=1, source_target_pairs={{0,1},{1,0},{2,3},{3,2},{4,5},{5,4},{6,7},{7,6},{8,9},{9,8},{10,11... | collective-permute-start | bytes 1179656 | tf_op jit(solution)/shard_map/ppermute | solution.py:324
  33.6 2.1 %collective-permute-start.7 = (bf16[4,80,512]{2,1,0:T(8,128)(2,1)S(1)}, bf16[4,80,512]{2,1,0:T(8,128)(2,1)S(1)}, u32[]{:S(2)}, u32[]{:S(2)}) collective-permute-start(bf16[4,80,512]{2,1,0:T(8,128)(2,1)S(1)} %get-tuple-element.47), channel_id=1, source_target_pairs={{0,1},{1,0},{2,3},{3,2},{4,5},{5,4},{6,7},{7,6},{8,9},{9,8},{10,11... | collective-permute-start | bytes 983048 | tf_op jit(solution)/shard_map/ppermute | solution.py:324
  35.7 7.7 %collective-permute-start.10 = (bf16[80,512]{1,0:T(8,128)(2,1)S(1)}, bf16[80,512]{1,0:T(8,128)(2,1)S(1)}, u32[]{:S(2)}, u32[]{:S(2)}) collective-permute-start(bf16[80,512]{1,0:T(8,128)(2,1)S(1)} %get-tuple-element.51), channel_id=1, source_target_pairs={{0,6},{1,7},{2,4},{3,5},{4,2},{5,3},{6,0},{7,1},{8,14},{9,15},{10,... | collective-permute-start | bytes 245768 | tf_op jit(solution)/shard_map/ppermute | solution.py:324
  37.3 6.2 %collective-permute-start.8 = (bf16[80,512]{1,0:T(8,128)(2,1)S(1)}, bf16[80,512]{1,0:T(8,128)(2,1)S(1)}, u32[]{:S(2)}, u32[]{:S(2)}) collective-permute-start(bf16[80,512]{1,0:T(8,128)(2,1)S(1)} %get-tuple-element.49), channel_id=1, source_target_pairs={{0,2},{1,3},{2,0},{3,1},{4,6},{5,7},{6,4},{7,5},{8,10},{9,11},{10,... | collective-permute-start | bytes 245768 | tf_op jit(solution)/shard_map/ppermute | solution.py:324
  37.8 5.7 %collective-permute-start.9 = (bf16[80,512]{1,0:T(8,128)(2,1)S(1)}, bf16[80,512]{1,0:T(8,128)(2,1)S(1)}, u32[]{:S(2)}, u32[]{:S(2)}) collective-permute-start(bf16[80,512]{1,0:T(8,128)(2,1)S(1)} %get-tuple-element.50), channel_id=1, source_target_pairs={{0,4},{1,5},{2,6},{3,7},{4,0},{5,1},{6,2},{7,3},{8,12},{9,13},{10,... | collective-permute-start | bytes 245768 | tf_op jit(solution)/shard_map/ppermute | solution.py:324
  41.2 7.8 %collective-permute-start.15 = (bf16[384,512]{1,0:T(8,128)(2,1)S(1)}, bf16[384,512]{1,0:T(8,128)(2,1)S(1)}, u32[]{:S(2)}, u32[]{:S(2)}) collective-permute-start(bf16[384,512]{1,0:T(8,128)(2,1)S(1)} %get-tuple-element.55), channel_id=1, source_target_pairs={{0,2},{1,5},{2,0},{3,7},{4,6},{5,1},{6,4},{7,3},{8,10},{9,13},{10,... | collective-permute-start | bytes 1179656 | tf_op jit(solution)/shard_map/ppermute | solution.py:268
  42.8 7.0 %collective-permute-start.16 = (bf16[384,512]{1,0:T(8,128)(2,1)S(1)}, bf16[384,512]{1,0:T(8,128)(2,1)S(1)}, u32[]{:S(2)}, u32[]{:S(2)}) collective-permute-start(bf16[384,512]{1,0:T(8,128)(2,1)S(1)} %get-tuple-element.71), channel_id=1, source_target_pairs={{3,7},{11,15},{19,23},{27,31}} | collective-permute-start | bytes 1179656 | tf_op jit(solution)/shard_map/ppermute | solution.py:268
  43.5 12.1 %collective-permute-start.12 = (bf16[80,512]{1,0:T(8,128)(2,1)S(1)}, bf16[80,512]{1,0:T(8,128)(2,1)S(1)}, u32[]{:S(2)}, u32[]{:S(2)}) collective-permute-start(bf16[80,512]{1,0:T(8,128)(2,1)S(1)} %shard_map.126.refs_0_), channel_id=1, source_target_pairs={{0,8},{1,9},{2,10},{3,11},{4,12},{5,13},{6,14},{7,15},{8,0},{9,1},... | collective-permute-start | bytes 245768 | tf_op jit(solution)/shard_map/ppermute | solution.py:324
  44.2 11.5 %collective-permute-start.13 = (bf16[80,512]{1,0:T(8,128)(2,1)S(1)}, bf16[80,512]{1,0:T(8,128)(2,1)S(1)}, u32[]{:S(2)}, u32[]{:S(2)}) collective-permute-start(bf16[80,512]{1,0:T(8,128)(2,1)S(1)} %shard_map.126.refs_0_), channel_id=1, source_target_pairs={{0,16},{1,17},{2,18},{3,19},{4,20},{5,21},{6,22},{7,23},{8,24},{9,... | collective-permute-start | bytes 245768 | tf_op jit(solution)/shard_map/ppermute | solution.py:324
  46.3 9.3 %collective-permute-start.14 = (bf16[80,512]{1,0:T(8,128)(2,1)S(1)}, bf16[80,512]{1,0:T(8,128)(2,1)S(1)}, u32[]{:S(2)}, u32[]{:S(2)}) collective-permute-start(bf16[80,512]{1,0:T(8,128)(2,1)S(1)} %shard_map.126.refs_0_), channel_id=1, source_target_pairs={{0,24},{1,25},{2,26},{3,27},{4,28},{5,29},{6,30},{7,31},{8,16},{9,... | collective-permute-start | bytes 245768 | tf_op jit(solution)/shard_map/ppermute | solution.py:324
  49.1 10.7 %collective-permute-start.20 = (bf16[384,512]{1,0:T(8,128)(2,1)S(1)}, bf16[384,512]{1,0:T(8,128)(2,1)S(1)}, u32[]{:S(2)}, u32[]{:S(2)}) collective-permute-start(bf16[384,512]{1,0:T(8,128)(2,1)S(1)} %get-tuple-element.71), channel_id=1, source_target_pairs={{1,25},{9,1},{17,9},{25,17}} | collective-permute-start | bytes 1179656 | tf_op jit(solution)/shard_map/ppermute | solution.py:268
  50.0 11.3 %collective-permute-start.21 = (bf16[384,512]{1,0:T(8,128)(2,1)S(1)}, bf16[384,512]{1,0:T(8,128)(2,1)S(1)}, u32[]{:S(2)}, u32[]{:S(2)}) collective-permute-start(bf16[384,512]{1,0:T(8,128)(2,1)S(1)} %shard_map.127), channel_id=1, source_target_pairs={{0,24},{2,26},{3,11},{4,12},{5,29},{6,14},{7,31},{8,0},{10,2},{11,... | collective-permute-start | bytes 1179656 | tf_op jit(solution)/shard_map/ppermute | solution.py:268
  56.2 7.9 %collective-permute-start.17 = (bf16[64,512]{1,0:T(8,128)(2,1)S(1)}, bf16[64,512]{1,0:T(8,128)(2,1)S(1)}, u32[]{:S(2)}, u32[]{:S(2)}) collective-permute-start(bf16[64,512]{1,0:T(8,128)(2,1)S(1)} %get-tuple-element.67.refs_0_), channel_id=1, source_target_pairs={{0,2},{1,3},{2,0},{3,1},{4,6},{5,7},{6,4},{7,5},{8,10},{9,11},{10,... | collective-permute-start | bytes 196616 | tf_op jit(solution)/shard_map/ppermute | solution.py:324
  57.6 6.5 %collective-permute-start.18 = (bf16[64,512]{1,0:T(8,128)(2,1)S(1)}, bf16[64,512]{1,0:T(8,128)(2,1)S(1)}, u32[]{:S(2)}, u32[]{:S(2)}) collective-permute-start(bf16[64,512]{1,0:T(8,128)(2,1)S(1)} %get-tuple-element.67.refs_0_), channel_id=1, source_target_pairs={{0,4},{1,5},{2,6},{3,7},{4,0},{5,1},{6,2},{7,3},{8,12},{9,13},{10,... | collective-permute-start | bytes 196616 | tf_op jit(solution)/shard_map/ppermute | solution.py:324
  57.6 6.5 %collective-permute-start.19 = (bf16[64,512]{1,0:T(8,128)(2,1)S(1)}, bf16[64,512]{1,0:T(8,128)(2,1)S(1)}, u32[]{:S(2)}, u32[]{:S(2)}) collective-permute-start(bf16[64,512]{1,0:T(8,128)(2,1)S(1)} %get-tuple-element.67.refs_0_), channel_id=1, source_target_pairs={{0,6},{1,7},{2,4},{3,5},{4,2},{5,3},{6,0},{7,1},{8,14},{9,15},{10,... | collective-permute-start | bytes 196616 | tf_op jit(solution)/shard_map/ppermute | solution.py:324
  59.8 9.9 %collective-permute-start.23 = (bf16[384,512]{1,0:T(8,128)(2,1)S(1)}, bf16[384,512]{1,0:T(8,128)(2,1)S(1)}, u32[]{:S(2)}, u32[]{:S(2)}) collective-permute-start(bf16[384,512]{1,0:T(8,128)(2,1)S(1)} %shard_map.130), channel_id=1, source_target_pairs={{0,2},{1,5},{2,0},{3,7},{4,6},{5,1},{6,4},{7,3},{8,10},{9,13},{10,... | collective-permute-start | bytes 1179656 | tf_op jit(solution)/shard_map/ppermute | solution.py:268
  61.5 11.2 %collective-permute-start.24 = (bf16[384,512]{1,0:T(8,128)(2,1)S(1)}, bf16[384,512]{1,0:T(8,128)(2,1)S(1)}, u32[]{:S(2)}, u32[]{:S(2)}) collective-permute-start(bf16[384,512]{1,0:T(8,128)(2,1)S(1)} %shard_map.131), channel_id=1, source_target_pairs={{0,4},{1,3},{2,6},{3,1},{4,0},{5,7},{6,2},{7,5},{8,12},{9,11},{10,... | collective-permute-start | bytes 1179656 | tf_op jit(solution)/shard_map/ppermute | solution.py:268
  64.2 2.8 %collective-permute-start.22 = (bf16[256,512]{1,0:T(8,128)(2,1)S(1)}, bf16[256,512]{1,0:T(8,128)(2,1)S(1)}, u32[]{:S(2)}, u32[]{:S(2)}) collective-permute-start(bf16[256,512]{1,0:T(8,128)(2,1)S(1)} %shard_map.132.mine_ref), channel_id=1, source_target_pairs={{0,1},{1,0},{2,3},{3,2},{4,5},{5,4},{6,7},{7,6},{8,9},{9,8},{10,11... | collective-permute-start | bytes 786440 | tf_op jit(solution)/shard_map/ppermute | solution.py:324

commit v15 on v14

--- a/solution.py
+++ b/solution.py
@@ -177,7 +177,7 @@
         refs[-2][...] = parts[0][:piece].astype(BF16)
         refs[-1][...] = parts[0][piece : piece + 1]
 
-    return call(kernel, [((piece, hidden), BF16), ((1, hidden), F32)], list(values), cost=10)
+    return call(kernel, [((piece, hidden), BF16), ((1, hidden), F32)], list(values), cost=4)
 
 
 def scattered_sums(flipped, own, mate, columns, dtypes, spot=None, lookup=None, cost=10):
@@ -278,36 +278,36 @@
         if k == 0:
             _, mate = after(token, self.mate)
             self.to_last, self.to_plane, self.plane_rest, self.to_straight = take(
-                mate, (4, 3, 2), [[BF16], [BF16, F32], [F32]]
+                mate, (4, 3, 2), [[BF16], [BF16, F32], [BF16]]
             )
             self.from_last = self.routed(self.to_last, straight)
             self.from_side = self.routed(self.to_plane, {3: 4})
             return [self.to_last]
         if k == 1:
-            _, plane_rest, to_plane = after(token, self.plane_rest, self.to_plane)
-            self.from_plane = self.routed(to_plane, {1: -8})
+            _, plane_rest = after(token, self.plane_rest)
             out = summed_terms(
                 self.spot, [plane_rest, self.from_last, self.from_side], [self.EVEN, self.MIDDLE, 0b10000000]
             )
             self.from_planes = self.routed(out, {0: -8, 2: -8, 4: 8, 6: 8, 5: -8, 3: 8, 7: -8})
-            out, mate = after(out, self.mate)
+            out, mate, to_straight = after(out, self.mate, self.to_straight)
+            self.second = self.routed(to_straight, {spot: straight[spot] for spot in (0, 2, 4, 5, 6, 7)})
             self.kept, self.to_across = take(mate, (0, 1), [[F32]] * 2, cost=10)
             return [self.kept]
         if k == 2:
-            _, rest, to_straight = after(token, self.to_across, self.to_straight)
-            second = summed_terms(self.spot, [to_straight, self.from_plane], [None, 0b00000010])
-            self.second = self.routed(second, straight)
+            _, rest, to_plane, _ = after(token, self.to_across, self.to_plane, self.second)
+            from_plane = self.routed(to_plane, {1: -8})
+            self.passed = self.routed(from_plane, {1: 4})
             out = summed_terms(
                 self.spot, [rest, self.from_planes, self.from_last], [None, self.EVEN | 0b00101000, self.ENDS]
             )
             self.first = self.routed(out, across)
-            return [second, out]
+            return [out, from_plane]
         return []
 
     def finish(self, token):
         _, kept = after(token, self.kept)
-        terms = [kept, self.second, self.first, self.from_planes]
-        return summed_terms(self.spot, terms, [None, None, None, 0b10000000])
+        terms = [kept, self.second, self.first, self.from_planes, self.passed]
+        return summed_terms(self.spot, terms, [None, None, None, 0b10000000, 0b00100000])
 
 
 def local(features, tile_list, tile_count, tile_values, weight, bias, grad_out):

time: 73.9 us -> 77.8 us (1.053)
  the two profiles are of different devices: /device:TPU:0 before, /device:TPU:1 now
where the time goes in v15:
time: 77.8 us; the launch traced here: 77.5 us
  starting transfers between devices  40.6 us (52%)
  waiting for transfers between devices  18.8 us (24%)
  Pallas kernels  14.2 us (18%)
  local copies, waits for them, and re-layouts  2.39 us (3%)
  between operations  0.86 us (1%)
    ppermute x15, starting transfers between devices, swapped(): return lax.ppermute(value, 'blk', [(s, s ^ distance) for s in range(count)])  22.1 us
    pallas_call x14, Pallas kernels, call(): pl.pallas_call(kernel, out_shape=out_shape, in_specs=[spec(k) for k in ra...  14.2 us
    ppermute x7, starting transfers between devices, routed(): return lax.ppermute(value, 'blk', pairs)  10.1 us
    ppermute x4, starting transfers between devices, sent(): return lax.ppermute(value, 'blk', pairs)  8.42 us
    ppermute x15, waiting for transfers between devices, swapped(): return lax.ppermute(value, 'blk', [(s, s ^ distance) for s in range(count)])  7.07 us
    ppermute x7, waiting for transfers between devices, routed(): return lax.ppermute(value, 'blk', pairs)  5.98 us
    ppermute x4, waiting for transfers between devices, sent(): return lax.ppermute(value, 'blk', pairs)  5.73 us
  transfers between devices with their start and end apart: 26, of which 10 were waited for; matrix products, arithmetic and copies ran while one was open for 2% of the time, Pallas kernels for 15%

profile of v15, /device:TPU:1, one launch (start us, length us, event | category | flops | bytes accessed | tf_op | source)
XLA Modules:
  0.0 77.5 jit_solution(5890220516634519601)
XLA Ops:
  0.8 2.7 %collective-permute-start.2 = (bf16[384,512]{1,0:T(8,128)(2,1)}, bf16[384,512]{1,0:T(8,128)(2,1)S(1)}, u32[]{:S(2)}, u32[]{:S(2)}) collective-permute-start(bf16[384,512]{1,0:T(8,128)(2,1)} %refs_2_.1), channel_id=1, source_target_pairs={{0,4},{1,5},{2,6},{3,7},{4,8},{5,9},{6,10},{7,11},{8,12},{9,13},{1... | collective-permute-start | bytes 1179656 | tf_op jit(solution)/shard_map/ppermute | solution.py:221
  3.4 1.2 %collective-permute-start.3 = (bf16[384,512]{1,0:T(8,128)(2,1)}, bf16[384,512]{1,0:T(8,128)(2,1)S(1)}, u32[]{:S(2)}, u32[]{:S(2)}) collective-permute-start(bf16[384,512]{1,0:T(8,128)(2,1)} %refs_2_.1), channel_id=1, source_target_pairs={{0,2},{1,3},{2,4},{3,5},{4,6},{5,7},{6,8},{7,9},{8,10},{9,11},{10,... | collective-permute-start | bytes 1179656 | tf_op jit(solution)/shard_map/ppermute | solution.py:221
  4.7 3.9 %collective-permute-start.4 = (bf16[384,512]{1,0:T(8,128)(2,1)}, bf16[384,512]{1,0:T(8,128)(2,1)S(1)}, u32[]{:S(2)}, u32[]{:S(2)}) collective-permute-start(bf16[384,512]{1,0:T(8,128)(2,1)} %refs_2_.1), channel_id=1, source_target_pairs={{0,30},{1,31},{2,0},{3,1},{4,2},{5,3},{6,4},{7,5},{8,6},{9,7},{10,... | collective-permute-start | bytes 1179656 | tf_op jit(solution)/shard_map/ppermute | solution.py:221
  10.7 2.6 %collective-permute-start.1 = (s32[120]{0:T(128)S(1)}, s32[120]{0:T(128)S(1)}, u32[]{:S(2)}, u32[]{:S(2)}) collective-permute-start(s32[120]{0:T(128)S(1)} %reshape.27.own_meta_ref), channel_id=1, source_target_pairs={{0,1},{1,0},{2,3},{3,2},{4,5},{5,4},{6,7},{7,6},{8,9},{9,8},{10,11... | collective-permute-start | bytes 1448 | tf_op jit(solution)/shard_map/ppermute | solution.py:324
  14.1 1.5 %copy-done = bf16[1,8,7,128,128]{4,3,2,1,0:T(8,128)(2,1)S(1)} copy-done((bf16[1,8,7,128,128]{4,3,2,1,0:T(8,128)(2,1)S(1)}, bf16[1,8,7,128,128]{4,3,2,1,0:T(8,128)(2,1)}, u32[]{:S(2)}) %copy-start) | copy-done | bytes 1835032
  15.6 4.0 %shard_map.120 = (bf16[768,1920]{1,0:T(8,128)(2,1)S(1)}, bf16[1920,768]{1,0:T(8,128)(2,1)S(1)}) custom-call(s32[1]{0:T(128)} %bitcast.spot_ref.refs_0_, s32[120]{0:T(128)S(1)} %reshape.27.own_meta_ref, s32[120]{0:T(128)S(1)} %collective-permute-done.1.mate_meta_ref, bf16[8,7,128,128]{3,2,1,0:T(8,128)(2,1)S(1)} %bitcast.8, ...), custom_call_target="tpu_custom_call" | custom-call | tf_op jit(solution)/shard_map/pallas_call | solution.py:16
  19.7 0.9 %collective-permute-done.2.refs_0_ = bf16[384,512]{1,0:T(8,128)(2,1)S(1)} collective-permute-done((bf16[384,512]{1,0:T(8,128)(2,1)}, bf16[384,512]{1,0:T(8,128)(2,1)S(1)}, u32[]{:S(2)}, u32[]{:S(2)}) %collective-permute-start.2) | collective-permute-done | bytes 393248 | tf_op jit(solution)/shard_map/ppermute | solution.py:221
  20.6 4.8 %collective-permute-done.3.refs_1_ = bf16[384,512]{1,0:T(8,128)(2,1)S(1)} collective-permute-done((bf16[384,512]{1,0:T(8,128)(2,1)}, bf16[384,512]{1,0:T(8,128)(2,1)S(1)}, u32[]{:S(2)}, u32[]{:S(2)}) %collective-permute-start.3) | collective-permute-done | bytes 393248 | tf_op jit(solution)/shard_map/ppermute | solution.py:221
  25.4 1.8 %shard_map.121.refs_0_.own_ref = f32[768,512]{1,0:T(8,128)S(1)} custom-call(bf16[768,1920]{1,0:T(8,128)(2,1)S(1)} %get-tuple-element.44.dense_ref, bf16[384,512]{1,0:T(8,128)(2,1)S(1)} %collective-permute-done.2.refs_0_, bf16[384,512]{1,0:T(8,128)(2,1)S(1)} %collective-permute-done.3.refs_1_, bf16[384,512]{1,0:T(8,128)(2,1)S(1)} %copy-done.2, ...), custom_call_target="tpu_custom_call" | custom-call | tf_op jit(solution)/shard_map/pallas_call | solution.py:16
  27.6 2.2 %collective-permute-start.6 = (f32[384,512]{1,0:T(8,128)S(1)}, f32[384,512]{1,0:T(8,128)S(1)}, u32[]{:S(2)}, u32[]{:S(2)}) collective-permute-start(f32[384,512]{1,0:T(8,128)S(1)} %shard_map.122), channel_id=1, source_target_pairs={{0,1},{1,0},{2,3},{3,2},{4,5},{5,4},{6,7},{7,6},{8,9},{9,8},{10,11... | collective-permute-start | bytes 2359304 | tf_op jit(solution)/shard_map/ppermute | solution.py:324
  29.8 1.9 %collective-permute-done.6.mate_ref = f32[384,512]{1,0:T(8,128)S(1)} collective-permute-done((f32[384,512]{1,0:T(8,128)S(1)}, f32[384,512]{1,0:T(8,128)S(1)}, u32[]{:S(2)}, u32[]{:S(2)}) %collective-permute-start.6) | collective-permute-done | bytes 786464 | tf_op jit(solution)/shard_map/ppermute | solution.py:324
  31.8 1.4 %shard_map.123 = (bf16[384,512]{1,0:T(8,128)(2,1)}, bf16[384,512]{1,0:T(8,128)(2,1)S(1)}, f32[4,80,512]{2,1,0:T(8,128)S(1)}, bf16[4,80,512]{2,1,0:T(8,128)(2,1)S(1)}) custom-call(s32[1]{0:T(128)} %bitcast.spot_ref.refs_0_, f32[768,512]{1,0:T(8,128)S(1)} %shard_map.121.refs_0_.own_ref, f32[384,512]{1,0:T(8,128)S(1)} %collective-permute-done.6.mate_ref, ...), custom_call_target="tpu_custom_call" | custom-call | tf_op jit(solution)/shard_map/pallas_call | solution.py:16
  33.7 1.7 %collective-permute-done.7.got_ref = bf16[4,80,512]{2,1,0:T(8,128)(2,1)S(1)} collective-permute-done((bf16[4,80,512]{2,1,0:T(8,128)(2,1)S(1)}, bf16[4,80,512]{2,1,0:T(8,128)(2,1)S(1)}, u32[]{:S(2)}, u32[]{:S(2)}) %collective-permute-start.7) | collective-permute-done | bytes 327712 | tf_op jit(solution)/shard_map/ppermute | solution.py:324
  35.4 1.3 %collective-permute-start.10 = (bf16[80,512]{1,0:T(8,128)(2,1)S(1)}, bf16[80,512]{1,0:T(8,128)(2,1)S(1)}, u32[]{:S(2)}, u32[]{:S(2)}) collective-permute-start(bf16[80,512]{1,0:T(8,128)(2,1)S(1)} %get-tuple-element.51), channel_id=1, source_target_pairs={{0,6},{1,7},{2,4},{3,5},{4,2},{5,3},{6,0},{7,1},{8,14},{9,15},{10,... | collective-permute-start | bytes 245768 | tf_op jit(solution)/shard_map/ppermute | solution.py:324
  36.9 1.2 %collective-permute-start.9 = (bf16[80,512]{1,0:T(8,128)(2,1)S(1)}, bf16[80,512]{1,0:T(8,128)(2,1)S(1)}, u32[]{:S(2)}, u32[]{:S(2)}) collective-permute-start(bf16[80,512]{1,0:T(8,128)(2,1)S(1)} %get-tuple-element.50), channel_id=1, source_target_pairs={{0,4},{1,5},{2,6},{3,7},{4,0},{5,1},{6,2},{7,3},{8,12},{9,13},{10,... | collective-permute-start | bytes 245768 | tf_op jit(solution)/shard_map/ppermute | solution.py:324
  38.1 1.9 %shard_map.125 = (bf16[384,512]{1,0:T(8,128)(2,1)S(1)}, bf16[384,512]{1,0:T(8,128)(2,1)S(1)}, f32[384,512]{1,0:T(8,128)S(1)}, bf16[384,512]{1,0:T(8,128)(2,1)S(1)}) custom-call(s32[1]{0:T(128)} %bitcast.spot_ref.refs_0_, s32[40]{0:T(128)S(1)} %copy-done.5, bf16[1920,768]{1,0:T(8,128)(2,1)S(1)} %get-tuple-element.52.refs_2_, ...), custom_call_target="tpu_custom_call" | custom-call | flops 10000000000 | tf_op jit(solution)/shard_map/pallas_call | solution.py:16
  41.1 1.1 %collective-permute-done.9.refs_2_ = bf16[80,512]{1,0:T(8,128)(2,1)S(1)} collective-permute-done((bf16[80,512]{1,0:T(8,128)(2,1)S(1)}, bf16[80,512]{1,0:T(8,128)(2,1)S(1)}, u32[]{:S(2)}, u32[]{:S(2)}) %collective-permute-start.9) | collective-permute-done | bytes 81952 | tf_op jit(solution)/shard_map/ppermute | solution.py:324
  42.5 2.1 %collective-permute-start.13 = (bf16[80,512]{1,0:T(8,128)(2,1)S(1)}, bf16[80,512]{1,0:T(8,128)(2,1)S(1)}, u32[]{:S(2)}, u32[]{:S(2)}) collective-permute-start(bf16[80,512]{1,0:T(8,128)(2,1)S(1)} %shard_map.126.refs_0_), channel_id=1, source_target_pairs={{0,16},{1,17},{2,18},{3,19},{4,20},{5,21},{6,22},{7,23},{8,24},{9,... | collective-permute-start | bytes 245768 | tf_op jit(solution)/shard_map/ppermute | solution.py:324
  44.6 1.3 %collective-permute-start.14 = (bf16[80,512]{1,0:T(8,128)(2,1)S(1)}, bf16[80,512]{1,0:T(8,128)(2,1)S(1)}, u32[]{:S(2)}, u32[]{:S(2)}) collective-permute-start(bf16[80,512]{1,0:T(8,128)(2,1)S(1)} %shard_map.126.refs_0_), channel_id=1, source_target_pairs={{0,24},{1,25},{2,26},{3,27},{4,28},{5,29},{6,30},{7,31},{8,16},{9,... | collective-permute-start | bytes 245768 | tf_op jit(solution)/shard_map/ppermute | solution.py:324
  45.8 1.2 %collective-permute-done.15.refs_1_.refs_2_ = bf16[384,512]{1,0:T(8,128)(2,1)S(1)} collective-permute-done((bf16[384,512]{1,0:T(8,128)(2,1)S(1)}, bf16[384,512]{1,0:T(8,128)(2,1)S(1)}, u32[]{:S(2)}, u32[]{:S(2)}) %collective-permute-start.15) | collective-permute-done | bytes 393248 | tf_op jit(solution)/shard_map/ppermute | solution.py:268
  47.9 1.3 %collective-permute-start.20 = (bf16[384,512]{1,0:T(8,128)(2,1)S(1)}, bf16[384,512]{1,0:T(8,128)(2,1)S(1)}, u32[]{:S(2)}, u32[]{:S(2)}) collective-permute-start(bf16[384,512]{1,0:T(8,128)(2,1)S(1)} %get-tuple-element.70), channel_id=1, source_target_pairs={{0,2},{2,0},{4,6},{5,1},{6,4},{7,3},{8,10},{10,8},{12,14},{13,9},{... | collective-permute-start | bytes 1179656 | tf_op jit(solution)/shard_map/ppermute | solution.py:268
  49.2 1.5 %shard_map.128 = (f32[384,512]{1,0:T(8,128)S(1)}, f32[384,512]{1,0:T(8,128)S(1)}) custom-call(s32[1]{0:T(128)} %bitcast.spot_ref.refs_0_, s32[40]{0:T(128)S(1)} %copy-done.5, bf16[1920,768]{1,0:T(8,128)(2,1)S(1)} %get-tuple-element.52.refs_2_, bf16[384,512]{1,0:T(8,128)(2,1)S(1)} %get-tuple-element.53.refs_3_, ...), custom_call_target="tpu_custom_call" | custom-call | flops 10000000000 | tf_op jit(solution)/shard_map/pallas_call | solution.py:16
  51.4 6.0 %collective-permute-start.17 = (bf16[64,512]{1,0:T(8,128)(2,1)S(1)}, bf16[64,512]{1,0:T(8,128)(2,1)S(1)}, u32[]{:S(2)}, u32[]{:S(2)}) collective-permute-start(bf16[64,512]{1,0:T(8,128)(2,1)S(1)} %get-tuple-element.68.refs_0_), channel_id=1, source_target_pairs={{0,2},{1,3},{2,0},{3,1},{4,6},{5,7},{6,4},{7,5},{8,10},{9,11},{10,... | collective-permute-start | bytes 196616 | tf_op jit(solution)/shard_map/ppermute | solution.py:324
  57.4 4.3 %collective-permute-start.18 = (bf16[64,512]{1,0:T(8,128)(2,1)S(1)}, bf16[64,512]{1,0:T(8,128)(2,1)S(1)}, u32[]{:S(2)}, u32[]{:S(2)}) collective-permute-start(bf16[64,512]{1,0:T(8,128)(2,1)S(1)} %get-tuple-element.68.refs_0_), channel_id=1, source_target_pairs={{0,4},{1,5},{2,6},{3,7},{4,0},{5,1},{6,2},{7,3},{8,12},{9,13},{10,... | collective-permute-start | bytes 196616 | tf_op jit(solution)/shard_map/ppermute | solution.py:324
  61.6 1.9 %collective-permute-start.22 = (bf16[384,512]{1,0:T(8,128)(2,1)S(1)}, bf16[384,512]{1,0:T(8,128)(2,1)S(1)}, u32[]{:S(2)}, u32[]{:S(2)}) collective-permute-start(bf16[384,512]{1,0:T(8,128)(2,1)S(1)} %get-tuple-element.72), channel_id=1, source_target_pairs={{1,25},{9,1},{17,9},{25,17}} | collective-permute-start | bytes 1179656 | tf_op jit(solution)/shard_map/ppermute | solution.py:268
  63.8 3.9 %collective-permute-start.24 = (bf16[384,512]{1,0:T(8,128)(2,1)S(1)}, bf16[384,512]{1,0:T(8,128)(2,1)S(1)}, u32[]{:S(2)}, u32[]{:S(2)}) collective-permute-start(bf16[384,512]{1,0:T(8,128)(2,1)S(1)} %shard_map.130), channel_id=1, source_target_pairs={{0,4},{1,3},{2,6},{3,1},{4,0},{5,7},{6,2},{7,5},{8,12},{9,11},{10,... | collective-permute-start | bytes 1179656 | tf_op jit(solution)/shard_map/ppermute | solution.py:268
  67.7 2.8 %collective-permute-done.22 = bf16[384,512]{1,0:T(8,128)(2,1)S(1)} collective-permute-done((bf16[384,512]{1,0:T(8,128)(2,1)S(1)}, bf16[384,512]{1,0:T(8,128)(2,1)S(1)}, u32[]{:S(2)}, u32[]{:S(2)}) %collective-permute-start.22) | collective-permute-done | bytes 393248 | tf_op jit(solution)/shard_map/ppermute | solution.py:268
  70.4 1.3 %collective-permute-start.25 = (bf16[384,512]{1,0:T(8,128)(2,1)S(1)}, bf16[384,512]{1,0:T(8,128)(2,1)S(1)}, u32[]{:S(2)}, u32[]{:S(2)}) collective-permute-start(bf16[384,512]{1,0:T(8,128)(2,1)S(1)} %collective-permute-done.22), channel_id=1, source_target_pairs={{1,5},{9,13},{17,21},{25,29}} | collective-permute-start | bytes 1179656 | tf_op jit(solution)/shard_map/ppermute | solution.py:268
  71.9 1.5 %collective-permute-done.23.other_ref = bf16[256,512]{1,0:T(8,128)(2,1)S(1)} collective-permute-done((bf16[256,512]{1,0:T(8,128)(2,1)S(1)}, bf16[256,512]{1,0:T(8,128)(2,1)S(1)}, u32[]{:S(2)}, u32[]{:S(2)}) %collective-permute-start.23) | collective-permute-done | bytes 262176 | tf_op jit(solution)/shard_map/ppermute | solution.py:324
  73.4 1.0 %shard_map.132 = f32[512,512]{1,0:T(8,128)} custom-call(s32[1]{0:T(128)} %bitcast.spot_ref.refs_0_, bf16[256,512]{1,0:T(8,128)(2,1)S(1)} %shard_map.131.mine_ref, bf16[256,512]{1,0:T(8,128)(2,1)S(1)} %collective-permute-done.23.other_ref), custom_call_target="tpu_custom_call" | custom-call | tf_op jit(solution)/shard_map/pallas_call | solution.py:16
  74.4 2.0 %collective-permute-done.25.refs_4_ = bf16[384,512]{1,0:T(8,128)(2,1)S(1)} collective-permute-done((bf16[384,512]{1,0:T(8,128)(2,1)S(1)}, bf16[384,512]{1,0:T(8,128)(2,1)S(1)}, u32[]{:S(2)}, u32[]{:S(2)}) %collective-permute-start.25) | collective-permute-done | bytes 393248 | tf_op jit(solution)/shard_map/ppermute | solution.py:268
  76.4 1.0 %shard_map.133 = bf16[384,512]{1,0:T(8,128)(2,1)} custom-call(s32[1]{0:T(128)} %bitcast.spot_ref.refs_0_, f32[384,512]{1,0:T(8,128)S(1)} %get-tuple-element.76.refs_0_, bf16[384,512]{1,0:T(8,128)(2,1)S(1)} %collective-permute-done.20.refs_1_, bf16[384,512]{1,0:T(8,128)(2,1)S(1)} %collective-permute-done.24.refs_2_, ...), custom_call_target="tpu_custom_call" | custom-call | flops 10000000000 | tf_op jit(solution)/shard_map/pallas_call | solution.py:16
  (50 shorter events, 7.5 us)
Async XLA Ops:
  0.6 8.6 %collective-permute-start = (bf16[8,7,128,128]{3,2,1,0:T(8,128)(2,1)}, bf16[8,7,128,128]{3,2,1,0:T(8,128)(2,1)S(1)}, u32[]{:S(2)}, u32[]{:S(2)}) collective-permute-start(bf16[8,7,128,128]{3,2,1,0:T(8,128)(2,1)} %bitcast.7), channel_id=1, source_target_pairs={{0,1},{1,0},{2,3},{3,2},{4,5},{5,4},{6,7},{7,6},{8,9},{9,8},{10,11... | collective-permute-start | bytes 5505032 | tf_op jit(solution)/shard_map/ppermute | solution.py:324
  0.8 19.8 %collective-permute-start.2 = (bf16[384,512]{1,0:T(8,128)(2,1)}, bf16[384,512]{1,0:T(8,128)(2,1)S(1)}, u32[]{:S(2)}, u32[]{:S(2)}) collective-permute-start(bf16[384,512]{1,0:T(8,128)(2,1)} %refs_2_.1), channel_id=1, source_target_pairs={{0,4},{1,5},{2,6},{3,7},{4,8},{5,9},{6,10},{7,11},{8,12},{9,13},{1... | collective-permute-start | bytes 1179656 | tf_op jit(solution)/shard_map/ppermute | solution.py:221
  3.4 21.9 %collective-permute-start.3 = (bf16[384,512]{1,0:T(8,128)(2,1)}, bf16[384,512]{1,0:T(8,128)(2,1)S(1)}, u32[]{:S(2)}, u32[]{:S(2)}) collective-permute-start(bf16[384,512]{1,0:T(8,128)(2,1)} %refs_2_.1), channel_id=1, source_target_pairs={{0,2},{1,3},{2,4},{3,5},{4,6},{5,7},{6,8},{7,9},{8,10},{9,11},{10,... | collective-permute-start | bytes 1179656 | tf_op jit(solution)/shard_map/ppermute | solution.py:221
  4.7 20.7 %collective-permute-start.4 = (bf16[384,512]{1,0:T(8,128)(2,1)}, bf16[384,512]{1,0:T(8,128)(2,1)S(1)}, u32[]{:S(2)}, u32[]{:S(2)}) collective-permute-start(bf16[384,512]{1,0:T(8,128)(2,1)} %refs_2_.1), channel_id=1, source_target_pairs={{0,30},{1,31},{2,0},{3,1},{4,2},{5,3},{6,4},{7,5},{8,6},{9,7},{10,... | collective-permute-start | bytes 1179656 | tf_op jit(solution)/shard_map/ppermute | solution.py:221
  8.5 18.7 %collective-permute-start.5 = (bf16[384,512]{1,0:T(8,128)(2,1)}, bf16[384,512]{1,0:T(8,128)(2,1)S(1)}, u32[]{:S(2)}, u32[]{:S(2)}) collective-permute-start(bf16[384,512]{1,0:T(8,128)(2,1)} %refs_2_.1), channel_id=1, source_target_pairs={{0,28},{2,30},{4,0},{6,2},{8,4},{10,6},{12,8},{14,10},{16,12},{18,... | collective-permute-start | bytes 1179656 | tf_op jit(solution)/shard_map/ppermute | solution.py:221
  10.7 3.4 %collective-permute-start.1 = (s32[120]{0:T(128)S(1)}, s32[120]{0:T(128)S(1)}, u32[]{:S(2)}, u32[]{:S(2)}) collective-permute-start(s32[120]{0:T(128)S(1)} %reshape.27.own_meta_ref), channel_id=1, source_target_pairs={{0,1},{1,0},{2,3},{3,2},{4,5},{5,4},{6,7},{7,6},{8,9},{9,8},{10,11... | collective-permute-start | bytes 1448 | tf_op jit(solution)/shard_map/ppermute | solution.py:324
  14.1 1.5 %copy-start = (bf16[1,8,7,128,128]{4,3,2,1,0:T(8,128)(2,1)S(1)}, bf16[1,8,7,128,128]{4,3,2,1,0:T(8,128)(2,1)}, u32[]{:S(2)}) copy-start(bf16[1,8,7,128,128]{4,3,2,1,0:T(8,128)(2,1)} %param.12) | copy-start | bytes 5505028
  15.6 9.8 %copy-start.2 = (bf16[384,512]{1,0:T(8,128)(2,1)S(1)}, bf16[384,512]{1,0:T(8,128)(2,1)}, u32[]{:S(2)}) copy-start(bf16[384,512]{1,0:T(8,128)(2,1)} %refs_2_.1) | copy-start | bytes 1179652
  27.2 4.6 %copy-start.1 = (bf16[512,512]{1,0:T(8,128)(2,1)S(1)}, bf16[512,512]{1,0:T(8,128)(2,1)}, u32[]{:S(2)}) copy-start(bf16[512,512]{1,0:T(8,128)(2,1)} %weight_ref.1) | copy-start | bytes 1572868
  27.2 4.6 %copy-start.3 = (bf16[384,512]{1,0:T(8,128)(2,1)S(1)}, bf16[384,512]{1,0:T(8,128)(2,1)}, u32[]{:S(2)}) copy-start(bf16[384,512]{1,0:T(8,128)(2,1)} %grad_out_ref.1) | copy-start | bytes 1179652
  27.2 4.6 %copy-start.4 = (f32[512]{0:T(512)S(1)}, f32[512]{0:T(512)}, u32[]{:S(2)}) copy-start(f32[512]{0:T(512)} %param.14) | copy-start | bytes 6148
  27.6 4.2 %collective-permute-start.6 = (f32[384,512]{1,0:T(8,128)S(1)}, f32[384,512]{1,0:T(8,128)S(1)}, u32[]{:S(2)}, u32[]{:S(2)}) collective-permute-start(f32[384,512]{1,0:T(8,128)S(1)} %shard_map.122), channel_id=1, source_target_pairs={{0,1},{1,0},{2,3},{3,2},{4,5},{5,4},{6,7},{7,6},{8,9},{9,8},{10,11... | collective-permute-start | bytes 2359304 | tf_op jit(solution)/shard_map/ppermute | solution.py:324
  31.8 6.4 %copy-start.5 = (s32[40]{0:T(128)S(1)}, s32[40]{0:T(128)}, u32[]{:S(2)}) copy-start(s32[40]{0:T(128)} %constant.23.refs_1_) | copy-start | bytes 484
  33.2 5.0 %collective-permute-start.11 = (bf16[384,512]{1,0:T(8,128)(2,1)S(1)}, bf16[384,512]{1,0:T(8,128)(2,1)S(1)}, u32[]{:S(2)}, u32[]{:S(2)}) collective-permute-start(bf16[384,512]{1,0:T(8,128)(2,1)S(1)} %get-tuple-element.53.refs_3_), channel_id=1, source_target_pairs={{0,1},{1,0},{2,3},{3,2},{4,5},{5,4},{6,7},{7,6},{8,9},{9,8},{10,11... | collective-permute-start | bytes 1179656 | tf_op jit(solution)/shard_map/ppermute | solution.py:324
  33.6 1.8 %collective-permute-start.7 = (bf16[4,80,512]{2,1,0:T(8,128)(2,1)S(1)}, bf16[4,80,512]{2,1,0:T(8,128)(2,1)S(1)}, u32[]{:S(2)}, u32[]{:S(2)}) collective-permute-start(bf16[4,80,512]{2,1,0:T(8,128)(2,1)S(1)} %get-tuple-element.47), channel_id=1, source_target_pairs={{0,1},{1,0},{2,3},{3,2},{4,5},{5,4},{6,7},{7,6},{8,9},{9,8},{10,11... | collective-permute-start | bytes 983048 | tf_op jit(solution)/shard_map/ppermute | solution.py:324
  35.4 5.6 %collective-permute-start.10 = (bf16[80,512]{1,0:T(8,128)(2,1)S(1)}, bf16[80,512]{1,0:T(8,128)(2,1)S(1)}, u32[]{:S(2)}, u32[]{:S(2)}) collective-permute-start(bf16[80,512]{1,0:T(8,128)(2,1)S(1)} %get-tuple-element.51), channel_id=1, source_target_pairs={{0,6},{1,7},{2,4},{3,5},{4,2},{5,3},{6,0},{7,1},{8,14},{9,15},{10,... | collective-permute-start | bytes 245768 | tf_op jit(solution)/shard_map/ppermute | solution.py:324
  36.7 4.4 %collective-permute-start.8 = (bf16[80,512]{1,0:T(8,128)(2,1)S(1)}, bf16[80,512]{1,0:T(8,128)(2,1)S(1)}, u32[]{:S(2)}, u32[]{:S(2)}) collective-permute-start(bf16[80,512]{1,0:T(8,128)(2,1)S(1)} %get-tuple-element.49), channel_id=1, source_target_pairs={{0,2},{1,3},{2,0},{3,1},{4,6},{5,7},{6,4},{7,5},{8,10},{9,11},{10,... | collective-permute-start | bytes 245768 | tf_op jit(solution)/shard_map/ppermute | solution.py:324
  36.9 5.3 %collective-permute-start.9 = (bf16[80,512]{1,0:T(8,128)(2,1)S(1)}, bf16[80,512]{1,0:T(8,128)(2,1)S(1)}, u32[]{:S(2)}, u32[]{:S(2)}) collective-permute-start(bf16[80,512]{1,0:T(8,128)(2,1)S(1)} %get-tuple-element.50), channel_id=1, source_target_pairs={{0,4},{1,5},{2,6},{3,7},{4,0},{5,1},{6,2},{7,3},{8,12},{9,13},{10,... | collective-permute-start | bytes 245768 | tf_op jit(solution)/shard_map/ppermute | solution.py:324
  40.1 7.0 %collective-permute-start.15 = (bf16[384,512]{1,0:T(8,128)(2,1)S(1)}, bf16[384,512]{1,0:T(8,128)(2,1)S(1)}, u32[]{:S(2)}, u32[]{:S(2)}) collective-permute-start(bf16[384,512]{1,0:T(8,128)(2,1)S(1)} %get-tuple-element.55), channel_id=1, source_target_pairs={{0,2},{1,5},{2,0},{3,7},{4,6},{5,1},{6,4},{7,3},{8,10},{9,13},{10,... | collective-permute-start | bytes 1179656 | tf_op jit(solution)/shard_map/ppermute | solution.py:268
  40.4 6.7 %collective-permute-start.16 = (bf16[384,512]{1,0:T(8,128)(2,1)S(1)}, bf16[384,512]{1,0:T(8,128)(2,1)S(1)}, u32[]{:S(2)}, u32[]{:S(2)}) collective-permute-start(bf16[384,512]{1,0:T(8,128)(2,1)S(1)} %get-tuple-element.72), channel_id=1, source_target_pairs={{3,7},{11,15},{19,23},{27,31}} | collective-permute-start | bytes 1179656 | tf_op jit(solution)/shard_map/ppermute | solution.py:268
  42.2 8.5 %collective-permute-start.12 = (bf16[80,512]{1,0:T(8,128)(2,1)S(1)}, bf16[80,512]{1,0:T(8,128)(2,1)S(1)}, u32[]{:S(2)}, u32[]{:S(2)}) collective-permute-start(bf16[80,512]{1,0:T(8,128)(2,1)S(1)} %shard_map.126.refs_0_), channel_id=1, source_target_pairs={{0,8},{1,9},{2,10},{3,11},{4,12},{5,13},{6,14},{7,15},{8,0},{9,1},... | collective-permute-start | bytes 245768 | tf_op jit(solution)/shard_map/ppermute | solution.py:324
  42.5 8.2 %collective-permute-start.13 = (bf16[80,512]{1,0:T(8,128)(2,1)S(1)}, bf16[80,512]{1,0:T(8,128)(2,1)S(1)}, u32[]{:S(2)}, u32[]{:S(2)}) collective-permute-start(bf16[80,512]{1,0:T(8,128)(2,1)S(1)} %shard_map.126.refs_0_), channel_id=1, source_target_pairs={{0,16},{1,17},{2,18},{3,19},{4,20},{5,21},{6,22},{7,23},{8,24},{9,... | collective-permute-start | bytes 245768 | tf_op jit(solution)/shard_map/ppermute | solution.py:324
  44.6 6.2 %collective-permute-start.14 = (bf16[80,512]{1,0:T(8,128)(2,1)S(1)}, bf16[80,512]{1,0:T(8,128)(2,1)S(1)}, u32[]{:S(2)}, u32[]{:S(2)}) collective-permute-start(bf16[80,512]{1,0:T(8,128)(2,1)S(1)} %shard_map.126.refs_0_), channel_id=1, source_target_pairs={{0,24},{1,25},{2,26},{3,27},{4,28},{5,29},{6,30},{7,31},{8,16},{9,... | collective-permute-start | bytes 245768 | tf_op jit(solution)/shard_map/ppermute | solution.py:324
  47.2 16.3 %collective-permute-start.21 = (bf16[384,512]{1,0:T(8,128)(2,1)S(1)}, bf16[384,512]{1,0:T(8,128)(2,1)S(1)}, u32[]{:S(2)}, u32[]{:S(2)}) collective-permute-start(bf16[384,512]{1,0:T(8,128)(2,1)S(1)} %shard_map.127), channel_id=1, source_target_pairs={{0,24},{2,26},{3,11},{4,12},{5,29},{6,14},{7,31},{8,0},{10,2},{11,... | collective-permute-start | bytes 1179656 | tf_op jit(solution)/shard_map/ppermute | solution.py:268
  47.9 13.7 %collective-permute-start.20 = (bf16[384,512]{1,0:T(8,128)(2,1)S(1)}, bf16[384,512]{1,0:T(8,128)(2,1)S(1)}, u32[]{:S(2)}, u32[]{:S(2)}) collective-permute-start(bf16[384,512]{1,0:T(8,128)(2,1)S(1)} %get-tuple-element.70), channel_id=1, source_target_pairs={{0,2},{2,0},{4,6},{5,1},{6,4},{7,3},{8,10},{10,8},{12,14},{13,9},{... | collective-permute-start | bytes 1179656 | tf_op jit(solution)/shard_map/ppermute | solution.py:268
  51.4 16.3 %collective-permute-start.17 = (bf16[64,512]{1,0:T(8,128)(2,1)S(1)}, bf16[64,512]{1,0:T(8,128)(2,1)S(1)}, u32[]{:S(2)}, u32[]{:S(2)}) collective-permute-start(bf16[64,512]{1,0:T(8,128)(2,1)S(1)} %get-tuple-element.68.refs_0_), channel_id=1, source_target_pairs={{0,2},{1,3},{2,0},{3,1},{4,6},{5,7},{6,4},{7,5},{8,10},{9,11},{10,... | collective-permute-start | bytes 196616 | tf_op jit(solution)/shard_map/ppermute | solution.py:324
  57.4 10.3 %collective-permute-start.18 = (bf16[64,512]{1,0:T(8,128)(2,1)S(1)}, bf16[64,512]{1,0:T(8,128)(2,1)S(1)}, u32[]{:S(2)}, u32[]{:S(2)}) collective-permute-start(bf16[64,512]{1,0:T(8,128)(2,1)S(1)} %get-tuple-element.68.refs_0_), channel_id=1, source_target_pairs={{0,4},{1,5},{2,6},{3,7},{4,0},{5,1},{6,2},{7,3},{8,12},{9,13},{10,... | collective-permute-start | bytes 196616 | tf_op jit(solution)/shard_map/ppermute | solution.py:324
  61.6 6.0 %collective-permute-start.19 = (bf16[64,512]{1,0:T(8,128)(2,1)S(1)}, bf16[64,512]{1,0:T(8,128)(2,1)S(1)}, u32[]{:S(2)}, u32[]{:S(2)}) collective-permute-start(bf16[64,512]{1,0:T(8,128)(2,1)S(1)} %get-tuple-element.68.refs_0_), channel_id=1, source_target_pairs={{0,6},{1,7},{2,4},{3,5},{4,2},{5,3},{6,0},{7,1},{8,14},{9,15},{10,... | collective-permute-start | bytes 196616 | tf_op jit(solution)/shard_map/ppermute | solution.py:324
  61.6 8.8 %collective-permute-start.22 = (bf16[384,512]{1,0:T(8,128)(2,1)S(1)}, bf16[384,512]{1,0:T(8,128)(2,1)S(1)}, u32[]{:S(2)}, u32[]{:S(2)}) collective-permute-start(bf16[384,512]{1,0:T(8,128)(2,1)S(1)} %get-tuple-element.72), channel_id=1, source_target_pairs={{1,25},{9,1},{17,9},{25,17}} | collective-permute-start | bytes 1179656 | tf_op jit(solution)/shard_map/ppermute | solution.py:268
  63.8 10.7 %collective-permute-start.24 = (bf16[384,512]{1,0:T(8,128)(2,1)S(1)}, bf16[384,512]{1,0:T(8,128)(2,1)S(1)}, u32[]{:S(2)}, u32[]{:S(2)}) collective-permute-start(bf16[384,512]{1,0:T(8,128)(2,1)S(1)} %shard_map.130), channel_id=1, source_target_pairs={{0,4},{1,3},{2,6},{3,1},{4,0},{5,7},{6,2},{7,5},{8,12},{9,11},{10,... | collective-permute-start | bytes 1179656 | tf_op jit(solution)/shard_map/ppermute | solution.py:268
  70.4 6.0 %collective-permute-start.25 = (bf16[384,512]{1,0:T(8,128)(2,1)S(1)}, bf16[384,512]{1,0:T(8,128)(2,1)S(1)}, u32[]{:S(2)}, u32[]{:S(2)}) collective-permute-start(bf16[384,512]{1,0:T(8,128)(2,1)S(1)} %collective-permute-done.22), channel_id=1, source_target_pairs={{1,5},{9,13},{17,21},{25,29}} | collective-permute-start | bytes 1179656 | tf_op jit(solution)/shard_map/ppermute | solution.py:268
  71.8 1.6 %collective-permute-start.23 = (bf16[256,512]{1,0:T(8,128)(2,1)S(1)}, bf16[256,512]{1,0:T(8,128)(2,1)S(1)}, u32[]{:S(2)}, u32[]{:S(2)}) collective-permute-start(bf16[256,512]{1,0:T(8,128)(2,1)S(1)} %shard_map.131.mine_ref), channel_id=1, source_target_pairs={{0,1},{1,0},{2,3},{3,2},{4,5},{5,4},{6,7},{7,6},{8,9},{9,8},{10,11... | collective-permute-start | bytes 786440 | tf_op jit(solution)/shard_map/ppermute | solution.py:324

commit v16 on v13

--- a/solution.py
+++ b/solution.py
@@ -177,7 +177,7 @@
         refs[-2][...] = parts[0][:piece].astype(BF16)
         refs[-1][...] = parts[0][piece : piece + 1]
 
-    return call(kernel, [((piece, hidden), BF16), ((1, hidden), F32)], list(values), cost=10)
+    return call(kernel, [((piece, hidden), BF16), ((1, hidden), F32)], list(values), cost=4)
 
 
 def scattered_sums(flipped, own, mate, columns, dtypes, spot=None, lookup=None, cost=10):
@@ -257,8 +257,8 @@
 class Relayed(Direct):
     EVEN, MIDDLE, ENDS = 0b01010101, 0b00111100, 0b11000011
     LOOKUP = [
-        [2, 4, 3, 0, 1], [2, 3, 4, 0, 1],
-        [2, 4, 1, 0, 3], [2, 1, 4, 0, 3],
+        [2, 4, 3, 0, 1], [2, 3, 0, 4, 1],
+        [2, 4, 1, 0, 3], [2, 1, 0, 4, 3],
         [2, 0, 3, 4, 1], [2, 3, 0, 4, 1],
         [2, 0, 1, 4, 3], [2, 1, 0, 4, 3],
     ]
@@ -277,23 +277,17 @@
         )
         if k == 0:
             _, mate = after(token, self.mate)
-            self.to_last, self.to_plane, self.plane_rest, self.to_straight = take(
-                mate, (4, 3, 2), [[BF16], [BF16, F32], [F32]]
-            )
-            self.from_last = self.routed(self.to_last, straight)
-            self.from_plane = self.routed(self.to_plane, {1: -8, 3: 4})
-            return [self.to_last]
+            to_last, self.to_planes, self.to_second = take(mate, (4, 3, 2), [[BF16], [F32], [BF16]])
+            self.from_last = self.routed(to_last, straight)
+            return [to_last]
         if k == 1:
-            _, plane_rest = after(token, self.plane_rest)
-            out = summed_terms(
-                self.spot, [plane_rest, self.from_last, self.from_plane], [self.EVEN, self.MIDDLE, 0b10000000]
-            )
-            self.from_planes = self.routed(out, {0: -8, 2: -8, 4: 8, 6: 8, 5: -8, 3: 8, 7: -8})
-            out, to_straight, mate = after(out, self.to_straight, self.mate)
-            second = summed_terms(self.spot, [to_straight, self.from_plane], [None, 0b00000010])
-            self.second = self.routed(second, straight)
+            _, rest = after(token, self.to_planes)
+            out = summed_terms(self.spot, [rest, self.from_last], [self.EVEN, self.MIDDLE])
+            self.from_planes = self.routed(out, {0: -8, 2: -8, 4: 8, 6: 8, 5: -8, 3: 8})
+            out, mate, to_second = after(out, self.mate, self.to_second)
+            self.second = self.routed(to_second, {**straight, 1: -4, 3: -4})
             self.kept, self.to_across = take(mate, (0, 1), [[F32]] * 2, cost=10)
-            return [second, self.kept]
+            return [self.kept]
         if k == 2:
             _, rest, _ = after(token, self.to_across, self.second)
             out = summed_terms(
@@ -305,8 +299,7 @@
 
     def finish(self, token):
         _, kept = after(token, self.kept)
-        terms = [kept, self.second, self.first, self.from_planes]
-        return summed_terms(self.spot, terms, [None, None, None, 0b10000000])
+        return summed_terms(self.spot, [kept, self.second, self.first])
 
 
 def local(features, tile_list, tile_count, tile_values, weight, bias, grad_out):

time: 74.4 us -> 73.6 us (0.989)
  the two profiles are of different devices: /device:TPU:16 before, /device:TPU:2 now
where the time goes in v16:
time: 73.6 us; the launch traced here: 73.3 us
  waiting for transfers between devices  29.1 us (40%)
  starting transfers between devices  26.3 us (36%)
  Pallas kernels  14 us (19%)
  local copies, waits for them, and re-layouts  2.4 us (3%)
  between operations  0.87 us (1%)
    pallas_call x14, Pallas kernels, call(): pl.pallas_call(kernel, out_shape=out_shape, in_specs=[spec(k) for k in ra...  14 us
    ppermute x4, waiting for transfers between devices, routed(): return lax.ppermute(value, 'blk', pairs)  13 us
    ppermute x15, starting transfers between devices, swapped(): return lax.ppermute(value, 'blk', [(s, s ^ distance) for s in range(count)])  12.2 us
    ppermute x4, starting transfers between devices, sent(): return lax.ppermute(value, 'blk', pairs)  8.7 us
    ppermute x4, waiting for transfers between devices, sent(): return lax.ppermute(value, 'blk', pairs)  8.36 us
    ppermute x15, waiting for transfers between devices, swapped(): return lax.ppermute(value, 'blk', [(s, s ^ distance) for s in range(count)])  7.71 us
    ppermute x4, starting transfers between devices, routed(): return lax.ppermute(value, 'blk', pairs)  5.4 us
    unnamed x12, local copies, waits for them, and re-layouts  1.53 us
  transfers between devices with their start and end apart: 23, of which 12 were waited for; matrix products, arithmetic and copies ran while one was open for 2% of the time, Pallas kernels for 15%

profile of v16, /device:TPU:2, one launch (start us, length us, event | category | flops | bytes accessed | tf_op | source)
XLA Modules:
  0.0 73.3 jit_solution(16947944480502708850)
XLA Ops:
  0.7 1.6 %collective-permute-start.2 = (bf16[384,512]{1,0:T(8,128)(2,1)}, bf16[384,512]{1,0:T(8,128)(2,1)S(1)}, u32[]{:S(2)}, u32[]{:S(2)}) collective-permute-start(bf16[384,512]{1,0:T(8,128)(2,1)} %refs_2_.1), channel_id=1, source_target_pairs={{0,4},{1,5},{2,6},{3,7},{4,8},{5,9},{6,10},{7,11},{8,12},{9,13},{1... | collective-permute-start | bytes 1179656 | tf_op jit(solution)/shard_map/ppermute | solution.py:221
  2.3 1.5 %collective-permute-start.3 = (bf16[384,512]{1,0:T(8,128)(2,1)}, bf16[384,512]{1,0:T(8,128)(2,1)S(1)}, u32[]{:S(2)}, u32[]{:S(2)}) collective-permute-start(bf16[384,512]{1,0:T(8,128)(2,1)} %refs_2_.1), channel_id=1, source_target_pairs={{0,2},{1,3},{2,4},{3,5},{4,6},{5,7},{6,8},{7,9},{8,10},{9,11},{10,... | collective-permute-start | bytes 1179656 | tf_op jit(solution)/shard_map/ppermute | solution.py:221
  4.3 5.1 %collective-permute-start.5 = (bf16[384,512]{1,0:T(8,128)(2,1)}, bf16[384,512]{1,0:T(8,128)(2,1)S(1)}, u32[]{:S(2)}, u32[]{:S(2)}) collective-permute-start(bf16[384,512]{1,0:T(8,128)(2,1)} %refs_2_.1), channel_id=1, source_target_pairs={{0,28},{2,30},{4,0},{6,2},{8,4},{10,6},{12,8},{14,10},{16,12},{18,... | collective-permute-start | bytes 1179656 | tf_op jit(solution)/shard_map/ppermute | solution.py:221
  9.4 0.7 reshape_squeeze.3
  10.1 0.7 pad_add_fusion
  11.0 1.1 %collective-permute-done.1.mate_meta_ref = s32[120]{0:T(128)S(1)} collective-permute-done((s32[120]{0:T(128)S(1)}, s32[120]{0:T(128)S(1)}, u32[]{:S(2)}, u32[]{:S(2)}) %collective-permute-start.1) | collective-permute-done | bytes 512 | tf_op jit(solution)/shard_map/ppermute | solution.py:316
  12.1 1.5 %copy-done = bf16[1,8,7,128,128]{4,3,2,1,0:T(8,128)(2,1)S(1)} copy-done((bf16[1,8,7,128,128]{4,3,2,1,0:T(8,128)(2,1)S(1)}, bf16[1,8,7,128,128]{4,3,2,1,0:T(8,128)(2,1)}, u32[]{:S(2)}) %copy-start) | copy-done | bytes 1835032
  13.6 4.1 %shard_map.120 = (bf16[768,1920]{1,0:T(8,128)(2,1)S(1)}, bf16[1920,768]{1,0:T(8,128)(2,1)S(1)}) custom-call(s32[1]{0:T(128)} %bitcast.spot_ref.refs_0_, s32[120]{0:T(128)S(1)} %reshape.27.own_meta_ref, s32[120]{0:T(128)S(1)} %collective-permute-done.1.mate_meta_ref, bf16[8,7,128,128]{3,2,1,0:T(8,128)(2,1)S(1)} %bitcast.8, ...), custom_call_target="tpu_custom_call" | custom-call | tf_op jit(solution)/shard_map/pallas_call | solution.py:16
  17.7 6.5 %collective-permute-done.2.refs_0_ = bf16[384,512]{1,0:T(8,128)(2,1)S(1)} collective-permute-done((bf16[384,512]{1,0:T(8,128)(2,1)}, bf16[384,512]{1,0:T(8,128)(2,1)S(1)}, u32[]{:S(2)}, u32[]{:S(2)}) %collective-permute-start.2) | collective-permute-done | bytes 393248 | tf_op jit(solution)/shard_map/ppermute | solution.py:221
  24.2 1.8 %shard_map.121.refs_0_.own_ref = f32[768,512]{1,0:T(8,128)S(1)} custom-call(bf16[768,1920]{1,0:T(8,128)(2,1)S(1)} %get-tuple-element.42.dense_ref, bf16[384,512]{1,0:T(8,128)(2,1)S(1)} %collective-permute-done.2.refs_0_, bf16[384,512]{1,0:T(8,128)(2,1)S(1)} %collective-permute-done.3.refs_1_, bf16[384,512]{1,0:T(8,128)(2,1)S(1)} %copy-done.2, ...), custom_call_target="tpu_custom_call" | custom-call | tf_op jit(solution)/shard_map/pallas_call | solution.py:16
  26.1 1.8 %collective-permute-done.5.refs_1_ = bf16[384,512]{1,0:T(8,128)(2,1)S(1)} collective-permute-done((bf16[384,512]{1,0:T(8,128)(2,1)}, bf16[384,512]{1,0:T(8,128)(2,1)S(1)}, u32[]{:S(2)}, u32[]{:S(2)}) %collective-permute-start.5) | collective-permute-done | bytes 393248 | tf_op jit(solution)/shard_map/ppermute | solution.py:221
  28.3 2.3 %collective-permute-done.6.mate_ref = f32[384,512]{1,0:T(8,128)S(1)} collective-permute-done((f32[384,512]{1,0:T(8,128)S(1)}, f32[384,512]{1,0:T(8,128)S(1)}, u32[]{:S(2)}, u32[]{:S(2)}) %collective-permute-start.6) | collective-permute-done | bytes 786464 | tf_op jit(solution)/shard_map/ppermute | solution.py:316
  30.6 1.4 %shard_map.123 = (bf16[384,512]{1,0:T(8,128)(2,1)}, bf16[384,512]{1,0:T(8,128)(2,1)S(1)}, f32[4,80,512]{2,1,0:T(8,128)S(1)}, bf16[4,80,512]{2,1,0:T(8,128)(2,1)S(1)}) custom-call(s32[1]{0:T(128)} %bitcast.spot_ref.refs_0_, f32[768,512]{1,0:T(8,128)S(1)} %shard_map.121.refs_0_.own_ref, f32[384,512]{1,0:T(8,128)S(1)} %collective-permute-done.6.mate_ref, ...), custom_call_target="tpu_custom_call" | custom-call | tf_op jit(solution)/shard_map/pallas_call | solution.py:16
  32.6 1.7 %collective-permute-done.7.got_ref = bf16[4,80,512]{2,1,0:T(8,128)(2,1)S(1)} collective-permute-done((bf16[4,80,512]{2,1,0:T(8,128)(2,1)S(1)}, bf16[4,80,512]{2,1,0:T(8,128)(2,1)S(1)}, u32[]{:S(2)}, u32[]{:S(2)}) %collective-permute-start.7) | collective-permute-done | bytes 327712 | tf_op jit(solution)/shard_map/ppermute | solution.py:316
  34.9 1.5 %collective-permute-start.8 = (bf16[80,512]{1,0:T(8,128)(2,1)S(1)}, bf16[80,512]{1,0:T(8,128)(2,1)S(1)}, u32[]{:S(2)}, u32[]{:S(2)}) collective-permute-start(bf16[80,512]{1,0:T(8,128)(2,1)S(1)} %get-tuple-element.47), channel_id=1, source_target_pairs={{0,2},{1,3},{2,0},{3,1},{4,6},{5,7},{6,4},{7,5},{8,10},{9,11},{10,... | collective-permute-start | bytes 245768 | tf_op jit(solution)/shard_map/ppermute | solution.py:316
  36.4 1.5 %collective-permute-start.9 = (bf16[80,512]{1,0:T(8,128)(2,1)S(1)}, bf16[80,512]{1,0:T(8,128)(2,1)S(1)}, u32[]{:S(2)}, u32[]{:S(2)}) collective-permute-start(bf16[80,512]{1,0:T(8,128)(2,1)S(1)} %get-tuple-element.48), channel_id=1, source_target_pairs={{0,4},{1,5},{2,6},{3,7},{4,0},{5,1},{6,2},{7,3},{8,12},{9,13},{10,... | collective-permute-start | bytes 245768 | tf_op jit(solution)/shard_map/ppermute | solution.py:316
  37.9 1.9 %shard_map.125 = (bf16[384,512]{1,0:T(8,128)(2,1)S(1)}, f32[384,512]{1,0:T(8,128)S(1)}, bf16[384,512]{1,0:T(8,128)(2,1)S(1)}) custom-call(s32[1]{0:T(128)} %bitcast.spot_ref.refs_0_, s32[40]{0:T(128)S(1)} %copy-done.5, bf16[1920,768]{1,0:T(8,128)(2,1)S(1)} %get-tuple-element.50.refs_2_, bf16[384,512]{1,0:T(8,128)(2,1)S(1)} %get-tuple-element.51.refs_3_, ...), custom_call_target="tpu_custom_call" | custom-call | flops 10000000000 | tf_op jit(solution)/shard_map/pallas_call | solution.py:16
  40.6 0.9 %collective-permute-done.9.refs_2_ = bf16[80,512]{1,0:T(8,128)(2,1)S(1)} collective-permute-done((bf16[80,512]{1,0:T(8,128)(2,1)S(1)}, bf16[80,512]{1,0:T(8,128)(2,1)S(1)}, u32[]{:S(2)}, u32[]{:S(2)}) %collective-permute-start.9) | collective-permute-done | bytes 81952 | tf_op jit(solution)/shard_map/ppermute | solution.py:316
  41.5 1.3 %collective-permute-start.12 = (bf16[80,512]{1,0:T(8,128)(2,1)S(1)}, bf16[80,512]{1,0:T(8,128)(2,1)S(1)}, u32[]{:S(2)}, u32[]{:S(2)}) collective-permute-start(bf16[80,512]{1,0:T(8,128)(2,1)S(1)} %shard_map.126.refs_0_), channel_id=1, source_target_pairs={{0,8},{1,9},{2,10},{3,11},{4,12},{5,13},{6,14},{7,15},{8,0},{9,1},... | collective-permute-start | bytes 245768 | tf_op jit(solution)/shard_map/ppermute | solution.py:316
  42.8 2.6 %collective-permute-start.13 = (bf16[80,512]{1,0:T(8,128)(2,1)S(1)}, bf16[80,512]{1,0:T(8,128)(2,1)S(1)}, u32[]{:S(2)}, u32[]{:S(2)}) collective-permute-start(bf16[80,512]{1,0:T(8,128)(2,1)S(1)} %shard_map.126.refs_0_), channel_id=1, source_target_pairs={{0,16},{1,17},{2,18},{3,19},{4,20},{5,21},{6,22},{7,23},{8,24},{9,... | collective-permute-start | bytes 245768 | tf_op jit(solution)/shard_map/ppermute | solution.py:316
  46.0 1.6 %collective-permute-done.15.refs_1_.refs_2_ = bf16[384,512]{1,0:T(8,128)(2,1)S(1)} collective-permute-done((bf16[384,512]{1,0:T(8,128)(2,1)S(1)}, bf16[384,512]{1,0:T(8,128)(2,1)S(1)}, u32[]{:S(2)}, u32[]{:S(2)}) %collective-permute-start.15) | collective-permute-done | bytes 393248 | tf_op jit(solution)/shard_map/ppermute | solution.py:268
  47.7 4.0 %collective-permute-start.20 = (bf16[384,512]{1,0:T(8,128)(2,1)S(1)}, bf16[384,512]{1,0:T(8,128)(2,1)S(1)}, u32[]{:S(2)}, u32[]{:S(2)}) collective-permute-start(bf16[384,512]{1,0:T(8,128)(2,1)S(1)} %shard_map.127), channel_id=1, source_target_pairs={{0,24},{2,26},{3,11},{4,12},{5,29},{6,14},{8,0},{10,2},{11,19},{12... | collective-permute-start | bytes 1179656 | tf_op jit(solution)/shard_map/ppermute | solution.py:268
  51.8 0.7 collective-permute-start.19
  52.4 1.5 %shard_map.128 = (f32[384,512]{1,0:T(8,128)S(1)}, f32[384,512]{1,0:T(8,128)S(1)}) custom-call(s32[1]{0:T(128)} %bitcast.spot_ref.refs_0_, s32[40]{0:T(128)S(1)} %copy-done.5, bf16[1920,768]{1,0:T(8,128)(2,1)S(1)} %get-tuple-element.50.refs_2_, bf16[384,512]{1,0:T(8,128)(2,1)S(1)} %get-tuple-element.51.refs_3_, ...), custom_call_target="tpu_custom_call" | custom-call | flops 10000000000 | tf_op jit(solution)/shard_map/pallas_call | solution.py:16
  54.6 1.4 %collective-permute-start.16 = (bf16[64,512]{1,0:T(8,128)(2,1)S(1)}, bf16[64,512]{1,0:T(8,128)(2,1)S(1)}, u32[]{:S(2)}, u32[]{:S(2)}) collective-permute-start(bf16[64,512]{1,0:T(8,128)(2,1)S(1)} %get-tuple-element.65.refs_0_), channel_id=1, source_target_pairs={{0,2},{1,3},{2,0},{3,1},{4,6},{5,7},{6,4},{7,5},{8,10},{9,11},{10,... | collective-permute-start | bytes 196616 | tf_op jit(solution)/shard_map/ppermute | solution.py:316
  56.0 2.1 %collective-permute-start.18 = (bf16[64,512]{1,0:T(8,128)(2,1)S(1)}, bf16[64,512]{1,0:T(8,128)(2,1)S(1)}, u32[]{:S(2)}, u32[]{:S(2)}) collective-permute-start(bf16[64,512]{1,0:T(8,128)(2,1)S(1)} %get-tuple-element.65.refs_0_), channel_id=1, source_target_pairs={{0,6},{1,7},{2,4},{3,5},{4,2},{5,3},{6,0},{7,1},{8,14},{9,15},{10,... | collective-permute-start | bytes 196616 | tf_op jit(solution)/shard_map/ppermute | solution.py:316
  58.1 2.7 %collective-permute-done.19.refs_1_ = bf16[384,512]{1,0:T(8,128)(2,1)S(1)} collective-permute-done((bf16[384,512]{1,0:T(8,128)(2,1)S(1)}, bf16[384,512]{1,0:T(8,128)(2,1)S(1)}, u32[]{:S(2)}, u32[]{:S(2)}) %collective-permute-start.19) | collective-permute-done | bytes 393248 | tf_op jit(solution)/shard_map/ppermute | solution.py:268
  60.7 3.7 %collective-permute-done.20.refs_1_ = bf16[384,512]{1,0:T(8,128)(2,1)S(1)} collective-permute-done((bf16[384,512]{1,0:T(8,128)(2,1)S(1)}, bf16[384,512]{1,0:T(8,128)(2,1)S(1)}, u32[]{:S(2)}, u32[]{:S(2)}) %collective-permute-start.20) | collective-permute-done | bytes 393248 | tf_op jit(solution)/shard_map/ppermute | solution.py:268
  64.8 1.5 %collective-permute-done.21.other_ref = bf16[256,512]{1,0:T(8,128)(2,1)S(1)} collective-permute-done((bf16[256,512]{1,0:T(8,128)(2,1)S(1)}, bf16[256,512]{1,0:T(8,128)(2,1)S(1)}, u32[]{:S(2)}, u32[]{:S(2)}) %collective-permute-start.21) | collective-permute-done | bytes 262176 | tf_op jit(solution)/shard_map/ppermute | solution.py:316
  66.3 1.0 %shard_map.132 = f32[512,512]{1,0:T(8,128)} custom-call(s32[1]{0:T(128)} %bitcast.spot_ref.refs_0_, bf16[256,512]{1,0:T(8,128)(2,1)S(1)} %shard_map.131.mine_ref, bf16[256,512]{1,0:T(8,128)(2,1)S(1)} %collective-permute-done.21.other_ref), custom_call_target="tpu_custom_call" | custom-call | tf_op jit(solution)/shard_map/pallas_call | solution.py:16
  67.4 5.1 %collective-permute-done.22.refs_2_ = bf16[384,512]{1,0:T(8,128)(2,1)S(1)} collective-permute-done((bf16[384,512]{1,0:T(8,128)(2,1)S(1)}, bf16[384,512]{1,0:T(8,128)(2,1)S(1)}, u32[]{:S(2)}, u32[]{:S(2)}) %collective-permute-start.22) | collective-permute-done | bytes 393248 | tf_op jit(solution)/shard_map/ppermute | solution.py:268
  72.4 0.9 %shard_map.133 = bf16[384,512]{1,0:T(8,128)(2,1)} custom-call(s32[1]{0:T(128)} %bitcast.spot_ref.refs_0_, f32[384,512]{1,0:T(8,128)S(1)} %get-tuple-element.72.refs_0_, bf16[384,512]{1,0:T(8,128)(2,1)S(1)} %collective-permute-done.19.refs_1_, bf16[384,512]{1,0:T(8,128)(2,1)S(1)} %collective-permute-done.22.refs_2_), custom_call_target="tpu_custom_call" | custom-call | flops 10000000000 | tf_op jit(solution)/shard_map/pallas_call | solution.py:16
  (44 shorter events, 4.9 us)
Async XLA Ops:
  0.6 8.8 %collective-permute-start = (bf16[8,7,128,128]{3,2,1,0:T(8,128)(2,1)}, bf16[8,7,128,128]{3,2,1,0:T(8,128)(2,1)S(1)}, u32[]{:S(2)}, u32[]{:S(2)}) collective-permute-start(bf16[8,7,128,128]{3,2,1,0:T(8,128)(2,1)} %bitcast.7), channel_id=1, source_target_pairs={{0,1},{1,0},{2,3},{3,2},{4,5},{5,4},{6,7},{7,6},{8,9},{9,8},{10,11... | collective-permute-start | bytes 5505032 | tf_op jit(solution)/shard_map/ppermute | solution.py:316
  0.7 23.5 %collective-permute-start.2 = (bf16[384,512]{1,0:T(8,128)(2,1)}, bf16[384,512]{1,0:T(8,128)(2,1)S(1)}, u32[]{:S(2)}, u32[]{:S(2)}) collective-permute-start(bf16[384,512]{1,0:T(8,128)(2,1)} %refs_2_.1), channel_id=1, source_target_pairs={{0,4},{1,5},{2,6},{3,7},{4,8},{5,9},{6,10},{7,11},{8,12},{9,13},{1... | collective-permute-start | bytes 1179656 | tf_op jit(solution)/shard_map/ppermute | solution.py:221
  2.3 21.9 %collective-permute-start.3 = (bf16[384,512]{1,0:T(8,128)(2,1)}, bf16[384,512]{1,0:T(8,128)(2,1)S(1)}, u32[]{:S(2)}, u32[]{:S(2)}) collective-permute-start(bf16[384,512]{1,0:T(8,128)(2,1)} %refs_2_.1), channel_id=1, source_target_pairs={{0,2},{1,3},{2,4},{3,5},{4,6},{5,7},{6,8},{7,9},{8,10},{9,11},{10,... | collective-permute-start | bytes 1179656 | tf_op jit(solution)/shard_map/ppermute | solution.py:221
  3.8 20.5 %collective-permute-start.4 = (bf16[384,512]{1,0:T(8,128)(2,1)}, bf16[384,512]{1,0:T(8,128)(2,1)S(1)}, u32[]{:S(2)}, u32[]{:S(2)}) collective-permute-start(bf16[384,512]{1,0:T(8,128)(2,1)} %refs_2_.1), channel_id=1, source_target_pairs={{0,30},{1,31},{2,0},{3,1},{4,2},{5,3},{6,4},{7,5},{8,6},{9,7},{10,... | collective-permute-start | bytes 1179656 | tf_op jit(solution)/shard_map/ppermute | solution.py:221
  4.3 23.6 %collective-permute-start.5 = (bf16[384,512]{1,0:T(8,128)(2,1)}, bf16[384,512]{1,0:T(8,128)(2,1)S(1)}, u32[]{:S(2)}, u32[]{:S(2)}) collective-permute-start(bf16[384,512]{1,0:T(8,128)(2,1)} %refs_2_.1), channel_id=1, source_target_pairs={{0,28},{2,30},{4,0},{6,2},{8,4},{10,6},{12,8},{14,10},{16,12},{18,... | collective-permute-start | bytes 1179656 | tf_op jit(solution)/shard_map/ppermute | solution.py:221
  11.0 1.1 %collective-permute-start.1 = (s32[120]{0:T(128)S(1)}, s32[120]{0:T(128)S(1)}, u32[]{:S(2)}, u32[]{:S(2)}) collective-permute-start(s32[120]{0:T(128)S(1)} %reshape.27.own_meta_ref), channel_id=1, source_target_pairs={{0,1},{1,0},{2,3},{3,2},{4,5},{5,4},{6,7},{7,6},{8,9},{9,8},{10,11... | collective-permute-start | bytes 1448 | tf_op jit(solution)/shard_map/ppermute | solution.py:316
  12.1 1.5 %copy-start = (bf16[1,8,7,128,128]{4,3,2,1,0:T(8,128)(2,1)S(1)}, bf16[1,8,7,128,128]{4,3,2,1,0:T(8,128)(2,1)}, u32[]{:S(2)}) copy-start(bf16[1,8,7,128,128]{4,3,2,1,0:T(8,128)(2,1)} %param.12) | copy-start | bytes 5505028
  13.6 10.6 %copy-start.2 = (bf16[384,512]{1,0:T(8,128)(2,1)S(1)}, bf16[384,512]{1,0:T(8,128)(2,1)}, u32[]{:S(2)}) copy-start(bf16[384,512]{1,0:T(8,128)(2,1)} %refs_2_.1) | copy-start | bytes 1179652
  26.0 4.6 %copy-start.1 = (bf16[512,512]{1,0:T(8,128)(2,1)S(1)}, bf16[512,512]{1,0:T(8,128)(2,1)}, u32[]{:S(2)}) copy-start(bf16[512,512]{1,0:T(8,128)(2,1)} %weight_ref.1) | copy-start | bytes 1572868
  26.0 4.6 %copy-start.3 = (bf16[384,512]{1,0:T(8,128)(2,1)S(1)}, bf16[384,512]{1,0:T(8,128)(2,1)}, u32[]{:S(2)}) copy-start(bf16[384,512]{1,0:T(8,128)(2,1)} %grad_out_ref.1) | copy-start | bytes 1179652
  26.0 4.6 %copy-start.4 = (f32[512]{0:T(512)S(1)}, f32[512]{0:T(512)}, u32[]{:S(2)}) copy-start(f32[512]{0:T(512)} %param.14) | copy-start | bytes 6148
  28.3 2.4 %collective-permute-start.6 = (f32[384,512]{1,0:T(8,128)S(1)}, f32[384,512]{1,0:T(8,128)S(1)}, u32[]{:S(2)}, u32[]{:S(2)}) collective-permute-start(f32[384,512]{1,0:T(8,128)S(1)} %shard_map.122), channel_id=1, source_target_pairs={{0,1},{1,0},{2,3},{3,2},{4,5},{5,4},{6,7},{7,6},{8,9},{9,8},{10,11... | collective-permute-start | bytes 2359304 | tf_op jit(solution)/shard_map/ppermute | solution.py:316
  30.6 7.2 %copy-start.5 = (s32[40]{0:T(128)S(1)}, s32[40]{0:T(128)}, u32[]{:S(2)}) copy-start(s32[40]{0:T(128)} %constant.23.refs_1_) | copy-start | bytes 484
  32.0 5.8 %collective-permute-start.11 = (bf16[384,512]{1,0:T(8,128)(2,1)S(1)}, bf16[384,512]{1,0:T(8,128)(2,1)S(1)}, u32[]{:S(2)}, u32[]{:S(2)}) collective-permute-start(bf16[384,512]{1,0:T(8,128)(2,1)S(1)} %get-tuple-element.51.refs_3_), channel_id=1, source_target_pairs={{0,1},{1,0},{2,3},{3,2},{4,5},{5,4},{6,7},{7,6},{8,9},{9,8},{10,11... | collective-permute-start | bytes 1179656 | tf_op jit(solution)/shard_map/ppermute | solution.py:316
  32.2 2.1 %collective-permute-start.7 = (bf16[4,80,512]{2,1,0:T(8,128)(2,1)S(1)}, bf16[4,80,512]{2,1,0:T(8,128)(2,1)S(1)}, u32[]{:S(2)}, u32[]{:S(2)}) collective-permute-start(bf16[4,80,512]{2,1,0:T(8,128)(2,1)S(1)} %get-tuple-element.45), channel_id=1, source_target_pairs={{0,1},{1,0},{2,3},{3,2},{4,5},{5,4},{6,7},{7,6},{8,9},{9,8},{10,11... | collective-permute-start | bytes 983048 | tf_op jit(solution)/shard_map/ppermute | solution.py:316
  34.3 6.3 %collective-permute-start.10 = (bf16[80,512]{1,0:T(8,128)(2,1)S(1)}, bf16[80,512]{1,0:T(8,128)(2,1)S(1)}, u32[]{:S(2)}, u32[]{:S(2)}) collective-permute-start(bf16[80,512]{1,0:T(8,128)(2,1)S(1)} %get-tuple-element.49), channel_id=1, source_target_pairs={{0,6},{1,7},{2,4},{3,5},{4,2},{5,3},{6,0},{7,1},{8,14},{9,15},{10,... | collective-permute-start | bytes 245768 | tf_op jit(solution)/shard_map/ppermute | solution.py:316
  34.9 5.7 %collective-permute-start.8 = (bf16[80,512]{1,0:T(8,128)(2,1)S(1)}, bf16[80,512]{1,0:T(8,128)(2,1)S(1)}, u32[]{:S(2)}, u32[]{:S(2)}) collective-permute-start(bf16[80,512]{1,0:T(8,128)(2,1)S(1)} %get-tuple-element.47), channel_id=1, source_target_pairs={{0,2},{1,3},{2,0},{3,1},{4,6},{5,7},{6,4},{7,5},{8,10},{9,11},{10,... | collective-permute-start | bytes 245768 | tf_op jit(solution)/shard_map/ppermute | solution.py:316
  36.4 5.1 %collective-permute-start.9 = (bf16[80,512]{1,0:T(8,128)(2,1)S(1)}, bf16[80,512]{1,0:T(8,128)(2,1)S(1)}, u32[]{:S(2)}, u32[]{:S(2)}) collective-permute-start(bf16[80,512]{1,0:T(8,128)(2,1)S(1)} %get-tuple-element.48), channel_id=1, source_target_pairs={{0,4},{1,5},{2,6},{3,7},{4,0},{5,1},{6,2},{7,3},{8,12},{9,13},{10,... | collective-permute-start | bytes 245768 | tf_op jit(solution)/shard_map/ppermute | solution.py:316
  39.8 7.8 %collective-permute-start.15 = (bf16[384,512]{1,0:T(8,128)(2,1)S(1)}, bf16[384,512]{1,0:T(8,128)(2,1)S(1)}, u32[]{:S(2)}, u32[]{:S(2)}) collective-permute-start(bf16[384,512]{1,0:T(8,128)(2,1)S(1)} %get-tuple-element.53), channel_id=1, source_target_pairs={{0,2},{1,5},{2,0},{3,7},{4,6},{5,1},{6,4},{7,3},{8,10},{9,13},{10,... | collective-permute-start | bytes 1179656 | tf_op jit(solution)/shard_map/ppermute | solution.py:268
  41.5 12.4 %collective-permute-start.12 = (bf16[80,512]{1,0:T(8,128)(2,1)S(1)}, bf16[80,512]{1,0:T(8,128)(2,1)S(1)}, u32[]{:S(2)}, u32[]{:S(2)}) collective-permute-start(bf16[80,512]{1,0:T(8,128)(2,1)S(1)} %shard_map.126.refs_0_), channel_id=1, source_target_pairs={{0,8},{1,9},{2,10},{3,11},{4,12},{5,13},{6,14},{7,15},{8,0},{9,1},... | collective-permute-start | bytes 245768 | tf_op jit(solution)/shard_map/ppermute | solution.py:316
  42.8 11.1 %collective-permute-start.13 = (bf16[80,512]{1,0:T(8,128)(2,1)S(1)}, bf16[80,512]{1,0:T(8,128)(2,1)S(1)}, u32[]{:S(2)}, u32[]{:S(2)}) collective-permute-start(bf16[80,512]{1,0:T(8,128)(2,1)S(1)} %shard_map.126.refs_0_), channel_id=1, source_target_pairs={{0,16},{1,17},{2,18},{3,19},{4,20},{5,21},{6,22},{7,23},{8,24},{9,... | collective-permute-start | bytes 245768 | tf_op jit(solution)/shard_map/ppermute | solution.py:316
  45.4 8.6 %collective-permute-start.14 = (bf16[80,512]{1,0:T(8,128)(2,1)S(1)}, bf16[80,512]{1,0:T(8,128)(2,1)S(1)}, u32[]{:S(2)}, u32[]{:S(2)}) collective-permute-start(bf16[80,512]{1,0:T(8,128)(2,1)S(1)} %shard_map.126.refs_0_), channel_id=1, source_target_pairs={{0,24},{1,25},{2,26},{3,27},{4,28},{5,29},{6,30},{7,31},{8,16},{9,... | collective-permute-start | bytes 245768 | tf_op jit(solution)/shard_map/ppermute | solution.py:316
  47.7 16.7 %collective-permute-start.20 = (bf16[384,512]{1,0:T(8,128)(2,1)S(1)}, bf16[384,512]{1,0:T(8,128)(2,1)S(1)}, u32[]{:S(2)}, u32[]{:S(2)}) collective-permute-start(bf16[384,512]{1,0:T(8,128)(2,1)S(1)} %shard_map.127), channel_id=1, source_target_pairs={{0,24},{2,26},{3,11},{4,12},{5,29},{6,14},{8,0},{10,2},{11,19},{12... | collective-permute-start | bytes 1179656 | tf_op jit(solution)/shard_map/ppermute | solution.py:268
  51.8 9.0 %collective-permute-start.19 = (bf16[384,512]{1,0:T(8,128)(2,1)S(1)}, bf16[384,512]{1,0:T(8,128)(2,1)S(1)}, u32[]{:S(2)}, u32[]{:S(2)}) collective-permute-start(bf16[384,512]{1,0:T(8,128)(2,1)S(1)} %get-tuple-element.67), channel_id=1, source_target_pairs={{0,2},{1,29},{2,0},{3,31},{4,6},{5,1},{6,4},{7,3},{8,10},{9,5},{10... | collective-permute-start | bytes 1179656 | tf_op jit(solution)/shard_map/ppermute | solution.py:268
  54.6 10.1 %collective-permute-start.16 = (bf16[64,512]{1,0:T(8,128)(2,1)S(1)}, bf16[64,512]{1,0:T(8,128)(2,1)S(1)}, u32[]{:S(2)}, u32[]{:S(2)}) collective-permute-start(bf16[64,512]{1,0:T(8,128)(2,1)S(1)} %get-tuple-element.65.refs_0_), channel_id=1, source_target_pairs={{0,2},{1,3},{2,0},{3,1},{4,6},{5,7},{6,4},{7,5},{8,10},{9,11},{10,... | collective-permute-start | bytes 196616 | tf_op jit(solution)/shard_map/ppermute | solution.py:316
  56.0 8.7 %collective-permute-start.17 = (bf16[64,512]{1,0:T(8,128)(2,1)S(1)}, bf16[64,512]{1,0:T(8,128)(2,1)S(1)}, u32[]{:S(2)}, u32[]{:S(2)}) collective-permute-start(bf16[64,512]{1,0:T(8,128)(2,1)S(1)} %get-tuple-element.65.refs_0_), channel_id=1, source_target_pairs={{0,4},{1,5},{2,6},{3,7},{4,0},{5,1},{6,2},{7,3},{8,12},{9,13},{10,... | collective-permute-start | bytes 196616 | tf_op jit(solution)/shard_map/ppermute | solution.py:316
  56.0 8.7 %collective-permute-start.18 = (bf16[64,512]{1,0:T(8,128)(2,1)S(1)}, bf16[64,512]{1,0:T(8,128)(2,1)S(1)}, u32[]{:S(2)}, u32[]{:S(2)}) collective-permute-start(bf16[64,512]{1,0:T(8,128)(2,1)S(1)} %get-tuple-element.65.refs_0_), channel_id=1, source_target_pairs={{0,6},{1,7},{2,4},{3,5},{4,2},{5,3},{6,0},{7,1},{8,14},{9,15},{10,... | collective-permute-start | bytes 196616 | tf_op jit(solution)/shard_map/ppermute | solution.py:316
  64.6 7.8 %collective-permute-start.22 = (bf16[384,512]{1,0:T(8,128)(2,1)S(1)}, bf16[384,512]{1,0:T(8,128)(2,1)S(1)}, u32[]{:S(2)}, u32[]{:S(2)}) collective-permute-start(bf16[384,512]{1,0:T(8,128)(2,1)S(1)} %shard_map.130), channel_id=1, source_target_pairs={{0,4},{1,3},{2,6},{3,1},{4,0},{5,7},{6,2},{7,5},{8,12},{9,11},{10,... | collective-permute-start | bytes 1179656 | tf_op jit(solution)/shard_map/ppermute | solution.py:268
  64.7 1.6 %collective-permute-start.21 = (bf16[256,512]{1,0:T(8,128)(2,1)S(1)}, bf16[256,512]{1,0:T(8,128)(2,1)S(1)}, u32[]{:S(2)}, u32[]{:S(2)}) collective-permute-start(bf16[256,512]{1,0:T(8,128)(2,1)S(1)} %shard_map.131.mine_ref), channel_id=1, source_target_pairs={{0,1},{1,0},{2,3},{3,2},{4,5},{5,4},{6,7},{7,6},{8,9},{9,8},{10,11... | collective-permute-start | bytes 786440 | tf_op jit(solution)/shard_map/ppermute | solution.py:316

commit v17 on v16

--- a/solution.py
+++ b/solution.py
@@ -250,7 +250,7 @@
         ]
         return terms[:1]
 
-    def finish(self, token):
+    def finish(self, half, grad_weight):
         return summed_terms(self.spot, self.arriving)
 
 
@@ -286,8 +286,8 @@
             self.from_planes = self.routed(out, {0: -8, 2: -8, 4: 8, 6: 8, 5: -8, 3: 8})
             out, mate, to_second = after(out, self.mate, self.to_second)
             self.second = self.routed(to_second, {**straight, 1: -4, 3: -4})
-            self.kept, self.to_across = take(mate, (0, 1), [[F32]] * 2, cost=10)
-            return [self.kept]
+            self.to_across = take(mate, (1,), [[F32]], cost=10)[0]
+            return [self.to_across]
         if k == 2:
             _, rest, _ = after(token, self.to_across, self.second)
             out = summed_terms(
@@ -297,8 +297,10 @@
             return [out]
         return []
 
-    def finish(self, token):
-        _, kept = after(token, self.kept)
+    def finish(self, half, grad_weight):
+        _, mate = after(half, self.mate)
+        kept = scattered_sums(self.flipped, self.own, mate, (0,), [[F32]], self.spot, self.LOOKUP)[0]
+        _, kept = after(grad_weight, kept)
         return summed_terms(self.spot, [kept, self.second, self.first])
 
 
@@ -344,7 +346,7 @@
     total, bias_sum = finished(values, hidden // pieces)
     half = joined_pieces(spot, [total, *exchanged(k, [total] * len(in_plane), in_plane)])
     grad_weight = whole_weight(spot, half, swapped(half, 1))
-    return (output, route.finish(grad_weight), grad_weight, bias_sum.reshape(hidden))
+    return (output, route.finish(half, grad_weight), grad_weight, bias_sum.reshape(hidden))
 
 
 def solution(mesh):

time: 73.6 us -> 73.6 us (level)
    ppermute x15, waiting for transfers between devices: 7.71 us -> 6.61 us  [swapped(): return lax.ppermute(value, 'blk', [(s, s ^ distance) for s in range(count)])]
    pallas_call x14 -> x15, Pallas kernels: 14 us -> 14.4 us  [call(): pl.pallas_call(kernel, out_shape=out_shape, in_specs=[spec(k) for k in ra...]
  transfers between devices with their start and end apart: 23 -> 23, of which waited for: 12 -> 12; matrix products, arithmetic and copies ran while one was open for 2% -> 2% of each run, Pallas kernels for 15% -> 16%
where the time goes in v17:
time: 73.6 us; the launch traced here: 73.3 us
  waiting for transfers between devices  28.7 us (39%)
  starting transfers between devices  26.3 us (36%)
  Pallas kernels  14.4 us (20%)
  local copies, waits for them, and re-layouts  2.4 us (3%)
  between operations  0.88 us (1%)
    pallas_call x15, Pallas kernels, call(): pl.pallas_call(kernel, out_shape=out_shape, in_specs=[spec(k) for k in ra...  14.4 us
    ppermute x4, waiting for transfers between devices, routed(): return lax.ppermute(value, 'blk', pairs)  13.4 us
    ppermute x15, starting transfers between devices, swapped(): return lax.ppermute(value, 'blk', [(s, s ^ distance) for s in range(count)])  12.2 us
    ppermute x4, starting transfers between devices, sent(): return lax.ppermute(value, 'blk', pairs)  8.7 us
    ppermute x4, waiting for transfers between devices, sent(): return lax.ppermute(value, 'blk', pairs)  8.68 us
    ppermute x15, waiting for transfers between devices, swapped(): return lax.ppermute(value, 'blk', [(s, s ^ distance) for s in range(count)])  6.61 us
    ppermute x4, starting transfers between devices, routed(): return lax.ppermute(value, 'blk', pairs)  5.4 us
    unnamed x12, local copies, waits for them, and re-layouts  1.53 us
  transfers between devices with their start and end apart: 23, of which 12 were waited for; matrix products, arithmetic and copies ran while one was open for 2% of the time, Pallas kernels for 16%

profile of v17, /device:TPU:2, one launch (start us, length us, event | category | flops | bytes accessed | tf_op | source)
XLA Modules:
  0.0 73.3 jit_solution(5147780590467573327)
XLA Ops:
  0.7 1.6 %collective-permute-start.2 = (bf16[384,512]{1,0:T(8,128)(2,1)}, bf16[384,512]{1,0:T(8,128)(2,1)S(1)}, u32[]{:S(2)}, u32[]{:S(2)}) collective-permute-start(bf16[384,512]{1,0:T(8,128)(2,1)} %refs_2_.1), channel_id=1, source_target_pairs={{0,4},{1,5},{2,6},{3,7},{4,8},{5,9},{6,10},{7,11},{8,12},{9,13},{1... | collective-permute-start | bytes 1179656 | tf_op jit(solution)/shard_map/ppermute | solution.py:221
  2.3 1.5 %collective-permute-start.3 = (bf16[384,512]{1,0:T(8,128)(2,1)}, bf16[384,512]{1,0:T(8,128)(2,1)S(1)}, u32[]{:S(2)}, u32[]{:S(2)}) collective-permute-start(bf16[384,512]{1,0:T(8,128)(2,1)} %refs_2_.1), channel_id=1, source_target_pairs={{0,2},{1,3},{2,4},{3,5},{4,6},{5,7},{6,8},{7,9},{8,10},{9,11},{10,... | collective-permute-start | bytes 1179656 | tf_op jit(solution)/shard_map/ppermute | solution.py:221
  4.3 5.1 %collective-permute-start.5 = (bf16[384,512]{1,0:T(8,128)(2,1)}, bf16[384,512]{1,0:T(8,128)(2,1)S(1)}, u32[]{:S(2)}, u32[]{:S(2)}) collective-permute-start(bf16[384,512]{1,0:T(8,128)(2,1)} %refs_2_.1), channel_id=1, source_target_pairs={{0,28},{2,30},{4,0},{6,2},{8,4},{10,6},{12,8},{14,10},{16,12},{18,... | collective-permute-start | bytes 1179656 | tf_op jit(solution)/shard_map/ppermute | solution.py:221
  9.4 0.7 reshape_squeeze.3
  10.1 0.7 pad_add_fusion
  11.0 1.1 %collective-permute-done.1.mate_meta_ref = s32[120]{0:T(128)S(1)} collective-permute-done((s32[120]{0:T(128)S(1)}, s32[120]{0:T(128)S(1)}, u32[]{:S(2)}, u32[]{:S(2)}) %collective-permute-start.1) | collective-permute-done | bytes 512 | tf_op jit(solution)/shard_map/ppermute | solution.py:318
  12.1 1.5 %copy-done = bf16[1,8,7,128,128]{4,3,2,1,0:T(8,128)(2,1)S(1)} copy-done((bf16[1,8,7,128,128]{4,3,2,1,0:T(8,128)(2,1)S(1)}, bf16[1,8,7,128,128]{4,3,2,1,0:T(8,128)(2,1)}, u32[]{:S(2)}) %copy-start) | copy-done | bytes 1835032
  13.6 3.8 %shard_map.129 = (bf16[768,1920]{1,0:T(8,128)(2,1)S(1)}, bf16[1920,768]{1,0:T(8,128)(2,1)S(1)}) custom-call(s32[1]{0:T(128)} %bitcast.spot_ref.refs_0_, s32[120]{0:T(128)S(1)} %reshape.30.own_meta_ref, s32[120]{0:T(128)S(1)} %collective-permute-done.1.mate_meta_ref, bf16[8,7,128,128]{3,2,1,0:T(8,128)(2,1)S(1)} %bitcast.8, ...), custom_call_target="tpu_custom_call" | custom-call | tf_op jit(solution)/shard_map/pallas_call | solution.py:16
  17.4 6.8 %collective-permute-done.2.refs_0_ = bf16[384,512]{1,0:T(8,128)(2,1)S(1)} collective-permute-done((bf16[384,512]{1,0:T(8,128)(2,1)}, bf16[384,512]{1,0:T(8,128)(2,1)S(1)}, u32[]{:S(2)}, u32[]{:S(2)}) %collective-permute-start.2) | collective-permute-done | bytes 393248 | tf_op jit(solution)/shard_map/ppermute | solution.py:221
  24.2 1.8 %shard_map.130.refs_0_.own_ref = f32[768,512]{1,0:T(8,128)S(1)} custom-call(bf16[768,1920]{1,0:T(8,128)(2,1)S(1)} %get-tuple-element.41.dense_ref, bf16[384,512]{1,0:T(8,128)(2,1)S(1)} %collective-permute-done.2.refs_0_, bf16[384,512]{1,0:T(8,128)(2,1)S(1)} %collective-permute-done.3.refs_1_, bf16[384,512]{1,0:T(8,128)(2,1)S(1)} %copy-done.2, ...), custom_call_target="tpu_custom_call" | custom-call | tf_op jit(solution)/shard_map/pallas_call | solution.py:16
  26.1 1.8 %collective-permute-done.5.refs_1_ = bf16[384,512]{1,0:T(8,128)(2,1)S(1)} collective-permute-done((bf16[384,512]{1,0:T(8,128)(2,1)}, bf16[384,512]{1,0:T(8,128)(2,1)S(1)}, u32[]{:S(2)}, u32[]{:S(2)}) %collective-permute-start.5) | collective-permute-done | bytes 393248 | tf_op jit(solution)/shard_map/ppermute | solution.py:221
  28.3 2.3 %collective-permute-done.6.mate_ref = f32[384,512]{1,0:T(8,128)S(1)} collective-permute-done((f32[384,512]{1,0:T(8,128)S(1)}, f32[384,512]{1,0:T(8,128)S(1)}, u32[]{:S(2)}, u32[]{:S(2)}) %collective-permute-start.6) | collective-permute-done | bytes 786464 | tf_op jit(solution)/shard_map/ppermute | solution.py:318
  30.6 1.4 %shard_map.132 = (bf16[384,512]{1,0:T(8,128)(2,1)}, bf16[384,512]{1,0:T(8,128)(2,1)S(1)}, f32[4,80,512]{2,1,0:T(8,128)S(1)}, bf16[4,80,512]{2,1,0:T(8,128)(2,1)S(1)}) custom-call(s32[1]{0:T(128)} %bitcast.spot_ref.refs_0_, f32[768,512]{1,0:T(8,128)S(1)} %shard_map.130.refs_0_.own_ref, f32[384,512]{1,0:T(8,128)S(1)} %collective-permute-done.6.mate_ref, ...), custom_call_target="tpu_custom_call" | custom-call | tf_op jit(solution)/shard_map/pallas_call | solution.py:16
  32.6 1.7 %collective-permute-done.7.got_ref = bf16[4,80,512]{2,1,0:T(8,128)(2,1)S(1)} collective-permute-done((bf16[4,80,512]{2,1,0:T(8,128)(2,1)S(1)}, bf16[4,80,512]{2,1,0:T(8,128)(2,1)S(1)}, u32[]{:S(2)}, u32[]{:S(2)}) %collective-permute-start.7) | collective-permute-done | bytes 327712 | tf_op jit(solution)/shard_map/ppermute | solution.py:318
  34.9 1.5 %collective-permute-start.8 = (bf16[80,512]{1,0:T(8,128)(2,1)S(1)}, bf16[80,512]{1,0:T(8,128)(2,1)S(1)}, u32[]{:S(2)}, u32[]{:S(2)}) collective-permute-start(bf16[80,512]{1,0:T(8,128)(2,1)S(1)} %get-tuple-element.46), channel_id=1, source_target_pairs={{0,2},{1,3},{2,0},{3,1},{4,6},{5,7},{6,4},{7,5},{8,10},{9,11},{10,... | collective-permute-start | bytes 245768 | tf_op jit(solution)/shard_map/ppermute | solution.py:318
  36.4 1.5 %collective-permute-start.9 = (bf16[80,512]{1,0:T(8,128)(2,1)S(1)}, bf16[80,512]{1,0:T(8,128)(2,1)S(1)}, u32[]{:S(2)}, u32[]{:S(2)}) collective-permute-start(bf16[80,512]{1,0:T(8,128)(2,1)S(1)} %get-tuple-element.47), channel_id=1, source_target_pairs={{0,4},{1,5},{2,6},{3,7},{4,0},{5,1},{6,2},{7,3},{8,12},{9,13},{10,... | collective-permute-start | bytes 245768 | tf_op jit(solution)/shard_map/ppermute | solution.py:318
  37.9 1.9 %shard_map.134 = (bf16[384,512]{1,0:T(8,128)(2,1)S(1)}, f32[384,512]{1,0:T(8,128)S(1)}, bf16[384,512]{1,0:T(8,128)(2,1)S(1)}) custom-call(s32[1]{0:T(128)} %bitcast.spot_ref.refs_0_, s32[40]{0:T(128)S(1)} %copy-done.5, bf16[1920,768]{1,0:T(8,128)(2,1)S(1)} %get-tuple-element.49.refs_2_, bf16[384,512]{1,0:T(8,128)(2,1)S(1)} %get-tuple-element.50.refs_3_, ...), custom_call_target="tpu_custom_call" | custom-call | flops 10000000000 | tf_op jit(solution)/shard_map/pallas_call | solution.py:16
  40.6 0.9 %collective-permute-done.9.refs_2_ = bf16[80,512]{1,0:T(8,128)(2,1)S(1)} collective-permute-done((bf16[80,512]{1,0:T(8,128)(2,1)S(1)}, bf16[80,512]{1,0:T(8,128)(2,1)S(1)}, u32[]{:S(2)}, u32[]{:S(2)}) %collective-permute-start.9) | collective-permute-done | bytes 81952 | tf_op jit(solution)/shard_map/ppermute | solution.py:318
  41.5 1.3 %collective-permute-start.12 = (bf16[80,512]{1,0:T(8,128)(2,1)S(1)}, bf16[80,512]{1,0:T(8,128)(2,1)S(1)}, u32[]{:S(2)}, u32[]{:S(2)}) collective-permute-start(bf16[80,512]{1,0:T(8,128)(2,1)S(1)} %shard_map.135.refs_0_), channel_id=1, source_target_pairs={{0,8},{1,9},{2,10},{3,11},{4,12},{5,13},{6,14},{7,15},{8,0},{9,1},... | collective-permute-start | bytes 245768 | tf_op jit(solution)/shard_map/ppermute | solution.py:318
  42.8 2.6 %collective-permute-start.13 = (bf16[80,512]{1,0:T(8,128)(2,1)S(1)}, bf16[80,512]{1,0:T(8,128)(2,1)S(1)}, u32[]{:S(2)}, u32[]{:S(2)}) collective-permute-start(bf16[80,512]{1,0:T(8,128)(2,1)S(1)} %shard_map.135.refs_0_), channel_id=1, source_target_pairs={{0,16},{1,17},{2,18},{3,19},{4,20},{5,21},{6,22},{7,23},{8,24},{9,... | collective-permute-start | bytes 245768 | tf_op jit(solution)/shard_map/ppermute | solution.py:318
  46.0 1.6 %collective-permute-done.15.refs_1_.refs_2_ = bf16[384,512]{1,0:T(8,128)(2,1)S(1)} collective-permute-done((bf16[384,512]{1,0:T(8,128)(2,1)S(1)}, bf16[384,512]{1,0:T(8,128)(2,1)S(1)}, u32[]{:S(2)}, u32[]{:S(2)}) %collective-permute-start.15) | collective-permute-done | bytes 393248 | tf_op jit(solution)/shard_map/ppermute | solution.py:268
  47.7 4.0 %collective-permute-start.20 = (bf16[384,512]{1,0:T(8,128)(2,1)S(1)}, bf16[384,512]{1,0:T(8,128)(2,1)S(1)}, u32[]{:S(2)}, u32[]{:S(2)}) collective-permute-start(bf16[384,512]{1,0:T(8,128)(2,1)S(1)} %shard_map.136), channel_id=1, source_target_pairs={{0,24},{2,26},{3,11},{4,12},{5,29},{6,14},{8,0},{10,2},{11,19},{12... | collective-permute-start | bytes 1179656 | tf_op jit(solution)/shard_map/ppermute | solution.py:268
  51.8 0.7 collective-permute-start.19
  52.4 1.1 %shard_map.137.refs_0_ = f32[384,512]{1,0:T(8,128)S(1)} custom-call(s32[1]{0:T(128)} %bitcast.spot_ref.refs_0_, s32[40]{0:T(128)S(1)} %copy-done.5, bf16[1920,768]{1,0:T(8,128)(2,1)S(1)} %get-tuple-element.49.refs_2_, bf16[384,512]{1,0:T(8,128)(2,1)S(1)} %get-tuple-element.50.refs_3_, bf16[384,512]{1,0:T(8,128)(2,1)S(1)} %collective-permute-done.11.refs_4_), custom_call_target="tpu_custom_call" | custom-call | flops 10000000000 | tf_op jit(solution)/shard_map/pallas_call | solution.py:16
  54.2 1.4 %collective-permute-start.16 = (bf16[64,512]{1,0:T(8,128)(2,1)S(1)}, bf16[64,512]{1,0:T(8,128)(2,1)S(1)}, u32[]{:S(2)}, u32[]{:S(2)}) collective-permute-start(bf16[64,512]{1,0:T(8,128)(2,1)S(1)} %get-tuple-element.63.refs_0_), channel_id=1, source_target_pairs={{0,2},{1,3},{2,0},{3,1},{4,6},{5,7},{6,4},{7,5},{8,10},{9,11},{10,... | collective-permute-start | bytes 196616 | tf_op jit(solution)/shard_map/ppermute | solution.py:318
  55.6 2.1 %collective-permute-start.18 = (bf16[64,512]{1,0:T(8,128)(2,1)S(1)}, bf16[64,512]{1,0:T(8,128)(2,1)S(1)}, u32[]{:S(2)}, u32[]{:S(2)}) collective-permute-start(bf16[64,512]{1,0:T(8,128)(2,1)S(1)} %get-tuple-element.63.refs_0_), channel_id=1, source_target_pairs={{0,6},{1,7},{2,4},{3,5},{4,2},{5,3},{6,0},{7,1},{8,14},{9,15},{10,... | collective-permute-start | bytes 196616 | tf_op jit(solution)/shard_map/ppermute | solution.py:318
  57.7 2.7 %collective-permute-done.19.refs_1_ = bf16[384,512]{1,0:T(8,128)(2,1)S(1)} collective-permute-done((bf16[384,512]{1,0:T(8,128)(2,1)S(1)}, bf16[384,512]{1,0:T(8,128)(2,1)S(1)}, u32[]{:S(2)}, u32[]{:S(2)}) %collective-permute-start.19) | collective-permute-done | bytes 393248 | tf_op jit(solution)/shard_map/ppermute | solution.py:268
  60.3 4.1 %collective-permute-done.20.refs_1_ = bf16[384,512]{1,0:T(8,128)(2,1)S(1)} collective-permute-done((bf16[384,512]{1,0:T(8,128)(2,1)S(1)}, bf16[384,512]{1,0:T(8,128)(2,1)S(1)}, u32[]{:S(2)}, u32[]{:S(2)}) %collective-permute-start.20) | collective-permute-done | bytes 393248 | tf_op jit(solution)/shard_map/ppermute | solution.py:268
  64.8 1.1 %shard_map.142.refs_0_ = f32[384,512]{1,0:T(8,128)S(1)} custom-call(s32[1]{0:T(128)} %bitcast.spot_ref.refs_0_, s32[40]{0:T(128)S(1)} %copy-done.5, bf16[1920,768]{1,0:T(8,128)(2,1)S(1)} %get-tuple-element.49.refs_2_, bf16[384,512]{1,0:T(8,128)(2,1)S(1)} %get-tuple-element.50.refs_3_, bf16[384,512]{1,0:T(8,128)(2,1)S(1)} %collective-permute-done.11.refs_4_), custom_call_target="tpu_custom_call" | custom-call | flops 10000000000 | tf_op jit(solution)/shard_map/pallas_call | solution.py:16
  66.3 1.0 %shard_map.141 = f32[512,512]{1,0:T(8,128)} custom-call(s32[1]{0:T(128)} %bitcast.spot_ref.refs_0_, bf16[256,512]{1,0:T(8,128)(2,1)S(1)} %shard_map.140.mine_ref, bf16[256,512]{1,0:T(8,128)(2,1)S(1)} %collective-permute-done.21.other_ref), custom_call_target="tpu_custom_call" | custom-call | tf_op jit(solution)/shard_map/pallas_call | solution.py:16
  67.4 5.1 %collective-permute-done.22.refs_2_ = bf16[384,512]{1,0:T(8,128)(2,1)S(1)} collective-permute-done((bf16[384,512]{1,0:T(8,128)(2,1)S(1)}, bf16[384,512]{1,0:T(8,128)(2,1)S(1)}, u32[]{:S(2)}, u32[]{:S(2)}) %collective-permute-start.22) | collective-permute-done | bytes 393248 | tf_op jit(solution)/shard_map/ppermute | solution.py:268
  72.4 0.9 %shard_map.143 = bf16[384,512]{1,0:T(8,128)(2,1)} custom-call(s32[1]{0:T(128)} %bitcast.spot_ref.refs_0_, f32[384,512]{1,0:T(8,128)S(1)} %shard_map.142.refs_0_, bf16[384,512]{1,0:T(8,128)(2,1)S(1)} %collective-permute-done.19.refs_1_, bf16[384,512]{1,0:T(8,128)(2,1)S(1)} %collective-permute-done.22.refs_2_), custom_call_target="tpu_custom_call" | custom-call | flops 10000000000 | tf_op jit(solution)/shard_map/pallas_call | solution.py:16
  (45 shorter events, 5.3 us)
Async XLA Ops:
  0.6 8.8 %collective-permute-start = (bf16[8,7,128,128]{3,2,1,0:T(8,128)(2,1)}, bf16[8,7,128,128]{3,2,1,0:T(8,128)(2,1)S(1)}, u32[]{:S(2)}, u32[]{:S(2)}) collective-permute-start(bf16[8,7,128,128]{3,2,1,0:T(8,128)(2,1)} %bitcast.7), channel_id=1, source_target_pairs={{0,1},{1,0},{2,3},{3,2},{4,5},{5,4},{6,7},{7,6},{8,9},{9,8},{10,11... | collective-permute-start | bytes 5505032 | tf_op jit(solution)/shard_map/ppermute | solution.py:318
  0.7 23.5 %collective-permute-start.2 = (bf16[384,512]{1,0:T(8,128)(2,1)}, bf16[384,512]{1,0:T(8,128)(2,1)S(1)}, u32[]{:S(2)}, u32[]{:S(2)}) collective-permute-start(bf16[384,512]{1,0:T(8,128)(2,1)} %refs_2_.1), channel_id=1, source_target_pairs={{0,4},{1,5},{2,6},{3,7},{4,8},{5,9},{6,10},{7,11},{8,12},{9,13},{1... | collective-permute-start | bytes 1179656 | tf_op jit(solution)/shard_map/ppermute | solution.py:221
  2.3 21.9 %collective-permute-start.3 = (bf16[384,512]{1,0:T(8,128)(2,1)}, bf16[384,512]{1,0:T(8,128)(2,1)S(1)}, u32[]{:S(2)}, u32[]{:S(2)}) collective-permute-start(bf16[384,512]{1,0:T(8,128)(2,1)} %refs_2_.1), channel_id=1, source_target_pairs={{0,2},{1,3},{2,4},{3,5},{4,6},{5,7},{6,8},{7,9},{8,10},{9,11},{10,... | collective-permute-start | bytes 1179656 | tf_op jit(solution)/shard_map/ppermute | solution.py:221
  3.8 20.5 %collective-permute-start.4 = (bf16[384,512]{1,0:T(8,128)(2,1)}, bf16[384,512]{1,0:T(8,128)(2,1)S(1)}, u32[]{:S(2)}, u32[]{:S(2)}) collective-permute-start(bf16[384,512]{1,0:T(8,128)(2,1)} %refs_2_.1), channel_id=1, source_target_pairs={{0,30},{1,31},{2,0},{3,1},{4,2},{5,3},{6,4},{7,5},{8,6},{9,7},{10,... | collective-permute-start | bytes 1179656 | tf_op jit(solution)/shard_map/ppermute | solution.py:221
  4.3 23.6 %collective-permute-start.5 = (bf16[384,512]{1,0:T(8,128)(2,1)}, bf16[384,512]{1,0:T(8,128)(2,1)S(1)}, u32[]{:S(2)}, u32[]{:S(2)}) collective-permute-start(bf16[384,512]{1,0:T(8,128)(2,1)} %refs_2_.1), channel_id=1, source_target_pairs={{0,28},{2,30},{4,0},{6,2},{8,4},{10,6},{12,8},{14,10},{16,12},{18,... | collective-permute-start | bytes 1179656 | tf_op jit(solution)/shard_map/ppermute | solution.py:221
  11.0 1.1 %collective-permute-start.1 = (s32[120]{0:T(128)S(1)}, s32[120]{0:T(128)S(1)}, u32[]{:S(2)}, u32[]{:S(2)}) collective-permute-start(s32[120]{0:T(128)S(1)} %reshape.30.own_meta_ref), channel_id=1, source_target_pairs={{0,1},{1,0},{2,3},{3,2},{4,5},{5,4},{6,7},{7,6},{8,9},{9,8},{10,11... | collective-permute-start | bytes 1448 | tf_op jit(solution)/shard_map/ppermute | solution.py:318
  12.1 1.5 %copy-start = (bf16[1,8,7,128,128]{4,3,2,1,0:T(8,128)(2,1)S(1)}, bf16[1,8,7,128,128]{4,3,2,1,0:T(8,128)(2,1)}, u32[]{:S(2)}) copy-start(bf16[1,8,7,128,128]{4,3,2,1,0:T(8,128)(2,1)} %param.13) | copy-start | bytes 5505028
  13.6 10.6 %copy-start.2 = (bf16[384,512]{1,0:T(8,128)(2,1)S(1)}, bf16[384,512]{1,0:T(8,128)(2,1)}, u32[]{:S(2)}) copy-start(bf16[384,512]{1,0:T(8,128)(2,1)} %refs_2_.1) | copy-start | bytes 1179652
  26.0 4.6 %copy-start.1 = (bf16[512,512]{1,0:T(8,128)(2,1)S(1)}, bf16[512,512]{1,0:T(8,128)(2,1)}, u32[]{:S(2)}) copy-start(bf16[512,512]{1,0:T(8,128)(2,1)} %weight_ref.1) | copy-start | bytes 1572868
  26.0 4.6 %copy-start.3 = (bf16[384,512]{1,0:T(8,128)(2,1)S(1)}, bf16[384,512]{1,0:T(8,128)(2,1)}, u32[]{:S(2)}) copy-start(bf16[384,512]{1,0:T(8,128)(2,1)} %grad_out_ref.1) | copy-start | bytes 1179652
  26.0 4.6 %copy-start.4 = (f32[512]{0:T(512)S(1)}, f32[512]{0:T(512)}, u32[]{:S(2)}) copy-start(f32[512]{0:T(512)} %param.15) | copy-start | bytes 6148
  28.3 2.4 %collective-permute-start.6 = (f32[384,512]{1,0:T(8,128)S(1)}, f32[384,512]{1,0:T(8,128)S(1)}, u32[]{:S(2)}, u32[]{:S(2)}) collective-permute-start(f32[384,512]{1,0:T(8,128)S(1)} %shard_map.131), channel_id=1, source_target_pairs={{0,1},{1,0},{2,3},{3,2},{4,5},{5,4},{6,7},{7,6},{8,9},{9,8},{10,11... | collective-permute-start | bytes 2359304 | tf_op jit(solution)/shard_map/ppermute | solution.py:318
  30.6 7.2 %copy-start.5 = (s32[40]{0:T(128)S(1)}, s32[40]{0:T(128)}, u32[]{:S(2)}) copy-start(s32[40]{0:T(128)} %constant.23.refs_1_) | copy-start | bytes 484
  32.0 5.8 %collective-permute-start.11 = (bf16[384,512]{1,0:T(8,128)(2,1)S(1)}, bf16[384,512]{1,0:T(8,128)(2,1)S(1)}, u32[]{:S(2)}, u32[]{:S(2)}) collective-permute-start(bf16[384,512]{1,0:T(8,128)(2,1)S(1)} %get-tuple-element.50.refs_3_), channel_id=1, source_target_pairs={{0,1},{1,0},{2,3},{3,2},{4,5},{5,4},{6,7},{7,6},{8,9},{9,8},{10,11... | collective-permute-start | bytes 1179656 | tf_op jit(solution)/shard_map/ppermute | solution.py:318
  32.2 2.1 %collective-permute-start.7 = (bf16[4,80,512]{2,1,0:T(8,128)(2,1)S(1)}, bf16[4,80,512]{2,1,0:T(8,128)(2,1)S(1)}, u32[]{:S(2)}, u32[]{:S(2)}) collective-permute-start(bf16[4,80,512]{2,1,0:T(8,128)(2,1)S(1)} %get-tuple-element.44), channel_id=1, source_target_pairs={{0,1},{1,0},{2,3},{3,2},{4,5},{5,4},{6,7},{7,6},{8,9},{9,8},{10,11... | collective-permute-start | bytes 983048 | tf_op jit(solution)/shard_map/ppermute | solution.py:318
  34.3 6.3 %collective-permute-start.10 = (bf16[80,512]{1,0:T(8,128)(2,1)S(1)}, bf16[80,512]{1,0:T(8,128)(2,1)S(1)}, u32[]{:S(2)}, u32[]{:S(2)}) collective-permute-start(bf16[80,512]{1,0:T(8,128)(2,1)S(1)} %get-tuple-element.48), channel_id=1, source_target_pairs={{0,6},{1,7},{2,4},{3,5},{4,2},{5,3},{6,0},{7,1},{8,14},{9,15},{10,... | collective-permute-start | bytes 245768 | tf_op jit(solution)/shard_map/ppermute | solution.py:318
  34.9 5.7 %collective-permute-start.8 = (bf16[80,512]{1,0:T(8,128)(2,1)S(1)}, bf16[80,512]{1,0:T(8,128)(2,1)S(1)}, u32[]{:S(2)}, u32[]{:S(2)}) collective-permute-start(bf16[80,512]{1,0:T(8,128)(2,1)S(1)} %get-tuple-element.46), channel_id=1, source_target_pairs={{0,2},{1,3},{2,0},{3,1},{4,6},{5,7},{6,4},{7,5},{8,10},{9,11},{10,... | collective-permute-start | bytes 245768 | tf_op jit(solution)/shard_map/ppermute | solution.py:318
  36.4 5.1 %collective-permute-start.9 = (bf16[80,512]{1,0:T(8,128)(2,1)S(1)}, bf16[80,512]{1,0:T(8,128)(2,1)S(1)}, u32[]{:S(2)}, u32[]{:S(2)}) collective-permute-start(bf16[80,512]{1,0:T(8,128)(2,1)S(1)} %get-tuple-element.47), channel_id=1, source_target_pairs={{0,4},{1,5},{2,6},{3,7},{4,0},{5,1},{6,2},{7,3},{8,12},{9,13},{10,... | collective-permute-start | bytes 245768 | tf_op jit(solution)/shard_map/ppermute | solution.py:318
  39.8 7.8 %collective-permute-start.15 = (bf16[384,512]{1,0:T(8,128)(2,1)S(1)}, bf16[384,512]{1,0:T(8,128)(2,1)S(1)}, u32[]{:S(2)}, u32[]{:S(2)}) collective-permute-start(bf16[384,512]{1,0:T(8,128)(2,1)S(1)} %get-tuple-element.52), channel_id=1, source_target_pairs={{0,2},{1,5},{2,0},{3,7},{4,6},{5,1},{6,4},{7,3},{8,10},{9,13},{10,... | collective-permute-start | bytes 1179656 | tf_op jit(solution)/shard_map/ppermute | solution.py:268
  41.5 12.0 %collective-permute-start.12 = (bf16[80,512]{1,0:T(8,128)(2,1)S(1)}, bf16[80,512]{1,0:T(8,128)(2,1)S(1)}, u32[]{:S(2)}, u32[]{:S(2)}) collective-permute-start(bf16[80,512]{1,0:T(8,128)(2,1)S(1)} %shard_map.135.refs_0_), channel_id=1, source_target_pairs={{0,8},{1,9},{2,10},{3,11},{4,12},{5,13},{6,14},{7,15},{8,0},{9,1},... | collective-permute-start | bytes 245768 | tf_op jit(solution)/shard_map/ppermute | solution.py:318
  42.8 10.7 %collective-permute-start.13 = (bf16[80,512]{1,0:T(8,128)(2,1)S(1)}, bf16[80,512]{1,0:T(8,128)(2,1)S(1)}, u32[]{:S(2)}, u32[]{:S(2)}) collective-permute-start(bf16[80,512]{1,0:T(8,128)(2,1)S(1)} %shard_map.135.refs_0_), channel_id=1, source_target_pairs={{0,16},{1,17},{2,18},{3,19},{4,20},{5,21},{6,22},{7,23},{8,24},{9,... | collective-permute-start | bytes 245768 | tf_op jit(solution)/shard_map/ppermute | solution.py:318
  45.4 8.2 %collective-permute-start.14 = (bf16[80,512]{1,0:T(8,128)(2,1)S(1)}, bf16[80,512]{1,0:T(8,128)(2,1)S(1)}, u32[]{:S(2)}, u32[]{:S(2)}) collective-permute-start(bf16[80,512]{1,0:T(8,128)(2,1)S(1)} %shard_map.135.refs_0_), channel_id=1, source_target_pairs={{0,24},{1,25},{2,26},{3,27},{4,28},{5,29},{6,30},{7,31},{8,16},{9,... | collective-permute-start | bytes 245768 | tf_op jit(solution)/shard_map/ppermute | solution.py:318
  47.7 16.7 %collective-permute-start.20 = (bf16[384,512]{1,0:T(8,128)(2,1)S(1)}, bf16[384,512]{1,0:T(8,128)(2,1)S(1)}, u32[]{:S(2)}, u32[]{:S(2)}) collective-permute-start(bf16[384,512]{1,0:T(8,128)(2,1)S(1)} %shard_map.136), channel_id=1, source_target_pairs={{0,24},{2,26},{3,11},{4,12},{5,29},{6,14},{8,0},{10,2},{11,19},{12... | collective-permute-start | bytes 1179656 | tf_op jit(solution)/shard_map/ppermute | solution.py:268
  51.8 8.6 %collective-permute-start.19 = (bf16[384,512]{1,0:T(8,128)(2,1)S(1)}, bf16[384,512]{1,0:T(8,128)(2,1)S(1)}, u32[]{:S(2)}, u32[]{:S(2)}) collective-permute-start(bf16[384,512]{1,0:T(8,128)(2,1)S(1)} %get-tuple-element.64), channel_id=1, source_target_pairs={{0,2},{1,29},{2,0},{3,31},{4,6},{5,1},{6,4},{7,3},{8,10},{9,5},{10... | collective-permute-start | bytes 1179656 | tf_op jit(solution)/shard_map/ppermute | solution.py:268
  54.2 10.5 %collective-permute-start.16 = (bf16[64,512]{1,0:T(8,128)(2,1)S(1)}, bf16[64,512]{1,0:T(8,128)(2,1)S(1)}, u32[]{:S(2)}, u32[]{:S(2)}) collective-permute-start(bf16[64,512]{1,0:T(8,128)(2,1)S(1)} %get-tuple-element.63.refs_0_), channel_id=1, source_target_pairs={{0,2},{1,3},{2,0},{3,1},{4,6},{5,7},{6,4},{7,5},{8,10},{9,11},{10,... | collective-permute-start | bytes 196616 | tf_op jit(solution)/shard_map/ppermute | solution.py:318
  55.6 9.1 %collective-permute-start.17 = (bf16[64,512]{1,0:T(8,128)(2,1)S(1)}, bf16[64,512]{1,0:T(8,128)(2,1)S(1)}, u32[]{:S(2)}, u32[]{:S(2)}) collective-permute-start(bf16[64,512]{1,0:T(8,128)(2,1)S(1)} %get-tuple-element.63.refs_0_), channel_id=1, source_target_pairs={{0,4},{1,5},{2,6},{3,7},{4,0},{5,1},{6,2},{7,3},{8,12},{9,13},{10,... | collective-permute-start | bytes 196616 | tf_op jit(solution)/shard_map/ppermute | solution.py:318
  55.6 9.1 %collective-permute-start.18 = (bf16[64,512]{1,0:T(8,128)(2,1)S(1)}, bf16[64,512]{1,0:T(8,128)(2,1)S(1)}, u32[]{:S(2)}, u32[]{:S(2)}) collective-permute-start(bf16[64,512]{1,0:T(8,128)(2,1)S(1)} %get-tuple-element.63.refs_0_), channel_id=1, source_target_pairs={{0,6},{1,7},{2,4},{3,5},{4,2},{5,3},{6,0},{7,1},{8,14},{9,15},{10,... | collective-permute-start | bytes 196616 | tf_op jit(solution)/shard_map/ppermute | solution.py:318
  64.6 7.8 %collective-permute-start.22 = (bf16[384,512]{1,0:T(8,128)(2,1)S(1)}, bf16[384,512]{1,0:T(8,128)(2,1)S(1)}, u32[]{:S(2)}, u32[]{:S(2)}) collective-permute-start(bf16[384,512]{1,0:T(8,128)(2,1)S(1)} %shard_map.139), channel_id=1, source_target_pairs={{0,4},{1,3},{2,6},{3,1},{4,0},{5,7},{6,2},{7,5},{8,12},{9,11},{10,... | collective-permute-start | bytes 1179656 | tf_op jit(solution)/shard_map/ppermute | solution.py:268
  64.7 1.6 %collective-permute-start.21 = (bf16[256,512]{1,0:T(8,128)(2,1)S(1)}, bf16[256,512]{1,0:T(8,128)(2,1)S(1)}, u32[]{:S(2)}, u32[]{:S(2)}) collective-permute-start(bf16[256,512]{1,0:T(8,128)(2,1)S(1)} %shard_map.140.mine_ref), channel_id=1, source_target_pairs={{0,1},{1,0},{2,3},{3,2},{4,5},{5,4},{6,7},{7,6},{8,9},{9,8},{10,11... | collective-permute-start | bytes 786440 | tf_op jit(solution)/shard_map/ppermute | solution.py:318
